TPU v7x, 32 devices: a whole 2x2x4 slice. The times are simulated.
32 devices in a mesh: tp: 2 (over x), ep: 16 (over z, y, core).
Axes of the slice: x: 2, y: 2, z: 4, core: 2. Of those that a mesh axis runs over, the one named last changes fastest.
Arguments:
- hidden_in: bfloat16 [256, 4096], P(('ep', 'tp')), may hold values from -6 to 6
- norm_gain: bfloat16 [4096], replicated, may hold values from 0.099609375 to 1.8984375
- expert_ids: int32 [256, 8], P('ep'), may hold values from 0 to 63, all different within a row; in each aligned block of 16 rows (0 to 15, 16 to 31, ...) at most 4 rows name the same one
- gate_weights: float32 [256, 8], P('ep'), may hold values from 0.05 to 0.35
- w_gate: bfloat16 [64, 4096, 1024], P('ep', None, 'tp'), may hold values from -0.09375 to 0.09375
- w_up: bfloat16 [64, 4096, 1024], P('ep', None, 'tp'), may hold values from -0.09375 to 0.09375
- w_down: bfloat16 [64, 1024, 4096], P('ep', None, 'tp'), may hold values from -0.1875 to 0.1875
Outputs:
- mixed: bfloat16 [256, 4096], P('ep', 'tp')
Inputs may be any that keep to these rules, and one draw needn't show every extreme that they name: `expert_ids`: each row names 8 different experts. Tokens form groups of 16 consecutive rows; within one group no expert is named by more than 4 rows, and in every draw some expert is named by exactly 4 rows of some group.
All inputs are finite; a program needn't handle non-finite values.
Results may differ from a plain program's by a relative error of at most 0.0043.
Values may be sent and summed in bfloat16 or wider, within the bound.
No kernel may reach another device: no remote copies, remote signals or barrier semaphores. Data moves between devices by JAX's collectives and lax.ppermute only.
A program may use at most 128 MiB of HBM per device.

v0:
```python
import jax
import jax.numpy as jnp
from jax import lax
from jax.sharding import PartitionSpec as P


def shards(hidden_in, norm_gain, expert_ids, gate_weights, w_gate, w_up, w_down):
    n_ep = lax.axis_size("ep")
    tp_pos = lax.axis_index("tp")
    tok_dev, width = hidden_in.shape
    group, top = expert_ids.shape
    exp_loc, _, hid_part = w_gate.shape
    col_part = w_down.shape[2]
    experts = exp_loc * n_ep
    cap = max(2, 2 * top * group // experts)
    values = hidden_in.astype(jnp.float32)
    scale = lax.rsqrt(jnp.mean(values * values, axis=1, keepdims=True) + 1e-06)
    normed = (values * scale * norm_gain.astype(jnp.float32)).astype(jnp.bfloat16)
    flat_ids = expert_ids.reshape(-1)
    pairs = flat_ids.shape[0]
    hits = (flat_ids[:, None] == lax.broadcasted_iota(jnp.int32, (pairs, experts), 1)).astype(
        jnp.int32
    )
    before = jnp.cumsum(hits, axis=0) - hits
    position = jnp.sum(before * hits, axis=1)
    slot_index = flat_ids * cap + position
    places = lax.broadcasted_iota(jnp.int32, (experts * cap, group, top), 0)
    dispatch_map = jnp.any(places == slot_index.reshape(group, top)[None], axis=2).astype(
        jnp.bfloat16
    )
    whole_norm, whole_input = (
        lax.all_gather(normed, "tp", axis=0, tiled=True),
        lax.all_gather(hidden_in, "tp", axis=0, tiled=True),
    )
    residual = lax.dynamic_slice_in_dim(whole_input, tp_pos * col_part, col_part, 1)
    packed = jnp.dot(dispatch_map, whole_norm, preferred_element_type=jnp.float32).astype(
        jnp.bfloat16
    )
    packed = packed.reshape(n_ep, exp_loc, cap, width)
    arrived = lax.all_to_all(packed, "ep", split_axis=0, concat_axis=0, tiled=True)
    gate_act = jnp.einsum("secd,edh->sech", arrived, w_gate, preferred_element_type=jnp.float32)
    up_act = jnp.einsum("secd,edh->sech", arrived, w_up, preferred_element_type=jnp.float32)
    hidden = (jax.nn.silu(gate_act) * up_act).astype(jnp.bfloat16)
    outputs = jnp.einsum(
        "sech,ehf->secf",
        lax.all_gather(hidden, "tp", axis=3, tiled=True),
        w_down,
        preferred_element_type=jnp.float32,
    )
    returned = lax.all_to_all(
        outputs.astype(jnp.bfloat16), "ep", split_axis=0, concat_axis=0, tiled=True
    )
    flat_back = returned.reshape(experts * cap, col_part)
    picked = flat_back[slot_index].reshape(group, top, col_part).astype(jnp.float32)
    combined = jnp.sum(picked * gate_weights[:, :, None], axis=1)
    return (residual.astype(jnp.float32) + combined).astype(jnp.bfloat16)


def solution(mesh):
    in_specs = (
        P(("ep", "tp"), None),
        P(),
        P("ep", None),
        P("ep", None),
        P("ep", None, "tp"),
        P("ep", None, "tp"),
        P("ep", None, "tp"),
    )
    out_specs = P("ep", "tp")
    return jax.shard_map(shards, mesh=mesh, in_specs=in_specs, out_specs=out_specs, check_vma=False)
```

profile of v0, /device:TPU:0, one launch (start us, length us, event | category | flops | bytes accessed | tf_op | source)
XLA Modules:
  0.0 129.6 jit_solution(5807486364761746593)
XLA Ops:
  0.0 0.8 copy.23
  0.8 0.1 eq.18
  0.8 0.1 fusion.39
  0.9 0.2 reduce_window_sum.11
  1.1 0.2 select_reduce_fusion
  1.3 0.1 reduce_sum.32
  1.4 0.1 fusion.38
  1.5 0.7 convert_element_type.40
  2.2 1.0 fusion.35
  3.2 0.9 fusion.37
  4.2 5.8 %all_gather.10 = bf16[16,4096]{1,0:T(8,128)(2,1)S(1)} all-gather(bf16[8,4096]{1,0:T(8,128)(2,1)S(1)} %fusion.37), channel_id=1, replica_groups=mesh['tp'=2,'ep'=16] {'tp'}, dimensions={0}, use_global_device_ids=true | all-gather | bytes 196608 | tf_op jit(solution)/shard_map/all_gather | solution.py:32
  10.0 0.7 convolution_convert_fusion
  10.7 2.2 %reshape.55 = bf16[16,4,4,4096]{3,2,1,0:T(4,128)(2,1)} reshape(bf16[256,4096]{1,0:T(8,128)(2,1)S(1)} %convolution_convert_fusion) | data formatting | bytes 4194304 | tf_op jit(solution)/shard_map/reshape | solution.py:39
  13.0 53.8 %all_to_all.10 = bf16[16,4,4,4096]{3,2,1,0:T(4,128)(2,1)S(1)} all-to-all(bf16[16,4,4,4096]{3,2,1,0:T(4,128)(2,1)} %reshape.55), channel_id=1, replica_groups=mesh['tp'=2,'ep'=16] {'ep'}, dimensions={0} | all-to-all | bytes 4194304 | tf_op jit(solution)/shard_map/all_to_all | solution.py:40
  66.8 0.0 slice-start
  66.8 0.0 slice-start.1
  66.8 9.1 %fusion.14 = f32[16,4,4,512]{3,0,2,1:T(8,128)S(1)} fusion(bf16[4,4096,512]{2,1,0:T(8,128)(2,1)} %param.11, bf16[16,4,4,4096]{3,2,1,0:T(4,128)(2,1)S(1)} %all_to_all.10), kind=kOutput, calls=%fused_computation.12 | convolution fusion | flops 1073741824 | bytes 19398656 | tf_op jit(solution)/shard_map/secd,edh->sech/dot_general | solution.py:41
  75.9 0.0 slice-start.2
  75.9 0.0 slice-start.3
  75.9 9.2 %fusion.29 = bf16[16,4,4,512]{3,0,2,1:T(8,128)(2,1)S(1)} fusion(bf16[4,4096,512]{2,1,0:T(8,128)(2,1)} %param.12, bf16[16,4,4,4096]{3,2,1,0:T(4,128)(2,1)S(1)} %all_to_all.10, f32[16,4,4,512]{3,0,2,1:T(8,128)S(1)} %fusion.14), kind=kOutput, calls=%fused_computation.15 | convolution fusion | flops 1074528256 | bytes 19660800 | tf_op jit(solution)/shard_map/secd,edh->sech/dot_general | solution.py:42
  85.1 9.7 %all_gather.11 = bf16[16,4,4,1024]{3,0,2,1:T(8,128)(2,1)S(1)} all-gather(bf16[16,4,4,512]{3,0,2,1:T(8,128)(2,1)S(1)} %fusion.29), channel_id=1, replica_groups=mesh['tp'=2,'ep'=16] {'tp'}, dimensions={3}, use_global_device_ids=true | all-gather | bytes 786432 | tf_op jit(solution)/shard_map/all_gather | solution.py:46
  94.8 0.0 slice-done
  94.8 0.0 slice-done.1
  94.8 0.0 slice-done.2
  94.8 0.0 slice-done.3
  94.8 3.0 %fusion.9 = bf16[16,4,4,2048]{3,0,2,1:T(8,128)(2,1)S(1)} fusion(bf16[16,4,4,1024]{3,0,2,1:T(8,128)(2,1)S(1)} %all_gather.11, bf16[4,1024,2048]{2,1,0:T(8,128)(2,1)S(1)} %bitcast.50), kind=kOutput, calls=%fused_computation.9 | convolution fusion | flops 1074266112 | bytes 18350080 | tf_op jit(solution)/shard_map/sech,ehf->secf/dot_general | solution.py:44
  97.9 0.0 copy-start.1
  97.9 0.0 copy-start
  97.9 1.8 %copy.27 = bf16[16,4,4,2048]{3,2,1,0:T(4,128)(2,1)} copy(bf16[16,4,4,2048]{3,0,2,1:T(8,128)(2,1)S(1)} %fusion.9) | data formatting | bytes 2097152 | tf_op jit(solution)/shard_map/convert_element_type | solution.py:51
  99.7 4.6 %all-to-all-start.1 = ((bf16[16,4,4,2048]{3,2,1,0:T(4,128)(2,1)}), bf16[16,4,4,2048]{3,2,1,0:T(4,128)(2,1)S(1)}, u32[]{:S(2)}, u32[]{:S(2)}) async-start(bf16[16,4,4,2048]{3,2,1,0:T(4,128)(2,1)} %copy.27), calls=%async_computation.1 | async-start | bytes 2097152 | tf_op jit(solution)/shard_map/all_to_all | solution.py:50
  104.3 0.1 mul.69
  104.4 0.0 copy-done.1
  104.4 0.1 copy.28
  104.5 0.0 copy-done
  104.5 5.1 %all_gather.9 = bf16[16,4096]{1,0:T(8,128)(2,1)S(1)} all-gather(bf16[8,4096]{1,0:T(8,128)(2,1)S(1)} %copy-done), channel_id=1, replica_groups=mesh['tp'=2,'ep'=16] {'tp'}, dimensions={0}, use_global_device_ids=true | all-gather | bytes 196608 | tf_op jit(solution)/shard_map/all_gather | solution.py:33
  109.6 17.7 %all-to-all-done.1 = bf16[16,4,4,2048]{3,2,1,0:T(4,128)(2,1)S(1)} async-done(((bf16[16,4,4,2048]{3,2,1,0:T(4,128)(2,1)}), bf16[16,4,4,2048]{3,2,1,0:T(4,128)(2,1)S(1)}, u32[]{:S(2)}, u32[]{:S(2)}) %all-to-all-start.1) | async-done | bytes 1048608 | tf_op jit(solution)/shard_map/all_to_all | solution.py:50
  127.3 0.3 reshape.56
  127.5 0.9 gather_fusion
  128.5 0.4 fusion.34
  128.9 0.7 add_convert_fusion
  (5 shorter events, 0.0 us)
Async XLA Ops:
  66.8 28.0 %slice-start = ((s8[16777216]{0:T(1024)(128)(4,1)}), s8[4194304]{0:T(1024)(128)(4,1)S(1)}, s32[]{:S(2)}) async-start(s8[16777216]{0:T(1024)(128)(4,1)} %bitcast.49), calls=%async_computation.2 | async-start | bytes 8388608
  66.8 28.0 %slice-start.1 = ((s8[16777216]{0:T(1024)(128)(4,1)}), s8[4194304]{0:T(1024)(128)(4,1)S(1)}, s32[]{:S(2)}) async-start(s8[16777216]{0:T(1024)(128)(4,1)} %bitcast.49), calls=%async_computation.3 | async-start | bytes 8388608
  75.9 18.9 %slice-start.2 = ((s8[16777216]{0:T(1024)(128)(4,1)}), s8[4194304]{0:T(1024)(128)(4,1)S(1)}, s32[]{:S(2)}) async-start(s8[16777216]{0:T(1024)(128)(4,1)} %bitcast.49), calls=%async_computation.4 | async-start | bytes 8388608
  75.9 18.9 %slice-start.3 = ((s8[16777216]{0:T(1024)(128)(4,1)}), s8[4194304]{0:T(1024)(128)(4,1)S(1)}, s32[]{:S(2)}) async-start(s8[16777216]{0:T(1024)(128)(4,1)} %bitcast.49), calls=%async_computation.5 | async-start | bytes 8388608
  97.9 6.6 %copy-start.1 = (f32[16,8]{0,1:T(8,128)S(1)}, f32[16,8]{0,1:T(8,128)}, u32[]{:S(2)}) copy-start(f32[16,8]{0,1:T(8,128)} %param.10) | copy-start | bytes 1540
  97.9 6.6 %copy-start = (bf16[8,4096]{1,0:T(8,128)(2,1)S(1)}, bf16[8,4096]{1,0:T(8,128)(2,1)}, u32[]{:S(2)}) copy-start(bf16[8,4096]{1,0:T(8,128)(2,1)} %param.7) | copy-start | bytes 196612
  99.7 27.6 %all-to-all-start.1 = ((bf16[16,4,4,2048]{3,2,1,0:T(4,128)(2,1)}), bf16[16,4,4,2048]{3,2,1,0:T(4,128)(2,1)S(1)}, u32[]{:S(2)}, u32[]{:S(2)}) async-start(bf16[16,4,4,2048]{3,2,1,0:T(4,128)(2,1)} %copy.27), calls=%async_computation.1 | async-start | bytes 2097152 | tf_op jit(solution)/shard_map/all_to_all | solution.py:50
where the time goes:
time: 131 us; the launch traced here: 130 us
  blocking collectives  74.4 us (57%)
  matrix products  22.1 us (17%)
  waiting for transfers between devices  17.7 us (14%)
  local copies, waits for them, and re-layouts  6.34 us (5%)
  starting transfers between devices  4.63 us (4%)
  other arithmetic  4.31 us (3%)
    all_to_all x1, blocking collectives, shards(): lax.all_to_all(packed, 'ep', split_axis=0, concat_axis=0, tiled=True)  53.8 us
    all_to_all x1, waiting for transfers between devices, shards(): lax.all_to_all(outputs.astype(jnp.bfloat16), 'ep', split_axis=0, concat_a...  17.7 us
    all_gather x1, blocking collectives, shards(): lax.all_gather(hidden, 'tp', axis=3, tiled=True)  9.66 us
    dot_general x1, matrix products, shards(): jnp.einsum('secd,edh->sech', arrived, w_up, preferred_element_type=jnp.fl...  9.2 us
    dot_general x1, matrix products, shards(): jnp.einsum('secd,edh->sech', arrived, w_gate, preferred_element_type=jnp....  9.12 us
    all_gather x1, blocking collectives, shards(): lax.all_gather(normed, 'tp', axis=0, tiled=True)  5.84 us
    all_gather x1, blocking collectives, shards(): lax.all_gather(hidden_in, 'tp', axis=0, tiled=True)  5.1 us
    all_to_all x1, starting transfers between devices, shards(): lax.all_to_all(outputs.astype(jnp.bfloat16), 'ep', split_axis=0, concat_a...  4.63 us
  transfers between devices with their start and end apart: 1, of which 1 were waited for; matrix products, arithmetic and copies ran while one was open for 0% of the time, Pallas kernels for 0%

commit v1 on v0

v1 whole, which is shorter than its diff:
```python
import jax
import jax.numpy as jnp
from jax import lax
from jax.sharding import PartitionSpec as P


def shards(hidden_in, norm_gain, expert_ids, gate_weights, w_gate, w_up, w_down):
    n_ep = lax.axis_size("ep")
    ep_pos = lax.axis_index("ep")
    tp_pos = lax.axis_index("tp")
    tok_dev, width = hidden_in.shape
    group, top = expert_ids.shape
    exp_loc, _, hid_part = w_gate.shape
    col_part = w_down.shape[2]
    experts = exp_loc * n_ep
    cap = max(2, 2 * top * group // experts)
    rows = cap * n_ep
    tokens = group * n_ep

    whole = lax.all_gather(hidden_in, ("ep", "tp"), axis=0, tiled=True)
    routing = jnp.concatenate([expert_ids.astype(jnp.float32), gate_weights], axis=1)
    routing = lax.all_gather(routing, "ep", axis=0, tiled=True)
    ids = routing[:, :top].astype(jnp.int32)
    weights = routing[:, top:]
    local = ep_pos * exp_loc + lax.broadcasted_iota(jnp.int32, (tokens, top, exp_loc), 2)
    match = ids[:, :, None] == local
    weight_of = jnp.sum(jnp.where(match, weights[:, :, None], 0.0), axis=1)
    hit = jnp.any(match, axis=1).astype(jnp.int32)
    position = jnp.cumsum(hit, axis=0) - hit
    place = jnp.where(hit > 0, position, -1).T
    pick = (place[:, None, :] == lax.broadcasted_iota(jnp.int32, (exp_loc, rows, tokens), 1))
    select = pick.astype(jnp.bfloat16)
    picked = jnp.einsum("ert,td->erd", select, whole, preferred_element_type=jnp.float32)
    scale = lax.rsqrt(jnp.mean(picked * picked, axis=2, keepdims=True) + 1e-06)
    normed = (picked * scale * norm_gain.astype(jnp.float32)).astype(jnp.bfloat16)
    gate_act = jnp.einsum("erd,edh->erh", normed, w_gate, preferred_element_type=jnp.float32)
    up_act = jnp.einsum("erd,edh->erh", normed, w_up, preferred_element_type=jnp.float32)
    hidden = (jax.nn.silu(gate_act) * up_act).astype(jnp.bfloat16)
    hidden = lax.all_gather(hidden, "tp", axis=2, tiled=True)
    outputs = jnp.einsum("erh,ehf->erf", hidden, w_down, preferred_element_type=jnp.float32)
    outputs = outputs.astype(jnp.bfloat16)
    spread = jnp.where(pick, weight_of.T[:, None, :], 0.0)
    high = spread.astype(jnp.bfloat16)
    rest = spread - high.astype(jnp.float32)
    low = rest.astype(jnp.bfloat16)
    partial = jnp.einsum("ert,erf->tf", high, outputs, preferred_element_type=jnp.float32)
    partial = partial + jnp.einsum("ert,erf->tf", low, outputs, preferred_element_type=jnp.float32)
    combined = lax.psum_scatter(partial.astype(jnp.bfloat16), "ep", scatter_dimension=0, tiled=True)
    residual = lax.dynamic_slice(whole, (ep_pos * group, tp_pos * col_part), (group, col_part))
    return (residual.astype(jnp.float32) + combined.astype(jnp.float32)).astype(jnp.bfloat16)


def solution(mesh):
    in_specs = (
        P(("ep", "tp"), None),
        P(),
        P("ep", None),
        P("ep", None),
        P("ep", None, "tp"),
        P("ep", None, "tp"),
        P("ep", None, "tp"),
    )
    out_specs = P("ep", "tp")
    return jax.shard_map(shards, mesh=mesh, in_specs=in_specs, out_specs=out_specs, check_vma=False)
```

time: 131 us -> 170 us (1.30)
  waiting for transfers between devices: 17.7 us -> 91.8 us
  blocking collectives: 74.4 us -> 32.6 us
  between operations: 0.15 us -> 13.5 us
  local copies, waits for them, and re-layouts: 6.34 us -> 0.61 us
  starting transfers between devices: 4.63 us -> 0.04 us
  matrix products: 22.1 us -> 25.6 us
    reduce_scatter x0 -> x1, waiting for transfers between devices: none -> 56.4 us  [shards(): lax.psum_scatter(partial.astype(jnp.bfloat16), 'ep', scatter_dimension=0,...]
    all_to_all x1 -> x0, blocking collectives: 53.8 us -> none  [shards(): lax.all_to_all(packed, 'ep', split_axis=0, concat_axis=0, tiled=True)]
    all_gather x0 -> x1, waiting for transfers between devices: none -> 34.7 us  [shards(): whole = lax.all_gather(hidden_in, ('ep', 'tp'), axis=0, tiled=True)]
    all_to_all x1 -> x0, waiting for transfers between devices: 17.7 us -> none  [shards(): lax.all_to_all(outputs.astype(jnp.bfloat16), 'ep', split_axis=0, concat_a...]
    all_gather x3 -> x2, blocking collectives: 20.6 us -> 32.6 us  [the longest x1 23.4 us: shards(): routing = lax.all_gather(routing, 'ep', axis=0, tiled=True)]
    all_to_all x1 -> x0, starting transfers between devices: 4.63 us -> none  [shards(): lax.all_to_all(outputs.astype(jnp.bfloat16), 'ep', split_axis=0, concat_a...]
    dot_general x4 -> x6, matrix products: 22.1 us -> 25.6 us  [the longest x1 9.14 us: shards(): jnp.einsum('erd,edh->erh', normed, w_up, preferred_element_type=jnp.float32)]
    reshape x2 -> x1, local copies, waits for them, and re-layouts: 2.49 us -> 0.01 us  [the longest x1 2.23 us: shards(): packed = packed.reshape(n_ep, exp_loc, cap, width)]
  transfers between devices with their start and end apart: 1 -> 2, of which waited for: 1 -> 2; matrix products, arithmetic and copies ran while one was open for 0% -> 2% of each run, Pallas kernels for 0% -> 0%
where the time goes in v1:
time: 170 us; the launch traced here: 169 us
  waiting for transfers between devices  91.8 us (54%)
  blocking collectives  32.6 us (19%)
  matrix products  25.6 us (15%)
  between operations  13.5 us (8%)
  other arithmetic  5.16 us (3%)
    reduce_scatter x1, waiting for transfers between devices, shards(): lax.psum_scatter(partial.astype(jnp.bfloat16), 'ep', scatter_dimension=0,...  56.4 us
    all_gather x1, waiting for transfers between devices, shards(): whole = lax.all_gather(hidden_in, ('ep', 'tp'), axis=0, tiled=True)  34.7 us
    all_gather x1, blocking collectives, shards(): routing = lax.all_gather(routing, 'ep', axis=0, tiled=True)  23.4 us
    all_gather x1, blocking collectives, shards(): hidden = lax.all_gather(hidden, 'tp', axis=2, tiled=True)  9.14 us
    dot_general x1, matrix products, shards(): jnp.einsum('erd,edh->erh', normed, w_up, preferred_element_type=jnp.float32)  9.14 us
    dot_general x1, matrix products, shards(): jnp.einsum('erd,edh->erh', normed, w_gate, preferred_element_type=jnp.flo...  9.09 us
  transfers between devices with their start and end apart: 2, of which 2 were waited for; matrix products, arithmetic and copies ran while one was open for 2% of the time, Pallas kernels for 0%

profile of v1, /device:TPU:0, one launch (start us, length us, event | category | flops | bytes accessed | tf_op | source)
XLA Modules:
  0.0 169.3 jit_solution(9247970354422878311)
XLA Ops:
  6.5 0.0 all-gather.2.cloned.1.call-start
  6.5 0.7 all-gather.2.cloned.1.call-update
  7.3 0.0 reduce-scatter.2.cloned.1.call-start
  7.3 0.7 convert_element_type.49
  8.0 0.7 pad_maximum_fusion
  8.7 0.1 copy.22
  8.8 0.7 convert_element_type.54
  9.5 23.4 %all_gather.10 = f32[256,16]{1,0:T(8,128)S(1)} all-gather(f32[16,16]{1,0:T(8,128)S(1)} %copy.22), channel_id=1, replica_groups=mesh['tp'=2,'ep'=16] {'ep'}, dimensions={0}, use_global_device_ids=true | all-gather | bytes 17408 | tf_op jit(solution)/shard_map/all_gather | solution.py:22
  32.9 0.1 fusion.19
  33.0 0.1 copy.26
  33.1 0.1 copy.27
  33.1 0.1 compare_reduce_fusion
  33.3 1.2 reduce-window.6
  34.5 0.1 slice.17
  34.6 0.1 copy.24
  34.7 0.1 copy.25
  34.8 0.1 fusion.15
  34.9 0.1 add_bitcast_fusion
  35.0 34.7 %all-gather.2.cloned.1.call-done = bf16[256,4096]{1,0:T(8,128)(2,1)} async-done(((bf16[8,4096]{1,0:T(8,128)(2,1)}), bf16[256,4096]{1,0:T(8,128)(2,1)}) %all-gather.2.cloned.1.call-update) | async-done | bytes 2097168 | tf_op jit(solution)/shard_map/all_gather | solution.py:20
  69.6 2.4 %multiply_reduce_fusion = (f32[4,64]{1,0:T(4,128)S(1)}, f32[4,64,4096]{2,1,0:T(8,128)S(1)}) fusion(bf16[256,4096]{1,0:T(8,128)(2,1)} %all-gather.2.cloned.1.call-done, s32[4,256]{1,0:T(4,128)S(1)} %fusion.16), kind=kOutput, calls=%fused_computation.1 | convolution fusion | flops 539033344 | bytes 6296576 | tf_op jit(solution)/shard_map/ert,td->erd/dot_general | solution.py:33
  72.1 0.0 slice-start
  72.1 0.0 slice-start.1
  72.1 9.1 %fusion.5 = f32[4,64,512]{2,1,0:T(8,128)S(1)} fusion(bf16[4,4096,512]{2,1,0:T(8,128)(2,1)} %param.11, f32[4,64,4096]{2,1,0:T(8,128)S(1)} %get-tuple-element.8, f32[4096]{0:T(1024)S(1)} %convert_element_type.54, f32[4,64]{1,0:T(4,128)S(1)} %add_rsqrt_fusion), kind=kOutput, calls=%fused_computation.11 | convolution fusion | flops 1076887552 | bytes 21513216 | tf_op jit(solution)/shard_map/erd,edh->erh/dot_general | solution.py:36
  81.2 0.0 slice-start.2
  81.2 0.0 slice-start.3
  81.2 9.1 %fusion.4 = bf16[4,64,512]{2,1,0:T(8,128)(2,1)S(1)} fusion(bf16[4,4096,512]{2,1,0:T(8,128)(2,1)} %param.12, f32[4,64,4096]{2,1,0:T(8,128)S(1)} %get-tuple-element.8, f32[4096]{0:T(1024)S(1)} %convert_element_type.54, f32[4,64]{1,0:T(4,128)S(1)} %add_rsqrt_fusion, f32[4,64,512]{2,1,0:T(8,128)S(1)} %fusion.5), kind=kOutput, calls=%fused_computation.10 | convolution fusion | flops 1077673984 | bytes 21775360 | tf_op jit(solution)/shard_map/erd,edh->erh/dot_general | solution.py:37
  90.3 9.1 %all_gather.11 = bf16[4,64,1024]{2,1,0:T(8,128)(2,1)S(1)} all-gather(bf16[4,64,512]{2,1,0:T(8,128)(2,1)S(1)} %fusion.4), channel_id=1, replica_groups=mesh['tp'=2,'ep'=16] {'tp'}, dimensions={2}, use_global_device_ids=true | all-gather | bytes 786432 | tf_op jit(solution)/shard_map/all_gather | solution.py:39
  99.5 0.0 slice-done
  99.5 0.0 slice-done.1
  99.5 0.0 slice-done.2
  99.5 0.0 slice-done.3
  99.5 3.0 %convolution_convert_fusion = bf16[4,64,2048]{2,1,0:T(8,128)(2,1)S(1)} fusion(bf16[4,64,1024]{2,1,0:T(8,128)(2,1)S(1)} %all_gather.11, bf16[4,1024,2048]{2,1,0:T(8,128)(2,1)S(1)} %bitcast.32), kind=kOutput, calls=%fused_computation.6 | convolution fusion | flops 1074266112 | bytes 18350080 | tf_op jit(solution)/shard_map/erh,ehf->erf/dot_general | solution.py:40
  102.6 0.5 convolution_bitcast_fusion
  103.0 1.5 fusion.1
  104.5 0.0 reduce-scatter.2.cloned.1.call-update
  104.5 56.4 %reduce-scatter.2.cloned.1.call-done = bf16[16,2048]{1,0:T(8,128)(2,1)} async-done(((bf16[256,2048]{1,0:T(8,128)(2,1)}), bf16[16,2048]{1,0:T(8,128)(2,1)}) %reduce-scatter.2.cloned.1.call-update) | async-done | bytes 65552 | tf_op jit(solution)/shard_map/reduce_scatter | solution.py:48
  160.9 1.5 add_convert_fusion
  (9 shorter events, 0.1 us)
Async XLA Ops:
  6.5 63.1 %all-gather.2.cloned.1.call-start = ((), (), s32[]{:S(2)}) async-start(), calls=%async_computation.1 | async-start | bytes 2162688 | tf_op jit(solution)/shard_map/all_gather | solution.py:20
  7.3 153.7 %reduce-scatter.2.cloned.1.call-start = ((), (), s32[]{:S(2)}) async-start(), calls=%async_computation.2 | async-start | bytes 1114112 | tf_op jit(solution)/shard_map/reduce_scatter | solution.py:48
  72.1 27.4 %slice-start = ((s8[16777216]{0:T(1024)(128)(4,1)}), s8[4194304]{0:T(1024)(128)(4,1)S(1)}, s32[]{:S(2)}) async-start(s8[16777216]{0:T(1024)(128)(4,1)} %bitcast.31), calls=%async_computation.3 | async-start | bytes 8388608
  72.1 27.4 %slice-start.1 = ((s8[16777216]{0:T(1024)(128)(4,1)}), s8[4194304]{0:T(1024)(128)(4,1)S(1)}, s32[]{:S(2)}) async-start(s8[16777216]{0:T(1024)(128)(4,1)} %bitcast.31), calls=%async_computation.4 | async-start | bytes 8388608
  81.2 18.3 %slice-start.2 = ((s8[16777216]{0:T(1024)(128)(4,1)}), s8[4194304]{0:T(1024)(128)(4,1)S(1)}, s32[]{:S(2)}) async-start(s8[16777216]{0:T(1024)(128)(4,1)} %bitcast.31), calls=%async_computation.5 | async-start | bytes 8388608
  81.2 18.3 %slice-start.3 = ((s8[16777216]{0:T(1024)(128)(4,1)}), s8[4194304]{0:T(1024)(128)(4,1)S(1)}, s32[]{:S(2)}) async-start(s8[16777216]{0:T(1024)(128)(4,1)} %bitcast.31), calls=%async_computation.6 | async-start | bytes 8388608
Sparse Core Ops, SparseCore 0:
  10.3 59.2 all-gather.1
  104.6 56.2 reduce-scatter.1

commit v2 on v0

--- a/solution.py
+++ b/solution.py
@@ -3,8 +3,42 @@
 from jax import lax
 from jax.sharding import PartitionSpec as P
 
-
-def shards(hidden_in, norm_gain, expert_ids, gate_weights, w_gate, w_up, w_down):
+LANES = 128
+
+
+def factors_of(n):
+    digits, stride = [], 1
+    for _ in range(2):
+        if n % 2 == 0 and n > 1:
+            digits.append((stride, 2))
+            stride, n = stride * 2, n // 2
+    while n > 1:
+        radix = next(r for r in (4, 3, 2, n) if n % r == 0)
+        digits.append((stride, radix))
+        stride, n = stride * radix, n // radix
+    return digits
+
+
+def shifted(x, axis, size, stride, radix, by):
+    pairs = []
+    for i in range(size):
+        digit = i // stride % radix
+        pairs.append((i, i + ((digit + by) % radix - digit) * stride))
+    return lax.ppermute(x, axis, pairs)
+
+
+def gathered(x, axis, size, stride, radix):
+    return jnp.stack([x] + [shifted(x, axis, size, stride, radix, s) for s in range(1, radix)])
+
+
+def scattered(x, axis, size, stride, radix):
+    total = x[0].astype(jnp.float32)
+    for s in range(1, radix):
+        total = total + shifted(x[s], axis, size, stride, radix, radix - s).astype(jnp.float32)
+    return total.astype(x.dtype)
+
+
+def by_slots(hidden_in, norm_gain, expert_ids, gate_weights, w_gate, w_up, w_down):
     n_ep = lax.axis_size("ep")
     tp_pos = lax.axis_index("tp")
     tok_dev, width = hidden_in.shape
@@ -56,6 +90,124 @@
     return (residual.astype(jnp.float32) + combined).astype(jnp.bfloat16)
 
 
+def by_tokens(hidden_in, norm_gain, expert_ids, gate_weights, w_gate, w_up, w_down):
+    n_ep = lax.axis_size("ep")
+    n_tp = lax.axis_size("tp")
+    ep_pos = lax.axis_index("ep")
+    tp_pos = lax.axis_index("tp")
+    tok_dev, width = hidden_in.shape
+    group, top = expert_ids.shape
+    exp_loc, _, hid_part = w_gate.shape
+    col_part = w_down.shape[2]
+    experts = exp_loc * n_ep
+    cap = max(2, 2 * top * group // experts)
+    rows = cap * n_ep
+    tokens = group * n_ep
+    digits = factors_of(n_ep)
+    fast, mid, slow = digits[0], digits[1:2], digits[2:]
+    half = width // 2
+
+    mine = lambda a: lax.dynamic_slice_in_dim(a, tp_pos * tok_dev, tok_dev, 0)
+    w_own = mine(gate_weights)
+    w_hi = w_own.astype(jnp.bfloat16)
+    w_rest = w_own - w_hi.astype(jnp.float32)
+    w_mid = w_rest.astype(jnp.bfloat16)
+    w_lo = (w_rest - w_mid.astype(jnp.float32)).astype(jnp.bfloat16)
+    blank = jnp.zeros((tok_dev, LANES - 4 * top), jnp.bfloat16)
+    routing = [mine(expert_ids).astype(jnp.bfloat16), w_hi, w_mid, w_lo, blank]
+
+    first = jnp.concatenate([hidden_in[:, :half]] + routing, axis=1)
+    second = hidden_in[:, half:]
+    for digit in reversed(slow):
+        first = gathered(first, "ep", n_ep, *digit)
+        second = gathered(second, "ep", n_ep, *digit)
+    lead = [radix for _, radix in reversed(slow)]
+    count = len(lead)
+    along_tp = lambda a: gathered(a, "tp", n_tp, 1, n_tp)
+    for digit in mid:
+        first = gathered(first, "ep", n_ep, *digit)
+    first = along_tp(first)
+    second = along_tp(second)
+    for digit in mid:
+        second = gathered(second, "ep", n_ep, *digit)
+    first = gathered(first, "ep", n_ep, *fast)
+    second = gathered(second, "ep", n_ep, *fast)
+    mids = [radix for _, radix in mid]
+    slow_n = 1
+    for r in lead:
+        slow_n *= r
+    mid_n = mids[0] if mids else 1
+    first = first.reshape(fast[1], n_tp, mid_n, slow_n, tok_dev, -1).transpose(0, 2, 3, 1, 4, 5)
+    second = second.reshape(fast[1], mid_n, n_tp, slow_n, tok_dev, -1).transpose(0, 1, 3, 2, 4, 5)
+    whole = jnp.concatenate(
+        [first[..., :half], second], axis=-1
+    ).reshape(tokens, width)
+    routing = first[..., half:].reshape(tokens, -1).astype(jnp.float32)
+    ids = routing[:, :top].astype(jnp.int32)
+    weights = routing[:, top : 2 * top] + (routing[:, 2 * top : 3 * top] + routing[:, 3 * top : 4 * top])
+
+    local = ep_pos * exp_loc + lax.broadcasted_iota(jnp.int32, (tokens, top, exp_loc), 2)
+    match = ids[:, :, None] == local
+    weight_of = jnp.sum(jnp.where(match, weights[:, :, None], 0.0), axis=1)
+    hit = jnp.any(match, axis=1)
+    number = lax.broadcasted_iota(jnp.int32, (tokens, 1), 0)
+    tp_of = (number // tok_dev % n_tp) * -1 + tp_pos + n_tp
+    number = number + (tp_of % n_tp - number // tok_dev % n_tp) * tok_dev
+    before = (number.reshape(1, tokens) < number).astype(jnp.bfloat16)
+    position = jnp.dot(before, hit.astype(jnp.bfloat16), preferred_element_type=jnp.float32)
+    place = jnp.where(hit, position.astype(jnp.int32), -1).T
+    pick = place[:, None, :] == lax.broadcasted_iota(jnp.int32, (exp_loc, rows, tokens), 1)
+    select = pick.astype(jnp.bfloat16)
+    picked = jnp.einsum("ert,td->erd", select, whole, preferred_element_type=jnp.float32)
+    scale = lax.rsqrt(jnp.mean(picked * picked, axis=2, keepdims=True) + 1e-06)
+    normed = (picked * scale * norm_gain.astype(jnp.float32)).astype(jnp.bfloat16)
+    parts = []
+    for e in range(exp_loc):
+        gate_act = jnp.dot(normed[e], w_gate[e], preferred_element_type=jnp.float32)
+        up_act = jnp.dot(normed[e], w_up[e], preferred_element_type=jnp.float32)
+        hidden = (jax.nn.silu(gate_act) * up_act).astype(jnp.bfloat16)
+        around = gathered(hidden, "tp", n_tp, 1, n_tp)
+        total = 0.0
+        for s in range(n_tp):
+            start = (tp_pos - s + n_tp) % n_tp * hid_part
+            rows_of = lax.dynamic_slice_in_dim(w_down[e], start, hid_part, 0)
+            total = total + jnp.dot(around[s], rows_of, preferred_element_type=jnp.float32)
+        parts.append(total.astype(jnp.bfloat16))
+    outputs = jnp.stack(parts)
+    spread = jnp.where(pick, weight_of.T[:, None, :], 0.0)
+    high = spread.astype(jnp.bfloat16)
+    low = (spread - high.astype(jnp.float32)).astype(jnp.bfloat16)
+    partial = jnp.einsum("ert,erf->tf", high, outputs, preferred_element_type=jnp.float32)
+    partial = partial + jnp.einsum("ert,erf->tf", low, outputs, preferred_element_type=jnp.float32)
+    total = partial.astype(jnp.bfloat16).reshape([fast[1]] + mids + lead + [group, col_part])
+    total = scattered(total, "ep", n_ep, *fast)
+    for digit in mid:
+        total = scattered(total, "ep", n_ep, *digit)
+    for digit in reversed(slow):
+        total = scattered(total, "ep", n_ep, *digit)
+    combined = total
+    mine_rows = whole[:group]
+    residual = lax.dynamic_slice_in_dim(mine_rows, tp_pos * col_part, col_part, 1)
+    result = (residual.astype(jnp.float32) + combined.astype(jnp.float32)).astype(jnp.bfloat16)
+    result = result.reshape(n_tp, tok_dev, col_part)
+    order = (tp_pos - jnp.arange(n_tp)) % n_tp
+    turned = [result[0]] * n_tp
+    for j in range(n_tp):
+        piece = result[0]
+        for s in range(1, n_tp):
+            piece = jnp.where(order[s] == j, result[s], piece)
+        turned[j] = piece
+    return jnp.concatenate(turned, axis=0)
+
+
+def shards(hidden_in, norm_gain, expert_ids, gate_weights, w_gate, w_up, w_down):
+    group, top = expert_ids.shape
+    exp_loc = w_gate.shape[0]
+    cap = max(2, 2 * top * group // (exp_loc * lax.axis_size("ep")))
+    plan = by_tokens if exp_loc * cap >= group else by_slots
+    return plan(hidden_in, norm_gain, expert_ids, gate_weights, w_gate, w_up, w_down)
+
+
 def solution(mesh):
     in_specs = (
         P(("ep", "tp"), None),

time: 131 us -> 108 us (0.82)
  blocking collectives: 74.4 us -> 0 us
  starting transfers between devices: 4.63 us -> 24.3 us
  local copies, waits for them, and re-layouts: 6.34 us -> 17.7 us
  matrix products: 22.1 us -> 31.6 us
  waiting for transfers between devices: 17.7 us -> 26.3 us
  between operations: 0.15 us -> 1.77 us
    all_to_all x1 -> x0, blocking collectives: 53.8 us -> none  [shards(): lax.all_to_all(packed, 'ep', split_axis=0, concat_axis=0, tiled=True)]
    ppermute x0 -> x21, waiting for transfers between devices: none -> 26.3 us  [shifted(): return lax.ppermute(x, axis, pairs)]
    ppermute x0 -> x21, starting transfers between devices: none -> 24.3 us  [shifted(): return lax.ppermute(x, axis, pairs)]
    all_gather x3 -> x0, blocking collectives: 20.6 us -> none  [the longest x1 9.66 us: shards(): lax.all_gather(hidden, 'tp', axis=3, tiled=True)]
    all_to_all x1 -> x0, waiting for transfers between devices: 17.7 us -> none  [shards(): lax.all_to_all(outputs.astype(jnp.bfloat16), 'ep', split_axis=0, concat_a...]
    slice x0 -> x7, local copies, waits for them, and re-layouts: none -> 15 us  [the longest x1 12.4 us: by_tokens(): rows_of = lax.dynamic_slice_in_dim(w_down[e], start, hid_part, 0)]
    dot_general x4 -> x20, matrix products: 22.1 us -> 31.6 us  [the longest x4 12.8 us: by_tokens(): gate_act = jnp.dot(normed[e], w_gate[e], preferred_element_type=jnp.float32)]
    all_to_all x1 -> x0, starting transfers between devices: 4.63 us -> none  [shards(): lax.all_to_all(outputs.astype(jnp.bfloat16), 'ep', split_axis=0, concat_a...]
  transfers between devices with their start and end apart: 1 -> 21, of which waited for: 1 -> 11; matrix products, arithmetic and copies ran while one was open for 0% -> 27% of each run, Pallas kernels for 0% -> 0%
where the time goes in v2:
time: 108 us; the launch traced here: 107 us
  matrix products  31.6 us (29%)
  waiting for transfers between devices  26.3 us (24%)
  starting transfers between devices  24.3 us (22%)
  local copies, waits for them, and re-layouts  17.7 us (16%)
  other arithmetic  5.27 us (5%)
  between operations  1.77 us (2%)
    ppermute x21, waiting for transfers between devices, shifted(): return lax.ppermute(x, axis, pairs)  26.3 us
    ppermute x21, starting transfers between devices, shifted(): return lax.ppermute(x, axis, pairs)  24.3 us
    dot_general x4, matrix products, by_tokens(): gate_act = jnp.dot(normed[e], w_gate[e], preferred_element_type=jnp.float32)  12.8 us
    dot_general x4, matrix products, by_tokens(): up_act = jnp.dot(normed[e], w_up[e], preferred_element_type=jnp.float32)  12.7 us
    slice x1, local copies, waits for them, and re-layouts, by_tokens(): rows_of = lax.dynamic_slice_in_dim(w_down[e], start, hid_part, 0)  12.4 us
    dot_general x8, matrix products, by_tokens(): jnp.dot(around[s], rows_of, preferred_element_type=jnp.float32)  3.97 us
  transfers between devices with their start and end apart: 21, of which 11 were waited for; matrix products, arithmetic and copies ran while one was open for 27% of the time, Pallas kernels for 0%

profile of v2, /device:TPU:0, one launch (start us, length us, event | category | flops | bytes accessed | tf_op | source)
XLA Modules:
  0.0 107.0 jit_solution(10273824901697140241)
XLA Ops:
  0.0 0.8 fusion.124
  0.8 4.1 %collective-permute-start.7 = (bf16[8,2048]{1,0:T(8,128)(2,1)S(1)}, bf16[8,2048]{1,0:T(8,128)(2,1)S(1)}, u32[]{:S(2)}, u32[]{:S(2)}) collective-permute-start(bf16[8,2048]{1,0:T(8,128)(2,1)S(1)} %get-tuple-element.32), channel_id=1, source_target_pairs={{0,8},{1,9},{2,10},{3,11},{4,12},{5,13},{6,14},{7,15},{8,0},{9,1},... | collective-permute-start | bytes 98312 | tf_op jit(solution)/shard_map/ppermute | solution.py:27
  4.9 1.6 %collective-permute-start.6 = (bf16[8,2048]{1,0:T(8,128)(2,1)S(1)}, bf16[8,2048]{1,0:T(8,128)(2,1)S(1)}, u32[]{:S(2)}, u32[]{:S(2)}) collective-permute-start(bf16[8,2048]{1,0:T(8,128)(2,1)S(1)} %get-tuple-element.32), channel_id=1, source_target_pairs={{0,4},{1,5},{2,6},{3,7},{4,8},{5,9},{6,10},{7,11},{8,12},{9,13},{1... | collective-permute-start | bytes 98312 | tf_op jit(solution)/shard_map/ppermute | solution.py:27
  6.5 2.3 %collective-permute-start.8 = (bf16[8,2048]{1,0:T(8,128)(2,1)S(1)}, bf16[8,2048]{1,0:T(8,128)(2,1)S(1)}, u32[]{:S(2)}, u32[]{:S(2)}) collective-permute-start(bf16[8,2048]{1,0:T(8,128)(2,1)S(1)} %get-tuple-element.32), channel_id=1, source_target_pairs={{0,12},{1,13},{2,14},{3,15},{4,0},{5,1},{6,2},{7,3},{8,4},{9,5},{1... | collective-permute-start | bytes 98312 | tf_op jit(solution)/shard_map/ppermute | solution.py:27
  8.9 0.8 constant_dynamic-slice_fusion.1
  9.7 0.1 concatenate.9
  9.8 1.2 %collective-permute-start.1 = (bf16[8,2176]{1,0:T(8,128)(2,1)S(1)}, bf16[8,2176]{1,0:T(8,128)(2,1)S(1)}, u32[]{:S(2)}, u32[]{:S(2)}) collective-permute-start(bf16[8,2176]{1,0:T(8,128)(2,1)S(1)} %concatenate.9), channel_id=1, source_target_pairs={{0,8},{1,9},{2,10},{3,11},{4,12},{5,13},{6,14},{7,15},{8,0},{9,1},... | collective-permute-start | bytes 104456 | tf_op jit(solution)/shard_map/ppermute | solution.py:27
  11.1 0.8 collective-permute-start
  11.9 1.6 %collective-permute-start.9 = (bf16[4,8,2048]{2,1,0:T(8,128)(2,1)S(1)}, bf16[4,8,2048]{2,1,0:T(8,128)(2,1)S(1)}, u32[]{:S(2)}, u32[]{:S(2)}) collective-permute-start(bf16[4,8,2048]{2,1,0:T(8,128)(2,1)S(1)} %get-tuple-element.27), channel_id=1, source_target_pairs={{0,16},{16,0},{1,17},{17,1},{2,18},{18,2},{3,19},{19,3},{4,20},{20... | collective-permute-start | bytes 393224 | tf_op jit(solution)/shard_map/ppermute | solution.py:27
  13.4 0.3 collective-permute-done.2
  13.8 1.0 collective-permute-done.1
  14.7 2.1 %collective-permute-done = bf16[8,2176]{1,0:T(8,128)(2,1)S(1)} collective-permute-done((bf16[8,2176]{1,0:T(8,128)(2,1)S(1)}, bf16[8,2176]{1,0:T(8,128)(2,1)S(1)}, u32[]{:S(2)}, u32[]{:S(2)}) %collective-permute-start) | collective-permute-done | bytes 34848 | tf_op jit(solution)/shard_map/ppermute | solution.py:27
  16.8 1.6 %collective-permute-start.3 = (bf16[4,8,2176]{2,1,0:T(8,128)(2,1)S(1)}, bf16[4,8,2176]{2,1,0:T(8,128)(2,1)S(1)}, u32[]{:S(2)}, u32[]{:S(2)}) collective-permute-start(bf16[4,8,2176]{2,1,0:T(8,128)(2,1)S(1)} %get-tuple-element.23), channel_id=1, source_target_pairs={{0,2},{1,3},{2,0},{3,1},{4,6},{5,7},{6,4},{7,5},{8,10},{9,11},{10,... | collective-permute-start | bytes 417800 | tf_op jit(solution)/shard_map/ppermute | solution.py:27
  18.4 0.6 collective-permute-start.10
  19.0 3.5 %collective-permute-done.3 = bf16[4,8,2176]{2,1,0:T(8,128)(2,1)S(1)} collective-permute-done((bf16[4,8,2176]{2,1,0:T(8,128)(2,1)S(1)}, bf16[4,8,2176]{2,1,0:T(8,128)(2,1)S(1)}, u32[]{:S(2)}, u32[]{:S(2)}) %collective-permute-start.3) | collective-permute-done | bytes 139296 | tf_op jit(solution)/shard_map/ppermute | solution.py:27
  22.6 1.6 %collective-permute-start.4 = (bf16[2,4,8,2176]{3,2,1,0:T(8,128)(2,1)S(1)}, bf16[2,4,8,2176]{3,2,1,0:T(8,128)(2,1)S(1)}, u32[]{:S(2)}, u32[]{:S(2)}) collective-permute-start(bf16[2,4,8,2176]{3,2,1,0:T(8,128)(2,1)S(1)} %get-tuple-element.16), channel_id=1, source_target_pairs={{0,16},{16,0},{1,17},{17,1},{2,18},{18,2},{3,19},{19,3},{4,20},{20... | collective-permute-start | bytes 835592 | tf_op jit(solution)/shard_map/ppermute | solution.py:27
  24.2 1.2 %collective-permute-done.10 = bf16[2,4,8,2048]{3,2,0,1:T(8,128)(2,1)S(1)} collective-permute-done((bf16[2,4,8,2048]{3,2,0,1:T(8,128)(2,1)S(1)}, bf16[2,4,8,2048]{3,2,0,1:T(8,128)(2,1)S(1)}, u32[]{:S(2)}, u32[]{:S(2)}) %collective-permute-start.10) | collective-permute-done | bytes 262176 | tf_op jit(solution)/shard_map/ppermute | solution.py:27
  25.5 3.7 %collective-permute-done.4 = bf16[2,4,8,2176]{3,2,1,0:T(8,128)(2,1)S(1)} collective-permute-done((bf16[2,4,8,2176]{3,2,1,0:T(8,128)(2,1)S(1)}, bf16[2,4,8,2176]{3,2,1,0:T(8,128)(2,1)S(1)}, u32[]{:S(2)}, u32[]{:S(2)}) %collective-permute-start.4) | collective-permute-done | bytes 278560 | tf_op jit(solution)/shard_map/ppermute | solution.py:27
  29.2 0.1 fusion.121
  29.4 12.4 %fusion.122 = (bf16[1,1024,2048]{2,1,0:T(8,128)(2,1)}, bf16[1,1024,2048]{2,1,0:T(8,128)(2,1)}, bf16[1,1024,2048]{2,1,0:T(8,128)(2,1)}, bf16[1,1024,2048]{2,1,0:T(8,128)(2,1)}) fusion(bf16[4,1024,2048]{2,1,0:T(8,128)(2,1)} %param.13), kind=kLoop, calls=%fused_computation.169 | loop fusion | bytes 33554432 | tf_op jit(solution)/shard_map/slice | solution.py:173
  41.9 0.8 copy-done.8
  42.7 1.1 %maximum_bitcast_fusion.1 = bf16[2,2,4,2,8,2048]{5,4,3,2,1,0:T(8,128)(2,1)S(1)} fusion(bf16[1,2,2,4,8,2048]{5,4,2,3,1,0:T(8,128)(2,1)} %bitcast.176, bf16[1,2,2,4,8,2048]{5,4,2,3,1,0:T(8,128)(2,1)S(1)} %get-tuple-element.13), kind=kLoop, calls=%fused_computation.74 | loop fusion | flops 524288 | bytes 2097152 | tf_op jit(solution)/shard_map/transpose | solution.py:141
  43.8 1.2 %maximum_bitcast_fusion = bf16[2,2,4,2,8,2176]{5,4,3,2,1,0:T(8,128)(2,1)S(1)} fusion(bf16[1,2,2,4,8,2176]{5,4,1,3,2,0:T(8,128)(2,1)} %bitcast.11, bf16[1,2,2,4,8,2176]{5,4,1,3,2,0:T(8,128)(2,1)S(1)} %get-tuple-element.11), kind=kLoop, calls=%fused_computation.71 | loop fusion | flops 557056 | bytes 2228224 | tf_op jit(solution)/shard_map/transpose | solution.py:140
  45.0 1.1 %slice.159 = bf16[2,2,4,2,8,2048]{5,4,3,2,1,0:T(8,128)(2,1)} slice(bf16[2,2,4,2,8,2176]{5,4,3,2,1,0:T(8,128)(2,1)S(1)} %maximum_bitcast_fusion), slice={[0:2], [0:2], [0:4], [0:2], [0:8], [0:2048]} | slice | bytes 2097152 | tf_op jit(solution)/shard_map/slice | solution.py:143
  46.2 0.2 fusion.85
  46.4 1.4 %pad_maximum_fusion = bf16[2,2,4,2,8,4096]{5,4,3,2,1,0:T(8,128)(2,1)S(1)} fusion(bf16[2,2,4,2,8,2048]{5,4,3,2,1,0:T(8,128)(2,1)S(1)} %maximum_bitcast_fusion.1, bf16[2,2,4,2,8,2048]{5,4,3,2,1,0:T(8,128)(2,1)} %slice.159), kind=kLoop, calls=%fused_computation.42 | loop fusion | flops 4194304 | bytes 4194304 | tf_op jit(solution)/shard_map/concatenate | solution.py:142
  47.8 0.1 compare_reduce_fusion
  47.9 0.2 fusion.78
  48.1 0.9 multiply_reduce_fusion
  49.0 0.6 multiply_convert_fusion
  49.6 3.8 %fusion.2 = f32[64,512]{1,0:T(8,128)S(1)} fusion(bf16[4,4096,512]{2,1,0:T(8,128)(2,1)} %param.11, bf16[4,64,4096]{2,1,0:T(8,128)(2,1)S(1)} %multiply_convert_fusion), kind=kOutput, calls=%fused_computation.2 | convolution fusion | flops 268435456 | bytes 4849664 | tf_op jit(solution)/shard_map/dot_general | solution.py:166
  53.4 3.0 %fusion.6 = f32[64,512]{1,0:T(8,128)S(1)} fusion(bf16[4,4096,512]{2,1,0:T(8,128)(2,1)} %param.11, bf16[4,64,4096]{2,1,0:T(8,128)(2,1)S(1)} %multiply_convert_fusion), kind=kOutput, calls=%fused_computation.6 | convolution fusion | flops 268435456 | bytes 4849664 | tf_op jit(solution)/shard_map/dot_general | solution.py:166
  56.5 3.0 %fusion.10 = f32[64,512]{1,0:T(8,128)S(1)} fusion(bf16[4,4096,512]{2,1,0:T(8,128)(2,1)} %param.11, bf16[4,64,4096]{2,1,0:T(8,128)(2,1)S(1)} %multiply_convert_fusion), kind=kOutput, calls=%fused_computation.10 | convolution fusion | flops 268435456 | bytes 4849664 | tf_op jit(solution)/shard_map/dot_general | solution.py:166
  59.5 3.0 %fusion.14 = f32[64,512]{1,0:T(8,128)S(1)} fusion(bf16[4,4096,512]{2,1,0:T(8,128)(2,1)} %param.11, bf16[4,64,4096]{2,1,0:T(8,128)(2,1)S(1)} %multiply_convert_fusion), kind=kOutput, calls=%fused_computation.14 | convolution fusion | flops 268435456 | bytes 4849664 | tf_op jit(solution)/shard_map/dot_general | solution.py:166
  62.6 3.3 %fusion.66 = bf16[64,512]{1,0:T(8,128)(2,1)S(1)} fusion(bf16[4,4096,512]{2,1,0:T(8,128)(2,1)} %param.12, bf16[4,64,4096]{2,1,0:T(8,128)(2,1)} %copy-done.6, f32[64,512]{1,0:T(8,128)S(1)} %fusion.2), kind=kOutput, calls=%fused_computation.67 | convolution fusion | flops 268632064 | bytes 4915200 | tf_op jit(solution)/shard_map/dot_general | solution.py:167
  65.9 1.6 %collective-permute-start.15 = (bf16[64,512]{1,0:T(8,128)(2,1)S(1)}, bf16[64,512]{1,0:T(8,128)(2,1)S(1)}, u32[]{:S(2)}, u32[]{:S(2)}) collective-permute-start(bf16[64,512]{1,0:T(8,128)(2,1)S(1)} %fusion.66), channel_id=1, source_target_pairs={{0,16},{16,0},{1,17},{17,1},{2,18},{18,2},{3,19},{19,3},{4,20},{20... | collective-permute-start | bytes 196616 | tf_op jit(solution)/shard_map/ppermute | solution.py:27
  67.5 3.0 %fusion.69 = bf16[64,512]{1,0:T(8,128)(2,1)S(1)} fusion(bf16[4,4096,512]{2,1,0:T(8,128)(2,1)} %param.12, bf16[4,64,4096]{2,1,0:T(8,128)(2,1)S(1)} %copy-done.7, f32[64,512]{1,0:T(8,128)S(1)} %fusion.6), kind=kOutput, calls=%fused_computation.68 | convolution fusion | flops 268632064 | bytes 4915200 | tf_op jit(solution)/shard_map/dot_general | solution.py:167
  70.5 0.6 collective-permute-start.14
  71.1 3.2 %fusion.72 = bf16[64,512]{1,0:T(8,128)(2,1)S(1)} fusion(bf16[4,4096,512]{2,1,0:T(8,128)(2,1)} %param.12, bf16[4,64,4096]{2,1,0:T(8,128)(2,1)S(1)} %copy-done.7, f32[64,512]{1,0:T(8,128)S(1)} %fusion.10), kind=kOutput, calls=%fused_computation.69 | convolution fusion | flops 268632064 | bytes 4915200 | tf_op jit(solution)/shard_map/dot_general | solution.py:167
  74.3 1.6 %collective-permute-start.13 = (bf16[64,512]{1,0:T(8,128)(2,1)S(1)}, bf16[64,512]{1,0:T(8,128)(2,1)S(1)}, u32[]{:S(2)}, u32[]{:S(2)}) collective-permute-start(bf16[64,512]{1,0:T(8,128)(2,1)S(1)} %fusion.72), channel_id=1, source_target_pairs={{0,16},{16,0},{1,17},{17,1},{2,18},{18,2},{3,19},{19,3},{4,20},{20... | collective-permute-start | bytes 196616 | tf_op jit(solution)/shard_map/ppermute | solution.py:27
  75.9 3.2 %fusion.75 = bf16[64,512]{1,0:T(8,128)(2,1)S(1)} fusion(bf16[4,4096,512]{2,1,0:T(8,128)(2,1)} %param.12, bf16[4,64,4096]{2,1,0:T(8,128)(2,1)S(1)} %copy-done.7, f32[64,512]{1,0:T(8,128)S(1)} %fusion.14), kind=kOutput, calls=%fused_computation.70 | convolution fusion | flops 268632064 | bytes 4915200 | tf_op jit(solution)/shard_map/dot_general | solution.py:167
  79.1 0.7 collective-permute-start.12
  79.8 0.5 fusion.44
  80.3 0.5 fusion.41
  80.8 0.5 fusion.35
  81.3 0.5 fusion.38
  81.8 0.1 fusion.98
  81.9 1.5 %collective-permute-done.12 = bf16[64,512]{1,0:T(8,128)(2,1)S(1)} collective-permute-done((bf16[64,512]{1,0:T(8,128)(2,1)S(1)}, bf16[64,512]{1,0:T(8,128)(2,1)S(1)}, u32[]{:S(2)}, u32[]{:S(2)}) %collective-permute-start.12) | collective-permute-done | bytes 65568 | tf_op jit(solution)/shard_map/ppermute | solution.py:27
  83.4 0.5 fusion.33
  83.9 0.5 fusion.32
  84.4 0.5 fusion.30
  84.9 0.5 fusion.31
  85.4 0.5 convolution_bitcast_fusion
  85.9 0.5 fusion.25
  86.6 1.9 %collective-permute-done.16 = bf16[2,4,16,2048]{3,2,1,0:T(8,128)(2,1)S(1)} collective-permute-done((bf16[2,4,16,2048]{3,2,1,0:T(8,128)(2,1)S(1)}, bf16[2,4,16,2048]{3,2,1,0:T(8,128)(2,1)S(1)}, u32[]{:S(2)}, u32[]{:S(2)}) %collective-permute-start.16) | collective-permute-done | bytes 524320 | tf_op jit(solution)/shard_map/ppermute | solution.py:27
  88.5 0.1 fusion.79
  88.6 1.6 %collective-permute-start.17 = (bf16[4,16,2048]{2,1,0:T(8,128)(2,1)S(1)}, bf16[4,16,2048]{2,1,0:T(8,128)(2,1)S(1)}, u32[]{:S(2)}, u32[]{:S(2)}) collective-permute-start(bf16[4,16,2048]{2,1,0:T(8,128)(2,1)S(1)} %slice_bitcast_fusion.12), channel_id=1, source_target_pairs={{0,2},{1,3},{2,0},{3,1},{4,6},{5,7},{6,4},{7,5},{8,10},{9,11},{10,... | collective-permute-start | bytes 786440 | tf_op jit(solution)/shard_map/ppermute | solution.py:27
  90.2 6.8 %collective-permute-done.17 = bf16[4,16,2048]{2,1,0:T(8,128)(2,1)S(1)} collective-permute-done((bf16[4,16,2048]{2,1,0:T(8,128)(2,1)S(1)}, bf16[4,16,2048]{2,1,0:T(8,128)(2,1)S(1)}, u32[]{:S(2)}, u32[]{:S(2)}) %collective-permute-start.17) | collective-permute-done | bytes 262176 | tf_op jit(solution)/shard_map/ppermute | solution.py:27
  97.1 2.2 %collective-permute-start.18 = (bf16[16,2048]{1,0:T(8,128)(2,1)S(1)}, bf16[16,2048]{1,0:T(8,128)(2,1)S(1)}, u32[]{:S(2)}, u32[]{:S(2)}) collective-permute-start(bf16[16,2048]{1,0:T(8,128)(2,1)S(1)} %get-tuple-element.17), channel_id=1, source_target_pairs={{0,12},{1,13},{2,14},{3,15},{4,0},{5,1},{6,2},{7,3},{8,4},{9,5},{1... | collective-permute-start | bytes 196616 | tf_op jit(solution)/shard_map/ppermute | solution.py:27
  99.4 0.7 collective-permute-start.19
  100.0 0.6 slice.123
  101.9 3.6 %collective-permute-done.20 = bf16[16,2048]{1,0:T(8,128)(2,1)S(1)} collective-permute-done((bf16[16,2048]{1,0:T(8,128)(2,1)S(1)}, bf16[16,2048]{1,0:T(8,128)(2,1)S(1)}, u32[]{:S(2)}, u32[]{:S(2)}) %collective-permute-start.20) | collective-permute-done | bytes 65568 | tf_op jit(solution)/shard_map/ppermute | solution.py:27
  105.5 0.8 collective-permute-done.19
  106.4 0.6 copy-done.10
  (64 shorter events, 1.2 us)
Async XLA Ops:
  0.0 8.7 %copy-start = (f32[16,8]{0,1:T(8,128)S(1)}, f32[16,8]{0,1:T(8,128)}, u32[]{:S(2)}) copy-start(f32[16,8]{0,1:T(8,128)} %param.10) | copy-start | bytes 1540
  0.8 10.3 %collective-permute-start.7 = (bf16[8,2048]{1,0:T(8,128)(2,1)S(1)}, bf16[8,2048]{1,0:T(8,128)(2,1)S(1)}, u32[]{:S(2)}, u32[]{:S(2)}) collective-permute-start(bf16[8,2048]{1,0:T(8,128)(2,1)S(1)} %get-tuple-element.32), channel_id=1, source_target_pairs={{0,8},{1,9},{2,10},{3,11},{4,12},{5,13},{6,14},{7,15},{8,0},{9,1},... | collective-permute-start | bytes 98312 | tf_op jit(solution)/shard_map/ppermute | solution.py:27
  4.9 7.0 %collective-permute-start.6 = (bf16[8,2048]{1,0:T(8,128)(2,1)S(1)}, bf16[8,2048]{1,0:T(8,128)(2,1)S(1)}, u32[]{:S(2)}, u32[]{:S(2)}) collective-permute-start(bf16[8,2048]{1,0:T(8,128)(2,1)S(1)} %get-tuple-element.32), channel_id=1, source_target_pairs={{0,4},{1,5},{2,6},{3,7},{4,8},{5,9},{6,10},{7,11},{8,12},{9,13},{1... | collective-permute-start | bytes 98312 | tf_op jit(solution)/shard_map/ppermute | solution.py:27
  6.5 5.4 %collective-permute-start.8 = (bf16[8,2048]{1,0:T(8,128)(2,1)S(1)}, bf16[8,2048]{1,0:T(8,128)(2,1)S(1)}, u32[]{:S(2)}, u32[]{:S(2)}) collective-permute-start(bf16[8,2048]{1,0:T(8,128)(2,1)S(1)} %get-tuple-element.32), channel_id=1, source_target_pairs={{0,12},{1,13},{2,14},{3,15},{4,0},{5,1},{6,2},{7,3},{8,4},{9,5},{1... | collective-permute-start | bytes 98312 | tf_op jit(solution)/shard_map/ppermute | solution.py:27
  9.8 3.9 %collective-permute-start.2 = (bf16[8,2176]{1,0:T(8,128)(2,1)S(1)}, bf16[8,2176]{1,0:T(8,128)(2,1)S(1)}, u32[]{:S(2)}, u32[]{:S(2)}) collective-permute-start(bf16[8,2176]{1,0:T(8,128)(2,1)S(1)} %concatenate.9), channel_id=1, source_target_pairs={{0,12},{1,13},{2,14},{3,15},{4,0},{5,1},{6,2},{7,3},{8,4},{9,5},{1... | collective-permute-start | bytes 104456 | tf_op jit(solution)/shard_map/ppermute | solution.py:27
  9.8 4.9 %collective-permute-start.1 = (bf16[8,2176]{1,0:T(8,128)(2,1)S(1)}, bf16[8,2176]{1,0:T(8,128)(2,1)S(1)}, u32[]{:S(2)}, u32[]{:S(2)}) collective-permute-start(bf16[8,2176]{1,0:T(8,128)(2,1)S(1)} %concatenate.9), channel_id=1, source_target_pairs={{0,8},{1,9},{2,10},{3,11},{4,12},{5,13},{6,14},{7,15},{8,0},{9,1},... | collective-permute-start | bytes 104456 | tf_op jit(solution)/shard_map/ppermute | solution.py:27
  11.1 5.7 %collective-permute-start = (bf16[8,2176]{1,0:T(8,128)(2,1)S(1)}, bf16[8,2176]{1,0:T(8,128)(2,1)S(1)}, u32[]{:S(2)}, u32[]{:S(2)}) collective-permute-start(bf16[8,2176]{1,0:T(8,128)(2,1)S(1)} %concatenate.9), channel_id=1, source_target_pairs={{0,4},{1,5},{2,6},{3,7},{4,8},{5,9},{6,10},{7,11},{8,12},{9,13},{1... | collective-permute-start | bytes 104456 | tf_op jit(solution)/shard_map/ppermute | solution.py:27
  11.9 6.5 %collective-permute-start.9 = (bf16[4,8,2048]{2,1,0:T(8,128)(2,1)S(1)}, bf16[4,8,2048]{2,1,0:T(8,128)(2,1)S(1)}, u32[]{:S(2)}, u32[]{:S(2)}) collective-permute-start(bf16[4,8,2048]{2,1,0:T(8,128)(2,1)S(1)} %get-tuple-element.27), channel_id=1, source_target_pairs={{0,16},{16,0},{1,17},{17,1},{2,18},{18,2},{3,19},{19,3},{4,20},{20... | collective-permute-start | bytes 393224 | tf_op jit(solution)/shard_map/ppermute | solution.py:27
  16.8 5.7 %collective-permute-start.3 = (bf16[4,8,2176]{2,1,0:T(8,128)(2,1)S(1)}, bf16[4,8,2176]{2,1,0:T(8,128)(2,1)S(1)}, u32[]{:S(2)}, u32[]{:S(2)}) collective-permute-start(bf16[4,8,2176]{2,1,0:T(8,128)(2,1)S(1)} %get-tuple-element.23), channel_id=1, source_target_pairs={{0,2},{1,3},{2,0},{3,1},{4,6},{5,7},{6,4},{7,5},{8,10},{9,11},{10,... | collective-permute-start | bytes 417800 | tf_op jit(solution)/shard_map/ppermute | solution.py:27
  18.4 6.9 %collective-permute-start.10 = (bf16[2,4,8,2048]{3,2,0,1:T(8,128)(2,1)S(1)}, bf16[2,4,8,2048]{3,2,0,1:T(8,128)(2,1)S(1)}, u32[]{:S(2)}, u32[]{:S(2)}) collective-permute-start(bf16[2,4,8,2048]{3,2,0,1:T(8,128)(2,1)S(1)} %get-tuple-element.21), channel_id=1, source_target_pairs={{0,2},{1,3},{2,0},{3,1},{4,6},{5,7},{6,4},{7,5},{8,10},{9,11},{10,... | collective-permute-start | bytes 786440 | tf_op jit(solution)/shard_map/ppermute | solution.py:27
  22.6 6.6 %collective-permute-start.4 = (bf16[2,4,8,2176]{3,2,1,0:T(8,128)(2,1)S(1)}, bf16[2,4,8,2176]{3,2,1,0:T(8,128)(2,1)S(1)}, u32[]{:S(2)}, u32[]{:S(2)}) collective-permute-start(bf16[2,4,8,2176]{3,2,1,0:T(8,128)(2,1)S(1)} %get-tuple-element.16), channel_id=1, source_target_pairs={{0,16},{16,0},{1,17},{17,1},{2,18},{18,2},{3,19},{19,3},{4,20},{20... | collective-permute-start | bytes 835592 | tf_op jit(solution)/shard_map/ppermute | solution.py:27
  25.4 16.4 %collective-permute-start.11 = (bf16[2,2,4,8,2048]{4,3,1,2,0:T(8,128)(2,1)S(1)}, bf16[2,2,4,8,2048]{4,3,1,2,0:T(8,128)(2,1)S(1)}, u32[]{:S(2)}, u32[]{:S(2)}) collective-permute-start(bf16[2,2,4,8,2048]{4,3,1,2,0:T(8,128)(2,1)S(1)} %get-tuple-element.14), channel_id=1, source_target_pairs={{0,1},{1,0},{2,3},{3,2},{4,5},{5,4},{6,7},{7,6},{8,9},{9,8},{10,11... | collective-permute-start | bytes 1572872 | tf_op jit(solution)/shard_map/ppermute | solution.py:27
  29.3 12.5 %copy-start.9 = (bf16[4096]{0:T(1024)(128)(2,1)S(1)}, bf16[4096]{0:T(1024)(128)(2,1)}, u32[]{:S(2)}) copy-start(bf16[4096]{0:T(1024)(128)(2,1)} %param.8) | copy-start | bytes 24580
  29.3 14.5 %collective-permute-start.5 = (bf16[2,2,4,8,2176]{4,3,0,2,1:T(8,128)(2,1)S(1)}, bf16[2,2,4,8,2176]{4,3,0,2,1:T(8,128)(2,1)}, u32[]{:S(2)}, u32[]{:S(2)}) collective-permute-start(bf16[2,2,4,8,2176]{4,3,0,2,1:T(8,128)(2,1)S(1)} %get-tuple-element.12), channel_id=1, source_target_pairs={{0,1},{1,0},{2,3},{3,2},{4,5},{5,4},{6,7},{7,6},{8,9},{9,8},{10,11... | collective-permute-start | bytes 1671176 | tf_op jit(solution)/shard_map/ppermute | solution.py:27
  41.9 0.8 copy-start.8
  49.6 9.9 %copy-start.6 = (bf16[4,64,4096]{2,1,0:T(8,128)(2,1)}, bf16[4,64,4096]{2,1,0:T(8,128)(2,1)S(1)}, u32[]{:S(2)}) copy-start(bf16[4,64,4096]{2,1,0:T(8,128)(2,1)S(1)} %multiply_convert_fusion) | copy-start | bytes 6291460
  62.6 4.9 %copy-start.7 = (bf16[4,64,4096]{2,1,0:T(8,128)(2,1)S(1)}, bf16[4,64,4096]{2,1,0:T(8,128)(2,1)}, u32[]{:S(2)}) copy-start(bf16[4,64,4096]{2,1,0:T(8,128)(2,1)} %copy-done.6) | copy-start | bytes 6291460
  65.9 18.5 %collective-permute-start.15 = (bf16[64,512]{1,0:T(8,128)(2,1)S(1)}, bf16[64,512]{1,0:T(8,128)(2,1)S(1)}, u32[]{:S(2)}, u32[]{:S(2)}) collective-permute-start(bf16[64,512]{1,0:T(8,128)(2,1)S(1)} %fusion.66), channel_id=1, source_target_pairs={{0,16},{16,0},{1,17},{17,1},{2,18},{18,2},{3,19},{19,3},{4,20},{20... | collective-permute-start | bytes 196616 | tf_op jit(solution)/shard_map/ppermute | solution.py:27
  70.5 14.4 %collective-permute-start.14 = (bf16[64,512]{1,0:T(8,128)(2,1)S(1)}, bf16[64,512]{1,0:T(8,128)(2,1)S(1)}, u32[]{:S(2)}, u32[]{:S(2)}) collective-permute-start(bf16[64,512]{1,0:T(8,128)(2,1)S(1)} %fusion.69), channel_id=1, source_target_pairs={{0,16},{16,0},{1,17},{17,1},{2,18},{18,2},{3,19},{19,3},{4,20},{20... | collective-permute-start | bytes 196616 | tf_op jit(solution)/shard_map/ppermute | solution.py:27
  71.1 8.6 %copy-start.5 = (bf16[1,1024,2048]{2,1,0:T(8,128)(2,1)S(1)}, bf16[1,1024,2048]{2,1,0:T(8,128)(2,1)}, u32[]{:S(2)}) copy-start(bf16[1,1024,2048]{2,1,0:T(8,128)(2,1)} %get-tuple-element.5) | copy-start | bytes 12582916
  74.3 6.0 %copy-start.4 = (bf16[1,1024,2048]{2,1,0:T(8,128)(2,1)S(1)}, bf16[1,1024,2048]{2,1,0:T(8,128)(2,1)}, u32[]{:S(2)}) copy-start(bf16[1,1024,2048]{2,1,0:T(8,128)(2,1)} %get-tuple-element.6) | copy-start | bytes 12582916
  74.3 9.6 %collective-permute-start.13 = (bf16[64,512]{1,0:T(8,128)(2,1)S(1)}, bf16[64,512]{1,0:T(8,128)(2,1)S(1)}, u32[]{:S(2)}, u32[]{:S(2)}) collective-permute-start(bf16[64,512]{1,0:T(8,128)(2,1)S(1)} %fusion.72), channel_id=1, source_target_pairs={{0,16},{16,0},{1,17},{17,1},{2,18},{18,2},{3,19},{19,3},{4,20},{20... | collective-permute-start | bytes 196616 | tf_op jit(solution)/shard_map/ppermute | solution.py:27
  75.9 4.9 %copy-start.3 = (bf16[1,1024,2048]{2,1,0:T(8,128)(2,1)S(1)}, bf16[1,1024,2048]{2,1,0:T(8,128)(2,1)}, u32[]{:S(2)}) copy-start(bf16[1,1024,2048]{2,1,0:T(8,128)(2,1)} %get-tuple-element.7) | copy-start | bytes 12582916
  79.0 2.3 %copy-start.2 = (bf16[1,1024,2048]{2,1,0:T(8,128)(2,1)S(1)}, bf16[1,1024,2048]{2,1,0:T(8,128)(2,1)}, u32[]{:S(2)}) copy-start(bf16[1,1024,2048]{2,1,0:T(8,128)(2,1)} %get-tuple-element.8) | copy-start | bytes 12582916
  79.1 4.3 %collective-permute-start.12 = (bf16[64,512]{1,0:T(8,128)(2,1)S(1)}, bf16[64,512]{1,0:T(8,128)(2,1)S(1)}, u32[]{:S(2)}, u32[]{:S(2)}) collective-permute-start(bf16[64,512]{1,0:T(8,128)(2,1)S(1)} %fusion.75), channel_id=1, source_target_pairs={{0,16},{16,0},{1,17},{17,1},{2,18},{18,2},{3,19},{19,3},{4,20},{20... | collective-permute-start | bytes 196616 | tf_op jit(solution)/shard_map/ppermute | solution.py:27
  85.9 21.1 %copy-start.1 = (f32[16,8]{0,1:T(8,128)S(1)}, f32[16,8]{0,1:T(8,128)}, u32[]{:S(2)}) copy-start(f32[16,8]{0,1:T(8,128)} %param.10) | copy-start | bytes 1540
  86.5 2.0 %collective-permute-start.16 = (bf16[2,4,16,2048]{3,2,1,0:T(8,128)(2,1)S(1)}, bf16[2,4,16,2048]{3,2,1,0:T(8,128)(2,1)S(1)}, u32[]{:S(2)}, u32[]{:S(2)}) collective-permute-start(bf16[2,4,16,2048]{3,2,1,0:T(8,128)(2,1)S(1)} %bitcast.177), channel_id=1, source_target_pairs={{0,1},{1,0},{2,3},{3,2},{4,5},{5,4},{6,7},{7,6},{8,9},{9,8},{10,11... | collective-permute-start | bytes 1572872 | tf_op jit(solution)/shard_map/ppermute | solution.py:27
  88.6 8.4 %collective-permute-start.17 = (bf16[4,16,2048]{2,1,0:T(8,128)(2,1)S(1)}, bf16[4,16,2048]{2,1,0:T(8,128)(2,1)S(1)}, u32[]{:S(2)}, u32[]{:S(2)}) collective-permute-start(bf16[4,16,2048]{2,1,0:T(8,128)(2,1)S(1)} %slice_bitcast_fusion.12), channel_id=1, source_target_pairs={{0,2},{1,3},{2,0},{3,1},{4,6},{5,7},{6,4},{7,5},{8,10},{9,11},{10,... | collective-permute-start | bytes 786440 | tf_op jit(solution)/shard_map/ppermute | solution.py:27
  97.1 4.8 %collective-permute-start.18 = (bf16[16,2048]{1,0:T(8,128)(2,1)S(1)}, bf16[16,2048]{1,0:T(8,128)(2,1)S(1)}, u32[]{:S(2)}, u32[]{:S(2)}) collective-permute-start(bf16[16,2048]{1,0:T(8,128)(2,1)S(1)} %get-tuple-element.17), channel_id=1, source_target_pairs={{0,12},{1,13},{2,14},{3,15},{4,0},{5,1},{6,2},{7,3},{8,4},{9,5},{1... | collective-permute-start | bytes 196616 | tf_op jit(solution)/shard_map/ppermute | solution.py:27
  99.4 6.2 %collective-permute-start.20 = (bf16[16,2048]{1,0:T(8,128)(2,1)S(1)}, bf16[16,2048]{1,0:T(8,128)(2,1)S(1)}, u32[]{:S(2)}, u32[]{:S(2)}) collective-permute-start(bf16[16,2048]{1,0:T(8,128)(2,1)S(1)} %get-tuple-element.18), channel_id=1, source_target_pairs={{0,4},{1,5},{2,6},{3,7},{4,8},{5,9},{6,10},{7,11},{8,12},{9,13},{1... | collective-permute-start | bytes 196616 | tf_op jit(solution)/shard_map/ppermute | solution.py:27
  99.4 6.9 %collective-permute-start.19 = (bf16[16,2048]{1,0:T(8,128)(2,1)S(1)}, bf16[16,2048]{1,0:T(8,128)(2,1)S(1)}, u32[]{:S(2)}, u32[]{:S(2)}) collective-permute-start(bf16[16,2048]{1,0:T(8,128)(2,1)S(1)} %get-tuple-element.19), channel_id=1, source_target_pairs={{0,8},{1,9},{2,10},{3,11},{4,12},{5,13},{6,14},{7,15},{8,0},{9,1},... | collective-permute-start | bytes 196616 | tf_op jit(solution)/shard_map/ppermute | solution.py:27
  106.4 0.6 copy-start.10

commit v3 on v0

--- a/solution.py
+++ b/solution.py
@@ -1,10 +1,345 @@
+import functools
+
 import jax
 import jax.numpy as jnp
 from jax import lax
+from jax.experimental import pallas as pl
+from jax.experimental.pallas import tpu as pltpu
 from jax.sharding import PartitionSpec as P
 
-
-def shards(hidden_in, norm_gain, expert_ids, gate_weights, w_gate, w_up, w_down):
+LANES = 128
+
+
+def factors_of(n):
+    digits, stride = [], 1
+    for _ in range(2):
+        if n % 2 == 0 and n > 1:
+            digits.append((stride, 2))
+            stride, n = stride * 2, n // 2
+    while n > 1:
+        radix = next(r for r in (4, 3, 2, n) if n % r == 0)
+        digits.append((stride, radix))
+        stride, n = stride * radix, n // radix
+    return digits
+
+
+def shifted(x, axis, size, stride, radix, by):
+    pairs = []
+    for i in range(size):
+        digit = i // stride % radix
+        pairs.append((i, i + ((digit + by) % radix - digit) * stride))
+    return lax.ppermute(x, axis, pairs)
+
+
+def arrivals(x, axis, size, stride, radix):
+    return [x] + [shifted(x, axis, size, stride, radix, s) for s in range(1, radix)]
+
+
+def gathered(x, axis, size, stride, radix):
+    return jnp.stack(arrivals(x, axis, size, stride, radix))
+
+
+def scattered(x, axis, size, stride, radix):
+    total = x[0].astype(jnp.float32)
+    for s in range(1, radix):
+        total = total + shifted(x[s], axis, size, stride, radix, radix - s).astype(jnp.float32)
+    return total.astype(x.dtype)
+
+
+def up_copies(up_ref, held, sems, start, count):
+    copies = [pltpu.make_async_copy(up_ref.at[start + i], held.at[i], sems.at[i]) for i in range(count)]
+    for copy in copies:
+        copy.start()
+    return copies
+
+
+def swiglu(x_ref, gate_ref, held, hidden_ref, copies, start):
+    for i, copy in enumerate(copies):
+        x = x_ref[start + i]
+        gate_act = jnp.dot(x, gate_ref[start + i], preferred_element_type=jnp.float32)
+        copy.wait()
+        up_act = jnp.dot(x, held[i], preferred_element_type=jnp.float32)
+        hidden_ref[i] = (gate_act / (1.0 + jnp.exp(-gate_act)) * up_act).astype(jnp.bfloat16)
+
+
+def select_kernel(dims, pos_ref, gain_ref, *refs):
+    n_fast, n_mid, n_tp, slow_n, tok_dev, top, exp_loc, rows, half = dims
+    first, second = refs[:n_fast], refs[n_fast : 2 * n_fast]
+    gate_ref, up_ref, normed_ref, high_ref, low_ref, hidden_ref, held, sems = refs[2 * n_fast :]
+    count = hidden_ref.shape[0]
+    copies = up_copies(up_ref, held, sems, 0, count)
+    tp_pos, base = pos_ref[0], pos_ref[1]
+    run = slow_n * tok_dev
+    tokens = n_fast * n_mid * n_tp * run
+    routing = jnp.concatenate([ref[:, half:] for ref in first], axis=0).astype(jnp.float32)
+    ids = routing[:, :top]
+    weights = routing[:, top : 2 * top] + (
+        routing[:, 2 * top : 3 * top] + routing[:, 3 * top : 4 * top]
+    )
+
+    def number(shape, dim):
+        at = lax.broadcasted_iota(jnp.int32, shape, dim)
+        tp_at = lax.rem(lax.div(at, n_mid * run), n_tp)
+        return at + (lax.rem(tp_pos - tp_at + n_tp, n_tp) - tp_at) * (n_mid * run)
+
+    before = number((tokens, tokens), 1) < number((tokens, tokens), 0)
+    match = [ids == (base + e).astype(jnp.float32) for e in range(exp_loc)]
+    hits = [jnp.sum(m.astype(jnp.float32), axis=1, keepdims=True) for m in match]
+    gates = [jnp.sum(jnp.where(m, weights, 0.0), axis=1, keepdims=True) for m in match]
+    lane = lax.broadcasted_iota(jnp.int32, (tokens, 128), 1)
+    hit = functools.reduce(
+        lambda a, e: jnp.where(lane == e, hits[e], a), range(exp_loc), jnp.zeros((tokens, 128), jnp.float32)
+    )
+    position = jnp.dot(
+        before.astype(jnp.float32).astype(jnp.bfloat16),
+        hit.astype(jnp.bfloat16),
+        preferred_element_type=jnp.float32,
+    )
+    slot = lax.broadcasted_iota(jnp.int32, (tokens, rows), 1).astype(jnp.float32)
+    picks, spreads = [], []
+    for e in range(exp_loc):
+        place = jnp.where(hits[e] > 0, position[:, e : e + 1], -1.0)
+        pick = slot == place
+        picks.append(pick.astype(jnp.float32))
+        spreads.append(jnp.where(pick, gates[e], 0.0))
+    spread = jnp.concatenate(spreads, axis=1)
+    blocks = []
+    for f in range(n_fast):
+        for m in range(n_mid):
+            for s in range(slow_n):
+                for t in range(n_tp):
+                    start = (((f * n_tp + t) * n_mid + m) * slow_n + s) * tok_dev
+                    blocks.append(spread[start : start + tok_dev])
+    spread = jnp.concatenate(blocks, axis=0)
+    high = spread.astype(jnp.bfloat16)
+    high_ref[...] = high
+    low_ref[...] = (spread - high.astype(jnp.float32)).astype(jnp.bfloat16)
+
+    part = n_mid * n_tp * run
+    gain = gain_ref[...].astype(jnp.float32)
+    dims_of = (((0,), (0,)), ((), ()))
+    for e in range(exp_loc):
+        left, right = [], []
+        for f in range(n_fast):
+            pick = picks[e][f * part : (f + 1) * part]
+            turned = jnp.concatenate(
+                [
+                    pick[(t * n_mid + m) * run : (t * n_mid + m + 1) * run]
+                    for m in range(n_mid)
+                    for t in range(n_tp)
+                ],
+                axis=0,
+            )
+            left.append(
+                lax.dot_general(
+                    pick.astype(jnp.bfloat16), first[f][:, :half], dims_of, preferred_element_type=jnp.float32
+                )
+            )
+            right.append(
+                lax.dot_general(
+                    turned.astype(jnp.bfloat16), second[f][...], dims_of, preferred_element_type=jnp.float32
+                )
+            )
+        left, right = sum(left[1:], left[0]), sum(right[1:], right[0])
+        squares = jnp.sum(left * left, axis=1, keepdims=True) + jnp.sum(right * right, axis=1, keepdims=True)
+        scale = lax.rsqrt(squares / (2 * half) + 1e-06)
+        normed_ref[e, :, :half] = (right * scale * gain[:, :half]).astype(jnp.bfloat16)
+        normed_ref[e, :, half:] = (left * scale * gain[:, half:]).astype(jnp.bfloat16)
+    swiglu(normed_ref, gate_ref, held, hidden_ref, copies, 0)
+
+
+def up_kernel(start, x_ref, gate_ref, up_ref, hidden_ref, held, sems):
+    copies = up_copies(up_ref, held, sems, start, hidden_ref.shape[0])
+    swiglu(x_ref, gate_ref, held, hidden_ref, copies, start)
+
+
+def down_kernel(n_tp, splits, pos_ref, high_ref, low_ref, *refs):
+    pieces = refs[: len(splits) * n_tp]
+    down_ref, partial_ref, out_ref = refs[len(splits) * n_tp :]
+    _, rows, hid_part = pieces[0].shape
+    tp_pos = pos_ref[0]
+    done = 0
+    for g, count in enumerate(splits):
+        for i in range(count):
+            total = 0.0
+            for s in range(n_tp):
+                begin = pl.multiple_of(lax.rem(tp_pos - s + n_tp, n_tp) * hid_part, hid_part)
+                total = total + jnp.dot(
+                    pieces[g * n_tp + s][i],
+                    down_ref[done, pl.ds(begin, hid_part), :],
+                    preferred_element_type=jnp.float32,
+                )
+            out_ref[done * rows : (done + 1) * rows] = total.astype(jnp.bfloat16)
+            done += 1
+    out = out_ref[...]
+    partial = jnp.dot(high_ref[...], out, preferred_element_type=jnp.float32)
+    partial = partial + jnp.dot(low_ref[...], out, preferred_element_type=jnp.float32)
+    partial_ref[...] = partial.astype(jnp.bfloat16)
+
+
+def load_kernel(src_ref, dst_ref, sems):
+    copies = [
+        pltpu.make_async_copy(src_ref.at[i], dst_ref.at[i], sems.at[i]) for i in range(src_ref.shape[0])
+    ]
+    for copy in copies:
+        copy.start()
+    for copy in copies:
+        copy.wait()
+
+
+def loaded(array):
+    return pl.pallas_call(
+        load_kernel,
+        out_shape=pltpu.VMEM(array.shape, array.dtype),
+        in_specs=[pl.BlockSpec(memory_space=pltpu.HBM)],
+        out_specs=pl.BlockSpec(memory_space=pltpu.VMEM),
+        scratch_shapes=[pltpu.SemaphoreType.DMA((array.shape[0],))],
+        compiler_params=pltpu.CompilerParams(vmem_limit_bytes=1 << 20),
+        cost_estimate=pl.CostEstimate(
+            flops=0, bytes_accessed=2 * array.size, transcendentals=0
+        ),
+    )(pltpu.with_memory_space_constraint(array, pltpu.HBM))
+
+
+VMEM = pl.BlockSpec(memory_space=pltpu.VMEM)
+SMEM = pl.BlockSpec(memory_space=pltpu.SMEM)
+
+
+HBM = pl.BlockSpec(memory_space=pltpu.HBM)
+
+
+def local_call(kernel, shapes, operands, far=(), scratch=(), limit=16 << 20, flops=0, moved=0):
+    specs = [HBM if i in far else SMEM if a.dtype == jnp.int32 else VMEM for i, a in enumerate(operands)]
+    operands = [
+        pltpu.with_memory_space_constraint(a, pltpu.HBM) if i in far else a for i, a in enumerate(operands)
+    ]
+    return pl.pallas_call(
+        kernel,
+        out_shape=shapes,
+        in_specs=specs,
+        out_specs=jax.tree.map(lambda _: VMEM, shapes),
+        scratch_shapes=list(scratch),
+        compiler_params=pltpu.CompilerParams(vmem_limit_bytes=limit),
+        cost_estimate=pl.CostEstimate(flops=flops, bytes_accessed=moved, transcendentals=0),
+    )(*operands)
+
+
+def by_tokens(hidden_in, norm_gain, expert_ids, gate_weights, w_gate, w_up, w_down):
+    n_ep = lax.axis_size("ep")
+    n_tp = lax.axis_size("tp")
+    ep_pos = lax.axis_index("ep")
+    tp_pos = lax.axis_index("tp")
+    tok_dev, width = hidden_in.shape
+    group, top = expert_ids.shape
+    exp_loc, _, hid_part = w_gate.shape
+    col_part = w_down.shape[2]
+    experts = exp_loc * n_ep
+    cap = max(2, 2 * top * group // experts)
+    rows = cap * n_ep
+    tokens = group * n_ep
+    digits = factors_of(n_ep)
+    fast, mid, slow = digits[0], digits[1:2], digits[2:]
+    half = width // 2
+    slow_n = n_ep
+    for _, radix in [fast] + mid:
+        slow_n //= radix
+    n_fast, n_mid = fast[1], mid[0][1] if mid else 1
+
+    mine = lambda a: lax.dynamic_slice_in_dim(a, tp_pos * tok_dev, tok_dev, 0)
+    w_own = mine(gate_weights)
+    w_hi = w_own.astype(jnp.bfloat16)
+    w_rest = w_own - w_hi.astype(jnp.float32)
+    w_mid = w_rest.astype(jnp.bfloat16)
+    w_lo = (w_rest - w_mid.astype(jnp.float32)).astype(jnp.bfloat16)
+    blank = jnp.zeros((tok_dev, LANES - 4 * top), jnp.bfloat16)
+    routing = [mine(expert_ids).astype(jnp.bfloat16), w_hi, w_mid, w_lo, blank]
+
+    whole = jnp.concatenate([hidden_in] + routing, axis=1)
+    for digit in reversed(slow):
+        whole = gathered(whole, "ep", n_ep, *digit)
+    whole = whole.reshape(slow_n * tok_dev, -1)
+    second, first = whole[:, :half], whole[:, half:]
+    along_tp = lambda a: gathered(a, "tp", n_tp, 1, n_tp)
+    for digit in mid:
+        first = gathered(first, "ep", n_ep, *digit)
+    second = along_tp(second)
+    first = along_tp(first)
+    for digit in mid:
+        second = gathered(second, "ep", n_ep, *digit)
+    first = arrivals(first.reshape(tokens // n_fast, -1), "ep", n_ep, *fast)
+    second = arrivals(second.reshape(tokens // n_fast, -1), "ep", n_ep, *fast)
+
+    position = jnp.stack([tp_pos, ep_pos * exp_loc])
+    gain = norm_gain.reshape(1, width)
+    dims = (n_fast, n_mid, n_tp, slow_n, tok_dev, top, exp_loc, rows, half)
+    bf16 = functools.partial(jax.ShapeDtypeStruct, dtype=jnp.bfloat16)
+    slots = exp_loc * rows
+    splits = [exp_loc - exp_loc // 2, exp_loc // 2] if exp_loc > 1 else [1]
+    gate_w = loaded(w_gate)
+    held = lambda count: [
+        pltpu.VMEM((count,) + w_up.shape[1:], jnp.bfloat16),
+        pltpu.SemaphoreType.DMA((count,)),
+    ]
+    operands = [position, gain] + first + second + [gate_w, w_up]
+    normed, high, low, hidden = local_call(
+        functools.partial(select_kernel, dims),
+        [
+            bf16((exp_loc, rows, width)),
+            bf16((tokens, slots)),
+            bf16((tokens, slots)),
+            bf16((splits[0], rows, hid_part)),
+        ],
+        operands,
+        far=[len(operands) - 1],
+        scratch=held(splits[0]),
+        flops=2 * slots * tokens * width,
+        moved=4 * splits[0] * width * hid_part,
+    )
+    pieces, start = arrivals(hidden, "tp", n_tp, 1, n_tp), splits[0]
+    for count in splits[1:]:
+        hidden = local_call(
+            functools.partial(up_kernel, start),
+            bf16((count, rows, hid_part)),
+            [normed, gate_w, w_up],
+            far=[2],
+            scratch=held(count),
+            flops=4 * count * rows * width * hid_part,
+            moved=4 * count * width * hid_part,
+        )
+        pieces += arrivals(hidden, "tp", n_tp, 1, n_tp)
+        start += count
+    partial = local_call(
+        functools.partial(down_kernel, n_tp, splits),
+        bf16((tokens, col_part)),
+        [position, high, low] + pieces + [w_down],
+        scratch=[pltpu.VMEM((slots, col_part), jnp.bfloat16)],
+        flops=2 * slots * n_tp * hid_part * col_part,
+        moved=2 * exp_loc * n_tp * hid_part * col_part,
+    )
+    total = partial.reshape(n_fast, -1, group, col_part)
+    total = scattered(total, "ep", n_ep, *fast)
+    for digit in mid:
+        total = scattered(total.reshape(digit[1], -1, group, col_part), "ep", n_ep, *digit)
+    for digit in reversed(slow):
+        total = scattered(total.reshape(digit[1], -1, group, col_part), "ep", n_ep, *digit)
+    combined = total.reshape(n_tp, tok_dev, col_part)
+    column = lambda a, at: lax.dynamic_slice_in_dim(a, at, col_part, 1)
+    near = first[0].reshape(n_tp, -1, first[0].shape[1])[:, :tok_dev]
+    far = second[0].reshape(n_mid, n_tp, -1, half)[0, :, :tok_dev]
+    own = jnp.concatenate([far, near[:, :, :half]], axis=2)
+    residual = lax.dynamic_slice_in_dim(own, tp_pos * col_part, col_part, 2)
+    result = (residual.astype(jnp.float32) + combined.astype(jnp.float32)).astype(jnp.bfloat16)
+    order = [lax.rem(tp_pos - s + n_tp, n_tp) for s in range(n_tp)]
+    turned = []
+    for j in range(n_tp):
+        piece = result[0]
+        for s in range(1, n_tp):
+            piece = jnp.where(order[s] == j, result[s], piece)
+        turned.append(piece)
+    return jnp.concatenate(turned, axis=0)
+
+
+def by_slots(hidden_in, norm_gain, expert_ids, gate_weights, w_gate, w_up, w_down):
     n_ep = lax.axis_size("ep")
     tp_pos = lax.axis_index("tp")
     tok_dev, width = hidden_in.shape
@@ -56,6 +391,14 @@
     return (residual.astype(jnp.float32) + combined).astype(jnp.bfloat16)
 
 
+def shards(hidden_in, norm_gain, expert_ids, gate_weights, w_gate, w_up, w_down):
+    group, top = expert_ids.shape
+    exp_loc = w_gate.shape[0]
+    cap = max(2, 2 * top * group // (exp_loc * lax.axis_size("ep")))
+    plan = by_tokens if exp_loc * cap >= group else by_slots
+    return plan(hidden_in, norm_gain, expert_ids, gate_weights, w_gate, w_up, w_down)
+
+
 def solution(mesh):
     in_specs = (
         P(("ep", "tp"), None),

time: 131 us -> 93.3 us (0.71)
  blocking collectives: 74.4 us -> 0 us
  Pallas kernels: 0 us -> 22.2 us
  matrix products: 22.1 us -> 0 us
  waiting for transfers between devices: 17.7 us -> 34.6 us
  starting transfers between devices: 4.63 us -> 19.4 us
  local copies, waits for them, and re-layouts: 6.34 us -> 13.7 us
  other arithmetic: 4.31 us -> 2.87 us
    all_to_all x1 -> x0, blocking collectives: 53.8 us -> none  [shards(): lax.all_to_all(packed, 'ep', split_axis=0, concat_axis=0, tiled=True)]
    ppermute x0 -> x16, waiting for transfers between devices: none -> 34.6 us  [shifted(): return lax.ppermute(x, axis, pairs)]
    pallas_call x0 -> x4, Pallas kernels: none -> 22.2 us  [the longest x3 16.3 us: local_call(): pl.pallas_call(kernel, out_shape=shapes, in_specs=specs, out_specs=jax.tr...]
    dot_general x4 -> x0, matrix products: 22.1 us -> none  [the longest x1 9.2 us: shards(): jnp.einsum('secd,edh->sech', arrived, w_up, preferred_element_type=jnp.fl...]
    all_gather x3 -> x0, blocking collectives: 20.6 us -> none  [the longest x1 9.66 us: shards(): lax.all_gather(hidden, 'tp', axis=3, tiled=True)]
    ppermute x0 -> x16, starting transfers between devices: none -> 19.4 us  [shifted(): return lax.ppermute(x, axis, pairs)]
    all_to_all x1 -> x0, waiting for transfers between devices: 17.7 us -> none  [shards(): lax.all_to_all(outputs.astype(jnp.bfloat16), 'ep', split_axis=0, concat_a...]
    unnamed x14 -> x12, local copies, waits for them, and re-layouts: 0.86 us -> 11.5 us
  transfers between devices with their start and end apart: 1 -> 16, of which waited for: 1 -> 12; matrix products, arithmetic and copies ran while one was open for 0% -> 1% of each run, Pallas kernels for 0% -> 6%
where the time goes in v3:
time: 93.3 us; the launch traced here: 93 us
  waiting for transfers between devices  34.6 us (37%)
  Pallas kernels  22.2 us (24%)
  starting transfers between devices  19.4 us (21%)
  local copies, waits for them, and re-layouts  13.7 us (15%)
  other arithmetic  2.87 us (3%)
    ppermute x16, waiting for transfers between devices, shifted(): return lax.ppermute(x, axis, pairs)  34.6 us
    ppermute x16, starting transfers between devices, shifted(): return lax.ppermute(x, axis, pairs)  19.4 us
    pallas_call x3, Pallas kernels, local_call(): pl.pallas_call(kernel, out_shape=shapes, in_specs=specs, out_specs=jax.tr...  16.3 us
    unnamed x12, local copies, waits for them, and re-layouts  11.5 us
    pallas_call x1, Pallas kernels, loaded(): pl.pallas_call(load_kernel, out_shape=pltpu.VMEM(array.shape, array.dtype...  5.89 us
  transfers between devices with their start and end apart: 16, of which 12 were waited for; matrix products, arithmetic and copies ran while one was open for 1% of the time, Pallas kernels for 6%

profile of v3, /device:TPU:0, one launch (start us, length us, event | category | flops | bytes accessed | tf_op | source)
XLA Modules:
  0.0 93.0 jit_solution(9522051650915269046)
XLA Ops:
  0.0 0.8 dynamic-slice_convert_fusion
  0.8 0.1 copy.8
  0.8 0.8 subtract_convert_fusion
  1.7 0.1 copy.11
  1.8 0.1 copy.10
  1.9 0.1 copy.9
  1.9 0.9 concatenate.10
  2.9 5.0 %collective-permute-start.2 = (bf16[8,4224]{1,0:T(8,128)(2,1)S(1)}, bf16[8,4224]{1,0:T(8,128)(2,1)S(1)}, u32[]{:S(2)}, u32[]{:S(2)}) collective-permute-start(bf16[8,4224]{1,0:T(8,128)(2,1)S(1)} %concatenate.10), channel_id=1, source_target_pairs={{0,12},{1,13},{2,14},{3,15},{4,0},{5,1},{6,2},{7,3},{8,4},{9,5},{1... | collective-permute-start | bytes 202760 | tf_op jit(solution)/shard_map/ppermute | solution.py:31
  7.9 0.0 collective-permute-start.1
  7.9 1.0 %collective-permute-start = (bf16[8,4224]{1,0:T(8,128)(2,1)S(1)}, bf16[8,4224]{1,0:T(8,128)(2,1)S(1)}, u32[]{:S(2)}, u32[]{:S(2)}) collective-permute-start(bf16[8,4224]{1,0:T(8,128)(2,1)S(1)} %concatenate.10), channel_id=1, source_target_pairs={{0,4},{1,5},{2,6},{3,7},{4,8},{5,9},{6,10},{7,11},{8,12},{9,13},{1... | collective-permute-start | bytes 202760 | tf_op jit(solution)/shard_map/ppermute | solution.py:31
  8.9 1.5 %collective-permute-done.2 = bf16[8,4224]{1,0:T(8,128)(2,1)S(1)} collective-permute-done((bf16[8,4224]{1,0:T(8,128)(2,1)S(1)}, bf16[8,4224]{1,0:T(8,128)(2,1)S(1)}, u32[]{:S(2)}, u32[]{:S(2)}) %collective-permute-start.2) | collective-permute-done | bytes 67616 | tf_op jit(solution)/shard_map/ppermute | solution.py:31
  10.5 4.1 %collective-permute-done.1 = bf16[8,4224]{1,0:T(8,128)(2,1)S(1)} collective-permute-done((bf16[8,4224]{1,0:T(8,128)(2,1)S(1)}, bf16[8,4224]{1,0:T(8,128)(2,1)S(1)}, u32[]{:S(2)}, u32[]{:S(2)}) %collective-permute-start.1) | collective-permute-done | bytes 67616 | tf_op jit(solution)/shard_map/ppermute | solution.py:31
  14.6 0.0 collective-permute-done
  14.6 1.6 %collective-permute-start.4 = (bf16[32,2176]{1,0:T(8,128)(2,1)S(1)}, bf16[32,2176]{1,0:T(8,128)(2,1)S(1)}, u32[]{:S(2)}, u32[]{:S(2)}) collective-permute-start(bf16[32,2176]{1,0:T(8,128)(2,1)S(1)} %get-tuple-element.23), channel_id=1, source_target_pairs={{0,2},{1,3},{2,0},{3,1},{4,6},{5,7},{6,4},{7,5},{8,10},{9,11},{10,... | collective-permute-start | bytes 417800 | tf_op jit(solution)/shard_map/ppermute | solution.py:31
  16.3 1.6 %collective-permute-start.3 = (bf16[32,2048]{1,0:T(8,128)(2,1)S(1)}, bf16[32,2048]{1,0:T(8,128)(2,1)S(1)}, u32[]{:S(2)}, u32[]{:S(2)}) collective-permute-start(bf16[32,2048]{1,0:T(8,128)(2,1)S(1)} %get-tuple-element.21), channel_id=1, source_target_pairs={{0,16},{16,0},{1,17},{17,1},{2,18},{18,2},{3,19},{19,3},{4,20},{20... | collective-permute-start | bytes 393224 | tf_op jit(solution)/shard_map/ppermute | solution.py:31
  17.8 2.4 %collective-permute-done.4 = bf16[32,2176]{1,0:T(8,128)(2,1)S(1)} collective-permute-done((bf16[32,2176]{1,0:T(8,128)(2,1)S(1)}, bf16[32,2176]{1,0:T(8,128)(2,1)S(1)}, u32[]{:S(2)}, u32[]{:S(2)}) %collective-permute-start.4) | collective-permute-done | bytes 139296 | tf_op jit(solution)/shard_map/ppermute | solution.py:31
  20.2 1.6 %collective-permute-start.5 = (bf16[2,32,2176]{2,1,0:T(8,128)(2,1)S(1)}, bf16[2,32,2176]{2,1,0:T(8,128)(2,1)S(1)}, u32[]{:S(2)}, u32[]{:S(2)}) collective-permute-start(bf16[2,32,2176]{2,1,0:T(8,128)(2,1)S(1)} %get-tuple-element.19), channel_id=1, source_target_pairs={{0,16},{16,0},{1,17},{17,1},{2,18},{18,2},{3,19},{19,3},{4,20},{20... | collective-permute-start | bytes 835592 | tf_op jit(solution)/shard_map/ppermute | solution.py:31
  21.8 0.0 collective-permute-done.3
  21.8 1.6 %collective-permute-start.7 = (bf16[2,32,2048]{2,1,0:T(8,128)(2,1)S(1)}, bf16[2,32,2048]{2,1,0:T(8,128)(2,1)S(1)}, u32[]{:S(2)}, u32[]{:S(2)}) collective-permute-start(bf16[2,32,2048]{2,1,0:T(8,128)(2,1)S(1)} %get-tuple-element.28), channel_id=1, source_target_pairs={{0,2},{1,3},{2,0},{3,1},{4,6},{5,7},{6,4},{7,5},{8,10},{9,11},{10,... | collective-permute-start | bytes 786440 | tf_op jit(solution)/shard_map/ppermute | solution.py:31
  23.4 4.5 %collective-permute-done.5 = bf16[2,32,2176]{2,1,0:T(8,128)(2,1)S(1)} collective-permute-done((bf16[2,32,2176]{2,1,0:T(8,128)(2,1)S(1)}, bf16[2,32,2176]{2,1,0:T(8,128)(2,1)S(1)}, u32[]{:S(2)}, u32[]{:S(2)}) %collective-permute-start.5) | collective-permute-done | bytes 278560 | tf_op jit(solution)/shard_map/ppermute | solution.py:31
  27.9 0.1 pad_maximum_fusion
  28.0 0.1 collective-permute-start.6
  28.1 0.8 collective-permute-done.7
  28.9 0.1 pad_maximum_fusion.1
  28.9 0.1 collective-permute-start.8
  29.0 0.7 reshape.47.gain_ref
  29.7 5.9 %shard_map.73.refs_4_.gate_ref = bf16[4,4096,512]{2,1,0:T(8,128)(2,1)S(1)} custom-call(bf16[4,4096,512]{2,1,0:T(8,128)(2,1)} %src_ref.1), custom_call_target="tpu_custom_call" | custom-call | bytes 16777216 | tf_op jit(solution)/shard_map/pallas_call | solution.py:191
  35.6 0.0 copy-start
  35.7 5.7 %copy-done = bf16[4,4096,512]{2,1,0:T(8,128)(2,1)} copy-done((bf16[4,4096,512]{2,1,0:T(8,128)(2,1)}, bf16[4,4096,512]{2,1,0:T(8,128)(2,1)S(1)}, u32[]{:S(2)}) %copy-start) | copy-done | bytes 16777240
  41.4 0.1 pad_add_fusion.pos_ref
  41.5 0.0 collective-permute-done.8.refs_3_
  41.5 0.0 collective-permute-done.6.refs_1_
  41.5 0.0 copy-start.1
  41.5 5.8 %copy-done.1 = bf16[4,4096,512]{2,1,0:T(8,128)(2,1)S(1)} copy-done((bf16[4,4096,512]{2,1,0:T(8,128)(2,1)S(1)}, bf16[4,4096,512]{2,1,0:T(8,128)(2,1)}, u32[]{:S(2)}) %copy-start.1) | copy-done | bytes 16777240
  47.3 0.0 slice-start
  47.3 0.0 slice-start.1
  47.3 7.4 %shard_map.74 = (bf16[4,64,4096]{2,1,0:T(8,128)(2,1)S(1)}, bf16[256,256]{1,0:T(8,128)(2,1)S(1)}, bf16[256,256]{1,0:T(8,128)(2,1)S(1)}, bf16[2,64,512]{2,1,0:T(8,128)(2,1)S(1)}) custom-call(s32[2]{0:T(128)S(1)} %pad_add_fusion.pos_ref, bf16[1,4096]{1,0:T(2,128)(2,1)S(1)} %reshape.47.gain_ref, bf16[128,2176]{1,0:T(8,128)(2,1)S(1)} %bitcast.41, ...), custom_call_target="tpu_custom_call" | custom-call | flops 536870912 | bytes 16777216 | tf_op jit(solution)/shard_map/pallas_call | solution.py:216
  54.6 0.0 slice-start.2
  54.6 0.0 slice-start.3
  54.7 4.8 %shard_map.75.refs_2_ = bf16[2,64,512]{2,1,0:T(8,128)(2,1)S(1)} custom-call(bf16[4,64,4096]{2,1,0:T(8,128)(2,1)S(1)} %get-tuple-element.12.x_ref, bf16[4,4096,512]{2,1,0:T(8,128)(2,1)S(1)} %copy-done.1, bf16[4,4096,512]{2,1,0:T(8,128)(2,1)} %up_ref.1), custom_call_target="tpu_custom_call" | custom-call | flops 1073741824 | bytes 16777216 | tf_op jit(solution)/shard_map/pallas_call | solution.py:216
  59.4 1.2 %collective-permute-start.10 = (bf16[2,64,512]{2,1,0:T(8,128)(2,1)S(1)}, bf16[2,64,512]{2,1,0:T(8,128)(2,1)S(1)}, u32[]{:S(2)}, u32[]{:S(2)}) collective-permute-start(bf16[2,64,512]{2,1,0:T(8,128)(2,1)S(1)} %shard_map.75.refs_2_), channel_id=1, source_target_pairs={{0,16},{16,0},{1,17},{17,1},{2,18},{18,2},{3,19},{19,3},{4,20},{20... | collective-permute-start | bytes 393224 | tf_op jit(solution)/shard_map/ppermute | solution.py:31
  60.6 0.9 collective-permute-start.9
  61.5 4.3 %collective-permute-done.10.refs_3_ = bf16[2,64,512]{2,1,0:T(8,128)(2,1)S(1)} collective-permute-done((bf16[2,64,512]{2,1,0:T(8,128)(2,1)S(1)}, bf16[2,64,512]{2,1,0:T(8,128)(2,1)S(1)}, u32[]{:S(2)}, u32[]{:S(2)}) %collective-permute-start.10) | collective-permute-done | bytes 131104 | tf_op jit(solution)/shard_map/ppermute | solution.py:31
  65.8 2.4 %collective-permute-done.9.refs_1_ = bf16[2,64,512]{2,1,0:T(8,128)(2,1)S(1)} collective-permute-done((bf16[2,64,512]{2,1,0:T(8,128)(2,1)S(1)}, bf16[2,64,512]{2,1,0:T(8,128)(2,1)S(1)}, u32[]{:S(2)}, u32[]{:S(2)}) %collective-permute-start.9) | collective-permute-done | bytes 131104 | tf_op jit(solution)/shard_map/ppermute | solution.py:31
  68.2 0.0 slice-done
  68.2 0.0 slice-done.1
  68.2 0.0 slice-done.2
  68.2 0.0 slice-done.3
  68.2 4.2 %shard_map.76 = bf16[256,2048]{1,0:T(8,128)(2,1)S(1)} custom-call(s32[2]{0:T(128)S(1)} %pad_add_fusion.pos_ref, bf16[256,256]{1,0:T(8,128)(2,1)S(1)} %get-tuple-element.9.high_ref, bf16[256,256]{1,0:T(8,128)(2,1)S(1)} %get-tuple-element.10.low_ref, bf16[2,64,512]{2,1,0:T(8,128)(2,1)S(1)} %get-tuple-element.11.refs_0_, ...), custom_call_target="tpu_custom_call" | custom-call | flops 1073741824 | bytes 16777216 | tf_op jit(solution)/shard_map/pallas_call | solution.py:216
  72.4 0.1 fusion.9
  72.5 0.1 collective-permute-start.11
  72.6 1.9 %collective-permute-done.11 = bf16[8,16,2048]{2,1,0:T(8,128)(2,1)S(1)} collective-permute-done((bf16[8,16,2048]{2,1,0:T(8,128)(2,1)S(1)}, bf16[8,16,2048]{2,1,0:T(8,128)(2,1)S(1)}, u32[]{:S(2)}, u32[]{:S(2)}) %collective-permute-start.11) | collective-permute-done | bytes 524320 | tf_op jit(solution)/shard_map/ppermute | solution.py:31
  74.5 0.1 fusion
  74.6 1.6 %collective-permute-start.12 = (bf16[4,16,2048]{2,1,0:T(8,128)(2,1)S(1)}, bf16[4,16,2048]{2,1,0:T(8,128)(2,1)S(1)}, u32[]{:S(2)}, u32[]{:S(2)}) collective-permute-start(bf16[4,16,2048]{2,1,0:T(8,128)(2,1)S(1)} %slice.74), channel_id=1, source_target_pairs={{0,2},{1,3},{2,0},{3,1},{4,6},{5,7},{6,4},{7,5},{8,10},{9,11},{10,... | collective-permute-start | bytes 786440 | tf_op jit(solution)/shard_map/ppermute | solution.py:31
  76.2 6.8 %collective-permute-done.12 = bf16[4,16,2048]{2,1,0:T(8,128)(2,1)S(1)} collective-permute-done((bf16[4,16,2048]{2,1,0:T(8,128)(2,1)S(1)}, bf16[4,16,2048]{2,1,0:T(8,128)(2,1)S(1)}, u32[]{:S(2)}, u32[]{:S(2)}) %collective-permute-start.12) | collective-permute-done | bytes 262176 | tf_op jit(solution)/shard_map/ppermute | solution.py:31
  83.0 0.1 add_convert_fusion
  83.1 2.2 %collective-permute-start.13 = (bf16[1,16,2048]{2,1,0:T(8,128)(2,1)S(1)}, bf16[1,16,2048]{2,1,0:T(8,128)(2,1)S(1)}, u32[]{:S(2)}, u32[]{:S(2)}) collective-permute-start(bf16[1,16,2048]{2,1,0:T(8,128)(2,1)S(1)} %get-tuple-element.24), channel_id=1, source_target_pairs={{0,12},{1,13},{2,14},{3,15},{4,0},{5,1},{6,2},{7,3},{8,4},{9,5},{1... | collective-permute-start | bytes 196616 | tf_op jit(solution)/shard_map/ppermute | solution.py:31
  85.3 0.0 collective-permute-start.15
  85.3 1.0 %collective-permute-start.14 = (bf16[1,16,2048]{2,1,0:T(8,128)(2,1)S(1)}, bf16[1,16,2048]{2,1,0:T(8,128)(2,1)S(1)}, u32[]{:S(2)}, u32[]{:S(2)}) collective-permute-start(bf16[1,16,2048]{2,1,0:T(8,128)(2,1)S(1)} %get-tuple-element.26), channel_id=1, source_target_pairs={{0,8},{1,9},{2,10},{3,11},{4,12},{5,13},{6,14},{7,15},{8,0},{9,1},... | collective-permute-start | bytes 196616 | tf_op jit(solution)/shard_map/ppermute | solution.py:31
  86.4 1.2 %collective-permute-done.13 = bf16[1,16,2048]{2,1,0:T(8,128)(2,1)S(1)} collective-permute-done((bf16[1,16,2048]{2,1,0:T(8,128)(2,1)S(1)}, bf16[1,16,2048]{2,1,0:T(8,128)(2,1)S(1)}, u32[]{:S(2)}, u32[]{:S(2)}) %collective-permute-start.13) | collective-permute-done | bytes 65568 | tf_op jit(solution)/shard_map/ppermute | solution.py:31
  87.5 3.9 %collective-permute-done.15 = bf16[1,16,2048]{2,1,0:T(8,128)(2,1)S(1)} collective-permute-done((bf16[1,16,2048]{2,1,0:T(8,128)(2,1)S(1)}, bf16[1,16,2048]{2,1,0:T(8,128)(2,1)S(1)}, u32[]{:S(2)}, u32[]{:S(2)}) %collective-permute-start.15) | collective-permute-done | bytes 65568 | tf_op jit(solution)/shard_map/ppermute | solution.py:31
  91.5 0.8 collective-permute-done.14
  92.2 0.1 fusion.1
  92.4 0.6 pad_maximum_fusion.4
  (11 shorter events, 0.2 us)
Async XLA Ops:
  2.9 7.6 %collective-permute-start.2 = (bf16[8,4224]{1,0:T(8,128)(2,1)S(1)}, bf16[8,4224]{1,0:T(8,128)(2,1)S(1)}, u32[]{:S(2)}, u32[]{:S(2)}) collective-permute-start(bf16[8,4224]{1,0:T(8,128)(2,1)S(1)} %concatenate.10), channel_id=1, source_target_pairs={{0,12},{1,13},{2,14},{3,15},{4,0},{5,1},{6,2},{7,3},{8,4},{9,5},{1... | collective-permute-start | bytes 202760 | tf_op jit(solution)/shard_map/ppermute | solution.py:31
  7.9 6.6 %collective-permute-start.1 = (bf16[8,4224]{1,0:T(8,128)(2,1)S(1)}, bf16[8,4224]{1,0:T(8,128)(2,1)S(1)}, u32[]{:S(2)}, u32[]{:S(2)}) collective-permute-start(bf16[8,4224]{1,0:T(8,128)(2,1)S(1)} %concatenate.10), channel_id=1, source_target_pairs={{0,8},{1,9},{2,10},{3,11},{4,12},{5,13},{6,14},{7,15},{8,0},{9,1},... | collective-permute-start | bytes 202760 | tf_op jit(solution)/shard_map/ppermute | solution.py:31
  7.9 6.6 %collective-permute-start = (bf16[8,4224]{1,0:T(8,128)(2,1)S(1)}, bf16[8,4224]{1,0:T(8,128)(2,1)S(1)}, u32[]{:S(2)}, u32[]{:S(2)}) collective-permute-start(bf16[8,4224]{1,0:T(8,128)(2,1)S(1)} %concatenate.10), channel_id=1, source_target_pairs={{0,4},{1,5},{2,6},{3,7},{4,8},{5,9},{6,10},{7,11},{8,12},{9,13},{1... | collective-permute-start | bytes 202760 | tf_op jit(solution)/shard_map/ppermute | solution.py:31
  14.6 5.6 %collective-permute-start.4 = (bf16[32,2176]{1,0:T(8,128)(2,1)S(1)}, bf16[32,2176]{1,0:T(8,128)(2,1)S(1)}, u32[]{:S(2)}, u32[]{:S(2)}) collective-permute-start(bf16[32,2176]{1,0:T(8,128)(2,1)S(1)} %get-tuple-element.23), channel_id=1, source_target_pairs={{0,2},{1,3},{2,0},{3,1},{4,6},{5,7},{6,4},{7,5},{8,10},{9,11},{10,... | collective-permute-start | bytes 417800 | tf_op jit(solution)/shard_map/ppermute | solution.py:31
  16.3 5.6 %collective-permute-start.3 = (bf16[32,2048]{1,0:T(8,128)(2,1)S(1)}, bf16[32,2048]{1,0:T(8,128)(2,1)S(1)}, u32[]{:S(2)}, u32[]{:S(2)}) collective-permute-start(bf16[32,2048]{1,0:T(8,128)(2,1)S(1)} %get-tuple-element.21), channel_id=1, source_target_pairs={{0,16},{16,0},{1,17},{17,1},{2,18},{18,2},{3,19},{19,3},{4,20},{20... | collective-permute-start | bytes 393224 | tf_op jit(solution)/shard_map/ppermute | solution.py:31
  20.2 7.7 %collective-permute-start.5 = (bf16[2,32,2176]{2,1,0:T(8,128)(2,1)S(1)}, bf16[2,32,2176]{2,1,0:T(8,128)(2,1)S(1)}, u32[]{:S(2)}, u32[]{:S(2)}) collective-permute-start(bf16[2,32,2176]{2,1,0:T(8,128)(2,1)S(1)} %get-tuple-element.19), channel_id=1, source_target_pairs={{0,16},{16,0},{1,17},{17,1},{2,18},{18,2},{3,19},{19,3},{4,20},{20... | collective-permute-start | bytes 835592 | tf_op jit(solution)/shard_map/ppermute | solution.py:31
  21.8 7.0 %collective-permute-start.7 = (bf16[2,32,2048]{2,1,0:T(8,128)(2,1)S(1)}, bf16[2,32,2048]{2,1,0:T(8,128)(2,1)S(1)}, u32[]{:S(2)}, u32[]{:S(2)}) collective-permute-start(bf16[2,32,2048]{2,1,0:T(8,128)(2,1)S(1)} %get-tuple-element.28), channel_id=1, source_target_pairs={{0,2},{1,3},{2,0},{3,1},{4,6},{5,7},{6,4},{7,5},{8,10},{9,11},{10,... | collective-permute-start | bytes 786440 | tf_op jit(solution)/shard_map/ppermute | solution.py:31
  28.0 13.5 %collective-permute-start.6 = (bf16[128,2176]{1,0:T(8,128)(2,1)S(1)}, bf16[128,2176]{1,0:T(8,128)(2,1)S(1)}, u32[]{:S(2)}, u32[]{:S(2)}) collective-permute-start(bf16[128,2176]{1,0:T(8,128)(2,1)S(1)} %bitcast.40), channel_id=1, source_target_pairs={{0,1},{1,0},{2,3},{3,2},{4,5},{5,4},{6,7},{7,6},{8,9},{9,8},{10,11... | collective-permute-start | bytes 1671176 | tf_op jit(solution)/shard_map/ppermute | solution.py:31
  28.9 12.5 %collective-permute-start.8 = (bf16[128,2048]{1,0:T(8,128)(2,1)S(1)}, bf16[128,2048]{1,0:T(8,128)(2,1)S(1)}, u32[]{:S(2)}, u32[]{:S(2)}) collective-permute-start(bf16[128,2048]{1,0:T(8,128)(2,1)S(1)} %bitcast.42), channel_id=1, source_target_pairs={{0,1},{1,0},{2,3},{3,2},{4,5},{5,4},{6,7},{7,6},{8,9},{9,8},{10,11... | collective-permute-start | bytes 1572872 | tf_op jit(solution)/shard_map/ppermute | solution.py:31
  35.6 5.8 %copy-start = (bf16[4,4096,512]{2,1,0:T(8,128)(2,1)}, bf16[4,4096,512]{2,1,0:T(8,128)(2,1)S(1)}, u32[]{:S(2)}) copy-start(bf16[4,4096,512]{2,1,0:T(8,128)(2,1)S(1)} %shard_map.73.refs_4_.gate_ref) | copy-start | bytes 50331652
  41.5 5.8 %copy-start.1 = (bf16[4,4096,512]{2,1,0:T(8,128)(2,1)S(1)}, bf16[4,4096,512]{2,1,0:T(8,128)(2,1)}, u32[]{:S(2)}) copy-start(bf16[4,4096,512]{2,1,0:T(8,128)(2,1)} %copy-done) | copy-start | bytes 50331652
  47.3 21.0 %slice-start = ((s8[16777216]{0:T(1024)(128)(4,1)}), s8[4194304]{0:T(1024)(128)(4,1)S(1)}, s32[]{:S(2)}) async-start(s8[16777216]{0:T(1024)(128)(4,1)} %bitcast.38), calls=%async_computation | async-start | bytes 8388608
  47.3 21.0 %slice-start.1 = ((s8[16777216]{0:T(1024)(128)(4,1)}), s8[4194304]{0:T(1024)(128)(4,1)S(1)}, s32[]{:S(2)}) async-start(s8[16777216]{0:T(1024)(128)(4,1)} %bitcast.38), calls=%async_computation.1 | async-start | bytes 8388608
  54.6 13.6 %slice-start.2 = ((s8[16777216]{0:T(1024)(128)(4,1)}), s8[4194304]{0:T(1024)(128)(4,1)S(1)}, s32[]{:S(2)}) async-start(s8[16777216]{0:T(1024)(128)(4,1)} %bitcast.38), calls=%async_computation.2 | async-start | bytes 8388608
  54.6 13.6 %slice-start.3 = ((s8[16777216]{0:T(1024)(128)(4,1)}), s8[4194304]{0:T(1024)(128)(4,1)S(1)}, s32[]{:S(2)}) async-start(s8[16777216]{0:T(1024)(128)(4,1)} %bitcast.38), calls=%async_computation.3 | async-start | bytes 8388608
  59.4 6.4 %collective-permute-start.10 = (bf16[2,64,512]{2,1,0:T(8,128)(2,1)S(1)}, bf16[2,64,512]{2,1,0:T(8,128)(2,1)S(1)}, u32[]{:S(2)}, u32[]{:S(2)}) collective-permute-start(bf16[2,64,512]{2,1,0:T(8,128)(2,1)S(1)} %shard_map.75.refs_2_), channel_id=1, source_target_pairs={{0,16},{16,0},{1,17},{17,1},{2,18},{18,2},{3,19},{19,3},{4,20},{20... | collective-permute-start | bytes 393224 | tf_op jit(solution)/shard_map/ppermute | solution.py:31
  60.6 7.6 %collective-permute-start.9 = (bf16[2,64,512]{2,1,0:T(8,128)(2,1)S(1)}, bf16[2,64,512]{2,1,0:T(8,128)(2,1)S(1)}, u32[]{:S(2)}, u32[]{:S(2)}) collective-permute-start(bf16[2,64,512]{2,1,0:T(8,128)(2,1)S(1)} %get-tuple-element.11.refs_0_), channel_id=1, source_target_pairs={{0,16},{16,0},{1,17},{17,1},{2,18},{18,2},{3,19},{19,3},{4,20},{20... | collective-permute-start | bytes 393224 | tf_op jit(solution)/shard_map/ppermute | solution.py:31
  72.5 2.0 %collective-permute-start.11 = (bf16[8,16,2048]{2,1,0:T(8,128)(2,1)S(1)}, bf16[8,16,2048]{2,1,0:T(8,128)(2,1)S(1)}, u32[]{:S(2)}, u32[]{:S(2)}) collective-permute-start(bf16[8,16,2048]{2,1,0:T(8,128)(2,1)S(1)} %bitcast.48), channel_id=1, source_target_pairs={{0,1},{1,0},{2,3},{3,2},{4,5},{5,4},{6,7},{7,6},{8,9},{9,8},{10,11... | collective-permute-start | bytes 1572872 | tf_op jit(solution)/shard_map/ppermute | solution.py:31
  74.6 8.4 %collective-permute-start.12 = (bf16[4,16,2048]{2,1,0:T(8,128)(2,1)S(1)}, bf16[4,16,2048]{2,1,0:T(8,128)(2,1)S(1)}, u32[]{:S(2)}, u32[]{:S(2)}) collective-permute-start(bf16[4,16,2048]{2,1,0:T(8,128)(2,1)S(1)} %slice.74), channel_id=1, source_target_pairs={{0,2},{1,3},{2,0},{3,1},{4,6},{5,7},{6,4},{7,5},{8,10},{9,11},{10,... | collective-permute-start | bytes 786440 | tf_op jit(solution)/shard_map/ppermute | solution.py:31
  83.1 4.4 %collective-permute-start.13 = (bf16[1,16,2048]{2,1,0:T(8,128)(2,1)S(1)}, bf16[1,16,2048]{2,1,0:T(8,128)(2,1)S(1)}, u32[]{:S(2)}, u32[]{:S(2)}) collective-permute-start(bf16[1,16,2048]{2,1,0:T(8,128)(2,1)S(1)} %get-tuple-element.24), channel_id=1, source_target_pairs={{0,12},{1,13},{2,14},{3,15},{4,0},{5,1},{6,2},{7,3},{8,4},{9,5},{1... | collective-permute-start | bytes 196616 | tf_op jit(solution)/shard_map/ppermute | solution.py:31
  85.3 6.2 %collective-permute-start.15 = (bf16[1,16,2048]{2,1,0:T(8,128)(2,1)S(1)}, bf16[1,16,2048]{2,1,0:T(8,128)(2,1)S(1)}, u32[]{:S(2)}, u32[]{:S(2)}) collective-permute-start(bf16[1,16,2048]{2,1,0:T(8,128)(2,1)S(1)} %get-tuple-element.25), channel_id=1, source_target_pairs={{0,4},{1,5},{2,6},{3,7},{4,8},{5,9},{6,10},{7,11},{8,12},{9,13},{1... | collective-permute-start | bytes 196616 | tf_op jit(solution)/shard_map/ppermute | solution.py:31
  85.3 6.9 %collective-permute-start.14 = (bf16[1,16,2048]{2,1,0:T(8,128)(2,1)S(1)}, bf16[1,16,2048]{2,1,0:T(8,128)(2,1)S(1)}, u32[]{:S(2)}, u32[]{:S(2)}) collective-permute-start(bf16[1,16,2048]{2,1,0:T(8,128)(2,1)S(1)} %get-tuple-element.26), channel_id=1, source_target_pairs={{0,8},{1,9},{2,10},{3,11},{4,12},{5,13},{6,14},{7,15},{8,0},{9,1},... | collective-permute-start | bytes 196616 | tf_op jit(solution)/shard_map/ppermute | solution.py:31

commit v4 on v3

--- a/solution.py
+++ b/solution.py
@@ -46,28 +46,80 @@
     return total.astype(x.dtype)
 
 
-def up_copies(up_ref, held, sems, start, count):
-    copies = [pltpu.make_async_copy(up_ref.at[start + i], held.at[i], sems.at[i]) for i in range(count)]
+def pack_kernel(top, pos_ref, ids_ref, weights_ref, values_ref, message_ref, ids, weights, sems):
+    tok_dev, width = values_ref.shape
+    copies = [
+        pltpu.make_async_copy(ids_ref, ids, sems.at[0]),
+        pltpu.make_async_copy(weights_ref, weights, sems.at[1]),
+        pltpu.make_async_copy(values_ref, message_ref.at[:, pl.ds(0, width)], sems.at[2]),
+    ]
+    for copy in copies:
+        copy.start()
+    copies[0].wait()
+    copies[1].wait()
+    group = ids.shape[1]
+    high = weights[...].astype(jnp.bfloat16).astype(jnp.float32)
+    rest = weights[...] - high
+    mid = rest.astype(jnp.bfloat16).astype(jnp.float32)
+    terms = [ids[...].astype(jnp.float32), high, mid, rest - mid]
+    terms.append(jnp.zeros((LANES - 4 * top, group), jnp.float32))
+    table = jnp.concatenate(terms, axis=0).astype(jnp.bfloat16)
+    own = lax.broadcasted_iota(jnp.int32, (tok_dev, group), 0) + pos_ref[0] * tok_dev
+    own = (own == lax.broadcasted_iota(jnp.int32, (tok_dev, group), 1)).astype(jnp.float32)
+    routing = lax.dot_general(
+        own.astype(jnp.bfloat16), table, (((1,), (1,)), ((), ())), preferred_element_type=jnp.float32
+    )
+    message_ref[:, width:] = routing.astype(jnp.bfloat16)
+    copies[2].wait()
+
+
+def split_kernel(half, *refs):
+    pieces, (first_ref, second_ref, token_ref) = refs[:-3], refs[-3:]
+    pieces = [ref for ref in pieces if ref.shape[1] > 2 * half]
+    whole = jnp.concatenate([ref[...].astype(jnp.float32) for ref in pieces], axis=0).astype(jnp.bfloat16)
+    second_ref[...] = whole[:, :half]
+    first_ref[...] = whole[:, half:]
+    token_ref[...] = jnp.zeros_like(token_ref)
+
+
+def join_kernel(count, *refs):
+    out_ref, token_ref = refs[-2:]
+    rows = refs[0].shape[0]
+    for i, ref in enumerate(refs[:count]):
+        out_ref[i * rows : (i + 1) * rows] = ref[...]
+    token_ref[...] = jnp.zeros_like(token_ref)
+
+
+def load_kernel(start, src_ref, *refs):
+    dst_ref, token_ref, sems = refs[-3:]
+    copies = load_copies(src_ref, dst_ref, sems, start)
+    token_ref[...] = jnp.zeros_like(token_ref)
+    for copy in copies:
+        copy.wait()
+
+
+def load_copies(src_ref, dst_ref, sems, start):
+    copies = [
+        pltpu.make_async_copy(src_ref.at[start + i], dst_ref.at[i], sems.at[i]) for i in range(dst_ref.shape[0])
+    ]
     for copy in copies:
         copy.start()
     return copies
 
 
-def swiglu(x_ref, gate_ref, held, hidden_ref, copies, start):
-    for i, copy in enumerate(copies):
-        x = x_ref[start + i]
-        gate_act = jnp.dot(x, gate_ref[start + i], preferred_element_type=jnp.float32)
-        copy.wait()
-        up_act = jnp.dot(x, held[i], preferred_element_type=jnp.float32)
+def swiglu(normed_ref, gate_ref, up_ref, hidden_ref, start):
+    for i in range(hidden_ref.shape[0]):
+        x = normed_ref[start + i]
+        gate_act = jnp.dot(x, gate_ref[i], preferred_element_type=jnp.float32)
+        up_act = jnp.dot(x, up_ref[i], preferred_element_type=jnp.float32)
         hidden_ref[i] = (gate_act / (1.0 + jnp.exp(-gate_act)) * up_act).astype(jnp.bfloat16)
 
 
 def select_kernel(dims, pos_ref, gain_ref, *refs):
     n_fast, n_mid, n_tp, slow_n, tok_dev, top, exp_loc, rows, half = dims
     first, second = refs[:n_fast], refs[n_fast : 2 * n_fast]
-    gate_ref, up_ref, normed_ref, high_ref, low_ref, hidden_ref, held, sems = refs[2 * n_fast :]
-    count = hidden_ref.shape[0]
-    copies = up_copies(up_ref, held, sems, 0, count)
+    gate_ref, up_ref, far_ref, hidden_ref, near_ref, normed_ref, high_ref, low_ref, sems = refs[2 * n_fast :]
+    copies = load_copies(far_ref, near_ref, sems, 0)
     tp_pos, base = pos_ref[0], pos_ref[1]
     run = slow_n * tok_dev
     tokens = n_fast * n_mid * n_tp * run
@@ -86,9 +138,11 @@
     match = [ids == (base + e).astype(jnp.float32) for e in range(exp_loc)]
     hits = [jnp.sum(m.astype(jnp.float32), axis=1, keepdims=True) for m in match]
     gates = [jnp.sum(jnp.where(m, weights, 0.0), axis=1, keepdims=True) for m in match]
-    lane = lax.broadcasted_iota(jnp.int32, (tokens, 128), 1)
+    lane = lax.broadcasted_iota(jnp.int32, (tokens, LANES), 1)
     hit = functools.reduce(
-        lambda a, e: jnp.where(lane == e, hits[e], a), range(exp_loc), jnp.zeros((tokens, 128), jnp.float32)
+        lambda a, e: jnp.where(lane == e, hits[e], a),
+        range(exp_loc),
+        jnp.zeros((tokens, LANES), jnp.float32),
     )
     position = jnp.dot(
         before.astype(jnp.float32).astype(jnp.bfloat16),
@@ -132,96 +186,115 @@
             )
             left.append(
                 lax.dot_general(
-                    pick.astype(jnp.bfloat16), first[f][:, :half], dims_of, preferred_element_type=jnp.float32
+                    turned.astype(jnp.bfloat16), second[f][...], dims_of, preferred_element_type=jnp.float32
                 )
             )
             right.append(
                 lax.dot_general(
-                    turned.astype(jnp.bfloat16), second[f][...], dims_of, preferred_element_type=jnp.float32
+                    pick.astype(jnp.bfloat16), first[f][:, :half], dims_of, preferred_element_type=jnp.float32
                 )
             )
         left, right = sum(left[1:], left[0]), sum(right[1:], right[0])
         squares = jnp.sum(left * left, axis=1, keepdims=True) + jnp.sum(right * right, axis=1, keepdims=True)
         scale = lax.rsqrt(squares / (2 * half) + 1e-06)
-        normed_ref[e, :, :half] = (right * scale * gain[:, :half]).astype(jnp.bfloat16)
-        normed_ref[e, :, half:] = (left * scale * gain[:, half:]).astype(jnp.bfloat16)
-    swiglu(normed_ref, gate_ref, held, hidden_ref, copies, 0)
-
-
-def up_kernel(start, x_ref, gate_ref, up_ref, hidden_ref, held, sems):
-    copies = up_copies(up_ref, held, sems, start, hidden_ref.shape[0])
-    swiglu(x_ref, gate_ref, held, hidden_ref, copies, start)
-
-
-def down_kernel(n_tp, splits, pos_ref, high_ref, low_ref, *refs):
-    pieces = refs[: len(splits) * n_tp]
-    down_ref, partial_ref, out_ref = refs[len(splits) * n_tp :]
-    _, rows, hid_part = pieces[0].shape
-    tp_pos = pos_ref[0]
-    done = 0
-    for g, count in enumerate(splits):
-        for i in range(count):
-            total = 0.0
-            for s in range(n_tp):
-                begin = pl.multiple_of(lax.rem(tp_pos - s + n_tp, n_tp) * hid_part, hid_part)
-                total = total + jnp.dot(
-                    pieces[g * n_tp + s][i],
-                    down_ref[done, pl.ds(begin, hid_part), :],
-                    preferred_element_type=jnp.float32,
-                )
-            out_ref[done * rows : (done + 1) * rows] = total.astype(jnp.bfloat16)
-            done += 1
+        normed_ref[e, :, :half] = (left * scale * gain[:, :half]).astype(jnp.bfloat16)
+        normed_ref[e, :, half:] = (right * scale * gain[:, half:]).astype(jnp.bfloat16)
+    swiglu(normed_ref, gate_ref, up_ref, hidden_ref, 0)
+    for copy in copies:
+        copy.wait()
+
+
+def up_kernel(start, normed_ref, gate_ref, up_ref, far_ref, hidden_ref, near_ref, sems):
+    copies = load_copies(far_ref, near_ref, sems, start)
+    swiglu(normed_ref, gate_ref, up_ref, hidden_ref, start)
+    for copy in copies:
+        copy.wait()
+
+
+def lower(n_tp, tp_pos, pieces, down_ref, i):
+    hid_part = pieces[0].shape[2]
+    total = 0.0
+    for s in range(n_tp):
+        begin = pl.multiple_of(lax.rem(tp_pos - s + n_tp, n_tp) * hid_part, hid_part)
+        total = total + jnp.dot(
+            pieces[s][i], down_ref[i, pl.ds(begin, hid_part), :], preferred_element_type=jnp.float32
+        )
+    return total.astype(jnp.bfloat16)
+
+
+def down_kernel(n_tp, pos_ref, *refs):
+    pieces, (down_ref, out_ref) = refs[:n_tp], refs[n_tp:]
+    rows = pieces[0].shape[1]
+    for i in range(down_ref.shape[0]):
+        out_ref[i * rows : (i + 1) * rows] = lower(n_tp, pos_ref[0], pieces, down_ref, i)
+
+
+def mix_kernel(n_tp, pos_ref, high_ref, low_ref, *refs):
+    pieces, down_ref, done, (partial_ref, out_ref) = refs[:n_tp], refs[n_tp], refs[n_tp + 1 : -2], refs[-2:]
+    rows, at = pieces[0].shape[1], 0
+    for ref in done:
+        out_ref[at : at + ref.shape[0]] = ref[...]
+        at += ref.shape[0]
+    for i in range(down_ref.shape[0]):
+        out_ref[at : at + rows] = lower(n_tp, pos_ref[0], pieces, down_ref, i)
+        at += rows
     out = out_ref[...]
     partial = jnp.dot(high_ref[...], out, preferred_element_type=jnp.float32)
     partial = partial + jnp.dot(low_ref[...], out, preferred_element_type=jnp.float32)
     partial_ref[...] = partial.astype(jnp.bfloat16)
 
 
-def load_kernel(src_ref, dst_ref, sems):
-    copies = [
-        pltpu.make_async_copy(src_ref.at[i], dst_ref.at[i], sems.at[i]) for i in range(src_ref.shape[0])
-    ]
-    for copy in copies:
-        copy.start()
-    for copy in copies:
-        copy.wait()
-
-
-def loaded(array):
-    return pl.pallas_call(
-        load_kernel,
-        out_shape=pltpu.VMEM(array.shape, array.dtype),
-        in_specs=[pl.BlockSpec(memory_space=pltpu.HBM)],
-        out_specs=pl.BlockSpec(memory_space=pltpu.VMEM),
-        scratch_shapes=[pltpu.SemaphoreType.DMA((array.shape[0],))],
-        compiler_params=pltpu.CompilerParams(vmem_limit_bytes=1 << 20),
-        cost_estimate=pl.CostEstimate(
-            flops=0, bytes_accessed=2 * array.size, transcendentals=0
-        ),
-    )(pltpu.with_memory_space_constraint(array, pltpu.HBM))
-
-
 VMEM = pl.BlockSpec(memory_space=pltpu.VMEM)
 SMEM = pl.BlockSpec(memory_space=pltpu.SMEM)
-
-
 HBM = pl.BlockSpec(memory_space=pltpu.HBM)
-
-
-def local_call(kernel, shapes, operands, far=(), scratch=(), limit=16 << 20, flops=0, moved=0):
-    specs = [HBM if i in far else SMEM if a.dtype == jnp.int32 else VMEM for i, a in enumerate(operands)]
-    operands = [
-        pltpu.with_memory_space_constraint(a, pltpu.HBM) if i in far else a for i, a in enumerate(operands)
-    ]
+KEPT = pltpu.VMEM
+
+
+def local_call(kernel, shapes, operands, far=(), scratch=(), limit=8 << 20, flops=0, moved=0):
+    specs, given = [], []
+    for i, a in enumerate(operands):
+        if i in far:
+            specs.append(HBM)
+            given.append(pltpu.with_memory_space_constraint(a, pltpu.HBM))
+        else:
+            specs.append(SMEM if a.dtype == jnp.int32 else VMEM)
+            given.append(a)
     return pl.pallas_call(
         kernel,
         out_shape=shapes,
         in_specs=specs,
-        out_specs=jax.tree.map(lambda _: VMEM, shapes),
+        out_specs=[VMEM] * len(shapes),
         scratch_shapes=list(scratch),
         compiler_params=pltpu.CompilerParams(vmem_limit_bytes=limit),
         cost_estimate=pl.CostEstimate(flops=flops, bytes_accessed=moved, transcendentals=0),
-    )(*operands)
+    )(*given)
+
+
+TOKEN = jax.ShapeDtypeStruct((8, LANES), jnp.float32)
+
+
+def loaded(array, start, count, after):
+    size = (count,) + array.shape[1:]
+    return local_call(
+        functools.partial(load_kernel, start),
+        [KEPT(size, array.dtype), TOKEN],
+        [array] + after,
+        far=[0],
+        scratch=[pltpu.SemaphoreType.DMA((count,))],
+        limit=1 << 20,
+        moved=2 * count * array.size // array.shape[0],
+    )
+
+
+def joined(pieces, after):
+    rows, columns = pieces[0].shape
+    return local_call(
+        functools.partial(join_kernel, len(pieces)),
+        [jax.ShapeDtypeStruct((len(pieces) * rows, columns), pieces[0].dtype), TOKEN],
+        list(pieces) + after,
+        limit=4 << 20,
+        moved=4 * len(pieces) * rows * columns,
+    )
 
 
 def by_tokens(hidden_in, norm_gain, expert_ids, gate_weights, w_gate, w_up, w_down):
@@ -245,77 +318,97 @@
         slow_n //= radix
     n_fast, n_mid = fast[1], mid[0][1] if mid else 1
 
-    mine = lambda a: lax.dynamic_slice_in_dim(a, tp_pos * tok_dev, tok_dev, 0)
-    w_own = mine(gate_weights)
-    w_hi = w_own.astype(jnp.bfloat16)
-    w_rest = w_own - w_hi.astype(jnp.float32)
-    w_mid = w_rest.astype(jnp.bfloat16)
-    w_lo = (w_rest - w_mid.astype(jnp.float32)).astype(jnp.bfloat16)
-    blank = jnp.zeros((tok_dev, LANES - 4 * top), jnp.bfloat16)
-    routing = [mine(expert_ids).astype(jnp.bfloat16), w_hi, w_mid, w_lo, blank]
-
-    whole = jnp.concatenate([hidden_in] + routing, axis=1)
-    for digit in reversed(slow):
-        whole = gathered(whole, "ep", n_ep, *digit)
-    whole = whole.reshape(slow_n * tok_dev, -1)
-    second, first = whole[:, :half], whole[:, half:]
-    along_tp = lambda a: gathered(a, "tp", n_tp, 1, n_tp)
-    for digit in mid:
-        first = gathered(first, "ep", n_ep, *digit)
-    second = along_tp(second)
-    first = along_tp(first)
-    for digit in mid:
-        second = gathered(second, "ep", n_ep, *digit)
-    first = arrivals(first.reshape(tokens // n_fast, -1), "ep", n_ep, *fast)
-    second = arrivals(second.reshape(tokens // n_fast, -1), "ep", n_ep, *fast)
-
-    position = jnp.stack([tp_pos, ep_pos * exp_loc])
-    gain = norm_gain.reshape(1, width)
-    dims = (n_fast, n_mid, n_tp, slow_n, tok_dev, top, exp_loc, rows, half)
     bf16 = functools.partial(jax.ShapeDtypeStruct, dtype=jnp.bfloat16)
     slots = exp_loc * rows
-    splits = [exp_loc - exp_loc // 2, exp_loc // 2] if exp_loc > 1 else [1]
-    gate_w = loaded(w_gate)
-    held = lambda count: [
-        pltpu.VMEM((count,) + w_up.shape[1:], jnp.bfloat16),
-        pltpu.SemaphoreType.DMA((count,)),
-    ]
-    operands = [position, gain] + first + second + [gate_w, w_up]
-    normed, high, low, hidden = local_call(
+    counts = [exp_loc - exp_loc // 2, exp_loc // 2] if exp_loc > 1 else [1]
+    lead = counts[0]
+    tail = counts[1:]
+    gain = norm_gain.reshape(1, width)
+    position = jnp.stack([tp_pos, ep_pos * exp_loc])
+    (message,) = local_call(
+        functools.partial(pack_kernel, top),
+        [bf16((tok_dev, width + LANES))],
+        [position, expert_ids.T, gate_weights.T, hidden_in],
+        far=[1, 2, 3],
+        scratch=[
+            pltpu.VMEM((top, group), jnp.int32),
+            pltpu.VMEM((top, group), jnp.float32),
+            pltpu.SemaphoreType.DMA((3,)),
+        ],
+        limit=4 << 20,
+    )
+    around = [message]
+    for digit in reversed(slow):
+        around = [a for piece in around for a in arrivals(piece, "ep", n_ep, *digit)]
+    gate_lead, sign = loaded(w_gate, 0, lead, [gain])
+    first, second, sign = local_call(
+        functools.partial(split_kernel, half),
+        [bf16((slow_n * tok_dev, width + LANES - half)), bf16((slow_n * tok_dev, half)), TOKEN],
+        around + [sign],
+        limit=4 << 20,
+    )
+    up_lead, up_sign = loaded(w_up, 0, lead, [sign])
+    along_tp = lambda a: arrivals(a, "tp", n_tp, 1, n_tp)
+    along_mid = lambda a: arrivals(a, "ep", n_ep, *mid[0]) if mid else [a]
+    first, second = along_mid(first), along_tp(second)
+    first, sign = joined(first, [up_sign])
+    second, _ = joined(second, [])
+    gate_tail = [loaded(w_gate, lead, count, [sign]) for count in tail]
+    first, second = along_tp(first), along_mid(second)
+    first, sign = joined(first, [sign for _, sign in gate_tail])
+    second, _ = joined(second, [])
+    up_tail = [loaded(w_up, lead, count, [sign]) for count in tail]
+    first = arrivals(first, "ep", n_ep, *fast)
+    second = arrivals(second, "ep", n_ep, *fast)
+
+    dims = (n_fast, n_mid, n_tp, slow_n, tok_dev, top, exp_loc, rows, half)
+    down_size = lambda count: KEPT((count,) + w_down.shape[1:], w_down.dtype)
+    operands = [position, gain] + first + second + [gate_lead, up_lead, w_down]
+    hidden, down_lead, normed, high, low = local_call(
         functools.partial(select_kernel, dims),
         [
+            bf16((lead, rows, hid_part)),
+            down_size(lead),
             bf16((exp_loc, rows, width)),
             bf16((tokens, slots)),
             bf16((tokens, slots)),
-            bf16((splits[0], rows, hid_part)),
         ],
         operands,
         far=[len(operands) - 1],
-        scratch=held(splits[0]),
-        flops=2 * slots * tokens * width,
-        moved=4 * splits[0] * width * hid_part,
-    )
-    pieces, start = arrivals(hidden, "tp", n_tp, 1, n_tp), splits[0]
-    for count in splits[1:]:
-        hidden = local_call(
-            functools.partial(up_kernel, start),
-            bf16((count, rows, hid_part)),
-            [normed, gate_w, w_up],
-            far=[2],
-            scratch=held(count),
-            flops=4 * count * rows * width * hid_part,
-            moved=4 * count * width * hid_part,
-        )
-        pieces += arrivals(hidden, "tp", n_tp, 1, n_tp)
-        start += count
-    partial = local_call(
-        functools.partial(down_kernel, n_tp, splits),
-        bf16((tokens, col_part)),
-        [position, high, low] + pieces + [w_down],
+        scratch=[pltpu.SemaphoreType.DMA((lead,))],
+        flops=2 * slots * tokens * width + 4 * lead * rows * width * hid_part,
+        moved=4 * lead * width * hid_part,
+    )
+    pieces = along_tp(hidden)
+    partial_of = lambda pieces, down, done: local_call(
+        functools.partial(mix_kernel, n_tp),
+        [bf16((tokens, col_part))],
+        [position, high, low] + pieces + [down] + done,
         scratch=[pltpu.VMEM((slots, col_part), jnp.bfloat16)],
         flops=2 * slots * n_tp * hid_part * col_part,
         moved=2 * exp_loc * n_tp * hid_part * col_part,
-    )
+    )[0]
+    if not tail:
+        partial = partial_of(pieces, down_lead, [])
+    else:
+        hidden, down_tail = local_call(
+            functools.partial(up_kernel, lead),
+            [bf16((tail[0], rows, hid_part)), down_size(tail[0])],
+            [normed, gate_tail[0][0], up_tail[0][0], w_down],
+            far=[3],
+            scratch=[pltpu.SemaphoreType.DMA((tail[0],))],
+            flops=4 * tail[0] * rows * width * hid_part,
+            moved=4 * tail[0] * width * hid_part,
+        )
+        late = along_tp(hidden)
+        (done,) = local_call(
+            functools.partial(down_kernel, n_tp),
+            [bf16((lead * rows, col_part))],
+            [position] + pieces + [down_lead],
+            flops=2 * lead * rows * n_tp * hid_part * col_part,
+            moved=2 * lead * n_tp * hid_part * col_part,
+        )
+        partial = partial_of(late, down_tail, [done])
     total = partial.reshape(n_fast, -1, group, col_part)
     total = scattered(total, "ep", n_ep, *fast)
     for digit in mid:
@@ -324,9 +417,9 @@
         total = scattered(total.reshape(digit[1], -1, group, col_part), "ep", n_ep, *digit)
     combined = total.reshape(n_tp, tok_dev, col_part)
     column = lambda a, at: lax.dynamic_slice_in_dim(a, at, col_part, 1)
-    near = first[0].reshape(n_tp, -1, first[0].shape[1])[:, :tok_dev]
-    far = second[0].reshape(n_mid, n_tp, -1, half)[0, :, :tok_dev]
-    own = jnp.concatenate([far, near[:, :, :half]], axis=2)
+    right = first[0].reshape(n_tp, -1, first[0].shape[1])[:, :tok_dev, :half]
+    left = second[0].reshape(n_mid, n_tp, -1, half)[0, :, :tok_dev]
+    own = jnp.concatenate([left, right], axis=2)
     residual = lax.dynamic_slice_in_dim(own, tp_pos * col_part, col_part, 2)
     result = (residual.astype(jnp.float32) + combined.astype(jnp.float32)).astype(jnp.bfloat16)
     order = [lax.rem(tp_pos - s + n_tp, n_tp) for s in range(n_tp)]

time: 93.3 us -> 75.3 us (0.81)
  waiting for transfers between devices: 34.6 us -> 19.1 us
  Pallas kernels: 22.2 us -> 31.5 us
  local copies, waits for them, and re-layouts: 13.7 us -> 5.52 us
  other arithmetic: 2.87 us -> 1.03 us
  starting transfers between devices: 19.4 us -> 17.7 us
    ppermute x16, waiting for transfers between devices: 34.6 us -> 19.1 us  [shifted(): return lax.ppermute(x, axis, pairs)]
    pallas_call x4 -> x14, Pallas kernels: 22.2 us -> 31.5 us  [local_call(): pl.pallas_call(kernel, out_shape=shapes, in_specs=specs, out_specs=[VMEM]...]
    unnamed x12 -> x4, local copies, waits for them, and re-layouts: 11.5 us -> 4.66 us
    ppermute x16, starting transfers between devices: 19.4 us -> 17.7 us  [shifted(): return lax.ppermute(x, axis, pairs)]
    convert_element_type x2 -> x0, other arithmetic: 1.6 us -> none  [the longest x1 0.84 us: by_tokens(): w_lo = (w_rest - w_mid.astype(jnp.float32)).astype(jnp.bfloat16)]
  transfers between devices with their start and end apart: 16 -> 16, of which waited for: 12 -> 9; matrix products, arithmetic and copies ran while one was open for 1% -> 1% of each run, Pallas kernels for 6% -> 29%
where the time goes in v4:
time: 75.3 us; the launch traced here: 75.1 us
  Pallas kernels  31.5 us (42%)
  waiting for transfers between devices  19.1 us (25%)
  starting transfers between devices  17.7 us (24%)
  local copies, waits for them, and re-layouts  5.52 us (7%)
  other arithmetic  1.03 us (1%)
    pallas_call x14, Pallas kernels, local_call(): pl.pallas_call(kernel, out_shape=shapes, in_specs=specs, out_specs=[VMEM]...  31.5 us
    ppermute x16, waiting for transfers between devices, shifted(): return lax.ppermute(x, axis, pairs)  19.1 us
    ppermute x16, starting transfers between devices, shifted(): return lax.ppermute(x, axis, pairs)  17.7 us
    unnamed x4, local copies, waits for them, and re-layouts  4.66 us
  transfers between devices with their start and end apart: 16, of which 9 were waited for; matrix products, arithmetic and copies ran while one was open for 1% of the time, Pallas kernels for 29%

profile of v4, /device:TPU:0, one launch (start us, length us, event | category | flops | bytes accessed | tf_op | source)
XLA Modules:
  0.0 75.1 jit_solution(5578487665872129605)
XLA Ops:
  0.0 0.1 pad_add_fusion.pos_ref
  0.1 1.4 %shard_map.73.refs_0_ = bf16[8,4224]{1,0:T(8,128)(2,1)S(1)} custom-call(s32[2]{0:T(128)S(1)} %pad_add_fusion.pos_ref, s32[8,16]{1,0:T(8,128)} %bitcast.24, f32[8,16]{1,0:T(8,128)} %bitcast.25, bf16[8,4096]{1,0:T(8,128)(2,1)} %values_ref.1), custom_call_target="tpu_custom_call" | custom-call | tf_op jit(solution)/shard_map/pallas_call | solution.py:262
  1.5 3.1 %collective-permute-start = (bf16[8,4224]{1,0:T(8,128)(2,1)S(1)}, bf16[8,4224]{1,0:T(8,128)(2,1)S(1)}, u32[]{:S(2)}, u32[]{:S(2)}) collective-permute-start(bf16[8,4224]{1,0:T(8,128)(2,1)S(1)} %shard_map.73.refs_0_), channel_id=1, source_target_pairs={{0,4},{1,5},{2,6},{3,7},{4,8},{5,9},{6,10},{7,11},{8,12},{9,13},{1... | collective-permute-start | bytes 202760 | tf_op jit(solution)/shard_map/ppermute | solution.py:31
  4.6 2.6 %collective-permute-start.1 = (bf16[8,4224]{1,0:T(8,128)(2,1)S(1)}, bf16[8,4224]{1,0:T(8,128)(2,1)S(1)}, u32[]{:S(2)}, u32[]{:S(2)}) collective-permute-start(bf16[8,4224]{1,0:T(8,128)(2,1)S(1)} %shard_map.73.refs_0_), channel_id=1, source_target_pairs={{0,8},{1,9},{2,10},{3,11},{4,12},{5,13},{6,14},{7,15},{8,0},{9,1},... | collective-permute-start | bytes 202760 | tf_op jit(solution)/shard_map/ppermute | solution.py:31
  7.2 1.3 %collective-permute-start.2 = (bf16[8,4224]{1,0:T(8,128)(2,1)S(1)}, bf16[8,4224]{1,0:T(8,128)(2,1)S(1)}, u32[]{:S(2)}, u32[]{:S(2)}) collective-permute-start(bf16[8,4224]{1,0:T(8,128)(2,1)S(1)} %shard_map.73.refs_0_), channel_id=1, source_target_pairs={{0,12},{1,13},{2,14},{3,15},{4,0},{5,1},{6,2},{7,3},{8,4},{9,5},{1... | collective-permute-start | bytes 202760 | tf_op jit(solution)/shard_map/ppermute | solution.py:31
  8.5 0.7 reshape.39.refs_0_.gain_ref
  9.2 3.5 %shard_map.74 = (bf16[2,4096,512]{2,1,0:T(8,128)(2,1)S(1)}, f32[8,128]{1,0:T(8,128)S(1)}) custom-call(bf16[4,4096,512]{2,1,0:T(8,128)(2,1)} %src_ref.6, bf16[1,4096]{1,0:T(2,128)(2,1)S(1)} %reshape.39.refs_0_.gain_ref), custom_call_target="tpu_custom_call" | custom-call | bytes 8388608 | tf_op jit(solution)/shard_map/pallas_call | solution.py:262
  12.7 0.0 collective-permute-done.refs_1_
  12.8 0.0 collective-permute-done.1.refs_2_
  12.8 0.0 collective-permute-done.2.refs_3_
  12.8 1.6 %collective-permute-start.5 = (bf16[32,2176]{1,0:T(8,128)(2,1)S(1)}, bf16[32,2176]{1,0:T(8,128)(2,1)S(1)}, u32[]{:S(2)}, u32[]{:S(2)}) collective-permute-start(bf16[32,2176]{1,0:T(8,128)(2,1)S(1)} %get-tuple-element.32.refs_0_), channel_id=1, source_target_pairs={{0,2},{1,3},{2,0},{3,1},{4,6},{5,7},{6,4},{7,5},{8,10},{9,11},{10,... | collective-permute-start | bytes 417800 | tf_op jit(solution)/shard_map/ppermute | solution.py:31
  14.4 1.5 %collective-permute-start.3 = (bf16[32,2048]{1,0:T(8,128)(2,1)S(1)}, bf16[32,2048]{1,0:T(8,128)(2,1)S(1)}, u32[]{:S(2)}, u32[]{:S(2)}) collective-permute-start(bf16[32,2048]{1,0:T(8,128)(2,1)S(1)} %get-tuple-element.29.refs_0_), channel_id=1, source_target_pairs={{0,16},{16,0},{1,17},{17,1},{2,18},{18,2},{3,19},{19,3},{4,20},{20... | collective-permute-start | bytes 393224 | tf_op jit(solution)/shard_map/ppermute | solution.py:31
  15.9 3.5 %shard_map.78 = (bf16[2,4096,512]{2,1,0:T(8,128)(2,1)S(1)}, f32[8,128]{1,0:T(8,128)S(1)}) custom-call(bf16[4,4096,512]{2,1,0:T(8,128)(2,1)} %src_ref.7, f32[8,128]{1,0:T(8,128)S(1)} %get-tuple-element.33.refs_0_), custom_call_target="tpu_custom_call" | custom-call | bytes 8388608 | tf_op jit(solution)/shard_map/pallas_call | solution.py:262
  19.4 0.0 collective-permute-done.5.refs_1_
  19.4 0.6 collective-permute-start.6
  20.0 0.0 collective-permute-done.3.refs_1_
  20.0 0.6 shard_map.76
  20.6 1.0 %collective-permute-start.4 = (bf16[64,2048]{1,0:T(8,128)(2,1)S(1)}, bf16[64,2048]{1,0:T(8,128)(2,1)S(1)}, u32[]{:S(2)}, u32[]{:S(2)}) collective-permute-start(bf16[64,2048]{1,0:T(8,128)(2,1)S(1)} %get-tuple-element.30.refs_0_), channel_id=1, source_target_pairs={{0,2},{1,3},{2,0},{3,1},{4,6},{5,7},{6,4},{7,5},{8,10},{9,11},{10,... | collective-permute-start | bytes 786440 | tf_op jit(solution)/shard_map/ppermute | solution.py:31
  21.6 3.5 %shard_map.80 = (bf16[2,4096,512]{2,1,0:T(8,128)(2,1)S(1)}, f32[8,128]{1,0:T(8,128)S(1)}) custom-call(bf16[4,4096,512]{2,1,0:T(8,128)(2,1)} %src_ref.6, f32[8,128]{1,0:T(8,128)S(1)} %get-tuple-element.36.refs_0_), custom_call_target="tpu_custom_call" | custom-call | bytes 8388608 | tf_op jit(solution)/shard_map/pallas_call | solution.py:262
  25.1 1.3 %collective-permute-done.6.refs_1_ = bf16[64,2176]{1,0:T(8,128)(2,1)S(1)} collective-permute-done((bf16[64,2176]{1,0:T(8,128)(2,1)S(1)}, bf16[64,2176]{1,0:T(8,128)(2,1)S(1)}, u32[]{:S(2)}, u32[]{:S(2)}) %collective-permute-start.6) | collective-permute-done | bytes 278560 | tf_op jit(solution)/shard_map/ppermute | solution.py:31
  26.5 0.1 collective-permute-start.7
  26.6 0.4 collective-permute-done.4.refs_1_
  27.0 0.6 shard_map.77
  27.6 0.1 collective-permute-start.8
  27.7 4.1 %shard_map.83 = (bf16[2,4096,512]{2,1,0:T(8,128)(2,1)S(1)}, f32[8,128]{1,0:T(8,128)}) custom-call(bf16[4,4096,512]{2,1,0:T(8,128)(2,1)} %src_ref.7, f32[8,128]{1,0:T(8,128)S(1)} %get-tuple-element.45.refs_0_), custom_call_target="tpu_custom_call" | custom-call | bytes 8388608 | tf_op jit(solution)/shard_map/pallas_call | solution.py:262
  31.8 0.0 collective-permute-done.8.refs_3_
  31.8 0.0 collective-permute-done.7.refs_1_
  31.8 5.7 %shard_map.82 = (bf16[2,64,512]{2,1,0:T(8,128)(2,1)S(1)}, bf16[2,1024,2048]{2,1,0:T(8,128)(2,1)S(1)}, bf16[4,64,4096]{2,1,0:T(8,128)(2,1)S(1)}, bf16[256,256]{1,0:T(8,128)(2,1)S(1)}, bf16[256,256]{1,0:T(8,128)(2,1)S(1)}) custom-call(s32[2]{0:T(128)S(1)} %pad_add_fusion.pos_ref, bf16[1,4096]{1,0:T(2,128)(2,1)S(1)} %reshape.39.refs_0_.gain_ref, ...), custom_call_target="tpu_custom_call" | custom-call | flops 1610612736 | bytes 16777216 | tf_op jit(solution)/shard_map/pallas_call | solution.py:262
  37.5 0.0 copy-start
  37.6 3.3 %copy-done = bf16[2,1024,2048]{2,1,0:T(8,128)(2,1)} copy-done((bf16[2,1024,2048]{2,1,0:T(8,128)(2,1)}, bf16[2,1024,2048]{2,1,0:T(8,128)(2,1)S(1)}, u32[]{:S(2)}) %copy-start) | copy-done | bytes 8388632
  40.8 1.4 %collective-permute-start.10 = (bf16[2,64,512]{2,1,0:T(8,128)(2,1)S(1)}, bf16[2,64,512]{2,1,0:T(8,128)(2,1)S(1)}, u32[]{:S(2)}, u32[]{:S(2)}) collective-permute-start(bf16[2,64,512]{2,1,0:T(8,128)(2,1)S(1)} %get-tuple-element.49.refs_0_), channel_id=1, source_target_pairs={{0,16},{16,0},{1,17},{17,1},{2,18},{18,2},{3,19},{19,3},{4,20},{20... | collective-permute-start | bytes 393224 | tf_op jit(solution)/shard_map/ppermute | solution.py:31
  42.2 0.0 copy-start.1
  42.2 3.6 %shard_map.84 = (bf16[2,64,512]{2,1,0:T(8,128)(2,1)S(1)}, bf16[2,1024,2048]{2,1,0:T(8,128)(2,1)S(1)}) custom-call(bf16[4,64,4096]{2,1,0:T(8,128)(2,1)S(1)} %get-tuple-element.43.normed_ref, bf16[2,4096,512]{2,1,0:T(8,128)(2,1)S(1)} %get-tuple-element.44.gate_ref, bf16[2,4096,512]{2,1,0:T(8,128)(2,1)S(1)} %get-tuple-element.46.up_ref, ...), custom_call_target="tpu_custom_call" | custom-call | flops 1073741824 | bytes 16777216 | tf_op jit(solution)/shard_map/pallas_call | solution.py:262
  45.9 0.7 collective-permute-start.9
  46.5 0.1 collective-permute-done.10.refs_1_
  46.6 1.4 %copy-done.1 = bf16[2,1024,2048]{2,1,0:T(8,128)(2,1)S(1)} copy-done((bf16[2,1024,2048]{2,1,0:T(8,128)(2,1)S(1)}, bf16[2,1024,2048]{2,1,0:T(8,128)(2,1)}, u32[]{:S(2)}) %copy-start.1) | copy-done | bytes 8388632
  48.0 2.1 %shard_map.85.refs_3_ = bf16[128,2048]{1,0:T(8,128)(2,1)S(1)} custom-call(s32[2]{0:T(128)S(1)} %pad_add_fusion.pos_ref, bf16[2,64,512]{2,1,0:T(8,128)(2,1)S(1)} %get-tuple-element.49.refs_0_, bf16[2,64,512]{2,1,0:T(8,128)(2,1)S(1)} %collective-permute-done.10.refs_1_, bf16[2,1024,2048]{2,1,0:T(8,128)(2,1)S(1)} %copy-done.1), custom_call_target="tpu_custom_call" | custom-call | flops 536870912 | bytes 8388608 | tf_op jit(solution)/shard_map/pallas_call | solution.py:262
  50.2 1.4 %collective-permute-done.9.refs_1_ = bf16[2,64,512]{2,1,0:T(8,128)(2,1)S(1)} collective-permute-done((bf16[2,64,512]{2,1,0:T(8,128)(2,1)S(1)}, bf16[2,64,512]{2,1,0:T(8,128)(2,1)S(1)}, u32[]{:S(2)}, u32[]{:S(2)}) %collective-permute-start.9) | collective-permute-done | bytes 131104 | tf_op jit(solution)/shard_map/ppermute | solution.py:31
  51.5 2.7 %shard_map.86 = bf16[256,2048]{1,0:T(8,128)(2,1)S(1)} custom-call(s32[2]{0:T(128)S(1)} %pad_add_fusion.pos_ref, bf16[256,256]{1,0:T(8,128)(2,1)S(1)} %get-tuple-element.41.high_ref, bf16[256,256]{1,0:T(8,128)(2,1)S(1)} %get-tuple-element.42.low_ref, bf16[2,64,512]{2,1,0:T(8,128)(2,1)S(1)} %get-tuple-element.47.refs_0_, ...), custom_call_target="tpu_custom_call" | custom-call | flops 1073741824 | bytes 16777216 | tf_op jit(solution)/shard_map/pallas_call | solution.py:262
  54.3 0.1 fusion.4
  54.4 0.1 collective-permute-start.11
  54.5 1.9 %collective-permute-done.11 = bf16[8,16,2048]{2,1,0:T(8,128)(2,1)S(1)} collective-permute-done((bf16[8,16,2048]{2,1,0:T(8,128)(2,1)S(1)}, bf16[8,16,2048]{2,1,0:T(8,128)(2,1)S(1)}, u32[]{:S(2)}, u32[]{:S(2)}) %collective-permute-start.11) | collective-permute-done | bytes 524320 | tf_op jit(solution)/shard_map/ppermute | solution.py:31
  56.4 0.1 fusion
  56.5 0.6 collective-permute-start.12
  57.1 7.8 %collective-permute-done.12 = bf16[4,16,2048]{2,1,0:T(8,128)(2,1)S(1)} collective-permute-done((bf16[4,16,2048]{2,1,0:T(8,128)(2,1)S(1)}, bf16[4,16,2048]{2,1,0:T(8,128)(2,1)S(1)}, u32[]{:S(2)}, u32[]{:S(2)}) %collective-permute-start.12) | collective-permute-done | bytes 262176 | tf_op jit(solution)/shard_map/ppermute | solution.py:31
  64.9 0.1 add_convert_fusion
  65.0 2.4 %collective-permute-start.13 = (bf16[1,16,2048]{2,1,0:T(8,128)(2,1)S(1)}, bf16[1,16,2048]{2,1,0:T(8,128)(2,1)S(1)}, u32[]{:S(2)}, u32[]{:S(2)}) collective-permute-start(bf16[1,16,2048]{2,1,0:T(8,128)(2,1)S(1)} %get-tuple-element.53), channel_id=1, source_target_pairs={{0,12},{1,13},{2,14},{3,15},{4,0},{5,1},{6,2},{7,3},{8,4},{9,5},{1... | collective-permute-start | bytes 196616 | tf_op jit(solution)/shard_map/ppermute | solution.py:31
  67.5 0.7 collective-permute-start.14
  68.1 0.0 collective-permute-start.15
  68.2 1.5 %collective-permute-done.13 = bf16[1,16,2048]{2,1,0:T(8,128)(2,1)S(1)} collective-permute-done((bf16[1,16,2048]{2,1,0:T(8,128)(2,1)S(1)}, bf16[1,16,2048]{2,1,0:T(8,128)(2,1)S(1)}, u32[]{:S(2)}, u32[]{:S(2)}) %collective-permute-start.13) | collective-permute-done | bytes 65568 | tf_op jit(solution)/shard_map/ppermute | solution.py:31
  69.7 3.9 %collective-permute-done.14 = bf16[1,16,2048]{2,1,0:T(8,128)(2,1)S(1)} collective-permute-done((bf16[1,16,2048]{2,1,0:T(8,128)(2,1)S(1)}, bf16[1,16,2048]{2,1,0:T(8,128)(2,1)S(1)}, u32[]{:S(2)}, u32[]{:S(2)}) %collective-permute-start.14) | collective-permute-done | bytes 65568 | tf_op jit(solution)/shard_map/ppermute | solution.py:31
  73.6 0.7 collective-permute-done.15
  74.3 0.1 fusion.1
  74.4 0.6 pad_maximum_fusion
  (8 shorter events, 0.1 us)
Async XLA Ops:
  1.5 11.2 %collective-permute-start = (bf16[8,4224]{1,0:T(8,128)(2,1)S(1)}, bf16[8,4224]{1,0:T(8,128)(2,1)S(1)}, u32[]{:S(2)}, u32[]{:S(2)}) collective-permute-start(bf16[8,4224]{1,0:T(8,128)(2,1)S(1)} %shard_map.73.refs_0_), channel_id=1, source_target_pairs={{0,4},{1,5},{2,6},{3,7},{4,8},{5,9},{6,10},{7,11},{8,12},{9,13},{1... | collective-permute-start | bytes 202760 | tf_op jit(solution)/shard_map/ppermute | solution.py:31
  4.6 8.2 %collective-permute-start.1 = (bf16[8,4224]{1,0:T(8,128)(2,1)S(1)}, bf16[8,4224]{1,0:T(8,128)(2,1)S(1)}, u32[]{:S(2)}, u32[]{:S(2)}) collective-permute-start(bf16[8,4224]{1,0:T(8,128)(2,1)S(1)} %shard_map.73.refs_0_), channel_id=1, source_target_pairs={{0,8},{1,9},{2,10},{3,11},{4,12},{5,13},{6,14},{7,15},{8,0},{9,1},... | collective-permute-start | bytes 202760 | tf_op jit(solution)/shard_map/ppermute | solution.py:31
  7.2 5.6 %collective-permute-start.2 = (bf16[8,4224]{1,0:T(8,128)(2,1)S(1)}, bf16[8,4224]{1,0:T(8,128)(2,1)S(1)}, u32[]{:S(2)}, u32[]{:S(2)}) collective-permute-start(bf16[8,4224]{1,0:T(8,128)(2,1)S(1)} %shard_map.73.refs_0_), channel_id=1, source_target_pairs={{0,12},{1,13},{2,14},{3,15},{4,0},{5,1},{6,2},{7,3},{8,4},{9,5},{1... | collective-permute-start | bytes 202760 | tf_op jit(solution)/shard_map/ppermute | solution.py:31
  12.8 6.6 %collective-permute-start.5 = (bf16[32,2176]{1,0:T(8,128)(2,1)S(1)}, bf16[32,2176]{1,0:T(8,128)(2,1)S(1)}, u32[]{:S(2)}, u32[]{:S(2)}) collective-permute-start(bf16[32,2176]{1,0:T(8,128)(2,1)S(1)} %get-tuple-element.32.refs_0_), channel_id=1, source_target_pairs={{0,2},{1,3},{2,0},{3,1},{4,6},{5,7},{6,4},{7,5},{8,10},{9,11},{10,... | collective-permute-start | bytes 417800 | tf_op jit(solution)/shard_map/ppermute | solution.py:31
  14.4 5.6 %collective-permute-start.3 = (bf16[32,2048]{1,0:T(8,128)(2,1)S(1)}, bf16[32,2048]{1,0:T(8,128)(2,1)S(1)}, u32[]{:S(2)}, u32[]{:S(2)}) collective-permute-start(bf16[32,2048]{1,0:T(8,128)(2,1)S(1)} %get-tuple-element.29.refs_0_), channel_id=1, source_target_pairs={{0,16},{16,0},{1,17},{17,1},{2,18},{18,2},{3,19},{19,3},{4,20},{20... | collective-permute-start | bytes 393224 | tf_op jit(solution)/shard_map/ppermute | solution.py:31
  19.4 7.1 %collective-permute-start.6 = (bf16[64,2176]{1,0:T(8,128)(2,1)S(1)}, bf16[64,2176]{1,0:T(8,128)(2,1)S(1)}, u32[]{:S(2)}, u32[]{:S(2)}) collective-permute-start(bf16[64,2176]{1,0:T(8,128)(2,1)S(1)} %get-tuple-element.35.refs_0_), channel_id=1, source_target_pairs={{0,16},{16,0},{1,17},{17,1},{2,18},{18,2},{3,19},{19,3},{4,20},{20... | collective-permute-start | bytes 835592 | tf_op jit(solution)/shard_map/ppermute | solution.py:31
  20.6 6.4 %collective-permute-start.4 = (bf16[64,2048]{1,0:T(8,128)(2,1)S(1)}, bf16[64,2048]{1,0:T(8,128)(2,1)S(1)}, u32[]{:S(2)}, u32[]{:S(2)}) collective-permute-start(bf16[64,2048]{1,0:T(8,128)(2,1)S(1)} %get-tuple-element.30.refs_0_), channel_id=1, source_target_pairs={{0,2},{1,3},{2,0},{3,1},{4,6},{5,7},{6,4},{7,5},{8,10},{9,11},{10,... | collective-permute-start | bytes 786440 | tf_op jit(solution)/shard_map/ppermute | solution.py:31
  26.5 5.3 %collective-permute-start.7 = (bf16[128,2176]{1,0:T(8,128)(2,1)S(1)}, bf16[128,2176]{1,0:T(8,128)(2,1)S(1)}, u32[]{:S(2)}, u32[]{:S(2)}) collective-permute-start(bf16[128,2176]{1,0:T(8,128)(2,1)S(1)} %get-tuple-element.38.refs_0_), channel_id=1, source_target_pairs={{0,1},{1,0},{2,3},{3,2},{4,5},{5,4},{6,7},{7,6},{8,9},{9,8},{10,11... | collective-permute-start | bytes 1671176 | tf_op jit(solution)/shard_map/ppermute | solution.py:31
  27.6 4.2 %collective-permute-start.8 = (bf16[128,2048]{1,0:T(8,128)(2,1)S(1)}, bf16[128,2048]{1,0:T(8,128)(2,1)S(1)}, u32[]{:S(2)}, u32[]{:S(2)}) collective-permute-start(bf16[128,2048]{1,0:T(8,128)(2,1)S(1)} %get-tuple-element.31.refs_2_), channel_id=1, source_target_pairs={{0,1},{1,0},{2,3},{3,2},{4,5},{5,4},{6,7},{7,6},{8,9},{9,8},{10,11... | collective-permute-start | bytes 1572872 | tf_op jit(solution)/shard_map/ppermute | solution.py:31
  37.5 3.3 %copy-start = (bf16[2,1024,2048]{2,1,0:T(8,128)(2,1)}, bf16[2,1024,2048]{2,1,0:T(8,128)(2,1)S(1)}, u32[]{:S(2)}) copy-start(bf16[2,1024,2048]{2,1,0:T(8,128)(2,1)S(1)} %get-tuple-element.50.refs_2_) | copy-start | bytes 25165828
  40.8 5.8 %collective-permute-start.10 = (bf16[2,64,512]{2,1,0:T(8,128)(2,1)S(1)}, bf16[2,64,512]{2,1,0:T(8,128)(2,1)S(1)}, u32[]{:S(2)}, u32[]{:S(2)}) collective-permute-start(bf16[2,64,512]{2,1,0:T(8,128)(2,1)S(1)} %get-tuple-element.49.refs_0_), channel_id=1, source_target_pairs={{0,16},{16,0},{1,17},{17,1},{2,18},{18,2},{3,19},{19,3},{4,20},{20... | collective-permute-start | bytes 393224 | tf_op jit(solution)/shard_map/ppermute | solution.py:31
  42.2 5.8 %copy-start.1 = (bf16[2,1024,2048]{2,1,0:T(8,128)(2,1)S(1)}, bf16[2,1024,2048]{2,1,0:T(8,128)(2,1)}, u32[]{:S(2)}) copy-start(bf16[2,1024,2048]{2,1,0:T(8,128)(2,1)} %copy-done) | copy-start | bytes 25165828
  45.9 5.7 %collective-permute-start.9 = (bf16[2,64,512]{2,1,0:T(8,128)(2,1)S(1)}, bf16[2,64,512]{2,1,0:T(8,128)(2,1)S(1)}, u32[]{:S(2)}, u32[]{:S(2)}) collective-permute-start(bf16[2,64,512]{2,1,0:T(8,128)(2,1)S(1)} %get-tuple-element.47.refs_0_), channel_id=1, source_target_pairs={{0,16},{16,0},{1,17},{17,1},{2,18},{18,2},{3,19},{19,3},{4,20},{20... | collective-permute-start | bytes 393224 | tf_op jit(solution)/shard_map/ppermute | solution.py:31
  54.4 2.0 %collective-permute-start.11 = (bf16[8,16,2048]{2,1,0:T(8,128)(2,1)S(1)}, bf16[8,16,2048]{2,1,0:T(8,128)(2,1)S(1)}, u32[]{:S(2)}, u32[]{:S(2)}) collective-permute-start(bf16[8,16,2048]{2,1,0:T(8,128)(2,1)S(1)} %bitcast.23), channel_id=1, source_target_pairs={{0,1},{1,0},{2,3},{3,2},{4,5},{5,4},{6,7},{7,6},{8,9},{9,8},{10,11... | collective-permute-start | bytes 1572872 | tf_op jit(solution)/shard_map/ppermute | solution.py:31
  56.5 8.4 %collective-permute-start.12 = (bf16[4,16,2048]{2,1,0:T(8,128)(2,1)S(1)}, bf16[4,16,2048]{2,1,0:T(8,128)(2,1)S(1)}, u32[]{:S(2)}, u32[]{:S(2)}) collective-permute-start(bf16[4,16,2048]{2,1,0:T(8,128)(2,1)S(1)} %slice.63), channel_id=1, source_target_pairs={{0,2},{1,3},{2,0},{3,1},{4,6},{5,7},{6,4},{7,5},{8,10},{9,11},{10,... | collective-permute-start | bytes 786440 | tf_op jit(solution)/shard_map/ppermute | solution.py:31
  65.0 4.7 %collective-permute-start.13 = (bf16[1,16,2048]{2,1,0:T(8,128)(2,1)S(1)}, bf16[1,16,2048]{2,1,0:T(8,128)(2,1)S(1)}, u32[]{:S(2)}, u32[]{:S(2)}) collective-permute-start(bf16[1,16,2048]{2,1,0:T(8,128)(2,1)S(1)} %get-tuple-element.53), channel_id=1, source_target_pairs={{0,12},{1,13},{2,14},{3,15},{4,0},{5,1},{6,2},{7,3},{8,4},{9,5},{1... | collective-permute-start | bytes 196616 | tf_op jit(solution)/shard_map/ppermute | solution.py:31
  67.5 6.1 %collective-permute-start.14 = (bf16[1,16,2048]{2,1,0:T(8,128)(2,1)S(1)}, bf16[1,16,2048]{2,1,0:T(8,128)(2,1)S(1)}, u32[]{:S(2)}, u32[]{:S(2)}) collective-permute-start(bf16[1,16,2048]{2,1,0:T(8,128)(2,1)S(1)} %get-tuple-element.55), channel_id=1, source_target_pairs={{0,8},{1,9},{2,10},{3,11},{4,12},{5,13},{6,14},{7,15},{8,0},{9,1},... | collective-permute-start | bytes 196616 | tf_op jit(solution)/shard_map/ppermute | solution.py:31
  68.1 6.1 %collective-permute-start.15 = (bf16[1,16,2048]{2,1,0:T(8,128)(2,1)S(1)}, bf16[1,16,2048]{2,1,0:T(8,128)(2,1)S(1)}, u32[]{:S(2)}, u32[]{:S(2)}) collective-permute-start(bf16[1,16,2048]{2,1,0:T(8,128)(2,1)S(1)} %get-tuple-element.54), channel_id=1, source_target_pairs={{0,4},{1,5},{2,6},{3,7},{4,8},{5,9},{6,10},{7,11},{8,12},{9,13},{1... | collective-permute-start | bytes 196616 | tf_op jit(solution)/shard_map/ppermute | solution.py:31

commit v5 on v4

--- a/solution.py
+++ b/solution.py
@@ -118,8 +118,11 @@
 def select_kernel(dims, pos_ref, gain_ref, *refs):
     n_fast, n_mid, n_tp, slow_n, tok_dev, top, exp_loc, rows, half = dims
     first, second = refs[:n_fast], refs[n_fast : 2 * n_fast]
-    gate_ref, up_ref, far_ref, hidden_ref, near_ref, normed_ref, high_ref, low_ref, sems = refs[2 * n_fast :]
-    copies = load_copies(far_ref, near_ref, sems, 0)
+    (gate_ref, up_ref, gate_far, up_far, hidden_ref, normed_ref, high_ref, low_ref, gate_near, up_near, sems) = refs[
+        2 * n_fast :
+    ]
+    lead = gate_ref.shape[0]
+    copies = load_copies(gate_far, gate_near, sems.at[0], lead) + load_copies(up_far, up_near, sems.at[1], lead)
     tp_pos, base = pos_ref[0], pos_ref[1]
     run = slow_n * tok_dev
     tokens = n_fast * n_mid * n_tp * run
@@ -205,7 +208,7 @@
 
 
 def up_kernel(start, normed_ref, gate_ref, up_ref, far_ref, hidden_ref, near_ref, sems):
-    copies = load_copies(far_ref, near_ref, sems, start)
+    copies = load_copies(far_ref, near_ref, sems, 0)
     swiglu(normed_ref, gate_ref, up_ref, hidden_ref, start)
     for copy in copies:
         copy.wait()
@@ -223,10 +226,13 @@
 
 
 def down_kernel(n_tp, pos_ref, *refs):
-    pieces, (down_ref, out_ref) = refs[:n_tp], refs[n_tp:]
+    pieces, (down_ref, far_ref, out_ref, near_ref, sems) = refs[:n_tp], refs[n_tp:]
     rows = pieces[0].shape[1]
+    copies = load_copies(far_ref, near_ref, sems, down_ref.shape[0])
     for i in range(down_ref.shape[0]):
         out_ref[i * rows : (i + 1) * rows] = lower(n_tp, pos_ref[0], pieces, down_ref, i)
+    for copy in copies:
+        copy.wait()
 
 
 def mix_kernel(n_tp, pos_ref, high_ref, low_ref, *refs):
@@ -347,35 +353,35 @@
         around + [sign],
         limit=4 << 20,
     )
-    up_lead, up_sign = loaded(w_up, 0, lead, [sign])
     along_tp = lambda a: arrivals(a, "tp", n_tp, 1, n_tp)
     along_mid = lambda a: arrivals(a, "ep", n_ep, *mid[0]) if mid else [a]
     first, second = along_mid(first), along_tp(second)
-    first, sign = joined(first, [up_sign])
+    first, join_sign = joined(first, [])
     second, _ = joined(second, [])
-    gate_tail = [loaded(w_gate, lead, count, [sign]) for count in tail]
+    up_lead, up_sign = loaded(w_up, 0, lead, [join_sign])
     first, second = along_tp(first), along_mid(second)
-    first, sign = joined(first, [sign for _, sign in gate_tail])
+    first, _ = joined(first, [up_sign])
     second, _ = joined(second, [])
-    up_tail = [loaded(w_up, lead, count, [sign]) for count in tail]
     first = arrivals(first, "ep", n_ep, *fast)
     second = arrivals(second, "ep", n_ep, *fast)
 
     dims = (n_fast, n_mid, n_tp, slow_n, tok_dev, top, exp_loc, rows, half)
     down_size = lambda count: KEPT((count,) + w_down.shape[1:], w_down.dtype)
-    operands = [position, gain] + first + second + [gate_lead, up_lead, w_down]
-    hidden, down_lead, normed, high, low = local_call(
+    operands = [position, gain] + first + second + [gate_lead, up_lead, w_gate, w_up]
+    up_size = lambda array: KEPT((exp_loc - lead,) + array.shape[1:], array.dtype)
+    hidden, normed, high, low, gate_tail, up_tail = local_call(
         functools.partial(select_kernel, dims),
         [
             bf16((lead, rows, hid_part)),
-            down_size(lead),
             bf16((exp_loc, rows, width)),
             bf16((tokens, slots)),
             bf16((tokens, slots)),
+            up_size(w_gate),
+            up_size(w_up),
         ],
         operands,
-        far=[len(operands) - 1],
-        scratch=[pltpu.SemaphoreType.DMA((lead,))],
+        far=[len(operands) - 2, len(operands) - 1],
+        scratch=[pltpu.SemaphoreType.DMA((2, exp_loc - lead))],
         flops=2 * slots * tokens * width + 4 * lead * rows * width * hid_part,
         moved=4 * lead * width * hid_part,
     )
@@ -389,22 +395,24 @@
         moved=2 * exp_loc * n_tp * hid_part * col_part,
     )[0]
     if not tail:
-        partial = partial_of(pieces, down_lead, [])
+        partial = partial_of(pieces, loaded(w_down, 0, lead, [])[0], [])
     else:
-        hidden, down_tail = local_call(
+        hidden, down_lead = local_call(
             functools.partial(up_kernel, lead),
-            [bf16((tail[0], rows, hid_part)), down_size(tail[0])],
-            [normed, gate_tail[0][0], up_tail[0][0], w_down],
+            [bf16((tail[0], rows, hid_part)), down_size(lead)],
+            [normed, gate_tail, up_tail, w_down],
             far=[3],
-            scratch=[pltpu.SemaphoreType.DMA((tail[0],))],
+            scratch=[pltpu.SemaphoreType.DMA((lead,))],
             flops=4 * tail[0] * rows * width * hid_part,
             moved=4 * tail[0] * width * hid_part,
         )
         late = along_tp(hidden)
-        (done,) = local_call(
+        done, down_tail = local_call(
             functools.partial(down_kernel, n_tp),
-            [bf16((lead * rows, col_part))],
-            [position] + pieces + [down_lead],
+            [bf16((lead * rows, col_part)), down_size(tail[0])],
+            [position] + pieces + [down_lead, w_down],
+            far=[len(pieces) + 2],
+            scratch=[pltpu.SemaphoreType.DMA((tail[0],))],
             flops=2 * lead * rows * n_tp * hid_part * col_part,
             moved=2 * lead * n_tp * hid_part * col_part,
         )
@@ -488,7 +496,7 @@
     group, top = expert_ids.shape
     exp_loc = w_gate.shape[0]
     cap = max(2, 2 * top * group // (exp_loc * lax.axis_size("ep")))
-    plan = by_tokens if exp_loc * cap >= group else by_slots
+    plan = by_tokens if exp_loc > 1 and exp_loc * cap >= group else by_slots
     return plan(hidden_in, norm_gain, expert_ids, gate_weights, w_gate, w_up, w_down)
 
 

time: 75.3 us -> 73.1 us (0.971)
  local copies, waits for them, and re-layouts: 5.52 us -> 0.82 us
  waiting for transfers between devices: 19.1 us -> 21.3 us
  starting transfers between devices: 17.7 us -> 18.6 us
    unnamed x4 -> x0, local copies, waits for them, and re-layouts: 4.66 us -> none
    ppermute x16, waiting for transfers between devices: 19.1 us -> 21.3 us  [shifted(): return lax.ppermute(x, axis, pairs)]
    ppermute x16, starting transfers between devices: 17.7 us -> 18.6 us  [shifted(): return lax.ppermute(x, axis, pairs)]
    pallas_call x14 -> x12, Pallas kernels: 31.5 us -> 30.9 us  [local_call(): pl.pallas_call(kernel, out_shape=shapes, in_specs=specs, out_specs=[VMEM]...]
  transfers between devices with their start and end apart: 16 -> 16, of which waited for: 9 -> 10; matrix products, arithmetic and copies ran while one was open for 1% -> 1% of each run, Pallas kernels for 29% -> 24%
where the time goes in v5:
time: 73.1 us; the launch traced here: 72.9 us
  Pallas kernels  30.9 us (42%)
  waiting for transfers between devices  21.3 us (29%)
  starting transfers between devices  18.6 us (25%)
  other arithmetic  1.03 us (1%)
  local copies, waits for them, and re-layouts  0.82 us (1%)
    pallas_call x12, Pallas kernels, local_call(): pl.pallas_call(kernel, out_shape=shapes, in_specs=specs, out_specs=[VMEM]...  30.9 us
    ppermute x16, waiting for transfers between devices, shifted(): return lax.ppermute(x, axis, pairs)  21.3 us
    ppermute x16, starting transfers between devices, shifted(): return lax.ppermute(x, axis, pairs)  18.6 us
  transfers between devices with their start and end apart: 16, of which 10 were waited for; matrix products, arithmetic and copies ran while one was open for 1% of the time, Pallas kernels for 24%

profile of v5, /device:TPU:0, one launch (start us, length us, event | category | flops | bytes accessed | tf_op | source)
XLA Modules:
  0.0 72.9 jit_solution(485556409480900452)
XLA Ops:
  0.0 0.1 pad_add_fusion.pos_ref
  0.1 1.4 %shard_map.73.refs_0_ = bf16[8,4224]{1,0:T(8,128)(2,1)S(1)} custom-call(s32[2]{0:T(128)S(1)} %pad_add_fusion.pos_ref, s32[8,16]{1,0:T(8,128)} %bitcast.24, f32[8,16]{1,0:T(8,128)} %bitcast.25, bf16[8,4096]{1,0:T(8,128)(2,1)} %values_ref.1), custom_call_target="tpu_custom_call" | custom-call | tf_op jit(solution)/shard_map/pallas_call | solution.py:268
  1.5 3.1 %collective-permute-start = (bf16[8,4224]{1,0:T(8,128)(2,1)S(1)}, bf16[8,4224]{1,0:T(8,128)(2,1)S(1)}, u32[]{:S(2)}, u32[]{:S(2)}) collective-permute-start(bf16[8,4224]{1,0:T(8,128)(2,1)S(1)} %shard_map.73.refs_0_), channel_id=1, source_target_pairs={{0,4},{1,5},{2,6},{3,7},{4,8},{5,9},{6,10},{7,11},{8,12},{9,13},{1... | collective-permute-start | bytes 202760 | tf_op jit(solution)/shard_map/ppermute | solution.py:31
  4.6 2.6 %collective-permute-start.1 = (bf16[8,4224]{1,0:T(8,128)(2,1)S(1)}, bf16[8,4224]{1,0:T(8,128)(2,1)S(1)}, u32[]{:S(2)}, u32[]{:S(2)}) collective-permute-start(bf16[8,4224]{1,0:T(8,128)(2,1)S(1)} %shard_map.73.refs_0_), channel_id=1, source_target_pairs={{0,8},{1,9},{2,10},{3,11},{4,12},{5,13},{6,14},{7,15},{8,0},{9,1},... | collective-permute-start | bytes 202760 | tf_op jit(solution)/shard_map/ppermute | solution.py:31
  7.2 1.3 %collective-permute-start.2 = (bf16[8,4224]{1,0:T(8,128)(2,1)S(1)}, bf16[8,4224]{1,0:T(8,128)(2,1)S(1)}, u32[]{:S(2)}, u32[]{:S(2)}) collective-permute-start(bf16[8,4224]{1,0:T(8,128)(2,1)S(1)} %shard_map.73.refs_0_), channel_id=1, source_target_pairs={{0,12},{1,13},{2,14},{3,15},{4,0},{5,1},{6,2},{7,3},{8,4},{9,5},{1... | collective-permute-start | bytes 202760 | tf_op jit(solution)/shard_map/ppermute | solution.py:31
  8.5 0.7 reshape.39.refs_0_.gain_ref
  9.2 3.5 %shard_map.74 = (bf16[2,4096,512]{2,1,0:T(8,128)(2,1)S(1)}, f32[8,128]{1,0:T(8,128)S(1)}) custom-call(bf16[4,4096,512]{2,1,0:T(8,128)(2,1)} %refs_6_.1, bf16[1,4096]{1,0:T(2,128)(2,1)S(1)} %reshape.39.refs_0_.gain_ref), custom_call_target="tpu_custom_call" | custom-call | bytes 8388608 | tf_op jit(solution)/shard_map/pallas_call | solution.py:268
  12.7 0.0 collective-permute-done.refs_1_
  12.8 0.0 collective-permute-done.1.refs_2_
  12.8 0.0 collective-permute-done.2.refs_3_
  12.8 0.6 shard_map.75
  13.4 1.5 %collective-permute-start.5 = (bf16[32,2176]{1,0:T(8,128)(2,1)S(1)}, bf16[32,2176]{1,0:T(8,128)(2,1)S(1)}, u32[]{:S(2)}, u32[]{:S(2)}) collective-permute-start(bf16[32,2176]{1,0:T(8,128)(2,1)S(1)} %get-tuple-element.30.refs_0_), channel_id=1, source_target_pairs={{0,2},{1,3},{2,0},{3,1},{4,6},{5,7},{6,4},{7,5},{8,10},{9,11},{10,... | collective-permute-start | bytes 417800 | tf_op jit(solution)/shard_map/ppermute | solution.py:31
  14.9 1.5 %collective-permute-start.3 = (bf16[32,2048]{1,0:T(8,128)(2,1)S(1)}, bf16[32,2048]{1,0:T(8,128)(2,1)S(1)}, u32[]{:S(2)}, u32[]{:S(2)}) collective-permute-start(bf16[32,2048]{1,0:T(8,128)(2,1)S(1)} %get-tuple-element.27.refs_0_), channel_id=1, source_target_pairs={{0,16},{16,0},{1,17},{17,1},{2,18},{18,2},{3,19},{19,3},{4,20},{20... | collective-permute-start | bytes 393224 | tf_op jit(solution)/shard_map/ppermute | solution.py:31
  16.4 2.0 %collective-permute-done.5.refs_1_ = bf16[32,2176]{1,0:T(8,128)(2,1)S(1)} collective-permute-done((bf16[32,2176]{1,0:T(8,128)(2,1)S(1)}, bf16[32,2176]{1,0:T(8,128)(2,1)S(1)}, u32[]{:S(2)}, u32[]{:S(2)}) %collective-permute-start.5) | collective-permute-done | bytes 139296 | tf_op jit(solution)/shard_map/ppermute | solution.py:31
  18.5 1.6 %collective-permute-start.6 = (bf16[64,2176]{1,0:T(8,128)(2,1)S(1)}, bf16[64,2176]{1,0:T(8,128)(2,1)S(1)}, u32[]{:S(2)}, u32[]{:S(2)}) collective-permute-start(bf16[64,2176]{1,0:T(8,128)(2,1)S(1)} %get-tuple-element.31.refs_0_), channel_id=1, source_target_pairs={{0,16},{16,0},{1,17},{17,1},{2,18},{18,2},{3,19},{19,3},{4,20},{20... | collective-permute-start | bytes 835592 | tf_op jit(solution)/shard_map/ppermute | solution.py:31
  20.0 0.8 %collective-permute-done.3.refs_1_ = bf16[32,2048]{1,0:T(8,128)(2,1)S(1)} collective-permute-done((bf16[32,2048]{1,0:T(8,128)(2,1)S(1)}, bf16[32,2048]{1,0:T(8,128)(2,1)S(1)}, u32[]{:S(2)}, u32[]{:S(2)}) %collective-permute-start.3) | collective-permute-done | bytes 131104 | tf_op jit(solution)/shard_map/ppermute | solution.py:31
  20.8 0.6 shard_map.76
  21.5 0.7 collective-permute-start.4
  22.2 3.5 %shard_map.79 = (bf16[2,4096,512]{2,1,0:T(8,128)(2,1)S(1)}, f32[8,128]{1,0:T(8,128)S(1)}) custom-call(bf16[4,4096,512]{2,1,0:T(8,128)(2,1)} %refs_7_.1, f32[8,128]{1,0:T(8,128)S(1)} %get-tuple-element.32.refs_0_), custom_call_target="tpu_custom_call" | custom-call | bytes 8388608 | tf_op jit(solution)/shard_map/pallas_call | solution.py:268
  25.7 0.2 collective-permute-done.6.refs_1_
  25.8 0.6 shard_map.80
  26.5 0.0 collective-permute-start.7
  26.5 1.4 %collective-permute-done.4.refs_1_ = bf16[64,2048]{1,0:T(8,128)(2,1)S(1)} collective-permute-done((bf16[64,2048]{1,0:T(8,128)(2,1)S(1)}, bf16[64,2048]{1,0:T(8,128)(2,1)S(1)}, u32[]{:S(2)}, u32[]{:S(2)}) %collective-permute-start.4) | collective-permute-done | bytes 262176 | tf_op jit(solution)/shard_map/ppermute | solution.py:31
  27.8 0.6 shard_map.77
  28.5 0.0 collective-permute-start.8
  28.5 1.9 %collective-permute-done.8.refs_3_ = bf16[128,2048]{1,0:T(8,128)(2,1)S(1)} collective-permute-done((bf16[128,2048]{1,0:T(8,128)(2,1)S(1)}, bf16[128,2048]{1,0:T(8,128)(2,1)S(1)}, u32[]{:S(2)}, u32[]{:S(2)}) %collective-permute-start.8) | collective-permute-done | bytes 524320 | tf_op jit(solution)/shard_map/ppermute | solution.py:31
  30.4 0.0 collective-permute-done.7.refs_1_
  30.4 8.3 %shard_map.81 = (bf16[2,64,512]{2,1,0:T(8,128)(2,1)S(1)}, bf16[4,64,4096]{2,1,0:T(8,128)(2,1)S(1)}, bf16[256,256]{1,0:T(8,128)(2,1)S(1)}, bf16[256,256]{1,0:T(8,...) custom-call(s32[2]{0:T(128)S(1)} %pad_add_fusion.pos_ref, ...), custom_call_target="tpu_custom_call" | custom-call | flops 1610612736 | bytes 16777216 | tf_op jit(solution)/shard_map/pallas_call | solution.py:268
  38.7 1.6 %collective-permute-start.10 = (bf16[2,64,512]{2,1,0:T(8,128)(2,1)S(1)}, bf16[2,64,512]{2,1,0:T(8,128)(2,1)S(1)}, u32[]{:S(2)}, u32[]{:S(2)}) collective-permute-start(bf16[2,64,512]{2,1,0:T(8,128)(2,1)S(1)} %get-tuple-element.43.refs_0_), channel_id=1, source_target_pairs={{0,16},{16,0},{1,17},{17,1},{2,18},{18,2},{3,19},{19,3},{4,20},{20... | collective-permute-start | bytes 393224 | tf_op jit(solution)/shard_map/ppermute | solution.py:31
  40.3 3.5 %shard_map.82 = (bf16[2,64,512]{2,1,0:T(8,128)(2,1)S(1)}, bf16[2,1024,2048]{2,1,0:T(8,128)(2,1)S(1)}) custom-call(bf16[4,64,4096]{2,1,0:T(8,128)(2,1)S(1)} %get-tuple-element.39.normed_ref, bf16[2,4096,512]{2,1,0:T(8,128)(2,1)S(1)} %get-tuple-element.40.gate_ref, bf16[2,4096,512]{2,1,0:T(8,128)(2,1)S(1)} %get-tuple-element.41.up_ref, ...), custom_call_target="tpu_custom_call" | custom-call | flops 1073741824 | bytes 16777216 | tf_op jit(solution)/shard_map/pallas_call | solution.py:268
  43.8 0.6 collective-permute-start.9
  44.4 0.0 collective-permute-done.10.refs_1_
  44.4 5.5 %shard_map.83 = (bf16[128,2048]{1,0:T(8,128)(2,1)S(1)}, bf16[2,1024,2048]{2,1,0:T(8,128)(2,1)S(1)}) custom-call(s32[2]{0:T(128)S(1)} %pad_add_fusion.pos_ref, bf16[2,64,512]{2,1,0:T(8,128)(2,1)S(1)} %get-tuple-element.43.refs_0_, bf16[2,64,512]{2,1,0:T(8,128)(2,1)S(1)} %collective-permute-done.10.refs_1_, ...), custom_call_target="tpu_custom_call" | custom-call | flops 536870912 | bytes 8388608 | tf_op jit(solution)/shard_map/pallas_call | solution.py:268
  49.9 0.0 collective-permute-done.9.refs_1_
  49.9 2.7 %shard_map.84 = bf16[256,2048]{1,0:T(8,128)(2,1)S(1)} custom-call(s32[2]{0:T(128)S(1)} %pad_add_fusion.pos_ref, bf16[256,256]{1,0:T(8,128)(2,1)S(1)} %get-tuple-element.37.high_ref, bf16[256,256]{1,0:T(8,128)(2,1)S(1)} %get-tuple-element.38.low_ref, bf16[2,64,512]{2,1,0:T(8,128)(2,1)S(1)} %get-tuple-element.42.refs_0_, ...), custom_call_target="tpu_custom_call" | custom-call | flops 1073741824 | bytes 16777216 | tf_op jit(solution)/shard_map/pallas_call | solution.py:268
  52.6 0.1 fusion.4
  52.7 0.1 collective-permute-start.11
  52.8 1.9 %collective-permute-done.11 = bf16[8,16,2048]{2,1,0:T(8,128)(2,1)S(1)} collective-permute-done((bf16[8,16,2048]{2,1,0:T(8,128)(2,1)S(1)}, bf16[8,16,2048]{2,1,0:T(8,128)(2,1)S(1)}, u32[]{:S(2)}, u32[]{:S(2)}) %collective-permute-start.11) | collective-permute-done | bytes 524320 | tf_op jit(solution)/shard_map/ppermute | solution.py:31
  54.7 0.1 fusion
  54.8 0.8 %collective-permute-start.12 = (bf16[4,16,2048]{2,1,0:T(8,128)(2,1)S(1)}, bf16[4,16,2048]{2,1,0:T(8,128)(2,1)S(1)}, u32[]{:S(2)}, u32[]{:S(2)}) collective-permute-start(bf16[4,16,2048]{2,1,0:T(8,128)(2,1)S(1)} %slice.63), channel_id=1, source_target_pairs={{0,2},{1,3},{2,0},{3,1},{4,6},{5,7},{6,4},{7,5},{8,10},{9,11},{10,... | collective-permute-start | bytes 786440 | tf_op jit(solution)/shard_map/ppermute | solution.py:31
  55.6 7.6 %collective-permute-done.12 = bf16[4,16,2048]{2,1,0:T(8,128)(2,1)S(1)} collective-permute-done((bf16[4,16,2048]{2,1,0:T(8,128)(2,1)S(1)}, bf16[4,16,2048]{2,1,0:T(8,128)(2,1)S(1)}, u32[]{:S(2)}, u32[]{:S(2)}) %collective-permute-start.12) | collective-permute-done | bytes 262176 | tf_op jit(solution)/shard_map/ppermute | solution.py:31
  63.2 0.1 add_convert_fusion
  63.3 2.7 %collective-permute-start.13 = (bf16[1,16,2048]{2,1,0:T(8,128)(2,1)S(1)}, bf16[1,16,2048]{2,1,0:T(8,128)(2,1)S(1)}, u32[]{:S(2)}, u32[]{:S(2)}) collective-permute-start(bf16[1,16,2048]{2,1,0:T(8,128)(2,1)S(1)} %get-tuple-element.49), channel_id=1, source_target_pairs={{0,12},{1,13},{2,14},{3,15},{4,0},{5,1},{6,2},{7,3},{8,4},{9,5},{1... | collective-permute-start | bytes 196616 | tf_op jit(solution)/shard_map/ppermute | solution.py:31
  66.0 0.0 collective-permute-start.14
  66.0 0.6 collective-permute-start.15
  66.7 1.6 %collective-permute-done.13 = bf16[1,16,2048]{2,1,0:T(8,128)(2,1)S(1)} collective-permute-done((bf16[1,16,2048]{2,1,0:T(8,128)(2,1)S(1)}, bf16[1,16,2048]{2,1,0:T(8,128)(2,1)S(1)}, u32[]{:S(2)}, u32[]{:S(2)}) %collective-permute-start.13) | collective-permute-done | bytes 65568 | tf_op jit(solution)/shard_map/ppermute | solution.py:31
  68.3 3.1 %collective-permute-done.14 = bf16[1,16,2048]{2,1,0:T(8,128)(2,1)S(1)} collective-permute-done((bf16[1,16,2048]{2,1,0:T(8,128)(2,1)S(1)}, bf16[1,16,2048]{2,1,0:T(8,128)(2,1)S(1)}, u32[]{:S(2)}, u32[]{:S(2)}) %collective-permute-start.14) | collective-permute-done | bytes 65568 | tf_op jit(solution)/shard_map/ppermute | solution.py:31
  71.4 0.7 collective-permute-done.15
  72.1 0.1 fusion.1
  72.3 0.6 pad_maximum_fusion
  (6 shorter events, 0.1 us)
Async XLA Ops:
  1.5 11.2 %collective-permute-start = (bf16[8,4224]{1,0:T(8,128)(2,1)S(1)}, bf16[8,4224]{1,0:T(8,128)(2,1)S(1)}, u32[]{:S(2)}, u32[]{:S(2)}) collective-permute-start(bf16[8,4224]{1,0:T(8,128)(2,1)S(1)} %shard_map.73.refs_0_), channel_id=1, source_target_pairs={{0,4},{1,5},{2,6},{3,7},{4,8},{5,9},{6,10},{7,11},{8,12},{9,13},{1... | collective-permute-start | bytes 202760 | tf_op jit(solution)/shard_map/ppermute | solution.py:31
  4.6 8.2 %collective-permute-start.1 = (bf16[8,4224]{1,0:T(8,128)(2,1)S(1)}, bf16[8,4224]{1,0:T(8,128)(2,1)S(1)}, u32[]{:S(2)}, u32[]{:S(2)}) collective-permute-start(bf16[8,4224]{1,0:T(8,128)(2,1)S(1)} %shard_map.73.refs_0_), channel_id=1, source_target_pairs={{0,8},{1,9},{2,10},{3,11},{4,12},{5,13},{6,14},{7,15},{8,0},{9,1},... | collective-permute-start | bytes 202760 | tf_op jit(solution)/shard_map/ppermute | solution.py:31
  7.2 5.6 %collective-permute-start.2 = (bf16[8,4224]{1,0:T(8,128)(2,1)S(1)}, bf16[8,4224]{1,0:T(8,128)(2,1)S(1)}, u32[]{:S(2)}, u32[]{:S(2)}) collective-permute-start(bf16[8,4224]{1,0:T(8,128)(2,1)S(1)} %shard_map.73.refs_0_), channel_id=1, source_target_pairs={{0,12},{1,13},{2,14},{3,15},{4,0},{5,1},{6,2},{7,3},{8,4},{9,5},{1... | collective-permute-start | bytes 202760 | tf_op jit(solution)/shard_map/ppermute | solution.py:31
  13.4 5.1 %collective-permute-start.5 = (bf16[32,2176]{1,0:T(8,128)(2,1)S(1)}, bf16[32,2176]{1,0:T(8,128)(2,1)S(1)}, u32[]{:S(2)}, u32[]{:S(2)}) collective-permute-start(bf16[32,2176]{1,0:T(8,128)(2,1)S(1)} %get-tuple-element.30.refs_0_), channel_id=1, source_target_pairs={{0,2},{1,3},{2,0},{3,1},{4,6},{5,7},{6,4},{7,5},{8,10},{9,11},{10,... | collective-permute-start | bytes 417800 | tf_op jit(solution)/shard_map/ppermute | solution.py:31
  14.9 5.9 %collective-permute-start.3 = (bf16[32,2048]{1,0:T(8,128)(2,1)S(1)}, bf16[32,2048]{1,0:T(8,128)(2,1)S(1)}, u32[]{:S(2)}, u32[]{:S(2)}) collective-permute-start(bf16[32,2048]{1,0:T(8,128)(2,1)S(1)} %get-tuple-element.27.refs_0_), channel_id=1, source_target_pairs={{0,16},{16,0},{1,17},{17,1},{2,18},{18,2},{3,19},{19,3},{4,20},{20... | collective-permute-start | bytes 393224 | tf_op jit(solution)/shard_map/ppermute | solution.py:31
  18.5 7.4 %collective-permute-start.6 = (bf16[64,2176]{1,0:T(8,128)(2,1)S(1)}, bf16[64,2176]{1,0:T(8,128)(2,1)S(1)}, u32[]{:S(2)}, u32[]{:S(2)}) collective-permute-start(bf16[64,2176]{1,0:T(8,128)(2,1)S(1)} %get-tuple-element.31.refs_0_), channel_id=1, source_target_pairs={{0,16},{16,0},{1,17},{17,1},{2,18},{18,2},{3,19},{19,3},{4,20},{20... | collective-permute-start | bytes 835592 | tf_op jit(solution)/shard_map/ppermute | solution.py:31
  21.5 6.4 %collective-permute-start.4 = (bf16[64,2048]{1,0:T(8,128)(2,1)S(1)}, bf16[64,2048]{1,0:T(8,128)(2,1)S(1)}, u32[]{:S(2)}, u32[]{:S(2)}) collective-permute-start(bf16[64,2048]{1,0:T(8,128)(2,1)S(1)} %get-tuple-element.28.refs_0_), channel_id=1, source_target_pairs={{0,2},{1,3},{2,0},{3,1},{4,6},{5,7},{6,4},{7,5},{8,10},{9,11},{10,... | collective-permute-start | bytes 786440 | tf_op jit(solution)/shard_map/ppermute | solution.py:31
  26.5 3.9 %collective-permute-start.7 = (bf16[128,2176]{1,0:T(8,128)(2,1)S(1)}, bf16[128,2176]{1,0:T(8,128)(2,1)S(1)}, u32[]{:S(2)}, u32[]{:S(2)}) collective-permute-start(bf16[128,2176]{1,0:T(8,128)(2,1)S(1)} %get-tuple-element.34.refs_0_), channel_id=1, source_target_pairs={{0,1},{1,0},{2,3},{3,2},{4,5},{5,4},{6,7},{7,6},{8,9},{9,8},{10,11... | collective-permute-start | bytes 1671176 | tf_op jit(solution)/shard_map/ppermute | solution.py:31
  28.5 1.9 %collective-permute-start.8 = (bf16[128,2048]{1,0:T(8,128)(2,1)S(1)}, bf16[128,2048]{1,0:T(8,128)(2,1)S(1)}, u32[]{:S(2)}, u32[]{:S(2)}) collective-permute-start(bf16[128,2048]{1,0:T(8,128)(2,1)S(1)} %get-tuple-element.29.refs_2_), channel_id=1, source_target_pairs={{0,1},{1,0},{2,3},{3,2},{4,5},{5,4},{6,7},{7,6},{8,9},{9,8},{10,11... | collective-permute-start | bytes 1572872 | tf_op jit(solution)/shard_map/ppermute | solution.py:31
  38.7 5.7 %collective-permute-start.10 = (bf16[2,64,512]{2,1,0:T(8,128)(2,1)S(1)}, bf16[2,64,512]{2,1,0:T(8,128)(2,1)S(1)}, u32[]{:S(2)}, u32[]{:S(2)}) collective-permute-start(bf16[2,64,512]{2,1,0:T(8,128)(2,1)S(1)} %get-tuple-element.43.refs_0_), channel_id=1, source_target_pairs={{0,16},{16,0},{1,17},{17,1},{2,18},{18,2},{3,19},{19,3},{4,20},{20... | collective-permute-start | bytes 393224 | tf_op jit(solution)/shard_map/ppermute | solution.py:31
  43.8 6.1 %collective-permute-start.9 = (bf16[2,64,512]{2,1,0:T(8,128)(2,1)S(1)}, bf16[2,64,512]{2,1,0:T(8,128)(2,1)S(1)}, u32[]{:S(2)}, u32[]{:S(2)}) collective-permute-start(bf16[2,64,512]{2,1,0:T(8,128)(2,1)S(1)} %get-tuple-element.42.refs_0_), channel_id=1, source_target_pairs={{0,16},{16,0},{1,17},{17,1},{2,18},{18,2},{3,19},{19,3},{4,20},{20... | collective-permute-start | bytes 393224 | tf_op jit(solution)/shard_map/ppermute | solution.py:31
  52.7 2.0 %collective-permute-start.11 = (bf16[8,16,2048]{2,1,0:T(8,128)(2,1)S(1)}, bf16[8,16,2048]{2,1,0:T(8,128)(2,1)S(1)}, u32[]{:S(2)}, u32[]{:S(2)}) collective-permute-start(bf16[8,16,2048]{2,1,0:T(8,128)(2,1)S(1)} %bitcast.23), channel_id=1, source_target_pairs={{0,1},{1,0},{2,3},{3,2},{4,5},{5,4},{6,7},{7,6},{8,9},{9,8},{10,11... | collective-permute-start | bytes 1572872 | tf_op jit(solution)/shard_map/ppermute | solution.py:31
  54.8 8.4 %collective-permute-start.12 = (bf16[4,16,2048]{2,1,0:T(8,128)(2,1)S(1)}, bf16[4,16,2048]{2,1,0:T(8,128)(2,1)S(1)}, u32[]{:S(2)}, u32[]{:S(2)}) collective-permute-start(bf16[4,16,2048]{2,1,0:T(8,128)(2,1)S(1)} %slice.63), channel_id=1, source_target_pairs={{0,2},{1,3},{2,0},{3,1},{4,6},{5,7},{6,4},{7,5},{8,10},{9,11},{10,... | collective-permute-start | bytes 786440 | tf_op jit(solution)/shard_map/ppermute | solution.py:31
  63.3 4.9 %collective-permute-start.13 = (bf16[1,16,2048]{2,1,0:T(8,128)(2,1)S(1)}, bf16[1,16,2048]{2,1,0:T(8,128)(2,1)S(1)}, u32[]{:S(2)}, u32[]{:S(2)}) collective-permute-start(bf16[1,16,2048]{2,1,0:T(8,128)(2,1)S(1)} %get-tuple-element.49), channel_id=1, source_target_pairs={{0,12},{1,13},{2,14},{3,15},{4,0},{5,1},{6,2},{7,3},{8,4},{9,5},{1... | collective-permute-start | bytes 196616 | tf_op jit(solution)/shard_map/ppermute | solution.py:31
  66.0 5.4 %collective-permute-start.14 = (bf16[1,16,2048]{2,1,0:T(8,128)(2,1)S(1)}, bf16[1,16,2048]{2,1,0:T(8,128)(2,1)S(1)}, u32[]{:S(2)}, u32[]{:S(2)}) collective-permute-start(bf16[1,16,2048]{2,1,0:T(8,128)(2,1)S(1)} %get-tuple-element.51), channel_id=1, source_target_pairs={{0,8},{1,9},{2,10},{3,11},{4,12},{5,13},{6,14},{7,15},{8,0},{9,1},... | collective-permute-start | bytes 196616 | tf_op jit(solution)/shard_map/ppermute | solution.py:31
  66.0 6.1 %collective-permute-start.15 = (bf16[1,16,2048]{2,1,0:T(8,128)(2,1)S(1)}, bf16[1,16,2048]{2,1,0:T(8,128)(2,1)S(1)}, u32[]{:S(2)}, u32[]{:S(2)}) collective-permute-start(bf16[1,16,2048]{2,1,0:T(8,128)(2,1)S(1)} %get-tuple-element.50), channel_id=1, source_target_pairs={{0,4},{1,5},{2,6},{3,7},{4,8},{5,9},{6,10},{7,11},{8,12},{9,13},{1... | collective-permute-start | bytes 196616 | tf_op jit(solution)/shard_map/ppermute | solution.py:31

commit v6 on v4

--- a/solution.py
+++ b/solution.py
@@ -82,44 +82,51 @@
     token_ref[...] = jnp.zeros_like(token_ref)
 
 
-def join_kernel(count, *refs):
-    out_ref, token_ref = refs[-2:]
+def join_kernel(count, signs, *refs):
+    out_ref = refs[count + signs]
     rows = refs[0].shape[0]
     for i, ref in enumerate(refs[:count]):
         out_ref[i * rows : (i + 1) * rows] = ref[...]
-    token_ref[...] = jnp.zeros_like(token_ref)
-
-
-def load_kernel(start, src_ref, *refs):
-    dst_ref, token_ref, sems = refs[-3:]
-    copies = load_copies(src_ref, dst_ref, sems, start)
-    token_ref[...] = jnp.zeros_like(token_ref)
+    for ref in refs[count + signs + 1 :]:
+        ref[...] = jnp.zeros_like(ref)
+
+
+def load_kernel(start, signs, src_ref, *refs):
+    sign_ref, *near, sems = refs[signs:]
+    copies = load_copies(src_ref, near, sems, start)
+    sign_ref[...] = jnp.zeros_like(sign_ref)
     for copy in copies:
         copy.wait()
 
 
-def load_copies(src_ref, dst_ref, sems, start):
-    copies = [
-        pltpu.make_async_copy(src_ref.at[start + i], dst_ref.at[i], sems.at[i]) for i in range(dst_ref.shape[0])
-    ]
+def load_copies(src_ref, near, sems, start):
+    count, runs = sems.shape
+    size = src_ref.shape[1] // runs
+    copies = []
+    for i in range(count):
+        for r in range(runs):
+            at = pl.ds(r * size, size)
+            copies.append(pltpu.make_async_copy(src_ref.at[start + i, at], near[i].at[at], sems.at[i, r]))
     for copy in copies:
         copy.start()
     return copies
 
 
-def swiglu(normed_ref, gate_ref, up_ref, hidden_ref, start):
-    for i in range(hidden_ref.shape[0]):
+def swiglu(normed_ref, gates, ups, hidden_ref, start):
+    for i, (gate_ref, up_ref) in enumerate(zip(gates, ups)):
         x = normed_ref[start + i]
-        gate_act = jnp.dot(x, gate_ref[i], preferred_element_type=jnp.float32)
-        up_act = jnp.dot(x, up_ref[i], preferred_element_type=jnp.float32)
+        gate_act = jnp.dot(x, gate_ref[...], preferred_element_type=jnp.float32)
+        up_act = jnp.dot(x, up_ref[...], preferred_element_type=jnp.float32)
         hidden_ref[i] = (gate_act / (1.0 + jnp.exp(-gate_act)) * up_act).astype(jnp.bfloat16)
 
 
-def select_kernel(dims, pos_ref, gain_ref, *refs):
+def select_kernel(dims, lead, tail, pos_ref, gain_ref, *refs):
     n_fast, n_mid, n_tp, slow_n, tok_dev, top, exp_loc, rows, half = dims
     first, second = refs[:n_fast], refs[n_fast : 2 * n_fast]
-    gate_ref, up_ref, far_ref, hidden_ref, near_ref, normed_ref, high_ref, low_ref, sems = refs[2 * n_fast :]
-    copies = load_copies(far_ref, near_ref, sems, 0)
+    refs = refs[2 * n_fast :]
+    gates, ups, refs = refs[:lead], refs[lead : 2 * lead], refs[2 * lead :]
+    far_ref, hidden_ref, normed_ref, mix_ref, turned_ref, *near, sems = refs
+    copies = load_copies(far_ref, near, sems, lead)
     tp_pos, base = pos_ref[0], pos_ref[1]
     run = slow_n * tok_dev
     tokens = n_fast * n_mid * n_tp * run
@@ -137,7 +144,7 @@
     before = number((tokens, tokens), 1) < number((tokens, tokens), 0)
     match = [ids == (base + e).astype(jnp.float32) for e in range(exp_loc)]
     hits = [jnp.sum(m.astype(jnp.float32), axis=1, keepdims=True) for m in match]
-    gates = [jnp.sum(jnp.where(m, weights, 0.0), axis=1, keepdims=True) for m in match]
+    shares = [jnp.sum(jnp.where(m, weights, 0.0), axis=1, keepdims=True) for m in match]
     lane = lax.broadcasted_iota(jnp.int32, (tokens, LANES), 1)
     hit = functools.reduce(
         lambda a, e: jnp.where(lane == e, hits[e], a),
@@ -155,19 +162,19 @@
         place = jnp.where(hits[e] > 0, position[:, e : e + 1], -1.0)
         pick = slot == place
         picks.append(pick.astype(jnp.float32))
-        spreads.append(jnp.where(pick, gates[e], 0.0))
+        spreads.append(jnp.where(pick, shares[e], 0.0))
     spread = jnp.concatenate(spreads, axis=1)
-    blocks = []
-    for f in range(n_fast):
-        for m in range(n_mid):
-            for s in range(slow_n):
-                for t in range(n_tp):
-                    start = (((f * n_tp + t) * n_mid + m) * slow_n + s) * tok_dev
-                    blocks.append(spread[start : start + tok_dev])
-    spread = jnp.concatenate(blocks, axis=0)
-    high = spread.astype(jnp.bfloat16)
-    high_ref[...] = high
-    low_ref[...] = (spread - high.astype(jnp.float32)).astype(jnp.bfloat16)
+    group = lambda f, m, s: [
+        spread[start : start + tok_dev]
+        for start in [(((f * n_tp + t) * n_mid + m) * slow_n + s) * tok_dev for t in range(n_tp)]
+    ]
+    blocks = [b for f in range(n_fast) for m in range(n_mid) for s in range(slow_n) for b in group(f, m, s)]
+    turned = [b for f in range(n_fast) for s in range(slow_n) for m in range(n_mid) for b in group(f, m, s)]
+    for ref, rows_of in ((mix_ref, blocks), (turned_ref, turned)):
+        exact = jnp.concatenate(rows_of, axis=0)
+        high = exact.astype(jnp.bfloat16)
+        ref[0] = high
+        ref[1] = (exact - high.astype(jnp.float32)).astype(jnp.bfloat16)
 
     part = n_mid * n_tp * run
     gain = gain_ref[...].astype(jnp.float32)
@@ -199,48 +206,53 @@
         scale = lax.rsqrt(squares / (2 * half) + 1e-06)
         normed_ref[e, :, :half] = (left * scale * gain[:, :half]).astype(jnp.bfloat16)
         normed_ref[e, :, half:] = (right * scale * gain[:, half:]).astype(jnp.bfloat16)
-    swiglu(normed_ref, gate_ref, up_ref, hidden_ref, 0)
+    swiglu(normed_ref, gates, ups, hidden_ref, 0)
     for copy in copies:
         copy.wait()
 
 
-def up_kernel(start, normed_ref, gate_ref, up_ref, far_ref, hidden_ref, near_ref, sems):
-    copies = load_copies(far_ref, near_ref, sems, start)
-    swiglu(normed_ref, gate_ref, up_ref, hidden_ref, start)
+def up_kernel(start, count, normed_ref, *refs):
+    gates, ups, (far_ref, hidden_ref, *near, sems) = refs[:count], refs[count : 2 * count], refs[2 * count :]
+    copies = load_copies(far_ref, near, sems, 0)
+    swiglu(normed_ref, gates, ups, hidden_ref, start)
     for copy in copies:
         copy.wait()
 
 
-def lower(n_tp, tp_pos, pieces, down_ref, i):
+def lower(n_tp, tp_pos, pieces, i, down_ref, columns):
     hid_part = pieces[0].shape[2]
     total = 0.0
     for s in range(n_tp):
         begin = pl.multiple_of(lax.rem(tp_pos - s + n_tp, n_tp) * hid_part, hid_part)
         total = total + jnp.dot(
-            pieces[s][i], down_ref[i, pl.ds(begin, hid_part), :], preferred_element_type=jnp.float32
+            pieces[s][i], down_ref[pl.ds(begin, hid_part), columns], preferred_element_type=jnp.float32
         )
     return total.astype(jnp.bfloat16)
 
 
-def down_kernel(n_tp, pos_ref, *refs):
-    pieces, (down_ref, out_ref) = refs[:n_tp], refs[n_tp:]
-    rows = pieces[0].shape[1]
-    for i in range(down_ref.shape[0]):
-        out_ref[i * rows : (i + 1) * rows] = lower(n_tp, pos_ref[0], pieces, down_ref, i)
-
-
-def mix_kernel(n_tp, pos_ref, high_ref, low_ref, *refs):
-    pieces, down_ref, done, (partial_ref, out_ref) = refs[:n_tp], refs[n_tp], refs[n_tp + 1 : -2], refs[-2:]
-    rows, at = pieces[0].shape[1], 0
-    for ref in done:
-        out_ref[at : at + ref.shape[0]] = ref[...]
-        at += ref.shape[0]
-    for i in range(down_ref.shape[0]):
-        out_ref[at : at + rows] = lower(n_tp, pos_ref[0], pieces, down_ref, i)
+def down_kernel(n_tp, done, pos_ref, *refs):
+    pieces, refs = refs[:n_tp], refs[n_tp:]
+    count, rows, _ = pieces[0].shape
+    downs, (far_ref, out_ref, *near, sems) = refs[:count], refs[count:]
+    copies = load_copies(far_ref, near, sems, done)
+    for i, ref in enumerate(downs):
+        out_ref[i * rows : (i + 1) * rows] = lower(n_tp, pos_ref[0], pieces, i, ref, slice(None))
+    for copy in copies:
+        copy.wait()
+
+
+def mix_kernel(n_tp, begin, pos_ref, mix_ref, done_ref, *refs):
+    pieces, (*downs, partial_ref, out_ref) = refs[:n_tp], refs[n_tp:]
+    columns = pl.ds(begin, partial_ref.shape[1])
+    _, rows, _ = pieces[0].shape
+    at = done_ref.shape[0]
+    out_ref[:at] = done_ref[:, columns]
+    for i, ref in enumerate(downs):
+        out_ref[at : at + rows] = lower(n_tp, pos_ref[0], pieces, i, ref, columns)
         at += rows
     out = out_ref[...]
-    partial = jnp.dot(high_ref[...], out, preferred_element_type=jnp.float32)
-    partial = partial + jnp.dot(low_ref[...], out, preferred_element_type=jnp.float32)
+    partial = jnp.dot(mix_ref[0], out, preferred_element_type=jnp.float32)
+    partial = partial + jnp.dot(mix_ref[1], out, preferred_element_type=jnp.float32)
     partial_ref[...] = partial.astype(jnp.bfloat16)
 
 
@@ -248,6 +260,7 @@
 SMEM = pl.BlockSpec(memory_space=pltpu.SMEM)
 HBM = pl.BlockSpec(memory_space=pltpu.HBM)
 KEPT = pltpu.VMEM
+TOKEN = jax.ShapeDtypeStruct((8, LANES), jnp.float32)
 
 
 def local_call(kernel, shapes, operands, far=(), scratch=(), limit=8 << 20, flops=0, moved=0):
@@ -270,27 +283,32 @@
     )(*given)
 
 
-TOKEN = jax.ShapeDtypeStruct((8, LANES), jnp.float32)
+def kept(array, count):
+    return [KEPT(array.shape[1:], array.dtype)] * count
+
+
+def runs_of(array):
+    return 4 if array.shape[1] % 64 == 0 else 1
 
 
 def loaded(array, start, count, after):
-    size = (count,) + array.shape[1:]
-    return local_call(
-        functools.partial(load_kernel, start),
-        [KEPT(size, array.dtype), TOKEN],
+    sign, *near = local_call(
+        functools.partial(load_kernel, start, len(after)),
+        [TOKEN] + kept(array, count),
         [array] + after,
         far=[0],
-        scratch=[pltpu.SemaphoreType.DMA((count,))],
+        scratch=[pltpu.SemaphoreType.DMA((count, runs_of(array)))],
         limit=1 << 20,
         moved=2 * count * array.size // array.shape[0],
     )
-
-
-def joined(pieces, after):
+    return near, sign
+
+
+def joined(pieces, after, signed):
     rows, columns = pieces[0].shape
     return local_call(
-        functools.partial(join_kernel, len(pieces)),
-        [jax.ShapeDtypeStruct((len(pieces) * rows, columns), pieces[0].dtype), TOKEN],
+        functools.partial(join_kernel, len(pieces), len(after)),
+        [jax.ShapeDtypeStruct((len(pieces) * rows, columns), pieces[0].dtype)] + [TOKEN] * signed,
         list(pieces) + after,
         limit=4 << 20,
         moved=4 * len(pieces) * rows * columns,
@@ -320,9 +338,8 @@
 
     bf16 = functools.partial(jax.ShapeDtypeStruct, dtype=jnp.bfloat16)
     slots = exp_loc * rows
-    counts = [exp_loc - exp_loc // 2, exp_loc // 2] if exp_loc > 1 else [1]
-    lead = counts[0]
-    tail = counts[1:]
+    lead = exp_loc - exp_loc // 2
+    tail = exp_loc - lead
     gain = norm_gain.reshape(1, width)
     position = jnp.stack([tp_pos, ep_pos * exp_loc])
     (message,) = local_call(
@@ -347,75 +364,79 @@
         around + [sign],
         limit=4 << 20,
     )
-    up_lead, up_sign = loaded(w_up, 0, lead, [sign])
+    gate_tail, sign = loaded(w_gate, lead, tail, [sign])
     along_tp = lambda a: arrivals(a, "tp", n_tp, 1, n_tp)
     along_mid = lambda a: arrivals(a, "ep", n_ep, *mid[0]) if mid else [a]
     first, second = along_mid(first), along_tp(second)
-    first, sign = joined(first, [up_sign])
-    second, _ = joined(second, [])
-    gate_tail = [loaded(w_gate, lead, count, [sign]) for count in tail]
+    first, sign = joined(first, [sign], 1)
+    (second,) = joined(second, [], 0)
+    up_lead, sign = loaded(w_up, 0, lead, [sign])
     first, second = along_tp(first), along_mid(second)
-    first, sign = joined(first, [sign for _, sign in gate_tail])
-    second, _ = joined(second, [])
-    up_tail = [loaded(w_up, lead, count, [sign]) for count in tail]
+    (first,) = joined(first, [sign], 0)
+    (second,) = joined(second, [], 0)
     first = arrivals(first, "ep", n_ep, *fast)
     second = arrivals(second, "ep", n_ep, *fast)
 
     dims = (n_fast, n_mid, n_tp, slow_n, tok_dev, top, exp_loc, rows, half)
-    down_size = lambda count: KEPT((count,) + w_down.shape[1:], w_down.dtype)
-    operands = [position, gain] + first + second + [gate_lead, up_lead, w_down]
-    hidden, down_lead, normed, high, low = local_call(
-        functools.partial(select_kernel, dims),
+    sems = lambda array, count: pltpu.SemaphoreType.DMA((count, runs_of(array)))
+    last = max(1, tail // 2)
+    early = exp_loc - last
+    operands = [position, gain] + first + second + gate_lead + up_lead + [w_up]
+    hidden, normed, mix, turned, *up_tail = local_call(
+        functools.partial(select_kernel, dims, lead, tail),
         [
             bf16((lead, rows, hid_part)),
-            down_size(lead),
             bf16((exp_loc, rows, width)),
-            bf16((tokens, slots)),
-            bf16((tokens, slots)),
-        ],
+            bf16((2, tokens, slots)),
+            bf16((2, tokens, slots)),
+        ]
+        + kept(w_up, tail),
         operands,
         far=[len(operands) - 1],
-        scratch=[pltpu.SemaphoreType.DMA((lead,))],
+        scratch=[sems(w_up, tail)],
         flops=2 * slots * tokens * width + 4 * lead * rows * width * hid_part,
         moved=4 * lead * width * hid_part,
     )
     pieces = along_tp(hidden)
-    partial_of = lambda pieces, down, done: local_call(
-        functools.partial(mix_kernel, n_tp),
-        [bf16((tokens, col_part))],
-        [position, high, low] + pieces + [down] + done,
-        scratch=[pltpu.VMEM((slots, col_part), jnp.bfloat16)],
-        flops=2 * slots * n_tp * hid_part * col_part,
-        moved=2 * exp_loc * n_tp * hid_part * col_part,
+    operands = [normed] + gate_tail + up_tail + [w_down]
+    hidden, *down_early = local_call(
+        functools.partial(up_kernel, lead, tail),
+        [bf16((tail, rows, hid_part))] + kept(w_down, early),
+        operands,
+        far=[len(operands) - 1],
+        scratch=[sems(w_down, early)],
+        flops=4 * tail * rows * width * hid_part,
+        moved=4 * tail * width * hid_part,
+    )
+    late = along_tp(hidden)
+    operands = [position] + pieces + down_early[:lead] + [w_down]
+    done, *down_last = local_call(
+        functools.partial(down_kernel, n_tp, early),
+        [bf16((lead * rows, col_part))] + kept(w_down, last),
+        operands,
+        far=[len(operands) - 1],
+        scratch=[sems(w_down, last)],
+        flops=2 * lead * rows * n_tp * hid_part * col_part,
+        moved=2 * lead * n_tp * hid_part * col_part,
+    )
+    col_half = col_part // 2
+    mixed_of = lambda table, begin: local_call(
+        functools.partial(mix_kernel, n_tp, begin),
+        [bf16((tokens, col_half))],
+        [position, table, done] + late + down_early[lead:] + down_last,
+        scratch=[pltpu.VMEM((slots, col_half), jnp.bfloat16)],
+        flops=slots * n_tp * hid_part * col_part,
+        moved=exp_loc * n_tp * hid_part * col_part,
     )[0]
-    if not tail:
-        partial = partial_of(pieces, down_lead, [])
-    else:
-        hidden, down_tail = local_call(
-            functools.partial(up_kernel, lead),
-            [bf16((tail[0], rows, hid_part)), down_size(tail[0])],
-            [normed, gate_tail[0][0], up_tail[0][0], w_down],
-            far=[3],
-            scratch=[pltpu.SemaphoreType.DMA((tail[0],))],
-            flops=4 * tail[0] * rows * width * hid_part,
-            moved=4 * tail[0] * width * hid_part,
-        )
-        late = along_tp(hidden)
-        (done,) = local_call(
-            functools.partial(down_kernel, n_tp),
-            [bf16((lead * rows, col_part))],
-            [position] + pieces + [down_lead],
-            flops=2 * lead * rows * n_tp * hid_part * col_part,
-            moved=2 * lead * n_tp * hid_part * col_part,
-        )
-        partial = partial_of(late, down_tail, [done])
-    total = partial.reshape(n_fast, -1, group, col_part)
-    total = scattered(total, "ep", n_ep, *fast)
-    for digit in mid:
-        total = scattered(total.reshape(digit[1], -1, group, col_part), "ep", n_ep, *digit)
-    for digit in reversed(slow):
-        total = scattered(total.reshape(digit[1], -1, group, col_part), "ep", n_ep, *digit)
-    combined = total.reshape(n_tp, tok_dev, col_part)
+
+    def over(total, digits):
+        for digit in digits:
+            total = scattered(total.reshape(digit[1], -1, group, col_half), "ep", n_ep, *digit)
+        return total.reshape(n_tp, tok_dev, col_half)
+
+    right = over(mixed_of(turned, col_half), [fast] + list(reversed(slow)) + mid)
+    left = over(mixed_of(mix, 0), [fast] + mid + list(reversed(slow)))
+    combined = jnp.concatenate([left, right], axis=2)
     column = lambda a, at: lax.dynamic_slice_in_dim(a, at, col_part, 1)
     right = first[0].reshape(n_tp, -1, first[0].shape[1])[:, :tok_dev, :half]
     left = second[0].reshape(n_mid, n_tp, -1, half)[0, :, :tok_dev]
@@ -488,7 +509,7 @@
     group, top = expert_ids.shape
     exp_loc = w_gate.shape[0]
     cap = max(2, 2 * top * group // (exp_loc * lax.axis_size("ep")))
-    plan = by_tokens if exp_loc * cap >= group else by_slots
+    plan = by_tokens if exp_loc > 1 and exp_loc * cap >= group else by_slots
     return plan(hidden_in, norm_gain, expert_ids, gate_weights, w_gate, w_up, w_down)
 
 

time: 75.3 us -> 89.7 us (1.19)
  local copies, waits for them, and re-layouts: 5.52 us -> 21.5 us
  waiting for transfers between devices: 19.1 us -> 11.3 us
  starting transfers between devices: 17.7 us -> 23.3 us
    unnamed x4 -> x24, local copies, waits for them, and re-layouts: 4.66 us -> 20.7 us
    ppermute x16 -> x21, waiting for transfers between devices: 19.1 us -> 11.3 us  [shifted(): return lax.ppermute(x, axis, pairs)]
    ppermute x16 -> x21, starting transfers between devices: 17.7 us -> 23.3 us  [shifted(): return lax.ppermute(x, axis, pairs)]
  transfers between devices with their start and end apart: 16 -> 21, of which waited for: 9 -> 7; matrix products, arithmetic and copies ran while one was open for 1% -> 1% of each run, Pallas kernels for 29% -> 24%
where the time goes in v6:
time: 89.7 us; the launch traced here: 89.3 us
  Pallas kernels  31.8 us (35%)
  starting transfers between devices  23.3 us (26%)
  local copies, waits for them, and re-layouts  21.5 us (24%)
  waiting for transfers between devices  11.3 us (13%)
  other arithmetic  1.09 us (1%)
    pallas_call x14, Pallas kernels, local_call(): pl.pallas_call(kernel, out_shape=shapes, in_specs=specs, out_specs=[VMEM]...  31.8 us
    ppermute x21, starting transfers between devices, shifted(): return lax.ppermute(x, axis, pairs)  23.3 us
    unnamed x24, local copies, waits for them, and re-layouts  20.7 us
    ppermute x21, waiting for transfers between devices, shifted(): return lax.ppermute(x, axis, pairs)  11.3 us
  transfers between devices with their start and end apart: 21, of which 7 were waited for; matrix products, arithmetic and copies ran while one was open for 1% of the time, Pallas kernels for 24%

profile of v6, /device:TPU:0, one launch (start us, length us, event | category | flops | bytes accessed | tf_op | source)
XLA Modules:
  0.0 89.3 jit_solution(3764040443767811584)
XLA Ops:
  0.0 0.1 pad_add_fusion.pos_ref
  0.1 1.4 %shard_map.73.refs_0_ = bf16[8,4224]{1,0:T(8,128)(2,1)S(1)} custom-call(s32[2]{0:T(128)S(1)} %pad_add_fusion.pos_ref, s32[8,16]{1,0:T(8,128)} %bitcast.28, f32[8,16]{1,0:T(8,128)} %bitcast.29, bf16[8,4096]{1,0:T(8,128)(2,1)} %values_ref.1), custom_call_target="tpu_custom_call" | custom-call | tf_op jit(solution)/shard_map/pallas_call | solution.py:275
  1.5 3.1 %collective-permute-start = (bf16[8,4224]{1,0:T(8,128)(2,1)S(1)}, bf16[8,4224]{1,0:T(8,128)(2,1)S(1)}, u32[]{:S(2)}, u32[]{:S(2)}) collective-permute-start(bf16[8,4224]{1,0:T(8,128)(2,1)S(1)} %shard_map.73.refs_0_), channel_id=1, source_target_pairs={{0,4},{1,5},{2,6},{3,7},{4,8},{5,9},{6,10},{7,11},{8,12},{9,13},{1... | collective-permute-start | bytes 202760 | tf_op jit(solution)/shard_map/ppermute | solution.py:31
  4.6 2.6 %collective-permute-start.1 = (bf16[8,4224]{1,0:T(8,128)(2,1)S(1)}, bf16[8,4224]{1,0:T(8,128)(2,1)S(1)}, u32[]{:S(2)}, u32[]{:S(2)}) collective-permute-start(bf16[8,4224]{1,0:T(8,128)(2,1)S(1)} %shard_map.73.refs_0_), channel_id=1, source_target_pairs={{0,8},{1,9},{2,10},{3,11},{4,12},{5,13},{6,14},{7,15},{8,0},{9,1},... | collective-permute-start | bytes 202760 | tf_op jit(solution)/shard_map/ppermute | solution.py:31
  7.2 1.3 %collective-permute-start.2 = (bf16[8,4224]{1,0:T(8,128)(2,1)S(1)}, bf16[8,4224]{1,0:T(8,128)(2,1)S(1)}, u32[]{:S(2)}, u32[]{:S(2)}) collective-permute-start(bf16[8,4224]{1,0:T(8,128)(2,1)S(1)} %shard_map.73.refs_0_), channel_id=1, source_target_pairs={{0,12},{1,13},{2,14},{3,15},{4,0},{5,1},{6,2},{7,3},{8,4},{9,5},{1... | collective-permute-start | bytes 202760 | tf_op jit(solution)/shard_map/ppermute | solution.py:31
  8.5 0.7 reshape.65.refs_0_.gain_ref
  9.2 3.5 %shard_map.74 = (f32[8,128]{1,0:T(8,128)S(1)}, bf16[4096,512]{1,0:T(8,128)(2,1)S(1)}, bf16[4096,512]{1,0:T(8,128)(2,1)S(1)}) custom-call(bf16[4,4096,512]{2,1,0:T(8,128)(2,1)} %src_ref.4, bf16[1,4096]{1,0:T(2,128)(2,1)S(1)} %reshape.65.refs_0_.gain_ref), custom_call_target="tpu_custom_call" | custom-call | bytes 8388608 | tf_op jit(solution)/shard_map/pallas_call | solution.py:275
  12.7 2.0 %copy-done = bf16[4096,512]{1,0:T(8,128)(2,1)} copy-done((bf16[4096,512]{1,0:T(8,128)(2,1)}, bf16[4096,512]{1,0:T(8,128)(2,1)S(1)}, u32[]{:S(2)}) %copy-start) | copy-done | bytes 4194328
  14.8 1.9 %copy-done.2 = bf16[4096,512]{1,0:T(8,128)(2,1)} copy-done((bf16[4096,512]{1,0:T(8,128)(2,1)}, bf16[4096,512]{1,0:T(8,128)(2,1)S(1)}, u32[]{:S(2)}) %copy-start.2) | copy-done | bytes 4194328
  16.7 0.0 collective-permute-done.refs_1_
  16.7 0.0 collective-permute-done.1.refs_2_
  16.7 0.0 collective-permute-done.2.refs_3_
  16.7 1.6 %collective-permute-start.5 = (bf16[32,2176]{1,0:T(8,128)(2,1)S(1)}, bf16[32,2176]{1,0:T(8,128)(2,1)S(1)}, u32[]{:S(2)}, u32[]{:S(2)}) collective-permute-start(bf16[32,2176]{1,0:T(8,128)(2,1)S(1)} %get-tuple-element.33.refs_0_), channel_id=1, source_target_pairs={{0,2},{1,3},{2,0},{3,1},{4,6},{5,7},{6,4},{7,5},{8,10},{9,11},{10,... | collective-permute-start | bytes 417800 | tf_op jit(solution)/shard_map/ppermute | solution.py:31
  18.3 1.5 %collective-permute-start.3 = (bf16[32,2048]{1,0:T(8,128)(2,1)S(1)}, bf16[32,2048]{1,0:T(8,128)(2,1)S(1)}, u32[]{:S(2)}, u32[]{:S(2)}) collective-permute-start(bf16[32,2048]{1,0:T(8,128)(2,1)S(1)} %get-tuple-element.32.refs_0_), channel_id=1, source_target_pairs={{0,16},{16,0},{1,17},{17,1},{2,18},{18,2},{3,19},{19,3},{4,20},{20... | collective-permute-start | bytes 393224 | tf_op jit(solution)/shard_map/ppermute | solution.py:31
  19.8 3.5 %shard_map.78 = (f32[8,128]{1,0:T(8,128)S(1)}, bf16[4096,512]{1,0:T(8,128)(2,1)S(1)}, bf16[4096,512]{1,0:T(8,128)(2,1)S(1)}) custom-call(bf16[4,4096,512]{2,1,0:T(8,128)(2,1)} %src_ref.4, f32[8,128]{1,0:T(8,128)S(1)} %get-tuple-element.34.refs_0_), custom_call_target="tpu_custom_call" | custom-call | bytes 8388608 | tf_op jit(solution)/shard_map/pallas_call | solution.py:275
  23.3 2.0 %copy-done.4 = bf16[4096,512]{1,0:T(8,128)(2,1)} copy-done((bf16[4096,512]{1,0:T(8,128)(2,1)}, bf16[4096,512]{1,0:T(8,128)(2,1)S(1)}, u32[]{:S(2)}) %copy-start.4) | copy-done | bytes 4194328
  25.3 2.0 %copy-done.6 = bf16[4096,512]{1,0:T(8,128)(2,1)} copy-done((bf16[4096,512]{1,0:T(8,128)(2,1)}, bf16[4096,512]{1,0:T(8,128)(2,1)S(1)}, u32[]{:S(2)}) %copy-start.6) | copy-done | bytes 4194328
  27.3 0.0 collective-permute-done.5.refs_1_
  27.3 0.6 collective-permute-start.6
  27.9 0.0 collective-permute-done.3.refs_1_
  27.9 0.6 collective-permute-start.4
  28.5 3.5 %shard_map.80 = (f32[8,128]{1,0:T(8,128)S(1)}, bf16[4096,512]{1,0:T(8,128)(2,1)S(1)}, bf16[4096,512]{1,0:T(8,128)(2,1)S(1)}) custom-call(bf16[4,4096,512]{2,1,0:T(8,128)(2,1)} %refs_8_.1, f32[8,128]{1,0:T(8,128)S(1)} %get-tuple-element.37.refs_0_), custom_call_target="tpu_custom_call" | custom-call | bytes 8388608 | tf_op jit(solution)/shard_map/pallas_call | solution.py:275
  32.0 2.0 %copy-done.8 = bf16[4096,512]{1,0:T(8,128)(2,1)} copy-done((bf16[4096,512]{1,0:T(8,128)(2,1)}, bf16[4096,512]{1,0:T(8,128)(2,1)S(1)}, u32[]{:S(2)}) %copy-start.8) | copy-done | bytes 4194328
  34.0 2.0 %copy-done.10 = bf16[4096,512]{1,0:T(8,128)(2,1)} copy-done((bf16[4096,512]{1,0:T(8,128)(2,1)}, bf16[4096,512]{1,0:T(8,128)(2,1)S(1)}, u32[]{:S(2)}) %copy-start.10) | copy-done | bytes 4194328
  36.0 0.0 collective-permute-done.6.refs_1_
  36.0 0.1 collective-permute-start.7
  36.1 0.0 collective-permute-done.4.refs_1_
  36.2 0.5 collective-permute-start.8
  36.7 2.1 %collective-permute-done.8.refs_3_ = bf16[128,2048]{1,0:T(8,128)(2,1)S(1)} collective-permute-done((bf16[128,2048]{1,0:T(8,128)(2,1)S(1)}, bf16[128,2048]{1,0:T(8,128)(2,1)S(1)}, u32[]{:S(2)}, u32[]{:S(2)}) %collective-permute-start.8) | collective-permute-done | bytes 524320 | tf_op jit(solution)/shard_map/ppermute | solution.py:31
  38.8 2.2 %copy-done.1 = bf16[4096,512]{1,0:T(8,128)(2,1)S(1)} copy-done((bf16[4096,512]{1,0:T(8,128)(2,1)S(1)}, bf16[4096,512]{1,0:T(8,128)(2,1)}, u32[]{:S(2)}) %copy-start.1) | copy-done | bytes 4194328
  41.0 2.2 %copy-done.3 = bf16[4096,512]{1,0:T(8,128)(2,1)S(1)} copy-done((bf16[4096,512]{1,0:T(8,128)(2,1)S(1)}, bf16[4096,512]{1,0:T(8,128)(2,1)}, u32[]{:S(2)}) %copy-start.3) | copy-done | bytes 4194328
  43.2 2.2 %copy-done.9 = bf16[4096,512]{1,0:T(8,128)(2,1)S(1)} copy-done((bf16[4096,512]{1,0:T(8,128)(2,1)S(1)}, bf16[4096,512]{1,0:T(8,128)(2,1)}, u32[]{:S(2)}) %copy-start.9) | copy-done | bytes 4194328
  45.4 2.2 %copy-done.11 = bf16[4096,512]{1,0:T(8,128)(2,1)S(1)} copy-done((bf16[4096,512]{1,0:T(8,128)(2,1)S(1)}, bf16[4096,512]{1,0:T(8,128)(2,1)}, u32[]{:S(2)}) %copy-start.11) | copy-done | bytes 4194328
  47.6 7.6 %shard_map.82 = (bf16[2,64,512]{2,1,0:T(8,128)(2,1)S(1)}, bf16[4,64,4096]{2,1,0:T(8,128)(2,1)S(1)}, bf16[2,256,256]{2,1,0:T(8,128)(2,1)S(1)}, bf16[2,256,256]{2,...) custom-call(s32[2]{0:T(128)S(1)} %pad_add_fusion.pos_ref, ...), custom_call_target="tpu_custom_call" | custom-call | flops 1610612736 | bytes 16777216 | tf_op jit(solution)/shard_map/pallas_call | solution.py:275
  55.2 1.6 %collective-permute-start.9 = (bf16[2,64,512]{2,1,0:T(8,128)(2,1)S(1)}, bf16[2,64,512]{2,1,0:T(8,128)(2,1)S(1)}, u32[]{:S(2)}, u32[]{:S(2)}) collective-permute-start(bf16[2,64,512]{2,1,0:T(8,128)(2,1)S(1)} %get-tuple-element.44.refs_0_), channel_id=1, source_target_pairs={{0,16},{16,0},{1,17},{17,1},{2,18},{18,2},{3,19},{19,3},{4,20},{20... | collective-permute-start | bytes 393224 | tf_op jit(solution)/shard_map/ppermute | solution.py:31
  56.8 4.9 %shard_map.83 = (bf16[2,64,512]{2,1,0:T(8,128)(2,1)S(1)}, bf16[1024,2048]{1,0:T(8,128)(2,1)S(1)}, bf16[1024,2048]{1,0:T(8,128)(2,1)S(1)}, bf16[1024,2048]{1,0:T(8,128)(2,1)S(1)}) custom-call(bf16[4,64,4096]{2,1,0:T(8,128)(2,1)S(1)} %get-tuple-element.45.normed_ref, bf16[4096,512]{1,0:T(8,128)(2,1)S(1)} %copy-done.5, bf16[4096,512]{1,0:T(8,128)(2,1)S(1)} %copy-done.7, ...), custom_call_target="tpu_custom_call" | custom-call | flops 1073741824 | bytes 16777216 | tf_op jit(solution)/shard_map/pallas_call | solution.py:275
  61.7 0.6 collective-permute-start.10
  62.3 0.0 collective-permute-done.9.refs_1_
  62.3 3.8 %shard_map.84 = (bf16[128,2048]{1,0:T(8,128)(2,1)S(1)}, bf16[1024,2048]{1,0:T(8,128)(2,1)S(1)}) custom-call(s32[2]{0:T(128)S(1)} %pad_add_fusion.pos_ref, bf16[2,64,512]{2,1,0:T(8,128)(2,1)S(1)} %get-tuple-element.44.refs_0_, bf16[2,64,512]{2,1,0:T(8,128)(2,1)S(1)} %collective-permute-done.9.refs_1_, bf16[1024,2048]{1,0:T(8,128)(2,1)S(1)} %get-tuple-element.50.refs_2_, ...), custom_call_target="tpu_custom_call" | custom-call | flops 536870912 | bytes 8388608 | tf_op jit(solution)/shard_map/pallas_call | solution.py:275
  66.2 0.8 collective-permute-done.10.refs_1_
  67.0 1.7 %shard_map.86 = bf16[256,1024]{1,0:T(8,128)(2,1)S(1)} custom-call(s32[2]{0:T(128)S(1)} %pad_add_fusion.pos_ref, bf16[2,256,256]{2,1,0:T(8,128)(2,1)S(1)} %get-tuple-element.56.mix_ref, bf16[128,2048]{1,0:T(8,128)(2,1)S(1)} %get-tuple-element.52.done_ref, bf16[2,64,512]{2,1,0:T(8,128)(2,1)S(1)} %get-tuple-element.53.refs_0_, ...), custom_call_target="tpu_custom_call" | custom-call | flops 536870912 | bytes 8388608 | tf_op jit(solution)/shard_map/pallas_call | solution.py:275
  68.8 0.1 collective-permute-start.16
  68.8 1.7 %shard_map.85 = bf16[256,1024]{1,0:T(8,128)(2,1)S(1)} custom-call(s32[2]{0:T(128)S(1)} %pad_add_fusion.pos_ref, bf16[2,256,256]{2,1,0:T(8,128)(2,1)S(1)} %get-tuple-element.43.mix_ref, bf16[128,2048]{1,0:T(8,128)(2,1)S(1)} %get-tuple-element.52.done_ref, bf16[2,64,512]{2,1,0:T(8,128)(2,1)S(1)} %get-tuple-element.53.refs_0_, ...), custom_call_target="tpu_custom_call" | custom-call | flops 536870912 | bytes 8388608 | tf_op jit(solution)/shard_map/pallas_call | solution.py:275
  70.6 0.6 collective-permute-start.11
  71.2 0.0 collective-permute-done.16
  71.2 0.1 fusion
  71.3 0.5 collective-permute-start.17
  71.8 1.7 %collective-permute-start.18 = (bf16[2,16,1024]{2,1,0:T(8,128)(2,1)S(1)}, bf16[2,16,1024]{2,1,0:T(8,128)(2,1)S(1)}, u32[]{:S(2)}, u32[]{:S(2)}) collective-permute-start(bf16[2,16,1024]{2,1,0:T(8,128)(2,1)S(1)} %get-tuple-element.63), channel_id=1, source_target_pairs={{0,8},{1,9},{2,10},{3,11},{4,12},{5,13},{6,14},{7,15},{8,0},{9,1},... | collective-permute-start | bytes 196616 | tf_op jit(solution)/shard_map/ppermute | solution.py:31
  73.5 0.2 collective-permute-start.19
  73.7 0.0 collective-permute-done.11
  73.7 0.1 fusion.1
  73.8 1.6 %collective-permute-start.12 = (bf16[4,16,1024]{2,1,0:T(8,128)(2,1)S(1)}, bf16[4,16,1024]{2,1,0:T(8,128)(2,1)S(1)}, u32[]{:S(2)}, u32[]{:S(2)}) collective-permute-start(bf16[4,16,1024]{2,1,0:T(8,128)(2,1)S(1)} %slice.103), channel_id=1, source_target_pairs={{0,2},{1,3},{2,0},{3,1},{4,6},{5,7},{6,4},{7,5},{8,10},{9,11},{10,... | collective-permute-start | bytes 393224 | tf_op jit(solution)/shard_map/ppermute | solution.py:31
  75.4 0.8 collective-permute-done.17
  76.2 3.8 %collective-permute-done.18 = bf16[2,16,1024]{2,1,0:T(8,128)(2,1)S(1)} collective-permute-done((bf16[2,16,1024]{2,1,0:T(8,128)(2,1)S(1)}, bf16[2,16,1024]{2,1,0:T(8,128)(2,1)S(1)}, u32[]{:S(2)}, u32[]{:S(2)}) %collective-permute-start.18) | collective-permute-done | bytes 65568 | tf_op jit(solution)/shard_map/ppermute | solution.py:31
  80.0 1.6 %collective-permute-start.20 = (bf16[1,16,1024]{2,1,0:T(8,128)(2,1)S(1)}, bf16[1,16,1024]{2,1,0:T(8,128)(2,1)S(1)}, u32[]{:S(2)}, u32[]{:S(2)}) collective-permute-start(bf16[1,16,1024]{2,1,0:T(8,128)(2,1)S(1)} %slice.115), channel_id=1, source_target_pairs={{0,2},{1,3},{2,0},{3,1},{4,6},{5,7},{6,4},{7,5},{8,10},{9,11},{10,... | collective-permute-start | bytes 98312 | tf_op jit(solution)/shard_map/ppermute | solution.py:31
  81.6 0.0 collective-permute-done.12
  81.6 0.9 %collective-permute-start.13 = (bf16[1,16,1024]{2,1,0:T(8,128)(2,1)S(1)}, bf16[1,16,1024]{2,1,0:T(8,128)(2,1)S(1)}, u32[]{:S(2)}, u32[]{:S(2)}) collective-permute-start(bf16[1,16,1024]{2,1,0:T(8,128)(2,1)S(1)} %get-tuple-element.64), channel_id=1, source_target_pairs={{0,12},{1,13},{2,14},{3,15},{4,0},{5,1},{6,2},{7,3},{8,4},{9,5},{1... | collective-permute-start | bytes 98312 | tf_op jit(solution)/shard_map/ppermute | solution.py:31
  82.6 0.2 collective-permute-start.14
  82.8 1.9 %collective-permute-start.15 = (bf16[1,16,1024]{2,1,0:T(8,128)(2,1)S(1)}, bf16[1,16,1024]{2,1,0:T(8,128)(2,1)S(1)}, u32[]{:S(2)}, u32[]{:S(2)}) collective-permute-start(bf16[1,16,1024]{2,1,0:T(8,128)(2,1)S(1)} %get-tuple-element.65), channel_id=1, source_target_pairs={{0,4},{1,5},{2,6},{3,7},{4,8},{5,9},{6,10},{7,11},{8,12},{9,13},{1... | collective-permute-start | bytes 98312 | tf_op jit(solution)/shard_map/ppermute | solution.py:31
  84.7 1.0 %collective-permute-done.13 = bf16[1,16,1024]{2,1,0:T(8,128)(2,1)S(1)} collective-permute-done((bf16[1,16,1024]{2,1,0:T(8,128)(2,1)S(1)}, bf16[1,16,1024]{2,1,0:T(8,128)(2,1)S(1)}, u32[]{:S(2)}, u32[]{:S(2)}) %collective-permute-start.13) | collective-permute-done | bytes 32800 | tf_op jit(solution)/shard_map/ppermute | solution.py:31
  85.7 1.7 %collective-permute-done.14 = bf16[1,16,1024]{2,1,0:T(8,128)(2,1)S(1)} collective-permute-done((bf16[1,16,1024]{2,1,0:T(8,128)(2,1)S(1)}, bf16[1,16,1024]{2,1,0:T(8,128)(2,1)S(1)}, u32[]{:S(2)}, u32[]{:S(2)}) %collective-permute-start.14) | collective-permute-done | bytes 32800 | tf_op jit(solution)/shard_map/ppermute | solution.py:31
  87.4 1.1 %collective-permute-done.15 = bf16[1,16,1024]{2,1,0:T(8,128)(2,1)S(1)} collective-permute-done((bf16[1,16,1024]{2,1,0:T(8,128)(2,1)S(1)}, bf16[1,16,1024]{2,1,0:T(8,128)(2,1)S(1)}, u32[]{:S(2)}, u32[]{:S(2)}) %collective-permute-start.15) | collective-permute-done | bytes 32800 | tf_op jit(solution)/shard_map/ppermute | solution.py:31
  88.5 0.1 add_convert_fusion.1
  88.7 0.6 pad_maximum_fusion
  (35 shorter events, 0.4 us)
Async XLA Ops:
  1.5 15.2 %collective-permute-start = (bf16[8,4224]{1,0:T(8,128)(2,1)S(1)}, bf16[8,4224]{1,0:T(8,128)(2,1)S(1)}, u32[]{:S(2)}, u32[]{:S(2)}) collective-permute-start(bf16[8,4224]{1,0:T(8,128)(2,1)S(1)} %shard_map.73.refs_0_), channel_id=1, source_target_pairs={{0,4},{1,5},{2,6},{3,7},{4,8},{5,9},{6,10},{7,11},{8,12},{9,13},{1... | collective-permute-start | bytes 202760 | tf_op jit(solution)/shard_map/ppermute | solution.py:31
  4.6 12.1 %collective-permute-start.1 = (bf16[8,4224]{1,0:T(8,128)(2,1)S(1)}, bf16[8,4224]{1,0:T(8,128)(2,1)S(1)}, u32[]{:S(2)}, u32[]{:S(2)}) collective-permute-start(bf16[8,4224]{1,0:T(8,128)(2,1)S(1)} %shard_map.73.refs_0_), channel_id=1, source_target_pairs={{0,8},{1,9},{2,10},{3,11},{4,12},{5,13},{6,14},{7,15},{8,0},{9,1},... | collective-permute-start | bytes 202760 | tf_op jit(solution)/shard_map/ppermute | solution.py:31
  7.2 9.5 %collective-permute-start.2 = (bf16[8,4224]{1,0:T(8,128)(2,1)S(1)}, bf16[8,4224]{1,0:T(8,128)(2,1)S(1)}, u32[]{:S(2)}, u32[]{:S(2)}) collective-permute-start(bf16[8,4224]{1,0:T(8,128)(2,1)S(1)} %shard_map.73.refs_0_), channel_id=1, source_target_pairs={{0,12},{1,13},{2,14},{3,15},{4,0},{5,1},{6,2},{7,3},{8,4},{9,5},{1... | collective-permute-start | bytes 202760 | tf_op jit(solution)/shard_map/ppermute | solution.py:31
  12.7 2.0 %copy-start = (bf16[4096,512]{1,0:T(8,128)(2,1)}, bf16[4096,512]{1,0:T(8,128)(2,1)S(1)}, u32[]{:S(2)}) copy-start(bf16[4096,512]{1,0:T(8,128)(2,1)S(1)} %get-tuple-element.39.refs_4_) | copy-start | bytes 12582916
  14.8 1.9 %copy-start.2 = (bf16[4096,512]{1,0:T(8,128)(2,1)}, bf16[4096,512]{1,0:T(8,128)(2,1)S(1)}, u32[]{:S(2)}) copy-start(bf16[4096,512]{1,0:T(8,128)(2,1)S(1)} %get-tuple-element.40.refs_5_) | copy-start | bytes 12582916
  16.7 10.5 %collective-permute-start.5 = (bf16[32,2176]{1,0:T(8,128)(2,1)S(1)}, bf16[32,2176]{1,0:T(8,128)(2,1)S(1)}, u32[]{:S(2)}, u32[]{:S(2)}) collective-permute-start(bf16[32,2176]{1,0:T(8,128)(2,1)S(1)} %get-tuple-element.33.refs_0_), channel_id=1, source_target_pairs={{0,2},{1,3},{2,0},{3,1},{4,6},{5,7},{6,4},{7,5},{8,10},{9,11},{10,... | collective-permute-start | bytes 417800 | tf_op jit(solution)/shard_map/ppermute | solution.py:31
  18.3 9.6 %collective-permute-start.3 = (bf16[32,2048]{1,0:T(8,128)(2,1)S(1)}, bf16[32,2048]{1,0:T(8,128)(2,1)S(1)}, u32[]{:S(2)}, u32[]{:S(2)}) collective-permute-start(bf16[32,2048]{1,0:T(8,128)(2,1)S(1)} %get-tuple-element.32.refs_0_), channel_id=1, source_target_pairs={{0,16},{16,0},{1,17},{17,1},{2,18},{18,2},{3,19},{19,3},{4,20},{20... | collective-permute-start | bytes 393224 | tf_op jit(solution)/shard_map/ppermute | solution.py:31
  23.3 2.0 %copy-start.4 = (bf16[4096,512]{1,0:T(8,128)(2,1)}, bf16[4096,512]{1,0:T(8,128)(2,1)S(1)}, u32[]{:S(2)}) copy-start(bf16[4096,512]{1,0:T(8,128)(2,1)S(1)} %get-tuple-element.46.refs_0_) | copy-start | bytes 12582916
  25.3 2.0 %copy-start.6 = (bf16[4096,512]{1,0:T(8,128)(2,1)}, bf16[4096,512]{1,0:T(8,128)(2,1)S(1)}, u32[]{:S(2)}) copy-start(bf16[4096,512]{1,0:T(8,128)(2,1)S(1)} %get-tuple-element.47.refs_1_) | copy-start | bytes 12582916
  27.3 8.7 %collective-permute-start.6 = (bf16[64,2176]{1,0:T(8,128)(2,1)S(1)}, bf16[64,2176]{1,0:T(8,128)(2,1)S(1)}, u32[]{:S(2)}, u32[]{:S(2)}) collective-permute-start(bf16[64,2176]{1,0:T(8,128)(2,1)S(1)} %get-tuple-element.36.refs_0_), channel_id=1, source_target_pairs={{0,16},{16,0},{1,17},{17,1},{2,18},{18,2},{3,19},{19,3},{4,20},{20... | collective-permute-start | bytes 835592 | tf_op jit(solution)/shard_map/ppermute | solution.py:31
  27.9 8.2 %collective-permute-start.4 = (bf16[64,2048]{1,0:T(8,128)(2,1)S(1)}, bf16[64,2048]{1,0:T(8,128)(2,1)S(1)}, u32[]{:S(2)}, u32[]{:S(2)}) collective-permute-start(bf16[64,2048]{1,0:T(8,128)(2,1)S(1)} %shard_map.76.refs_0_), channel_id=1, source_target_pairs={{0,2},{1,3},{2,0},{3,1},{4,6},{5,7},{6,4},{7,5},{8,10},{9,11},{10,... | collective-permute-start | bytes 786440 | tf_op jit(solution)/shard_map/ppermute | solution.py:31
  32.0 2.0 %copy-start.8 = (bf16[4096,512]{1,0:T(8,128)(2,1)}, bf16[4096,512]{1,0:T(8,128)(2,1)S(1)}, u32[]{:S(2)}) copy-start(bf16[4096,512]{1,0:T(8,128)(2,1)S(1)} %get-tuple-element.41.refs_6_) | copy-start | bytes 12582916
  34.0 2.0 %copy-start.10 = (bf16[4096,512]{1,0:T(8,128)(2,1)}, bf16[4096,512]{1,0:T(8,128)(2,1)S(1)}, u32[]{:S(2)}) copy-start(bf16[4096,512]{1,0:T(8,128)(2,1)S(1)} %get-tuple-element.42.refs_7_) | copy-start | bytes 12582916
  36.0 2.8 %collective-permute-start.7 = (bf16[128,2176]{1,0:T(8,128)(2,1)S(1)}, bf16[128,2176]{1,0:T(8,128)(2,1)S(1)}, u32[]{:S(2)}, u32[]{:S(2)}) collective-permute-start(bf16[128,2176]{1,0:T(8,128)(2,1)S(1)} %shard_map.81.refs_0_), channel_id=1, source_target_pairs={{0,1},{1,0},{2,3},{3,2},{4,5},{5,4},{6,7},{7,6},{8,9},{9,8},{10,11... | collective-permute-start | bytes 1671176 | tf_op jit(solution)/shard_map/ppermute | solution.py:31
  36.2 2.6 %collective-permute-start.8 = (bf16[128,2048]{1,0:T(8,128)(2,1)S(1)}, bf16[128,2048]{1,0:T(8,128)(2,1)S(1)}, u32[]{:S(2)}, u32[]{:S(2)}) collective-permute-start(bf16[128,2048]{1,0:T(8,128)(2,1)S(1)} %shard_map.77.refs_2_), channel_id=1, source_target_pairs={{0,1},{1,0},{2,3},{3,2},{4,5},{5,4},{6,7},{7,6},{8,9},{9,8},{10,11... | collective-permute-start | bytes 1572872 | tf_op jit(solution)/shard_map/ppermute | solution.py:31
  38.8 2.2 %copy-start.1 = (bf16[4096,512]{1,0:T(8,128)(2,1)S(1)}, bf16[4096,512]{1,0:T(8,128)(2,1)}, u32[]{:S(2)}) copy-start(bf16[4096,512]{1,0:T(8,128)(2,1)} %copy-done) | copy-start | bytes 12582916
  41.0 2.2 %copy-start.3 = (bf16[4096,512]{1,0:T(8,128)(2,1)S(1)}, bf16[4096,512]{1,0:T(8,128)(2,1)}, u32[]{:S(2)}) copy-start(bf16[4096,512]{1,0:T(8,128)(2,1)} %copy-done.2) | copy-start | bytes 12582916
  43.2 2.2 %copy-start.9 = (bf16[4096,512]{1,0:T(8,128)(2,1)S(1)}, bf16[4096,512]{1,0:T(8,128)(2,1)}, u32[]{:S(2)}) copy-start(bf16[4096,512]{1,0:T(8,128)(2,1)} %copy-done.8) | copy-start | bytes 12582916
  45.4 2.2 %copy-start.11 = (bf16[4096,512]{1,0:T(8,128)(2,1)S(1)}, bf16[4096,512]{1,0:T(8,128)(2,1)}, u32[]{:S(2)}) copy-start(bf16[4096,512]{1,0:T(8,128)(2,1)} %copy-done.10) | copy-start | bytes 12582916
  47.6 9.2 %copy-start.5 = (bf16[4096,512]{1,0:T(8,128)(2,1)S(1)}, bf16[4096,512]{1,0:T(8,128)(2,1)}, u32[]{:S(2)}) copy-start(bf16[4096,512]{1,0:T(8,128)(2,1)} %copy-done.4) | copy-start | bytes 12582916
  47.6 9.2 %copy-start.7 = (bf16[4096,512]{1,0:T(8,128)(2,1)S(1)}, bf16[4096,512]{1,0:T(8,128)(2,1)}, u32[]{:S(2)}) copy-start(bf16[4096,512]{1,0:T(8,128)(2,1)} %copy-done.6) | copy-start | bytes 12582916
  55.2 7.1 %collective-permute-start.9 = (bf16[2,64,512]{2,1,0:T(8,128)(2,1)S(1)}, bf16[2,64,512]{2,1,0:T(8,128)(2,1)S(1)}, u32[]{:S(2)}, u32[]{:S(2)}) collective-permute-start(bf16[2,64,512]{2,1,0:T(8,128)(2,1)S(1)} %get-tuple-element.44.refs_0_), channel_id=1, source_target_pairs={{0,16},{16,0},{1,17},{17,1},{2,18},{18,2},{3,19},{19,3},{4,20},{20... | collective-permute-start | bytes 393224 | tf_op jit(solution)/shard_map/ppermute | solution.py:31
  61.7 5.3 %collective-permute-start.10 = (bf16[2,64,512]{2,1,0:T(8,128)(2,1)S(1)}, bf16[2,64,512]{2,1,0:T(8,128)(2,1)S(1)}, u32[]{:S(2)}, u32[]{:S(2)}) collective-permute-start(bf16[2,64,512]{2,1,0:T(8,128)(2,1)S(1)} %get-tuple-element.53.refs_0_), channel_id=1, source_target_pairs={{0,16},{16,0},{1,17},{17,1},{2,18},{18,2},{3,19},{19,3},{4,20},{20... | collective-permute-start | bytes 393224 | tf_op jit(solution)/shard_map/ppermute | solution.py:31
  68.8 2.4 %collective-permute-start.16 = (bf16[8,16,1024]{2,1,0:T(8,128)(2,1)S(1)}, bf16[8,16,1024]{2,1,0:T(8,128)(2,1)S(1)}, u32[]{:S(2)}, u32[]{:S(2)}) collective-permute-start(bf16[8,16,1024]{2,1,0:T(8,128)(2,1)S(1)} %bitcast.27), channel_id=1, source_target_pairs={{0,1},{1,0},{2,3},{3,2},{4,5},{5,4},{6,7},{7,6},{8,9},{9,8},{10,11... | collective-permute-start | bytes 786440 | tf_op jit(solution)/shard_map/ppermute | solution.py:31
  70.6 3.1 %collective-permute-start.11 = (bf16[8,16,1024]{2,1,0:T(8,128)(2,1)S(1)}, bf16[8,16,1024]{2,1,0:T(8,128)(2,1)S(1)}, u32[]{:S(2)}, u32[]{:S(2)}) collective-permute-start(bf16[8,16,1024]{2,1,0:T(8,128)(2,1)S(1)} %bitcast.26), channel_id=1, source_target_pairs={{0,1},{1,0},{2,3},{3,2},{4,5},{5,4},{6,7},{7,6},{8,9},{9,8},{10,11... | collective-permute-start | bytes 786440 | tf_op jit(solution)/shard_map/ppermute | solution.py:31
  71.3 4.9 %collective-permute-start.17 = (bf16[2,16,1024]{2,1,0:T(8,128)(2,1)S(1)}, bf16[2,16,1024]{2,1,0:T(8,128)(2,1)S(1)}, u32[]{:S(2)}, u32[]{:S(2)}) collective-permute-start(bf16[2,16,1024]{2,1,0:T(8,128)(2,1)S(1)} %get-tuple-element.61), channel_id=1, source_target_pairs={{0,12},{1,13},{2,14},{3,15},{4,0},{5,1},{6,2},{7,3},{8,4},{9,5},{1... | collective-permute-start | bytes 196616 | tf_op jit(solution)/shard_map/ppermute | solution.py:31
  71.8 8.1 %collective-permute-start.18 = (bf16[2,16,1024]{2,1,0:T(8,128)(2,1)S(1)}, bf16[2,16,1024]{2,1,0:T(8,128)(2,1)S(1)}, u32[]{:S(2)}, u32[]{:S(2)}) collective-permute-start(bf16[2,16,1024]{2,1,0:T(8,128)(2,1)S(1)} %get-tuple-element.63), channel_id=1, source_target_pairs={{0,8},{1,9},{2,10},{3,11},{4,12},{5,13},{6,14},{7,15},{8,0},{9,1},... | collective-permute-start | bytes 196616 | tf_op jit(solution)/shard_map/ppermute | solution.py:31
  73.5 6.5 %collective-permute-start.19 = (bf16[2,16,1024]{2,1,0:T(8,128)(2,1)S(1)}, bf16[2,16,1024]{2,1,0:T(8,128)(2,1)S(1)}, u32[]{:S(2)}, u32[]{:S(2)}) collective-permute-start(bf16[2,16,1024]{2,1,0:T(8,128)(2,1)S(1)} %get-tuple-element.62), channel_id=1, source_target_pairs={{0,4},{1,5},{2,6},{3,7},{4,8},{5,9},{6,10},{7,11},{8,12},{9,13},{1... | collective-permute-start | bytes 196616 | tf_op jit(solution)/shard_map/ppermute | solution.py:31
  73.8 7.8 %collective-permute-start.12 = (bf16[4,16,1024]{2,1,0:T(8,128)(2,1)S(1)}, bf16[4,16,1024]{2,1,0:T(8,128)(2,1)S(1)}, u32[]{:S(2)}, u32[]{:S(2)}) collective-permute-start(bf16[4,16,1024]{2,1,0:T(8,128)(2,1)S(1)} %slice.103), channel_id=1, source_target_pairs={{0,2},{1,3},{2,0},{3,1},{4,6},{5,7},{6,4},{7,5},{8,10},{9,11},{10,... | collective-permute-start | bytes 393224 | tf_op jit(solution)/shard_map/ppermute | solution.py:31
  80.0 4.7 %collective-permute-start.20 = (bf16[1,16,1024]{2,1,0:T(8,128)(2,1)S(1)}, bf16[1,16,1024]{2,1,0:T(8,128)(2,1)S(1)}, u32[]{:S(2)}, u32[]{:S(2)}) collective-permute-start(bf16[1,16,1024]{2,1,0:T(8,128)(2,1)S(1)} %slice.115), channel_id=1, source_target_pairs={{0,2},{1,3},{2,0},{3,1},{4,6},{5,7},{6,4},{7,5},{8,10},{9,11},{10,... | collective-permute-start | bytes 98312 | tf_op jit(solution)/shard_map/ppermute | solution.py:31
  81.6 4.1 %collective-permute-start.13 = (bf16[1,16,1024]{2,1,0:T(8,128)(2,1)S(1)}, bf16[1,16,1024]{2,1,0:T(8,128)(2,1)S(1)}, u32[]{:S(2)}, u32[]{:S(2)}) collective-permute-start(bf16[1,16,1024]{2,1,0:T(8,128)(2,1)S(1)} %get-tuple-element.64), channel_id=1, source_target_pairs={{0,12},{1,13},{2,14},{3,15},{4,0},{5,1},{6,2},{7,3},{8,4},{9,5},{1... | collective-permute-start | bytes 98312 | tf_op jit(solution)/shard_map/ppermute | solution.py:31
  82.6 4.8 %collective-permute-start.14 = (bf16[1,16,1024]{2,1,0:T(8,128)(2,1)S(1)}, bf16[1,16,1024]{2,1,0:T(8,128)(2,1)S(1)}, u32[]{:S(2)}, u32[]{:S(2)}) collective-permute-start(bf16[1,16,1024]{2,1,0:T(8,128)(2,1)S(1)} %get-tuple-element.66), channel_id=1, source_target_pairs={{0,8},{1,9},{2,10},{3,11},{4,12},{5,13},{6,14},{7,15},{8,0},{9,1},... | collective-permute-start | bytes 98312 | tf_op jit(solution)/shard_map/ppermute | solution.py:31
  82.8 5.7 %collective-permute-start.15 = (bf16[1,16,1024]{2,1,0:T(8,128)(2,1)S(1)}, bf16[1,16,1024]{2,1,0:T(8,128)(2,1)S(1)}, u32[]{:S(2)}, u32[]{:S(2)}) collective-permute-start(bf16[1,16,1024]{2,1,0:T(8,128)(2,1)S(1)} %get-tuple-element.65), channel_id=1, source_target_pairs={{0,4},{1,5},{2,6},{3,7},{4,8},{5,9},{6,10},{7,11},{8,12},{9,13},{1... | collective-permute-start | bytes 98312 | tf_op jit(solution)/shard_map/ppermute | solution.py:31

commit v7 on v6

--- a/solution.py
+++ b/solution.py
@@ -33,17 +33,6 @@
 
 def arrivals(x, axis, size, stride, radix):
     return [x] + [shifted(x, axis, size, stride, radix, s) for s in range(1, radix)]
-
-
-def gathered(x, axis, size, stride, radix):
-    return jnp.stack(arrivals(x, axis, size, stride, radix))
-
-
-def scattered(x, axis, size, stride, radix):
-    total = x[0].astype(jnp.float32)
-    for s in range(1, radix):
-        total = total + shifted(x[s], axis, size, stride, radix, radix - s).astype(jnp.float32)
-    return total.astype(x.dtype)
 
 
 def pack_kernel(top, pos_ref, ids_ref, weights_ref, values_ref, message_ref, ids, weights, sems):
@@ -91,22 +80,24 @@
         ref[...] = jnp.zeros_like(ref)
 
 
-def load_kernel(start, signs, src_ref, *refs):
-    sign_ref, *near, sems = refs[signs:]
-    copies = load_copies(src_ref, near, sems, start)
+def load_kernel(experts, signs, *refs):
+    count = len(experts)
+    refs = refs[:count] + refs[count + signs :]
+    far, (sign_ref, *near, sems) = refs[:count], refs[count:]
+    copies = load_copies(far, near, sems, experts)
     sign_ref[...] = jnp.zeros_like(sign_ref)
     for copy in copies:
         copy.wait()
 
 
-def load_copies(src_ref, near, sems, start):
-    count, runs = sems.shape
-    size = src_ref.shape[1] // runs
+def load_copies(far, near, sems, experts):
     copies = []
-    for i in range(count):
+    for i, (src_ref, dst_ref, expert) in enumerate(zip(far, near, experts)):
+        runs = sems.shape[1]
+        size = dst_ref.shape[0] // runs
         for r in range(runs):
             at = pl.ds(r * size, size)
-            copies.append(pltpu.make_async_copy(src_ref.at[start + i, at], near[i].at[at], sems.at[i, r]))
+            copies.append(pltpu.make_async_copy(src_ref.at[expert, at], dst_ref.at[at], sems.at[i, r]))
     for copy in copies:
         copy.start()
     return copies
@@ -126,7 +117,7 @@
     refs = refs[2 * n_fast :]
     gates, ups, refs = refs[:lead], refs[lead : 2 * lead], refs[2 * lead :]
     far_ref, hidden_ref, normed_ref, mix_ref, turned_ref, *near, sems = refs
-    copies = load_copies(far_ref, near, sems, lead)
+    copies = load_copies([far_ref] * tail, near, sems, range(lead, lead + tail))
     tp_pos, base = pos_ref[0], pos_ref[1]
     run = slow_n * tok_dev
     tokens = n_fast * n_mid * n_tp * run
@@ -211,9 +202,9 @@
         copy.wait()
 
 
-def up_kernel(start, count, normed_ref, *refs):
+def up_kernel(start, count, wanted, normed_ref, *refs):
     gates, ups, (far_ref, hidden_ref, *near, sems) = refs[:count], refs[count : 2 * count], refs[2 * count :]
-    copies = load_copies(far_ref, near, sems, 0)
+    copies = load_copies([far_ref] * len(near), near, sems, wanted)
     swiglu(normed_ref, gates, ups, hidden_ref, start)
     for copy in copies:
         copy.wait()
@@ -230,20 +221,22 @@
     return total.astype(jnp.bfloat16)
 
 
-def down_kernel(n_tp, done, pos_ref, *refs):
-    pieces, refs = refs[:n_tp], refs[n_tp:]
-    count, rows, _ = pieces[0].shape
-    downs, (far_ref, out_ref, *near, sems) = refs[:count], refs[count:]
-    copies = load_copies(far_ref, near, sems, done)
+def down_kernel(n_tp, pos_ref, *refs):
+    pieces, (*downs, out_ref) = refs[:n_tp], refs[n_tp:]
+    _, rows, _ = pieces[0].shape
     for i, ref in enumerate(downs):
         out_ref[i * rows : (i + 1) * rows] = lower(n_tp, pos_ref[0], pieces, i, ref, slice(None))
-    for copy in copies:
-        copy.wait()
-
-
-def mix_kernel(n_tp, begin, pos_ref, mix_ref, done_ref, *refs):
-    pieces, (*downs, partial_ref, out_ref) = refs[:n_tp], refs[n_tp:]
-    columns = pl.ds(begin, partial_ref.shape[1])
+
+
+def in_blocks(total, refs):
+    rows = refs[0].shape[0]
+    for i, ref in enumerate(refs):
+        ref[...] = total[i * rows : (i + 1) * rows].astype(jnp.bfloat16)
+
+
+def mix_kernel(n_tp, count, begin, pos_ref, mix_ref, done_ref, *refs):
+    pieces, downs, (*partial_refs, out_ref) = refs[:n_tp], refs[n_tp : n_tp + count], refs[n_tp + count :]
+    columns = pl.ds(begin, out_ref.shape[1])
     _, rows, _ = pieces[0].shape
     at = done_ref.shape[0]
     out_ref[:at] = done_ref[:, columns]
@@ -253,7 +246,40 @@
     out = out_ref[...]
     partial = jnp.dot(mix_ref[0], out, preferred_element_type=jnp.float32)
     partial = partial + jnp.dot(mix_ref[1], out, preferred_element_type=jnp.float32)
-    partial_ref[...] = partial.astype(jnp.bfloat16)
+    in_blocks(partial, partial_refs)
+
+
+def total_of(refs):
+    return functools.reduce(lambda a, ref: a + ref[...].astype(jnp.float32), refs[1:], refs[0][...].astype(jnp.float32))
+
+
+def sum_kernel(count, signs, blocks, *refs):
+    out_refs = refs[count + signs :]
+    in_blocks(total_of(refs[:count]), out_refs[:blocks])
+    for ref in out_refs[blocks:]:
+        ref[...] = jnp.zeros_like(ref)
+
+
+def final_kernel(dims, count, pos_ref, first_ref, second_ref, *refs):
+    n_mid, n_tp, slow_n, tok_dev, half = dims
+    left, right, (out_ref, own_ref) = refs[:count], refs[count:-2], refs[-2:]
+    tp_pos = pos_ref[0]
+    col_part = out_ref.shape[1]
+    for s in range(n_tp):
+        at = s * n_mid * slow_n * tok_dev
+        own_ref[s * tok_dev : (s + 1) * tok_dev, half:] = first_ref[at : at + tok_dev, :half].astype(jnp.float32)
+        at = s * slow_n * tok_dev
+        own_ref[s * tok_dev : (s + 1) * tok_dev, :half] = second_ref[at : at + tok_dev].astype(jnp.float32)
+    total = jnp.concatenate([total_of(left), total_of(right)], axis=1)
+    total = total + own_ref[:, pl.ds(pl.multiple_of(tp_pos * col_part, col_part), col_part)]
+    rows = []
+    for j in range(n_tp):
+        row = total[:tok_dev]
+        for s in range(1, n_tp):
+            here = lax.rem(tp_pos - s + n_tp, n_tp) == j
+            row = jnp.where(here, total[s * tok_dev : (s + 1) * tok_dev], row)
+        rows.append(row)
+    out_ref[...] = jnp.concatenate(rows, axis=0).astype(jnp.bfloat16)
 
 
 VMEM = pl.BlockSpec(memory_space=pltpu.VMEM)
@@ -291,17 +317,28 @@
     return 4 if array.shape[1] % 64 == 0 else 1
 
 
-def loaded(array, start, count, after):
+def loaded(wanted, after):
     sign, *near = local_call(
-        functools.partial(load_kernel, start, len(after)),
-        [TOKEN] + kept(array, count),
-        [array] + after,
-        far=[0],
-        scratch=[pltpu.SemaphoreType.DMA((count, runs_of(array)))],
+        functools.partial(load_kernel, [expert for _, expert in wanted], len(after)),
+        [TOKEN] + [KEPT(array.shape[1:], array.dtype) for array, _ in wanted],
+        [array for array, _ in wanted] + after,
+        far=range(len(wanted)),
+        scratch=[pltpu.SemaphoreType.DMA((len(wanted), min(runs_of(array) for array, _ in wanted)))],
         limit=1 << 20,
-        moved=2 * count * array.size // array.shape[0],
+        moved=2 * sum(array.size // array.shape[0] for array, _ in wanted),
     )
     return near, sign
+
+
+def summed(pieces, blocks, after, signed):
+    rows, columns = pieces[0].shape
+    return local_call(
+        functools.partial(sum_kernel, len(pieces), len(after), blocks),
+        [jax.ShapeDtypeStruct((rows // blocks, columns), pieces[0].dtype)] * blocks + [TOKEN] * signed,
+        list(pieces) + after,
+        limit=4 << 20,
+        moved=2 * (len(pieces) + 1) * rows * columns,
+    )
 
 
 def joined(pieces, after, signed):
@@ -357,30 +394,31 @@
     around = [message]
     for digit in reversed(slow):
         around = [a for piece in around for a in arrivals(piece, "ep", n_ep, *digit)]
-    gate_lead, sign = loaded(w_gate, 0, lead, [gain])
+    gate_lead, sign = loaded([(w_gate, e) for e in range(lead)], [gain])
     first, second, sign = local_call(
         functools.partial(split_kernel, half),
         [bf16((slow_n * tok_dev, width + LANES - half)), bf16((slow_n * tok_dev, half)), TOKEN],
         around + [sign],
         limit=4 << 20,
     )
-    gate_tail, sign = loaded(w_gate, lead, tail, [sign])
+    gate_tail, sign = loaded([(w_gate, e) for e in range(lead, exp_loc)], [sign])
     along_tp = lambda a: arrivals(a, "tp", n_tp, 1, n_tp)
     along_mid = lambda a: arrivals(a, "ep", n_ep, *mid[0]) if mid else [a]
     first, second = along_mid(first), along_tp(second)
     first, sign = joined(first, [sign], 1)
     (second,) = joined(second, [], 0)
-    up_lead, sign = loaded(w_up, 0, lead, [sign])
+    up_lead, sign = loaded([(w_up, e) for e in range(lead)] + [(w_down, 0)], [sign])
+    *up_lead, down_first = up_lead
     first, second = along_tp(first), along_mid(second)
-    (first,) = joined(first, [sign], 0)
+    first, sign = joined(first, [sign], 1)
+    down_lead, _ = loaded([(w_down, e) for e in range(1, lead)], [sign]) if lead > 1 else ([], None)
+    down_lead = [down_first] + down_lead
     (second,) = joined(second, [], 0)
     first = arrivals(first, "ep", n_ep, *fast)
     second = arrivals(second, "ep", n_ep, *fast)
 
     dims = (n_fast, n_mid, n_tp, slow_n, tok_dev, top, exp_loc, rows, half)
     sems = lambda array, count: pltpu.SemaphoreType.DMA((count, runs_of(array)))
-    last = max(1, tail // 2)
-    early = exp_loc - last
     operands = [position, gain] + first + second + gate_lead + up_lead + [w_up]
     hidden, normed, mix, turned, *up_tail = local_call(
         functools.partial(select_kernel, dims, lead, tail),
@@ -399,58 +437,59 @@
     )
     pieces = along_tp(hidden)
     operands = [normed] + gate_tail + up_tail + [w_down]
-    hidden, *down_early = local_call(
-        functools.partial(up_kernel, lead, tail),
-        [bf16((tail, rows, hid_part))] + kept(w_down, early),
+    hidden, *down_tail = local_call(
+        functools.partial(up_kernel, lead, tail, range(lead, exp_loc)),
+        [bf16((tail, rows, hid_part))] + kept(w_down, tail),
         operands,
         far=[len(operands) - 1],
-        scratch=[sems(w_down, early)],
+        scratch=[sems(w_down, tail)],
         flops=4 * tail * rows * width * hid_part,
         moved=4 * tail * width * hid_part,
     )
     late = along_tp(hidden)
-    operands = [position] + pieces + down_early[:lead] + [w_down]
-    done, *down_last = local_call(
-        functools.partial(down_kernel, n_tp, early),
-        [bf16((lead * rows, col_part))] + kept(w_down, last),
-        operands,
-        far=[len(operands) - 1],
-        scratch=[sems(w_down, last)],
+    (done,) = local_call(
+        functools.partial(down_kernel, n_tp),
+        [bf16((lead * rows, col_part))],
+        [position] + pieces + down_lead,
         flops=2 * lead * rows * n_tp * hid_part * col_part,
         moved=2 * lead * n_tp * hid_part * col_part,
     )
     col_half = col_part // 2
     mixed_of = lambda table, begin: local_call(
-        functools.partial(mix_kernel, n_tp, begin),
-        [bf16((tokens, col_half))],
-        [position, table, done] + late + down_early[lead:] + down_last,
+        functools.partial(mix_kernel, n_tp, tail, begin),
+        [bf16((tokens // n_fast, col_half))] * n_fast,
+        [position, table, done] + late + down_tail,
         scratch=[pltpu.VMEM((slots, col_half), jnp.bfloat16)],
         flops=slots * n_tp * hid_part * col_part,
         moved=exp_loc * n_tp * hid_part * col_part,
-    )[0]
-
-    def over(total, digits):
-        for digit in digits:
-            total = scattered(total.reshape(digit[1], -1, group, col_half), "ep", n_ep, *digit)
-        return total.reshape(n_tp, tok_dev, col_half)
-
-    right = over(mixed_of(turned, col_half), [fast] + list(reversed(slow)) + mid)
-    left = over(mixed_of(mix, 0), [fast] + mid + list(reversed(slow)))
-    combined = jnp.concatenate([left, right], axis=2)
-    column = lambda a, at: lax.dynamic_slice_in_dim(a, at, col_part, 1)
-    right = first[0].reshape(n_tp, -1, first[0].shape[1])[:, :tok_dev, :half]
-    left = second[0].reshape(n_mid, n_tp, -1, half)[0, :, :tok_dev]
-    own = jnp.concatenate([left, right], axis=2)
-    residual = lax.dynamic_slice_in_dim(own, tp_pos * col_part, col_part, 2)
-    result = (residual.astype(jnp.float32) + combined.astype(jnp.float32)).astype(jnp.bfloat16)
-    order = [lax.rem(tp_pos - s + n_tp, n_tp) for s in range(n_tp)]
-    turned = []
-    for j in range(n_tp):
-        piece = result[0]
-        for s in range(1, n_tp):
-            piece = jnp.where(order[s] == j, result[s], piece)
-        turned.append(piece)
-    return jnp.concatenate(turned, axis=0)
+    )
+
+    def swapped(blocks, digit):
+        stride, radix = digit
+        return [blocks[0]] + [shifted(blocks[s], "ep", n_ep, stride, radix, radix - s) for s in range(1, radix)]
+
+    slow = list(reversed(slow))
+    right_way, left_way = slow + mid, mid + slow
+    right = summed(swapped(mixed_of(turned, col_half), fast), right_way[0][1], [], 0)
+    left = summed(swapped(mixed_of(mix, 0), fast), left_way[0][1], [], 0)
+    signs = []
+    for digit, later in zip(left_way[:-1], left_way[1:]):
+        *left, sign = summed(swapped(left, digit), later[1], [], 1)
+        signs.append(sign)
+    for digit, later in zip(right_way[:-1], right_way[1:]):
+        right = summed(swapped(right, digit), later[1], signs, 0)
+        signs = []
+    left = swapped(left, left_way[-1])
+    right = swapped(right, right_way[-1])
+    (mixed,) = local_call(
+        functools.partial(final_kernel, (n_mid, n_tp, slow_n, tok_dev, half), len(left)),
+        [bf16((group, col_part))],
+        [position, first[0], second[0]] + left + right,
+        scratch=[pltpu.VMEM((group, width), jnp.float32)],
+        limit=4 << 20,
+        moved=2 * group * (width + 6 * col_part),
+    )
+    return mixed
 
 
 def by_slots(hidden_in, norm_gain, expert_ids, gate_weights, w_gate, w_up, w_down):

time: 89.7 us -> 72 us (0.80)
  local copies, waits for them, and re-layouts: 21.5 us -> 0.71 us
  Pallas kernels: 31.8 us -> 36.4 us
  other arithmetic: 1.09 us -> 0.07 us
    unnamed x24 -> x0, local copies, waits for them, and re-layouts: 20.7 us -> none
    pallas_call x14 -> x20, Pallas kernels: 31.8 us -> 36.4 us  [local_call(): pl.pallas_call(kernel, out_shape=shapes, in_specs=specs, out_specs=[VMEM]...]
  transfers between devices with their start and end apart: 21 -> 21, of which waited for: 7 -> 9; matrix products, arithmetic and copies ran while one was open for 1% -> 1% of each run, Pallas kernels for 24% -> 34%
where the time goes in v7:
time: 72 us; the launch traced here: 71.8 us
  Pallas kernels  36.4 us (51%)
  starting transfers between devices  22.9 us (32%)
  waiting for transfers between devices  11.5 us (16%)
    pallas_call x20, Pallas kernels, local_call(): pl.pallas_call(kernel, out_shape=shapes, in_specs=specs, out_specs=[VMEM]...  36.4 us
    ppermute x21, starting transfers between devices, shifted(): return lax.ppermute(x, axis, pairs)  22.9 us
    ppermute x21, waiting for transfers between devices, shifted(): return lax.ppermute(x, axis, pairs)  11.5 us
  transfers between devices with their start and end apart: 21, of which 9 were waited for; matrix products, arithmetic and copies ran while one was open for 1% of the time, Pallas kernels for 34%

profile of v7, /device:TPU:0, one launch (start us, length us, event | category | flops | bytes accessed | tf_op | source)
XLA Modules:
  0.0 71.8 jit_solution(1876468136573198224)
XLA Ops:
  0.0 0.1 pad_add_fusion.pos_ref
  0.1 1.4 %shard_map.73.refs_0_ = bf16[8,4224]{1,0:T(8,128)(2,1)S(1)} custom-call(s32[2]{0:T(128)S(1)} %pad_add_fusion.pos_ref, s32[8,16]{1,0:T(8,128)} %bitcast.4, f32[8,16]{1,0:T(8,128)} %bitcast.5, bf16[8,4096]{1,0:T(8,128)(2,1)} %values_ref.1), custom_call_target="tpu_custom_call" | custom-call | tf_op jit(solution)/shard_map/pallas_call | solution.py:301
  1.5 5.1 %collective-permute-start.2 = (bf16[8,4224]{1,0:T(8,128)(2,1)S(1)}, bf16[8,4224]{1,0:T(8,128)(2,1)S(1)}, u32[]{:S(2)}, u32[]{:S(2)}) collective-permute-start(bf16[8,4224]{1,0:T(8,128)(2,1)S(1)} %shard_map.73.refs_0_), channel_id=1, source_target_pairs={{0,12},{1,13},{2,14},{3,15},{4,0},{5,1},{6,2},{7,3},{8,4},{9,5},{1... | collective-permute-start | bytes 202760 | tf_op jit(solution)/shard_map/ppermute | solution.py:31
  6.6 0.0 collective-permute-start.1
  6.6 1.0 %collective-permute-start = (bf16[8,4224]{1,0:T(8,128)(2,1)S(1)}, bf16[8,4224]{1,0:T(8,128)(2,1)S(1)}, u32[]{:S(2)}, u32[]{:S(2)}) collective-permute-start(bf16[8,4224]{1,0:T(8,128)(2,1)S(1)} %shard_map.73.refs_0_), channel_id=1, source_target_pairs={{0,4},{1,5},{2,6},{3,7},{4,8},{5,9},{6,10},{7,11},{8,12},{9,13},{1... | collective-permute-start | bytes 202760 | tf_op jit(solution)/shard_map/ppermute | solution.py:31
  7.6 0.7 reshape.3.refs_2_.gain_ref
  8.3 3.5 %shard_map.74 = (f32[8,128]{1,0:T(8,128)S(1)}, bf16[4096,512]{1,0:T(8,128)(2,1)S(1)}, bf16[4096,512]{1,0:T(8,128)(2,1)S(1)}) custom-call(bf16[4,4096,512]{2,1,0:T(8,128)(2,1)} %refs_1_.4, bf16[4,4096,512]{2,1,0:T(8,128)(2,1)} %refs_1_.4, bf16[1,4096]{1,0:T(2,128)(2,1)S(1)} %reshape.3.refs_2_.gain_ref), custom_call_target="tpu_custom_call" | custom-call | bytes 8388608 | tf_op jit(solution)/shard_map/pallas_call | solution.py:301
  11.8 0.0 collective-permute-done.2.refs_3_
  11.8 1.4 %collective-permute-done.1.refs_2_ = bf16[8,4224]{1,0:T(8,128)(2,1)S(1)} collective-permute-done((bf16[8,4224]{1,0:T(8,128)(2,1)S(1)}, bf16[8,4224]{1,0:T(8,128)(2,1)S(1)}, u32[]{:S(2)}, u32[]{:S(2)}) %collective-permute-start.1) | collective-permute-done | bytes 67616 | tf_op jit(solution)/shard_map/ppermute | solution.py:31
  13.3 0.0 collective-permute-done.refs_1_
  13.3 1.6 %collective-permute-start.3 = (bf16[32,2176]{1,0:T(8,128)(2,1)S(1)}, bf16[32,2176]{1,0:T(8,128)(2,1)S(1)}, u32[]{:S(2)}, u32[]{:S(2)}) collective-permute-start(bf16[32,2176]{1,0:T(8,128)(2,1)S(1)} %get-tuple-element.50.refs_0_), channel_id=1, source_target_pairs={{0,2},{1,3},{2,0},{3,1},{4,6},{5,7},{6,4},{7,5},{8,10},{9,11},{10,... | collective-permute-start | bytes 417800 | tf_op jit(solution)/shard_map/ppermute | solution.py:31
  14.9 1.5 %collective-permute-start.5 = (bf16[32,2048]{1,0:T(8,128)(2,1)S(1)}, bf16[32,2048]{1,0:T(8,128)(2,1)S(1)}, u32[]{:S(2)}, u32[]{:S(2)}) collective-permute-start(bf16[32,2048]{1,0:T(8,128)(2,1)S(1)} %get-tuple-element.57.refs_0_), channel_id=1, source_target_pairs={{0,16},{16,0},{1,17},{17,1},{2,18},{18,2},{3,19},{19,3},{4,20},{20... | collective-permute-start | bytes 393224 | tf_op jit(solution)/shard_map/ppermute | solution.py:31
  16.4 3.5 %shard_map.76 = (f32[8,128]{1,0:T(8,128)S(1)}, bf16[4096,512]{1,0:T(8,128)(2,1)S(1)}, bf16[4096,512]{1,0:T(8,128)(2,1)S(1)}) custom-call(bf16[4,4096,512]{2,1,0:T(8,128)(2,1)} %refs_1_.4, bf16[4,4096,512]{2,1,0:T(8,128)(2,1)} %refs_1_.4, f32[8,128]{1,0:T(8,128)S(1)} %get-tuple-element.51.refs_2_), custom_call_target="tpu_custom_call" | custom-call | bytes 8388608 | tf_op jit(solution)/shard_map/pallas_call | solution.py:301
  19.9 0.0 collective-permute-done.3.refs_1_
  19.9 0.6 collective-permute-start.4
  20.5 0.0 collective-permute-done.5.refs_1_
  20.5 1.5 %collective-permute-start.6 = (bf16[64,2048]{1,0:T(8,128)(2,1)S(1)}, bf16[64,2048]{1,0:T(8,128)(2,1)S(1)}, u32[]{:S(2)}, u32[]{:S(2)}) collective-permute-start(bf16[64,2048]{1,0:T(8,128)(2,1)S(1)} %shard_map.80.refs_0_), channel_id=1, source_target_pairs={{0,2},{1,3},{2,0},{3,1},{4,6},{5,7},{6,4},{7,5},{8,10},{9,11},{10,... | collective-permute-start | bytes 786440 | tf_op jit(solution)/shard_map/ppermute | solution.py:31
  22.0 4.7 %shard_map.78 = (f32[8,128]{1,0:T(8,128)S(1)}, bf16[4096,512]{1,0:T(8,128)(2,1)S(1)}, bf16[4096,512]{1,0:T(8,128)(2,1)S(1)}, bf16[1024,2048]{1,0:T(8,128)(2,1)S(1)}) custom-call(bf16[4,4096,512]{2,1,0:T(8,128)(2,1)} %refs_8_.1, bf16[4,4096,512]{2,1,0:T(8,128)(2,1)} %refs_8_.1, bf16[4,1024,2048]{2,1,0:T(8,128)(2,1)} %refs_4_.1, ...), custom_call_target="tpu_custom_call" | custom-call | bytes 12582912 | tf_op jit(solution)/shard_map/pallas_call | solution.py:301
  26.8 1.1 %collective-permute-done.4.refs_1_ = bf16[64,2176]{1,0:T(8,128)(2,1)S(1)} collective-permute-done((bf16[64,2176]{1,0:T(8,128)(2,1)S(1)}, bf16[64,2176]{1,0:T(8,128)(2,1)S(1)}, u32[]{:S(2)}, u32[]{:S(2)}) %collective-permute-start.4) | collective-permute-done | bytes 278560 | tf_op jit(solution)/shard_map/ppermute | solution.py:31
  27.9 0.1 collective-permute-start.7
  28.0 0.0 collective-permute-done.6.refs_1_
  28.1 0.6 collective-permute-start.8
  28.6 2.1 %collective-permute-done.8.refs_3_ = bf16[128,2048]{1,0:T(8,128)(2,1)S(1)} collective-permute-done((bf16[128,2048]{1,0:T(8,128)(2,1)S(1)}, bf16[128,2048]{1,0:T(8,128)(2,1)S(1)}, u32[]{:S(2)}, u32[]{:S(2)}) %collective-permute-start.8) | collective-permute-done | bytes 524320 | tf_op jit(solution)/shard_map/ppermute | solution.py:31
  30.7 0.0 collective-permute-done.7.refs_1_
  30.7 7.7 %shard_map.82 = (bf16[2,64,512]{2,1,0:T(8,128)(2,1)S(1)}, bf16[4,64,4096]{2,1,0:T(8,128)(2,1)S(1)}, bf16[2,256,256]{2,1,0:T(8,128)(2,1)S(1)}, bf16[2,256,256]{2,...) custom-call(s32[2]{0:T(128)S(1)} %pad_add_fusion.pos_ref, ...), custom_call_target="tpu_custom_call" | custom-call | flops 1610612736 | bytes 16777216 | tf_op jit(solution)/shard_map/pallas_call | solution.py:301
  38.4 0.8 %collective-permute-start.9 = (bf16[2,64,512]{2,1,0:T(8,128)(2,1)S(1)}, bf16[2,64,512]{2,1,0:T(8,128)(2,1)S(1)}, u32[]{:S(2)}, u32[]{:S(2)}) collective-permute-start(bf16[2,64,512]{2,1,0:T(8,128)(2,1)S(1)} %get-tuple-element.63.refs_0_), channel_id=1, source_target_pairs={{0,16},{16,0},{1,17},{17,1},{2,18},{18,2},{3,19},{19,3},{4,20},{20... | collective-permute-start | bytes 393224 | tf_op jit(solution)/shard_map/ppermute | solution.py:31
  39.2 5.6 %shard_map.85 = (bf16[2,64,512]{2,1,0:T(8,128)(2,1)S(1)}, bf16[1024,2048]{1,0:T(8,128)(2,1)S(1)}, bf16[1024,2048]{1,0:T(8,128)(2,1)S(1)}) custom-call(bf16[4,64,4096]{2,1,0:T(8,128)(2,1)S(1)} %get-tuple-element.67.normed_ref, bf16[4096,512]{1,0:T(8,128)(2,1)S(1)} %get-tuple-element.68.refs_0_, bf16[4096,512]{1,0:T(8,128)(2,1)S(1)} %get-tuple-element.69.refs_1_, ...), custom_call_target="tpu_custom_call" | custom-call | flops 1073741824 | bytes 16777216 | tf_op jit(solution)/shard_map/pallas_call | solution.py:301
  44.8 1.4 %collective-permute-start.10 = (bf16[2,64,512]{2,1,0:T(8,128)(2,1)S(1)}, bf16[2,64,512]{2,1,0:T(8,128)(2,1)S(1)}, u32[]{:S(2)}, u32[]{:S(2)}) collective-permute-start(bf16[2,64,512]{2,1,0:T(8,128)(2,1)S(1)} %get-tuple-element.72.refs_0_), channel_id=1, source_target_pairs={{0,16},{16,0},{1,17},{17,1},{2,18},{18,2},{3,19},{19,3},{4,20},{20... | collective-permute-start | bytes 393224 | tf_op jit(solution)/shard_map/ppermute | solution.py:31
  46.2 2.8 %shard_map.83 = (f32[8,128]{1,0:T(8,128)}, bf16[1024,2048]{1,0:T(8,128)(2,1)S(1)}) custom-call(bf16[4,1024,2048]{2,1,0:T(8,128)(2,1)} %refs_4_.1, f32[8,128]{1,0:T(8,128)S(1)} %get-tuple-element.65.refs_1_), custom_call_target="tpu_custom_call" | custom-call | bytes 4194304 | tf_op jit(solution)/shard_map/pallas_call | solution.py:301
  49.0 0.0 collective-permute-done.9.refs_1_
  49.0 2.1 %shard_map.84.done_ref = bf16[128,2048]{1,0:T(8,128)(2,1)S(1)} custom-call(s32[2]{0:T(128)S(1)} %pad_add_fusion.pos_ref, bf16[2,64,512]{2,1,0:T(8,128)(2,1)S(1)} %get-tuple-element.63.refs_0_, bf16[2,64,512]{2,1,0:T(8,128)(2,1)S(1)} %collective-permute-done.9.refs_1_, bf16[1024,2048]{1,0:T(8,128)(2,1)S(1)} %get-tuple-element.64.refs_2_, ...), custom_call_target="tpu_custom_call" | custom-call | flops 536870912 | bytes 8388608 | tf_op jit(solution)/shard_map/pallas_call | solution.py:301
  51.2 0.0 collective-permute-done.10.refs_1_
  51.2 1.7 %shard_map.86 = (bf16[128,1024]{1,0:T(8,128)(2,1)S(1)}, bf16[128,1024]{1,0:T(8,128)(2,1)S(1)}) custom-call(s32[2]{0:T(128)S(1)} %pad_add_fusion.pos_ref, bf16[2,256,256]{2,1,0:T(8,128)(2,1)S(1)} %get-tuple-element.62.mix_ref, bf16[128,2048]{1,0:T(8,128)(2,1)S(1)} %shard_map.84.done_ref, bf16[2,64,512]{2,1,0:T(8,128)(2,1)S(1)} %get-tuple-element.72.refs_0_, ...), custom_call_target="tpu_custom_call" | custom-call | flops 536870912 | bytes 8388608 | tf_op jit(solution)/shard_map/pallas_call | solution.py:301
  52.9 0.1 collective-permute-start.11
  53.0 1.7 %shard_map.89 = (bf16[128,1024]{1,0:T(8,128)(2,1)S(1)}, bf16[128,1024]{1,0:T(8,128)(2,1)S(1)}) custom-call(s32[2]{0:T(128)S(1)} %pad_add_fusion.pos_ref, bf16[2,256,256]{2,1,0:T(8,128)(2,1)S(1)} %get-tuple-element.83.mix_ref, bf16[128,2048]{1,0:T(8,128)(2,1)S(1)} %shard_map.84.done_ref, bf16[2,64,512]{2,1,0:T(8,128)(2,1)S(1)} %get-tuple-element.72.refs_0_, ...), custom_call_target="tpu_custom_call" | custom-call | flops 536870912 | bytes 8388608 | tf_op jit(solution)/shard_map/pallas_call | solution.py:301
  54.7 0.6 collective-permute-start.16
  55.3 0.0 collective-permute-done.11.refs_1_
  55.3 0.1 shard_map.87
  55.4 0.6 collective-permute-start.12
  55.9 0.5 collective-permute-done.16.refs_1_
  56.4 0.1 shard_map.90
  56.5 0.9 %collective-permute-start.17 = (bf16[32,1024]{1,0:T(8,128)(2,1)S(1)}, bf16[32,1024]{1,0:T(8,128)(2,1)S(1)}, u32[]{:S(2)}, u32[]{:S(2)}) collective-permute-start(bf16[32,1024]{1,0:T(8,128)(2,1)S(1)} %get-tuple-element.87), channel_id=1, source_target_pairs={{0,12},{1,13},{2,14},{3,15},{4,0},{5,1},{6,2},{7,3},{8,4},{9,5},{1... | collective-permute-start | bytes 196616 | tf_op jit(solution)/shard_map/ppermute | solution.py:31
  57.4 0.8 %collective-permute-start.18 = (bf16[32,1024]{1,0:T(8,128)(2,1)S(1)}, bf16[32,1024]{1,0:T(8,128)(2,1)S(1)}, u32[]{:S(2)}, u32[]{:S(2)}) collective-permute-start(bf16[32,1024]{1,0:T(8,128)(2,1)S(1)} %get-tuple-element.88), channel_id=1, source_target_pairs={{0,8},{1,9},{2,10},{3,11},{4,12},{5,13},{6,14},{7,15},{8,0},{9,1},... | collective-permute-start | bytes 196616 | tf_op jit(solution)/shard_map/ppermute | solution.py:31
  58.2 1.7 %collective-permute-start.19 = (bf16[32,1024]{1,0:T(8,128)(2,1)S(1)}, bf16[32,1024]{1,0:T(8,128)(2,1)S(1)}, u32[]{:S(2)}, u32[]{:S(2)}) collective-permute-start(bf16[32,1024]{1,0:T(8,128)(2,1)S(1)} %get-tuple-element.89), channel_id=1, source_target_pairs={{0,4},{1,5},{2,6},{3,7},{4,8},{5,9},{6,10},{7,11},{8,12},{9,13},{1... | collective-permute-start | bytes 196616 | tf_op jit(solution)/shard_map/ppermute | solution.py:31
  59.9 0.9 %collective-permute-done.12.refs_1_ = bf16[64,1024]{1,0:T(8,128)(2,1)S(1)} collective-permute-done((bf16[64,1024]{1,0:T(8,128)(2,1)S(1)}, bf16[64,1024]{1,0:T(8,128)(2,1)S(1)}, u32[]{:S(2)}, u32[]{:S(2)}) %collective-permute-start.12) | collective-permute-done | bytes 131104 | tf_op jit(solution)/shard_map/ppermute | solution.py:31
  60.9 1.2 %collective-permute-start.13 = (bf16[16,1024]{1,0:T(8,128)(2,1)S(1)}, bf16[16,1024]{1,0:T(8,128)(2,1)S(1)}, u32[]{:S(2)}, u32[]{:S(2)}) collective-permute-start(bf16[16,1024]{1,0:T(8,128)(2,1)S(1)} %get-tuple-element.80), channel_id=1, source_target_pairs={{0,12},{1,13},{2,14},{3,15},{4,0},{5,1},{6,2},{7,3},{8,4},{9,5},{1... | collective-permute-start | bytes 98312 | tf_op jit(solution)/shard_map/ppermute | solution.py:31
  62.1 0.4 collective-permute-start.14
  62.6 0.0 collective-permute-done.17.refs_1_
  62.6 1.7 %collective-permute-start.15 = (bf16[16,1024]{1,0:T(8,128)(2,1)S(1)}, bf16[16,1024]{1,0:T(8,128)(2,1)S(1)}, u32[]{:S(2)}, u32[]{:S(2)}) collective-permute-start(bf16[16,1024]{1,0:T(8,128)(2,1)S(1)} %get-tuple-element.82), channel_id=1, source_target_pairs={{0,4},{1,5},{2,6},{3,7},{4,8},{5,9},{6,10},{7,11},{8,12},{9,13},{1... | collective-permute-start | bytes 98312 | tf_op jit(solution)/shard_map/ppermute | solution.py:31
  64.3 2.3 %collective-permute-done.18.refs_2_ = bf16[32,1024]{1,0:T(8,128)(2,1)S(1)} collective-permute-done((bf16[32,1024]{1,0:T(8,128)(2,1)S(1)}, bf16[32,1024]{1,0:T(8,128)(2,1)S(1)}, u32[]{:S(2)}, u32[]{:S(2)}) %collective-permute-start.18) | collective-permute-done | bytes 65568 | tf_op jit(solution)/shard_map/ppermute | solution.py:31
  66.5 0.0 collective-permute-done.19.refs_3_
  66.6 0.8 %collective-permute-start.20 = (bf16[16,1024]{1,0:T(8,128)(2,1)S(1)}, bf16[16,1024]{1,0:T(8,128)(2,1)S(1)}, u32[]{:S(2)}, u32[]{:S(2)}) collective-permute-start(bf16[16,1024]{1,0:T(8,128)(2,1)S(1)} %get-tuple-element.92), channel_id=1, source_target_pairs={{0,2},{1,3},{2,0},{3,1},{4,6},{5,7},{6,4},{7,5},{8,10},{9,11},{10,... | collective-permute-start | bytes 98312 | tf_op jit(solution)/shard_map/ppermute | solution.py:31
  67.4 0.0 collective-permute-done.13.refs_1_
  67.4 0.3 collective-permute-done.14.refs_2_
  67.7 0.6 collective-permute-done.15.refs_3_
  68.3 2.3 %collective-permute-done.20.refs_5_ = bf16[16,1024]{1,0:T(8,128)(2,1)S(1)} collective-permute-done((bf16[16,1024]{1,0:T(8,128)(2,1)S(1)}, bf16[16,1024]{1,0:T(8,128)(2,1)S(1)}, u32[]{:S(2)}, u32[]{:S(2)}) %collective-permute-start.20) | collective-permute-done | bytes 32800 | tf_op jit(solution)/shard_map/ppermute | solution.py:31
  70.6 1.2 %shard_map.92 = bf16[16,2048]{1,0:T(8,128)(2,1)} custom-call(s32[2]{0:T(128)S(1)} %pad_add_fusion.pos_ref, bf16[128,2176]{1,0:T(8,128)(2,1)S(1)} %get-tuple-element.56.refs_0_.first_ref, bf16[128,2048]{1,0:T(8,128)(2,1)S(1)} %shard_map.81.refs_2_.second_ref, bf16[16,1024]{1,0:T(8,128)(2,1)S(1)} %get-tuple-element.79.refs_0_, ...), custom_call_target="tpu_custom_call" | custom-call | bytes 524288 | tf_op jit(solution)/shard_map/pallas_call | solution.py:301
  (7 shorter events, 0.2 us)
Async XLA Ops:
  1.5 10.3 %collective-permute-start.2 = (bf16[8,4224]{1,0:T(8,128)(2,1)S(1)}, bf16[8,4224]{1,0:T(8,128)(2,1)S(1)}, u32[]{:S(2)}, u32[]{:S(2)}) collective-permute-start(bf16[8,4224]{1,0:T(8,128)(2,1)S(1)} %shard_map.73.refs_0_), channel_id=1, source_target_pairs={{0,12},{1,13},{2,14},{3,15},{4,0},{5,1},{6,2},{7,3},{8,4},{9,5},{1... | collective-permute-start | bytes 202760 | tf_op jit(solution)/shard_map/ppermute | solution.py:31
  6.6 6.6 %collective-permute-start.1 = (bf16[8,4224]{1,0:T(8,128)(2,1)S(1)}, bf16[8,4224]{1,0:T(8,128)(2,1)S(1)}, u32[]{:S(2)}, u32[]{:S(2)}) collective-permute-start(bf16[8,4224]{1,0:T(8,128)(2,1)S(1)} %shard_map.73.refs_0_), channel_id=1, source_target_pairs={{0,8},{1,9},{2,10},{3,11},{4,12},{5,13},{6,14},{7,15},{8,0},{9,1},... | collective-permute-start | bytes 202760 | tf_op jit(solution)/shard_map/ppermute | solution.py:31
  6.6 6.6 %collective-permute-start = (bf16[8,4224]{1,0:T(8,128)(2,1)S(1)}, bf16[8,4224]{1,0:T(8,128)(2,1)S(1)}, u32[]{:S(2)}, u32[]{:S(2)}) collective-permute-start(bf16[8,4224]{1,0:T(8,128)(2,1)S(1)} %shard_map.73.refs_0_), channel_id=1, source_target_pairs={{0,4},{1,5},{2,6},{3,7},{4,8},{5,9},{6,10},{7,11},{8,12},{9,13},{1... | collective-permute-start | bytes 202760 | tf_op jit(solution)/shard_map/ppermute | solution.py:31
  13.3 6.6 %collective-permute-start.3 = (bf16[32,2176]{1,0:T(8,128)(2,1)S(1)}, bf16[32,2176]{1,0:T(8,128)(2,1)S(1)}, u32[]{:S(2)}, u32[]{:S(2)}) collective-permute-start(bf16[32,2176]{1,0:T(8,128)(2,1)S(1)} %get-tuple-element.50.refs_0_), channel_id=1, source_target_pairs={{0,2},{1,3},{2,0},{3,1},{4,6},{5,7},{6,4},{7,5},{8,10},{9,11},{10,... | collective-permute-start | bytes 417800 | tf_op jit(solution)/shard_map/ppermute | solution.py:31
  14.9 5.6 %collective-permute-start.5 = (bf16[32,2048]{1,0:T(8,128)(2,1)S(1)}, bf16[32,2048]{1,0:T(8,128)(2,1)S(1)}, u32[]{:S(2)}, u32[]{:S(2)}) collective-permute-start(bf16[32,2048]{1,0:T(8,128)(2,1)S(1)} %get-tuple-element.57.refs_0_), channel_id=1, source_target_pairs={{0,16},{16,0},{1,17},{17,1},{2,18},{18,2},{3,19},{19,3},{4,20},{20... | collective-permute-start | bytes 393224 | tf_op jit(solution)/shard_map/ppermute | solution.py:31
  19.9 8.0 %collective-permute-start.4 = (bf16[64,2176]{1,0:T(8,128)(2,1)S(1)}, bf16[64,2176]{1,0:T(8,128)(2,1)S(1)}, u32[]{:S(2)}, u32[]{:S(2)}) collective-permute-start(bf16[64,2176]{1,0:T(8,128)(2,1)S(1)} %get-tuple-element.53.refs_0_), channel_id=1, source_target_pairs={{0,16},{16,0},{1,17},{17,1},{2,18},{18,2},{3,19},{19,3},{4,20},{20... | collective-permute-start | bytes 835592 | tf_op jit(solution)/shard_map/ppermute | solution.py:31
  20.5 7.5 %collective-permute-start.6 = (bf16[64,2048]{1,0:T(8,128)(2,1)S(1)}, bf16[64,2048]{1,0:T(8,128)(2,1)S(1)}, u32[]{:S(2)}, u32[]{:S(2)}) collective-permute-start(bf16[64,2048]{1,0:T(8,128)(2,1)S(1)} %shard_map.80.refs_0_), channel_id=1, source_target_pairs={{0,2},{1,3},{2,0},{3,1},{4,6},{5,7},{6,4},{7,5},{8,10},{9,11},{10,... | collective-permute-start | bytes 786440 | tf_op jit(solution)/shard_map/ppermute | solution.py:31
  27.9 2.8 %collective-permute-start.7 = (bf16[128,2176]{1,0:T(8,128)(2,1)S(1)}, bf16[128,2176]{1,0:T(8,128)(2,1)S(1)}, u32[]{:S(2)}, u32[]{:S(2)}) collective-permute-start(bf16[128,2176]{1,0:T(8,128)(2,1)S(1)} %get-tuple-element.56.refs_0_.first_ref), channel_id=1, source_target_pairs={{0,1},{1,0},{2,3},{3,2},{4,5},{5,4},{6,7},{7,6},{8,9},{9,8},{10,11... | collective-permute-start | bytes 1671176 | tf_op jit(solution)/shard_map/ppermute | solution.py:31
  28.1 2.6 %collective-permute-start.8 = (bf16[128,2048]{1,0:T(8,128)(2,1)S(1)}, bf16[128,2048]{1,0:T(8,128)(2,1)S(1)}, u32[]{:S(2)}, u32[]{:S(2)}) collective-permute-start(bf16[128,2048]{1,0:T(8,128)(2,1)S(1)} %shard_map.81.refs_2_.second_ref), channel_id=1, source_target_pairs={{0,1},{1,0},{2,3},{3,2},{4,5},{5,4},{6,7},{7,6},{8,9},{9,8},{10,11... | collective-permute-start | bytes 1572872 | tf_op jit(solution)/shard_map/ppermute | solution.py:31
  38.4 10.6 %collective-permute-start.9 = (bf16[2,64,512]{2,1,0:T(8,128)(2,1)S(1)}, bf16[2,64,512]{2,1,0:T(8,128)(2,1)S(1)}, u32[]{:S(2)}, u32[]{:S(2)}) collective-permute-start(bf16[2,64,512]{2,1,0:T(8,128)(2,1)S(1)} %get-tuple-element.63.refs_0_), channel_id=1, source_target_pairs={{0,16},{16,0},{1,17},{17,1},{2,18},{18,2},{3,19},{19,3},{4,20},{20... | collective-permute-start | bytes 393224 | tf_op jit(solution)/shard_map/ppermute | solution.py:31
  44.8 6.4 %collective-permute-start.10 = (bf16[2,64,512]{2,1,0:T(8,128)(2,1)S(1)}, bf16[2,64,512]{2,1,0:T(8,128)(2,1)S(1)}, u32[]{:S(2)}, u32[]{:S(2)}) collective-permute-start(bf16[2,64,512]{2,1,0:T(8,128)(2,1)S(1)} %get-tuple-element.72.refs_0_), channel_id=1, source_target_pairs={{0,16},{16,0},{1,17},{17,1},{2,18},{18,2},{3,19},{19,3},{4,20},{20... | collective-permute-start | bytes 393224 | tf_op jit(solution)/shard_map/ppermute | solution.py:31
  52.9 2.4 %collective-permute-start.11 = (bf16[128,1024]{1,0:T(8,128)(2,1)S(1)}, bf16[128,1024]{1,0:T(8,128)(2,1)S(1)}, u32[]{:S(2)}, u32[]{:S(2)}) collective-permute-start(bf16[128,1024]{1,0:T(8,128)(2,1)S(1)} %get-tuple-element.76), channel_id=1, source_target_pairs={{0,1},{1,0},{2,3},{3,2},{4,5},{5,4},{6,7},{7,6},{8,9},{9,8},{10,11... | collective-permute-start | bytes 786440 | tf_op jit(solution)/shard_map/ppermute | solution.py:31
  54.7 1.7 %collective-permute-start.16 = (bf16[128,1024]{1,0:T(8,128)(2,1)S(1)}, bf16[128,1024]{1,0:T(8,128)(2,1)S(1)}, u32[]{:S(2)}, u32[]{:S(2)}) collective-permute-start(bf16[128,1024]{1,0:T(8,128)(2,1)S(1)} %get-tuple-element.85), channel_id=1, source_target_pairs={{0,1},{1,0},{2,3},{3,2},{4,5},{5,4},{6,7},{7,6},{8,9},{9,8},{10,11... | collective-permute-start | bytes 786440 | tf_op jit(solution)/shard_map/ppermute | solution.py:31
  55.4 5.5 %collective-permute-start.12 = (bf16[64,1024]{1,0:T(8,128)(2,1)S(1)}, bf16[64,1024]{1,0:T(8,128)(2,1)S(1)}, u32[]{:S(2)}, u32[]{:S(2)}) collective-permute-start(bf16[64,1024]{1,0:T(8,128)(2,1)S(1)} %get-tuple-element.78), channel_id=1, source_target_pairs={{0,2},{1,3},{2,0},{3,1},{4,6},{5,7},{6,4},{7,5},{8,10},{9,11},{10,... | collective-permute-start | bytes 393224 | tf_op jit(solution)/shard_map/ppermute | solution.py:31
  56.5 6.1 %collective-permute-start.17 = (bf16[32,1024]{1,0:T(8,128)(2,1)S(1)}, bf16[32,1024]{1,0:T(8,128)(2,1)S(1)}, u32[]{:S(2)}, u32[]{:S(2)}) collective-permute-start(bf16[32,1024]{1,0:T(8,128)(2,1)S(1)} %get-tuple-element.87), channel_id=1, source_target_pairs={{0,12},{1,13},{2,14},{3,15},{4,0},{5,1},{6,2},{7,3},{8,4},{9,5},{1... | collective-permute-start | bytes 196616 | tf_op jit(solution)/shard_map/ppermute | solution.py:31
  57.4 9.2 %collective-permute-start.18 = (bf16[32,1024]{1,0:T(8,128)(2,1)S(1)}, bf16[32,1024]{1,0:T(8,128)(2,1)S(1)}, u32[]{:S(2)}, u32[]{:S(2)}) collective-permute-start(bf16[32,1024]{1,0:T(8,128)(2,1)S(1)} %get-tuple-element.88), channel_id=1, source_target_pairs={{0,8},{1,9},{2,10},{3,11},{4,12},{5,13},{6,14},{7,15},{8,0},{9,1},... | collective-permute-start | bytes 196616 | tf_op jit(solution)/shard_map/ppermute | solution.py:31
  58.2 8.3 %collective-permute-start.19 = (bf16[32,1024]{1,0:T(8,128)(2,1)S(1)}, bf16[32,1024]{1,0:T(8,128)(2,1)S(1)}, u32[]{:S(2)}, u32[]{:S(2)}) collective-permute-start(bf16[32,1024]{1,0:T(8,128)(2,1)S(1)} %get-tuple-element.89), channel_id=1, source_target_pairs={{0,4},{1,5},{2,6},{3,7},{4,8},{5,9},{6,10},{7,11},{8,12},{9,13},{1... | collective-permute-start | bytes 196616 | tf_op jit(solution)/shard_map/ppermute | solution.py:31
  60.9 6.5 %collective-permute-start.13 = (bf16[16,1024]{1,0:T(8,128)(2,1)S(1)}, bf16[16,1024]{1,0:T(8,128)(2,1)S(1)}, u32[]{:S(2)}, u32[]{:S(2)}) collective-permute-start(bf16[16,1024]{1,0:T(8,128)(2,1)S(1)} %get-tuple-element.80), channel_id=1, source_target_pairs={{0,12},{1,13},{2,14},{3,15},{4,0},{5,1},{6,2},{7,3},{8,4},{9,5},{1... | collective-permute-start | bytes 98312 | tf_op jit(solution)/shard_map/ppermute | solution.py:31
  62.1 5.5 %collective-permute-start.14 = (bf16[16,1024]{1,0:T(8,128)(2,1)S(1)}, bf16[16,1024]{1,0:T(8,128)(2,1)S(1)}, u32[]{:S(2)}, u32[]{:S(2)}) collective-permute-start(bf16[16,1024]{1,0:T(8,128)(2,1)S(1)} %get-tuple-element.81), channel_id=1, source_target_pairs={{0,8},{1,9},{2,10},{3,11},{4,12},{5,13},{6,14},{7,15},{8,0},{9,1},... | collective-permute-start | bytes 98312 | tf_op jit(solution)/shard_map/ppermute | solution.py:31
  62.6 5.7 %collective-permute-start.15 = (bf16[16,1024]{1,0:T(8,128)(2,1)S(1)}, bf16[16,1024]{1,0:T(8,128)(2,1)S(1)}, u32[]{:S(2)}, u32[]{:S(2)}) collective-permute-start(bf16[16,1024]{1,0:T(8,128)(2,1)S(1)} %get-tuple-element.82), channel_id=1, source_target_pairs={{0,4},{1,5},{2,6},{3,7},{4,8},{5,9},{6,10},{7,11},{8,12},{9,13},{1... | collective-permute-start | bytes 98312 | tf_op jit(solution)/shard_map/ppermute | solution.py:31
  66.6 4.0 %collective-permute-start.20 = (bf16[16,1024]{1,0:T(8,128)(2,1)S(1)}, bf16[16,1024]{1,0:T(8,128)(2,1)S(1)}, u32[]{:S(2)}, u32[]{:S(2)}) collective-permute-start(bf16[16,1024]{1,0:T(8,128)(2,1)S(1)} %get-tuple-element.92), channel_id=1, source_target_pairs={{0,2},{1,3},{2,0},{3,1},{4,6},{5,7},{6,4},{7,5},{8,10},{9,11},{10,... | collective-permute-start | bytes 98312 | tf_op jit(solution)/shard_map/ppermute | solution.py:31

commit v8 on v7

--- a/solution.py
+++ b/solution.py
@@ -111,13 +111,8 @@
         hidden_ref[i] = (gate_act / (1.0 + jnp.exp(-gate_act)) * up_act).astype(jnp.bfloat16)
 
 
-def select_kernel(dims, lead, tail, pos_ref, gain_ref, *refs):
+def select_body(dims, pos_ref, gain_ref, first, second, gates, ups, hidden_ref, normed_ref, mix_ref, turned_ref):
     n_fast, n_mid, n_tp, slow_n, tok_dev, top, exp_loc, rows, half = dims
-    first, second = refs[:n_fast], refs[n_fast : 2 * n_fast]
-    refs = refs[2 * n_fast :]
-    gates, ups, refs = refs[:lead], refs[lead : 2 * lead], refs[2 * lead :]
-    far_ref, hidden_ref, normed_ref, mix_ref, turned_ref, *near, sems = refs
-    copies = load_copies([far_ref] * tail, near, sems, range(lead, lead + tail))
     tp_pos, base = pos_ref[0], pos_ref[1]
     run = slow_n * tok_dev
     tokens = n_fast * n_mid * n_tp * run
@@ -198,14 +193,31 @@
         normed_ref[e, :, :half] = (left * scale * gain[:, :half]).astype(jnp.bfloat16)
         normed_ref[e, :, half:] = (right * scale * gain[:, half:]).astype(jnp.bfloat16)
     swiglu(normed_ref, gates, ups, hidden_ref, 0)
+
+
+def select_kernel(dims, lead, tail, pos_ref, gain_ref, *refs):
+    n_fast = dims[0]
+    first, second, refs = refs[:n_fast], refs[n_fast : 2 * n_fast], refs[2 * n_fast :]
+    gates, ups, refs = refs[:lead], refs[lead : 2 * lead], refs[2 * lead :]
+    _, far_ref, hidden_ref, normed_ref, mix_ref, turned_ref, *near, sems = refs
+    copies = load_copies([far_ref] * tail, near, sems, range(lead, lead + tail))
+
+    @pl.when(pos_ref[0] >= 0)
+    def _():
+        select_body(dims, pos_ref, gain_ref, first, second, gates, ups, hidden_ref, normed_ref, mix_ref, turned_ref)
+
     for copy in copies:
         copy.wait()
 
 
-def up_kernel(start, count, wanted, normed_ref, *refs):
+def up_kernel(start, count, wanted, pos_ref, normed_ref, *refs):
     gates, ups, (far_ref, hidden_ref, *near, sems) = refs[:count], refs[count : 2 * count], refs[2 * count :]
     copies = load_copies([far_ref] * len(near), near, sems, wanted)
-    swiglu(normed_ref, gates, ups, hidden_ref, start)
+
+    @pl.when(pos_ref[0] >= 0)
+    def _():
+        swiglu(normed_ref, gates, ups, hidden_ref, start)
+
     for copy in copies:
         copy.wait()
 
@@ -411,7 +423,7 @@
     *up_lead, down_first = up_lead
     first, second = along_tp(first), along_mid(second)
     first, sign = joined(first, [sign], 1)
-    down_lead, _ = loaded([(w_down, e) for e in range(1, lead)], [sign]) if lead > 1 else ([], None)
+    down_lead, sign = loaded([(w_down, e) for e in range(1, lead)], [sign]) if lead > 1 else ([], sign)
     down_lead = [down_first] + down_lead
     (second,) = joined(second, [], 0)
     first = arrivals(first, "ep", n_ep, *fast)
@@ -419,7 +431,7 @@
 
     dims = (n_fast, n_mid, n_tp, slow_n, tok_dev, top, exp_loc, rows, half)
     sems = lambda array, count: pltpu.SemaphoreType.DMA((count, runs_of(array)))
-    operands = [position, gain] + first + second + gate_lead + up_lead + [w_up]
+    operands = [position, gain] + first + second + gate_lead + up_lead + [sign, w_up]
     hidden, normed, mix, turned, *up_tail = local_call(
         functools.partial(select_kernel, dims, lead, tail),
         [
@@ -436,7 +448,7 @@
         moved=4 * lead * width * hid_part,
     )
     pieces = along_tp(hidden)
-    operands = [normed] + gate_tail + up_tail + [w_down]
+    operands = [position, normed] + gate_tail + up_tail + [w_down]
     hidden, *down_tail = local_call(
         functools.partial(up_kernel, lead, tail, range(lead, exp_loc)),
         [bf16((tail, rows, hid_part))] + kept(w_down, tail),

time: 72 us -> 70.4 us (0.978)
  Pallas kernels: 36.4 us -> 32.4 us
  local copies, waits for them, and re-layouts: 0.71 us -> 2.68 us
    pallas_call x20, Pallas kernels: 36.4 us -> 32.4 us  [local_call(): pl.pallas_call(kernel, out_shape=shapes, in_specs=specs, out_specs=[VMEM]...]
    unnamed x0 -> x4, local copies, waits for them, and re-layouts: none -> 1.97 us
  transfers between devices with their start and end apart: 21 -> 21, of which waited for: 9 -> 9; matrix products, arithmetic and copies ran while one was open for 1% -> 1% of each run, Pallas kernels for 34% -> 32%
where the time goes in v8:
time: 70.4 us; the launch traced here: 70.1 us
  Pallas kernels  32.4 us (46%)
  starting transfers between devices  22.9 us (33%)
  waiting for transfers between devices  11.9 us (17%)
  local copies, waits for them, and re-layouts  2.68 us (4%)
    pallas_call x20, Pallas kernels, local_call(): pl.pallas_call(kernel, out_shape=shapes, in_specs=specs, out_specs=[VMEM]...  32.4 us
    ppermute x21, starting transfers between devices, shifted(): return lax.ppermute(x, axis, pairs)  22.9 us
    ppermute x21, waiting for transfers between devices, shifted(): return lax.ppermute(x, axis, pairs)  11.9 us
    unnamed x4, local copies, waits for them, and re-layouts  1.97 us
  transfers between devices with their start and end apart: 21, of which 9 were waited for; matrix products, arithmetic and copies ran while one was open for 1% of the time, Pallas kernels for 32%

profile of v8, /device:TPU:0, one launch (start us, length us, event | category | flops | bytes accessed | tf_op | source)
XLA Modules:
  0.0 70.1 jit_solution(14786657631134017560)
XLA Ops:
  0.0 0.1 pad_add_fusion.pos_ref
  0.1 1.4 %shard_map.73.refs_0_ = bf16[8,4224]{1,0:T(8,128)(2,1)S(1)} custom-call(s32[2]{0:T(128)S(1)} %pad_add_fusion.pos_ref, s32[8,16]{1,0:T(8,128)} %bitcast.4, f32[8,16]{1,0:T(8,128)} %bitcast.5, bf16[8,4096]{1,0:T(8,128)(2,1)} %values_ref.1), custom_call_target="tpu_custom_call" | custom-call | tf_op jit(solution)/shard_map/pallas_call | solution.py:313
  1.5 5.1 %collective-permute-start.2 = (bf16[8,4224]{1,0:T(8,128)(2,1)S(1)}, bf16[8,4224]{1,0:T(8,128)(2,1)S(1)}, u32[]{:S(2)}, u32[]{:S(2)}) collective-permute-start(bf16[8,4224]{1,0:T(8,128)(2,1)S(1)} %shard_map.73.refs_0_), channel_id=1, source_target_pairs={{0,12},{1,13},{2,14},{3,15},{4,0},{5,1},{6,2},{7,3},{8,4},{9,5},{1... | collective-permute-start | bytes 202760 | tf_op jit(solution)/shard_map/ppermute | solution.py:31
  6.6 0.0 collective-permute-start.1
  6.6 1.0 %collective-permute-start = (bf16[8,4224]{1,0:T(8,128)(2,1)S(1)}, bf16[8,4224]{1,0:T(8,128)(2,1)S(1)}, u32[]{:S(2)}, u32[]{:S(2)}) collective-permute-start(bf16[8,4224]{1,0:T(8,128)(2,1)S(1)} %shard_map.73.refs_0_), channel_id=1, source_target_pairs={{0,4},{1,5},{2,6},{3,7},{4,8},{5,9},{6,10},{7,11},{8,12},{9,13},{1... | collective-permute-start | bytes 202760 | tf_op jit(solution)/shard_map/ppermute | solution.py:31
  7.6 0.7 %reshape.3.refs_2_.gain_ref = bf16[1,4096]{1,0:T(2,128)(2,1)S(1)} reshape(bf16[4096]{0:T(1024)(128)(2,1)} %param.8) | data formatting | bytes 16384 | tf_op jit(solution)/shard_map/reshape | solution.py:392
  8.3 3.5 %shard_map.74 = (f32[8,128]{1,0:T(8,128)S(1)}, bf16[4096,512]{1,0:T(8,128)(2,1)S(1)}, bf16[4096,512]{1,0:T(8,128)(2,1)S(1)}) custom-call(bf16[4,4096,512]{2,1,0:T(8,128)(2,1)} %refs_1_.4, bf16[4,4096,512]{2,1,0:T(8,128)(2,1)} %refs_1_.4, bf16[1,4096]{1,0:T(2,128)(2,1)S(1)} %reshape.3.refs_2_.gain_ref), custom_call_target="tpu_custom_call" | custom-call | bytes 8388608 | tf_op jit(solution)/shard_map/pallas_call | solution.py:313
  11.8 0.0 collective-permute-done.2.refs_3_
  11.8 1.4 %collective-permute-done.1.refs_2_ = bf16[8,4224]{1,0:T(8,128)(2,1)S(1)} collective-permute-done((bf16[8,4224]{1,0:T(8,128)(2,1)S(1)}, bf16[8,4224]{1,0:T(8,128)(2,1)S(1)}, u32[]{:S(2)}, u32[]{:S(2)}) %collective-permute-start.1) | collective-permute-done | bytes 67616 | tf_op jit(solution)/shard_map/ppermute | solution.py:31
  13.3 0.0 collective-permute-done.refs_1_
  13.3 1.6 %collective-permute-start.3 = (bf16[32,2176]{1,0:T(8,128)(2,1)S(1)}, bf16[32,2176]{1,0:T(8,128)(2,1)S(1)}, u32[]{:S(2)}, u32[]{:S(2)}) collective-permute-start(bf16[32,2176]{1,0:T(8,128)(2,1)S(1)} %get-tuple-element.51.refs_0_), channel_id=1, source_target_pairs={{0,2},{1,3},{2,0},{3,1},{4,6},{5,7},{6,4},{7,5},{8,10},{9,11},{10,... | collective-permute-start | bytes 417800 | tf_op jit(solution)/shard_map/ppermute | solution.py:31
  14.9 1.5 %collective-permute-start.5 = (bf16[32,2048]{1,0:T(8,128)(2,1)S(1)}, bf16[32,2048]{1,0:T(8,128)(2,1)S(1)}, u32[]{:S(2)}, u32[]{:S(2)}) collective-permute-start(bf16[32,2048]{1,0:T(8,128)(2,1)S(1)} %get-tuple-element.58.refs_0_), channel_id=1, source_target_pairs={{0,16},{16,0},{1,17},{17,1},{2,18},{18,2},{3,19},{19,3},{4,20},{20... | collective-permute-start | bytes 393224 | tf_op jit(solution)/shard_map/ppermute | solution.py:31
  16.4 3.5 %shard_map.76 = (f32[8,128]{1,0:T(8,128)S(1)}, bf16[4096,512]{1,0:T(8,128)(2,1)S(1)}, bf16[4096,512]{1,0:T(8,128)(2,1)S(1)}) custom-call(bf16[4,4096,512]{2,1,0:T(8,128)(2,1)} %refs_1_.4, bf16[4,4096,512]{2,1,0:T(8,128)(2,1)} %refs_1_.4, f32[8,128]{1,0:T(8,128)S(1)} %get-tuple-element.52.refs_2_), custom_call_target="tpu_custom_call" | custom-call | bytes 8388608 | tf_op jit(solution)/shard_map/pallas_call | solution.py:313
  19.9 0.0 collective-permute-done.3.refs_1_
  19.9 0.6 collective-permute-start.4
  20.5 0.0 collective-permute-done.5.refs_1_
  20.5 1.5 %collective-permute-start.6 = (bf16[64,2048]{1,0:T(8,128)(2,1)S(1)}, bf16[64,2048]{1,0:T(8,128)(2,1)S(1)}, u32[]{:S(2)}, u32[]{:S(2)}) collective-permute-start(bf16[64,2048]{1,0:T(8,128)(2,1)S(1)} %shard_map.80.refs_0_), channel_id=1, source_target_pairs={{0,2},{1,3},{2,0},{3,1},{4,6},{5,7},{6,4},{7,5},{8,10},{9,11},{10,... | collective-permute-start | bytes 786440 | tf_op jit(solution)/shard_map/ppermute | solution.py:31
  22.0 4.7 %shard_map.78 = (f32[8,128]{1,0:T(8,128)S(1)}, bf16[4096,512]{1,0:T(8,128)(2,1)S(1)}, bf16[4096,512]{1,0:T(8,128)(2,1)S(1)}, bf16[1024,2048]{1,0:T(8,128)(2,1)S(1)}) custom-call(bf16[4,4096,512]{2,1,0:T(8,128)(2,1)} %refs_9_.1, bf16[4,4096,512]{2,1,0:T(8,128)(2,1)} %refs_9_.1, bf16[4,1024,2048]{2,1,0:T(8,128)(2,1)} %refs_4_.1, ...), custom_call_target="tpu_custom_call" | custom-call | bytes 12582912 | tf_op jit(solution)/shard_map/pallas_call | solution.py:313
  26.8 1.1 %collective-permute-done.4.refs_1_ = bf16[64,2176]{1,0:T(8,128)(2,1)S(1)} collective-permute-done((bf16[64,2176]{1,0:T(8,128)(2,1)S(1)}, bf16[64,2176]{1,0:T(8,128)(2,1)S(1)}, u32[]{:S(2)}, u32[]{:S(2)}) %collective-permute-start.4) | collective-permute-done | bytes 278560 | tf_op jit(solution)/shard_map/ppermute | solution.py:31
  27.9 0.1 collective-permute-start.7
  28.0 0.0 collective-permute-done.6.refs_1_
  28.1 0.6 collective-permute-start.8
  28.6 2.2 %shard_map.82 = (f32[8,128]{1,0:T(8,128)S(1)}, bf16[1024,2048]{1,0:T(8,128)(2,1)S(1)}) custom-call(bf16[4,1024,2048]{2,1,0:T(8,128)(2,1)} %refs_4_.1, f32[8,128]{1,0:T(8,128)S(1)} %get-tuple-element.63.refs_1_), custom_call_target="tpu_custom_call" | custom-call | bytes 4194304 | tf_op jit(solution)/shard_map/pallas_call | solution.py:313
  30.8 0.0 copy-start
  30.8 2.0 %copy-done = bf16[1024,2048]{1,0:T(8,128)(2,1)} copy-done((bf16[1024,2048]{1,0:T(8,128)(2,1)}, bf16[1024,2048]{1,0:T(8,128)(2,1)S(1)}, u32[]{:S(2)}) %copy-start) | copy-done | bytes 4194328
  32.8 0.0 collective-permute-done.8.refs_3_
  32.8 0.0 collective-permute-done.7.refs_1_
  32.8 5.8 %shard_map.83 = (bf16[2,64,512]{2,1,0:T(8,128)(2,1)S(1)}, bf16[4,64,4096]{2,1,0:T(8,128)(2,1)S(1)}, bf16[2,256,256]{2,1,0:T(8,128)(2,1)S(1)}, bf16[2,256,256]{2,...) custom-call(s32[2]{0:T(128)S(1)} %pad_add_fusion.pos_ref, ...), custom_call_target="tpu_custom_call" | custom-call | flops 1610612736 | bytes 16777216 | tf_op jit(solution)/shard_map/pallas_call | solution.py:313
  38.6 0.9 %collective-permute-start.9 = (bf16[2,64,512]{2,1,0:T(8,128)(2,1)S(1)}, bf16[2,64,512]{2,1,0:T(8,128)(2,1)S(1)}, u32[]{:S(2)}, u32[]{:S(2)}) collective-permute-start(bf16[2,64,512]{2,1,0:T(8,128)(2,1)S(1)} %get-tuple-element.66.refs_0_), channel_id=1, source_target_pairs={{0,16},{16,0},{1,17},{17,1},{2,18},{18,2},{3,19},{19,3},{4,20},{20... | collective-permute-start | bytes 393224 | tf_op jit(solution)/shard_map/ppermute | solution.py:31
  39.5 0.0 copy-start.1
  39.5 4.3 %shard_map.85 = (bf16[2,64,512]{2,1,0:T(8,128)(2,1)S(1)}, bf16[1024,2048]{1,0:T(8,128)(2,1)S(1)}, bf16[1024,2048]{1,0:T(8,128)(2,1)S(1)}) custom-call(s32[2]{0:T(128)S(1)} %pad_add_fusion.pos_ref, bf16[4,64,4096]{2,1,0:T(8,128)(2,1)S(1)} %get-tuple-element.69.normed_ref, bf16[4096,512]{1,0:T(8,128)(2,1)S(1)} %get-tuple-element.70.refs_0_, ...), custom_call_target="tpu_custom_call" | custom-call | flops 1073741824 | bytes 16777216 | tf_op jit(solution)/shard_map/pallas_call | solution.py:313
  43.8 1.2 %collective-permute-start.10 = (bf16[2,64,512]{2,1,0:T(8,128)(2,1)S(1)}, bf16[2,64,512]{2,1,0:T(8,128)(2,1)S(1)}, u32[]{:S(2)}, u32[]{:S(2)}) collective-permute-start(bf16[2,64,512]{2,1,0:T(8,128)(2,1)S(1)} %get-tuple-element.74.refs_0_), channel_id=1, source_target_pairs={{0,16},{16,0},{1,17},{17,1},{2,18},{18,2},{3,19},{19,3},{4,20},{20... | collective-permute-start | bytes 393224 | tf_op jit(solution)/shard_map/ppermute | solution.py:31
  45.0 0.0 collective-permute-done.9.refs_1_
  45.0 0.0 copy-done.1
  45.0 2.1 %shard_map.84.done_ref = bf16[128,2048]{1,0:T(8,128)(2,1)S(1)} custom-call(s32[2]{0:T(128)S(1)} %pad_add_fusion.pos_ref, bf16[2,64,512]{2,1,0:T(8,128)(2,1)S(1)} %get-tuple-element.66.refs_0_, bf16[2,64,512]{2,1,0:T(8,128)(2,1)S(1)} %collective-permute-done.9.refs_1_, bf16[1024,2048]{1,0:T(8,128)(2,1)S(1)} %get-tuple-element.67.refs_2_, ...), custom_call_target="tpu_custom_call" | custom-call | flops 536870912 | bytes 8388608 | tf_op jit(solution)/shard_map/pallas_call | solution.py:313
  47.1 2.3 %collective-permute-done.10.refs_1_ = bf16[2,64,512]{2,1,0:T(8,128)(2,1)S(1)} collective-permute-done((bf16[2,64,512]{2,1,0:T(8,128)(2,1)S(1)}, bf16[2,64,512]{2,1,0:T(8,128)(2,1)S(1)}, u32[]{:S(2)}, u32[]{:S(2)}) %collective-permute-start.10) | collective-permute-done | bytes 131104 | tf_op jit(solution)/shard_map/ppermute | solution.py:31
  49.5 1.7 %shard_map.86 = (bf16[128,1024]{1,0:T(8,128)(2,1)S(1)}, bf16[128,1024]{1,0:T(8,128)(2,1)S(1)}) custom-call(s32[2]{0:T(128)S(1)} %pad_add_fusion.pos_ref, bf16[2,256,256]{2,1,0:T(8,128)(2,1)S(1)} %get-tuple-element.65.mix_ref, bf16[128,2048]{1,0:T(8,128)(2,1)S(1)} %shard_map.84.done_ref, bf16[2,64,512]{2,1,0:T(8,128)(2,1)S(1)} %get-tuple-element.74.refs_0_, ...), custom_call_target="tpu_custom_call" | custom-call | flops 536870912 | bytes 8388608 | tf_op jit(solution)/shard_map/pallas_call | solution.py:313
  51.2 0.1 collective-permute-start.11
  51.3 1.7 %shard_map.89 = (bf16[128,1024]{1,0:T(8,128)(2,1)S(1)}, bf16[128,1024]{1,0:T(8,128)(2,1)S(1)}) custom-call(s32[2]{0:T(128)S(1)} %pad_add_fusion.pos_ref, bf16[2,256,256]{2,1,0:T(8,128)(2,1)S(1)} %get-tuple-element.85.mix_ref, bf16[128,2048]{1,0:T(8,128)(2,1)S(1)} %shard_map.84.done_ref, bf16[2,64,512]{2,1,0:T(8,128)(2,1)S(1)} %get-tuple-element.74.refs_0_, ...), custom_call_target="tpu_custom_call" | custom-call | flops 536870912 | bytes 8388608 | tf_op jit(solution)/shard_map/pallas_call | solution.py:313
  53.0 0.6 collective-permute-start.16
  53.6 0.0 collective-permute-done.11.refs_1_
  53.6 0.1 shard_map.87
  53.6 0.6 collective-permute-start.12
  54.2 0.5 collective-permute-done.16.refs_1_
  54.7 0.1 shard_map.90
  54.8 1.0 %collective-permute-start.17 = (bf16[32,1024]{1,0:T(8,128)(2,1)S(1)}, bf16[32,1024]{1,0:T(8,128)(2,1)S(1)}, u32[]{:S(2)}, u32[]{:S(2)}) collective-permute-start(bf16[32,1024]{1,0:T(8,128)(2,1)S(1)} %get-tuple-element.89), channel_id=1, source_target_pairs={{0,12},{1,13},{2,14},{3,15},{4,0},{5,1},{6,2},{7,3},{8,4},{9,5},{1... | collective-permute-start | bytes 196616 | tf_op jit(solution)/shard_map/ppermute | solution.py:31
  55.8 0.7 collective-permute-start.18
  56.5 1.7 %collective-permute-start.19 = (bf16[32,1024]{1,0:T(8,128)(2,1)S(1)}, bf16[32,1024]{1,0:T(8,128)(2,1)S(1)}, u32[]{:S(2)}, u32[]{:S(2)}) collective-permute-start(bf16[32,1024]{1,0:T(8,128)(2,1)S(1)} %get-tuple-element.91), channel_id=1, source_target_pairs={{0,4},{1,5},{2,6},{3,7},{4,8},{5,9},{6,10},{7,11},{8,12},{9,13},{1... | collective-permute-start | bytes 196616 | tf_op jit(solution)/shard_map/ppermute | solution.py:31
  58.2 0.9 %collective-permute-done.12.refs_1_ = bf16[64,1024]{1,0:T(8,128)(2,1)S(1)} collective-permute-done((bf16[64,1024]{1,0:T(8,128)(2,1)S(1)}, bf16[64,1024]{1,0:T(8,128)(2,1)S(1)}, u32[]{:S(2)}, u32[]{:S(2)}) %collective-permute-start.12) | collective-permute-done | bytes 131104 | tf_op jit(solution)/shard_map/ppermute | solution.py:31
  59.2 1.2 %collective-permute-start.13 = (bf16[16,1024]{1,0:T(8,128)(2,1)S(1)}, bf16[16,1024]{1,0:T(8,128)(2,1)S(1)}, u32[]{:S(2)}, u32[]{:S(2)}) collective-permute-start(bf16[16,1024]{1,0:T(8,128)(2,1)S(1)} %get-tuple-element.82), channel_id=1, source_target_pairs={{0,12},{1,13},{2,14},{3,15},{4,0},{5,1},{6,2},{7,3},{8,4},{9,5},{1... | collective-permute-start | bytes 98312 | tf_op jit(solution)/shard_map/ppermute | solution.py:31
  60.4 0.4 collective-permute-start.14
  60.8 0.0 collective-permute-done.17.refs_1_
  60.8 1.7 %collective-permute-start.15 = (bf16[16,1024]{1,0:T(8,128)(2,1)S(1)}, bf16[16,1024]{1,0:T(8,128)(2,1)S(1)}, u32[]{:S(2)}, u32[]{:S(2)}) collective-permute-start(bf16[16,1024]{1,0:T(8,128)(2,1)S(1)} %get-tuple-element.84), channel_id=1, source_target_pairs={{0,4},{1,5},{2,6},{3,7},{4,8},{5,9},{6,10},{7,11},{8,12},{9,13},{1... | collective-permute-start | bytes 98312 | tf_op jit(solution)/shard_map/ppermute | solution.py:31
  62.5 2.3 %collective-permute-done.18.refs_2_ = bf16[32,1024]{1,0:T(8,128)(2,1)S(1)} collective-permute-done((bf16[32,1024]{1,0:T(8,128)(2,1)S(1)}, bf16[32,1024]{1,0:T(8,128)(2,1)S(1)}, u32[]{:S(2)}, u32[]{:S(2)}) %collective-permute-start.18) | collective-permute-done | bytes 65568 | tf_op jit(solution)/shard_map/ppermute | solution.py:31
  64.9 0.0 collective-permute-done.19.refs_3_
  64.9 0.8 %collective-permute-start.20 = (bf16[16,1024]{1,0:T(8,128)(2,1)S(1)}, bf16[16,1024]{1,0:T(8,128)(2,1)S(1)}, u32[]{:S(2)}, u32[]{:S(2)}) collective-permute-start(bf16[16,1024]{1,0:T(8,128)(2,1)S(1)} %get-tuple-element.94), channel_id=1, source_target_pairs={{0,2},{1,3},{2,0},{3,1},{4,6},{5,7},{6,4},{7,5},{8,10},{9,11},{10,... | collective-permute-start | bytes 98312 | tf_op jit(solution)/shard_map/ppermute | solution.py:31
  65.7 0.0 collective-permute-done.13.refs_1_
  65.7 0.3 collective-permute-done.14.refs_2_
  66.0 0.5 collective-permute-done.15.refs_3_
  66.6 2.4 %collective-permute-done.20.refs_5_ = bf16[16,1024]{1,0:T(8,128)(2,1)S(1)} collective-permute-done((bf16[16,1024]{1,0:T(8,128)(2,1)S(1)}, bf16[16,1024]{1,0:T(8,128)(2,1)S(1)}, u32[]{:S(2)}, u32[]{:S(2)}) %collective-permute-start.20) | collective-permute-done | bytes 32800 | tf_op jit(solution)/shard_map/ppermute | solution.py:31
  68.9 1.2 %shard_map.92 = bf16[16,2048]{1,0:T(8,128)(2,1)} custom-call(s32[2]{0:T(128)S(1)} %pad_add_fusion.pos_ref, bf16[128,2176]{1,0:T(8,128)(2,1)S(1)} %get-tuple-element.57.refs_0_.first_ref, bf16[128,2048]{1,0:T(8,128)(2,1)S(1)} %shard_map.81.refs_2_.second_ref, bf16[16,1024]{1,0:T(8,128)(2,1)S(1)} %get-tuple-element.81.refs_0_, ...), custom_call_target="tpu_custom_call" | custom-call | bytes 524288 | tf_op jit(solution)/shard_map/pallas_call | solution.py:313
  (7 shorter events, 0.2 us)
Async XLA Ops:
  1.5 10.3 %collective-permute-start.2 = (bf16[8,4224]{1,0:T(8,128)(2,1)S(1)}, bf16[8,4224]{1,0:T(8,128)(2,1)S(1)}, u32[]{:S(2)}, u32[]{:S(2)}) collective-permute-start(bf16[8,4224]{1,0:T(8,128)(2,1)S(1)} %shard_map.73.refs_0_), channel_id=1, source_target_pairs={{0,12},{1,13},{2,14},{3,15},{4,0},{5,1},{6,2},{7,3},{8,4},{9,5},{1... | collective-permute-start | bytes 202760 | tf_op jit(solution)/shard_map/ppermute | solution.py:31
  6.6 6.6 %collective-permute-start.1 = (bf16[8,4224]{1,0:T(8,128)(2,1)S(1)}, bf16[8,4224]{1,0:T(8,128)(2,1)S(1)}, u32[]{:S(2)}, u32[]{:S(2)}) collective-permute-start(bf16[8,4224]{1,0:T(8,128)(2,1)S(1)} %shard_map.73.refs_0_), channel_id=1, source_target_pairs={{0,8},{1,9},{2,10},{3,11},{4,12},{5,13},{6,14},{7,15},{8,0},{9,1},... | collective-permute-start | bytes 202760 | tf_op jit(solution)/shard_map/ppermute | solution.py:31
  6.6 6.6 %collective-permute-start = (bf16[8,4224]{1,0:T(8,128)(2,1)S(1)}, bf16[8,4224]{1,0:T(8,128)(2,1)S(1)}, u32[]{:S(2)}, u32[]{:S(2)}) collective-permute-start(bf16[8,4224]{1,0:T(8,128)(2,1)S(1)} %shard_map.73.refs_0_), channel_id=1, source_target_pairs={{0,4},{1,5},{2,6},{3,7},{4,8},{5,9},{6,10},{7,11},{8,12},{9,13},{1... | collective-permute-start | bytes 202760 | tf_op jit(solution)/shard_map/ppermute | solution.py:31
  13.3 6.6 %collective-permute-start.3 = (bf16[32,2176]{1,0:T(8,128)(2,1)S(1)}, bf16[32,2176]{1,0:T(8,128)(2,1)S(1)}, u32[]{:S(2)}, u32[]{:S(2)}) collective-permute-start(bf16[32,2176]{1,0:T(8,128)(2,1)S(1)} %get-tuple-element.51.refs_0_), channel_id=1, source_target_pairs={{0,2},{1,3},{2,0},{3,1},{4,6},{5,7},{6,4},{7,5},{8,10},{9,11},{10,... | collective-permute-start | bytes 417800 | tf_op jit(solution)/shard_map/ppermute | solution.py:31
  14.9 5.6 %collective-permute-start.5 = (bf16[32,2048]{1,0:T(8,128)(2,1)S(1)}, bf16[32,2048]{1,0:T(8,128)(2,1)S(1)}, u32[]{:S(2)}, u32[]{:S(2)}) collective-permute-start(bf16[32,2048]{1,0:T(8,128)(2,1)S(1)} %get-tuple-element.58.refs_0_), channel_id=1, source_target_pairs={{0,16},{16,0},{1,17},{17,1},{2,18},{18,2},{3,19},{19,3},{4,20},{20... | collective-permute-start | bytes 393224 | tf_op jit(solution)/shard_map/ppermute | solution.py:31
  19.9 8.0 %collective-permute-start.4 = (bf16[64,2176]{1,0:T(8,128)(2,1)S(1)}, bf16[64,2176]{1,0:T(8,128)(2,1)S(1)}, u32[]{:S(2)}, u32[]{:S(2)}) collective-permute-start(bf16[64,2176]{1,0:T(8,128)(2,1)S(1)} %get-tuple-element.54.refs_0_), channel_id=1, source_target_pairs={{0,16},{16,0},{1,17},{17,1},{2,18},{18,2},{3,19},{19,3},{4,20},{20... | collective-permute-start | bytes 835592 | tf_op jit(solution)/shard_map/ppermute | solution.py:31
  20.5 7.5 %collective-permute-start.6 = (bf16[64,2048]{1,0:T(8,128)(2,1)S(1)}, bf16[64,2048]{1,0:T(8,128)(2,1)S(1)}, u32[]{:S(2)}, u32[]{:S(2)}) collective-permute-start(bf16[64,2048]{1,0:T(8,128)(2,1)S(1)} %shard_map.80.refs_0_), channel_id=1, source_target_pairs={{0,2},{1,3},{2,0},{3,1},{4,6},{5,7},{6,4},{7,5},{8,10},{9,11},{10,... | collective-permute-start | bytes 786440 | tf_op jit(solution)/shard_map/ppermute | solution.py:31
  27.9 4.9 %collective-permute-start.7 = (bf16[128,2176]{1,0:T(8,128)(2,1)S(1)}, bf16[128,2176]{1,0:T(8,128)(2,1)S(1)}, u32[]{:S(2)}, u32[]{:S(2)}) collective-permute-start(bf16[128,2176]{1,0:T(8,128)(2,1)S(1)} %get-tuple-element.57.refs_0_.first_ref), channel_id=1, source_target_pairs={{0,1},{1,0},{2,3},{3,2},{4,5},{5,4},{6,7},{7,6},{8,9},{9,8},{10,11... | collective-permute-start | bytes 1671176 | tf_op jit(solution)/shard_map/ppermute | solution.py:31
  28.1 4.7 %collective-permute-start.8 = (bf16[128,2048]{1,0:T(8,128)(2,1)S(1)}, bf16[128,2048]{1,0:T(8,128)(2,1)S(1)}, u32[]{:S(2)}, u32[]{:S(2)}) collective-permute-start(bf16[128,2048]{1,0:T(8,128)(2,1)S(1)} %shard_map.81.refs_2_.second_ref), channel_id=1, source_target_pairs={{0,1},{1,0},{2,3},{3,2},{4,5},{5,4},{6,7},{7,6},{8,9},{9,8},{10,11... | collective-permute-start | bytes 1572872 | tf_op jit(solution)/shard_map/ppermute | solution.py:31
  30.8 2.0 %copy-start = (bf16[1024,2048]{1,0:T(8,128)(2,1)}, bf16[1024,2048]{1,0:T(8,128)(2,1)S(1)}, u32[]{:S(2)}) copy-start(bf16[1024,2048]{1,0:T(8,128)(2,1)S(1)} %get-tuple-element.68.refs_3_) | copy-start | bytes 12582916
  38.6 6.4 %collective-permute-start.9 = (bf16[2,64,512]{2,1,0:T(8,128)(2,1)S(1)}, bf16[2,64,512]{2,1,0:T(8,128)(2,1)S(1)}, u32[]{:S(2)}, u32[]{:S(2)}) collective-permute-start(bf16[2,64,512]{2,1,0:T(8,128)(2,1)S(1)} %get-tuple-element.66.refs_0_), channel_id=1, source_target_pairs={{0,16},{16,0},{1,17},{17,1},{2,18},{18,2},{3,19},{19,3},{4,20},{20... | collective-permute-start | bytes 393224 | tf_op jit(solution)/shard_map/ppermute | solution.py:31
  39.5 5.5 %copy-start.1 = (bf16[1024,2048]{1,0:T(8,128)(2,1)S(1)}, bf16[1024,2048]{1,0:T(8,128)(2,1)}, u32[]{:S(2)}) copy-start(bf16[1024,2048]{1,0:T(8,128)(2,1)} %copy-done) | copy-start | bytes 12582916
  43.8 5.7 %collective-permute-start.10 = (bf16[2,64,512]{2,1,0:T(8,128)(2,1)S(1)}, bf16[2,64,512]{2,1,0:T(8,128)(2,1)S(1)}, u32[]{:S(2)}, u32[]{:S(2)}) collective-permute-start(bf16[2,64,512]{2,1,0:T(8,128)(2,1)S(1)} %get-tuple-element.74.refs_0_), channel_id=1, source_target_pairs={{0,16},{16,0},{1,17},{17,1},{2,18},{18,2},{3,19},{19,3},{4,20},{20... | collective-permute-start | bytes 393224 | tf_op jit(solution)/shard_map/ppermute | solution.py:31
  51.2 2.4 %collective-permute-start.11 = (bf16[128,1024]{1,0:T(8,128)(2,1)S(1)}, bf16[128,1024]{1,0:T(8,128)(2,1)S(1)}, u32[]{:S(2)}, u32[]{:S(2)}) collective-permute-start(bf16[128,1024]{1,0:T(8,128)(2,1)S(1)} %get-tuple-element.78), channel_id=1, source_target_pairs={{0,1},{1,0},{2,3},{3,2},{4,5},{5,4},{6,7},{7,6},{8,9},{9,8},{10,11... | collective-permute-start | bytes 786440 | tf_op jit(solution)/shard_map/ppermute | solution.py:31
  53.0 1.7 %collective-permute-start.16 = (bf16[128,1024]{1,0:T(8,128)(2,1)S(1)}, bf16[128,1024]{1,0:T(8,128)(2,1)S(1)}, u32[]{:S(2)}, u32[]{:S(2)}) collective-permute-start(bf16[128,1024]{1,0:T(8,128)(2,1)S(1)} %get-tuple-element.87), channel_id=1, source_target_pairs={{0,1},{1,0},{2,3},{3,2},{4,5},{5,4},{6,7},{7,6},{8,9},{9,8},{10,11... | collective-permute-start | bytes 786440 | tf_op jit(solution)/shard_map/ppermute | solution.py:31
  53.6 5.5 %collective-permute-start.12 = (bf16[64,1024]{1,0:T(8,128)(2,1)S(1)}, bf16[64,1024]{1,0:T(8,128)(2,1)S(1)}, u32[]{:S(2)}, u32[]{:S(2)}) collective-permute-start(bf16[64,1024]{1,0:T(8,128)(2,1)S(1)} %get-tuple-element.80), channel_id=1, source_target_pairs={{0,2},{1,3},{2,0},{3,1},{4,6},{5,7},{6,4},{7,5},{8,10},{9,11},{10,... | collective-permute-start | bytes 393224 | tf_op jit(solution)/shard_map/ppermute | solution.py:31
  54.8 6.1 %collective-permute-start.17 = (bf16[32,1024]{1,0:T(8,128)(2,1)S(1)}, bf16[32,1024]{1,0:T(8,128)(2,1)S(1)}, u32[]{:S(2)}, u32[]{:S(2)}) collective-permute-start(bf16[32,1024]{1,0:T(8,128)(2,1)S(1)} %get-tuple-element.89), channel_id=1, source_target_pairs={{0,12},{1,13},{2,14},{3,15},{4,0},{5,1},{6,2},{7,3},{8,4},{9,5},{1... | collective-permute-start | bytes 196616 | tf_op jit(solution)/shard_map/ppermute | solution.py:31
  55.8 9.1 %collective-permute-start.18 = (bf16[32,1024]{1,0:T(8,128)(2,1)S(1)}, bf16[32,1024]{1,0:T(8,128)(2,1)S(1)}, u32[]{:S(2)}, u32[]{:S(2)}) collective-permute-start(bf16[32,1024]{1,0:T(8,128)(2,1)S(1)} %get-tuple-element.90), channel_id=1, source_target_pairs={{0,8},{1,9},{2,10},{3,11},{4,12},{5,13},{6,14},{7,15},{8,0},{9,1},... | collective-permute-start | bytes 196616 | tf_op jit(solution)/shard_map/ppermute | solution.py:31
  56.5 8.4 %collective-permute-start.19 = (bf16[32,1024]{1,0:T(8,128)(2,1)S(1)}, bf16[32,1024]{1,0:T(8,128)(2,1)S(1)}, u32[]{:S(2)}, u32[]{:S(2)}) collective-permute-start(bf16[32,1024]{1,0:T(8,128)(2,1)S(1)} %get-tuple-element.91), channel_id=1, source_target_pairs={{0,4},{1,5},{2,6},{3,7},{4,8},{5,9},{6,10},{7,11},{8,12},{9,13},{1... | collective-permute-start | bytes 196616 | tf_op jit(solution)/shard_map/ppermute | solution.py:31
  59.2 6.6 %collective-permute-start.13 = (bf16[16,1024]{1,0:T(8,128)(2,1)S(1)}, bf16[16,1024]{1,0:T(8,128)(2,1)S(1)}, u32[]{:S(2)}, u32[]{:S(2)}) collective-permute-start(bf16[16,1024]{1,0:T(8,128)(2,1)S(1)} %get-tuple-element.82), channel_id=1, source_target_pairs={{0,12},{1,13},{2,14},{3,15},{4,0},{5,1},{6,2},{7,3},{8,4},{9,5},{1... | collective-permute-start | bytes 98312 | tf_op jit(solution)/shard_map/ppermute | solution.py:31
  60.4 5.6 %collective-permute-start.14 = (bf16[16,1024]{1,0:T(8,128)(2,1)S(1)}, bf16[16,1024]{1,0:T(8,128)(2,1)S(1)}, u32[]{:S(2)}, u32[]{:S(2)}) collective-permute-start(bf16[16,1024]{1,0:T(8,128)(2,1)S(1)} %get-tuple-element.83), channel_id=1, source_target_pairs={{0,8},{1,9},{2,10},{3,11},{4,12},{5,13},{6,14},{7,15},{8,0},{9,1},... | collective-permute-start | bytes 98312 | tf_op jit(solution)/shard_map/ppermute | solution.py:31
  60.8 5.7 %collective-permute-start.15 = (bf16[16,1024]{1,0:T(8,128)(2,1)S(1)}, bf16[16,1024]{1,0:T(8,128)(2,1)S(1)}, u32[]{:S(2)}, u32[]{:S(2)}) collective-permute-start(bf16[16,1024]{1,0:T(8,128)(2,1)S(1)} %get-tuple-element.84), channel_id=1, source_target_pairs={{0,4},{1,5},{2,6},{3,7},{4,8},{5,9},{6,10},{7,11},{8,12},{9,13},{1... | collective-permute-start | bytes 98312 | tf_op jit(solution)/shard_map/ppermute | solution.py:31
  64.9 4.0 %collective-permute-start.20 = (bf16[16,1024]{1,0:T(8,128)(2,1)S(1)}, bf16[16,1024]{1,0:T(8,128)(2,1)S(1)}, u32[]{:S(2)}, u32[]{:S(2)}) collective-permute-start(bf16[16,1024]{1,0:T(8,128)(2,1)S(1)} %get-tuple-element.94), channel_id=1, source_target_pairs={{0,2},{1,3},{2,0},{3,1},{4,6},{5,7},{6,4},{7,5},{8,10},{9,11},{10,... | collective-permute-start | bytes 98312 | tf_op jit(solution)/shard_map/ppermute | solution.py:31

commit v9 on v8

--- a/solution.py
+++ b/solution.py
@@ -163,35 +163,33 @@
         ref[1] = (exact - high.astype(jnp.float32)).astype(jnp.bfloat16)
 
     part = n_mid * n_tp * run
-    gain = gain_ref[...].astype(jnp.float32)
-    dims_of = (((0,), (0,)), ((), ()))
-    for e in range(exp_loc):
-        left, right = [], []
+    pick = jnp.concatenate(picks, axis=1)
+    chosen, swapped = [], []
+    for f in range(n_fast):
+        own = pick[f * part : (f + 1) * part]
+        runs = [
+            own[(t * n_mid + m) * run : (t * n_mid + m + 1) * run] for m in range(n_mid) for t in range(n_tp)
+        ]
+        chosen.append(own.T.astype(jnp.bfloat16))
+        swapped.append(jnp.concatenate(runs, axis=0).T.astype(jnp.bfloat16))
+    size = min(half, 4 * LANES)
+    squares = 0.0
+    for begin in range(0, 2 * half, size):
+        table, side, at = (swapped, second, begin) if begin < half else (chosen, first, begin - half)
+        values = 0.0
         for f in range(n_fast):
-            pick = picks[e][f * part : (f + 1) * part]
-            turned = jnp.concatenate(
-                [
-                    pick[(t * n_mid + m) * run : (t * n_mid + m + 1) * run]
-                    for m in range(n_mid)
-                    for t in range(n_tp)
-                ],
-                axis=0,
-            )
-            left.append(
-                lax.dot_general(
-                    turned.astype(jnp.bfloat16), second[f][...], dims_of, preferred_element_type=jnp.float32
-                )
-            )
-            right.append(
-                lax.dot_general(
-                    pick.astype(jnp.bfloat16), first[f][:, :half], dims_of, preferred_element_type=jnp.float32
-                )
-            )
-        left, right = sum(left[1:], left[0]), sum(right[1:], right[0])
-        squares = jnp.sum(left * left, axis=1, keepdims=True) + jnp.sum(right * right, axis=1, keepdims=True)
-        scale = lax.rsqrt(squares / (2 * half) + 1e-06)
-        normed_ref[e, :, :half] = (left * scale * gain[:, :half]).astype(jnp.bfloat16)
-        normed_ref[e, :, half:] = (right * scale * gain[:, half:]).astype(jnp.bfloat16)
+            values = values + jnp.dot(table[f], side[f][:, at : at + size], preferred_element_type=jnp.float32)
+        squares = squares + jnp.sum(values * values, axis=1, keepdims=True)
+        values = values.astype(jnp.bfloat16)
+        for e in range(exp_loc):
+            normed_ref[e, :, begin : begin + size] = values[e * rows : (e + 1) * rows]
+    scale = lax.rsqrt(squares / (2 * half) + 1e-06)
+    for begin in range(0, 2 * half, size):
+        gain = gain_ref[:, begin : begin + size].astype(jnp.float32)
+        for e in range(exp_loc):
+            values = normed_ref[e, :, begin : begin + size].astype(jnp.float32)
+            values = values * scale[e * rows : (e + 1) * rows] * gain
+            normed_ref[e, :, begin : begin + size] = values.astype(jnp.bfloat16)
     swiglu(normed_ref, gates, ups, hidden_ref, 0)
 
 
@@ -222,22 +220,21 @@
         copy.wait()
 
 
-def lower(n_tp, tp_pos, pieces, i, down_ref, columns):
-    hid_part = pieces[0].shape[2]
-    total = 0.0
-    for s in range(n_tp):
-        begin = pl.multiple_of(lax.rem(tp_pos - s + n_tp, n_tp) * hid_part, hid_part)
-        total = total + jnp.dot(
-            pieces[s][i], down_ref[pl.ds(begin, hid_part), columns], preferred_element_type=jnp.float32
-        )
-    return total.astype(jnp.bfloat16)
-
-
-def down_kernel(n_tp, pos_ref, *refs):
-    pieces, (*downs, out_ref) = refs[:n_tp], refs[n_tp:]
-    _, rows, _ = pieces[0].shape
-    for i, ref in enumerate(downs):
-        out_ref[i * rows : (i + 1) * rows] = lower(n_tp, pos_ref[0], pieces, i, ref, slice(None))
+def lower(tp_pos, n_tp, piece, s, down_ref, columns):
+    hid_part = piece.shape[1]
+    begin = pl.multiple_of(lax.rem(tp_pos - s + n_tp, n_tp) * hid_part, hid_part)
+    return jnp.dot(piece, down_ref[pl.ds(begin, hid_part), columns], preferred_element_type=jnp.float32)
+
+
+def down_kernel(n_tp, count, pos_ref, own_ref, *refs):
+    pieces, (*downs, out_ref, part_ref) = refs[:n_tp], refs[n_tp:]
+    _, rows, _ = own_ref.shape
+    every = slice(None)
+    for i, ref in enumerate(downs[:count]):
+        total = sum(lower(pos_ref[0], n_tp, pieces[s][i], s, ref, every) for s in range(n_tp))
+        out_ref[i * rows : (i + 1) * rows] = total.astype(jnp.bfloat16)
+    for i, ref in enumerate(downs[count:]):
+        part_ref[i * rows : (i + 1) * rows] = lower(pos_ref[0], n_tp, own_ref[i], 0, ref, every)
 
 
 def in_blocks(total, refs):
@@ -246,15 +243,18 @@
         ref[...] = total[i * rows : (i + 1) * rows].astype(jnp.bfloat16)
 
 
-def mix_kernel(n_tp, count, begin, pos_ref, mix_ref, done_ref, *refs):
-    pieces, downs, (*partial_refs, out_ref) = refs[:n_tp], refs[n_tp : n_tp + count], refs[n_tp + count :]
+def mix_kernel(n_tp, count, begin, pos_ref, mix_ref, done_ref, part_ref, *refs):
+    pieces, refs = refs[: n_tp - 1], refs[n_tp - 1 :]
+    downs, (*partial_refs, out_ref) = refs[:count], refs[count:]
     columns = pl.ds(begin, out_ref.shape[1])
-    _, rows, _ = pieces[0].shape
     at = done_ref.shape[0]
+    rows = part_ref.shape[0] // count
     out_ref[:at] = done_ref[:, columns]
     for i, ref in enumerate(downs):
-        out_ref[at : at + rows] = lower(n_tp, pos_ref[0], pieces, i, ref, columns)
-        at += rows
+        total = part_ref[i * rows : (i + 1) * rows, columns]
+        for s in range(1, n_tp):
+            total = total + lower(pos_ref[0], n_tp, pieces[s - 1][i], s, ref, columns)
+        out_ref[at + i * rows : at + (i + 1) * rows] = total.astype(jnp.bfloat16)
     out = out_ref[...]
     partial = jnp.dot(mix_ref[0], out, preferred_element_type=jnp.float32)
     partial = partial + jnp.dot(mix_ref[1], out, preferred_element_type=jnp.float32)
@@ -301,7 +301,7 @@
 TOKEN = jax.ShapeDtypeStruct((8, LANES), jnp.float32)
 
 
-def local_call(kernel, shapes, operands, far=(), scratch=(), limit=8 << 20, flops=0, moved=0):
+def local_call(kernel, shapes, operands, far=(), scratch=(), limit=6 << 20, flops=0, moved=0):
     specs, given = [], []
     for i, a in enumerate(operands):
         if i in far:
@@ -459,10 +459,10 @@
         moved=4 * tail * width * hid_part,
     )
     late = along_tp(hidden)
-    (done,) = local_call(
-        functools.partial(down_kernel, n_tp),
-        [bf16((lead * rows, col_part))],
-        [position] + pieces + down_lead,
+    done, part = local_call(
+        functools.partial(down_kernel, n_tp, lead),
+        [bf16((lead * rows, col_part)), jax.ShapeDtypeStruct((tail * rows, col_part), jnp.float32)],
+        [position, late[0]] + pieces + down_lead + down_tail,
         flops=2 * lead * rows * n_tp * hid_part * col_part,
         moved=2 * lead * n_tp * hid_part * col_part,
     )
@@ -470,7 +470,7 @@
     mixed_of = lambda table, begin: local_call(
         functools.partial(mix_kernel, n_tp, tail, begin),
         [bf16((tokens // n_fast, col_half))] * n_fast,
-        [position, table, done] + late + down_tail,
+        [position, table, done, part] + late[1:] + down_tail,
         scratch=[pltpu.VMEM((slots, col_half), jnp.bfloat16)],
         flops=slots * n_tp * hid_part * col_part,
         moved=exp_loc * n_tp * hid_part * col_part,

time: 70.4 us -> 67.7 us (0.962)
  local copies, waits for them, and re-layouts: 2.68 us -> 0.71 us
    unnamed x4 -> x0, local copies, waits for them, and re-layouts: 1.97 us -> none
  transfers between devices with their start and end apart: 21 -> 21, of which waited for: 9 -> 9; matrix products, arithmetic and copies ran while one was open for 1% -> 1% of each run, Pallas kernels for 32% -> 33%
where the time goes in v9:
time: 67.7 us; the launch traced here: 67.5 us
  Pallas kernels  32.5 us (48%)
  starting transfers between devices  22.8 us (34%)
  waiting for transfers between devices  11.2 us (17%)
  local copies, waits for them, and re-layouts  0.71 us (1%)
    pallas_call x20, Pallas kernels, local_call(): pl.pallas_call(kernel, out_shape=shapes, in_specs=specs, out_specs=[VMEM]...  32.5 us
    ppermute x21, starting transfers between devices, shifted(): return lax.ppermute(x, axis, pairs)  22.8 us
    ppermute x21, waiting for transfers between devices, shifted(): return lax.ppermute(x, axis, pairs)  11.2 us
  transfers between devices with their start and end apart: 21, of which 9 were waited for; matrix products, arithmetic and copies ran while one was open for 1% of the time, Pallas kernels for 33%

profile of v9, /device:TPU:0, one launch (start us, length us, event | category | flops | bytes accessed | tf_op | source)
XLA Modules:
  0.0 67.5 jit_solution(15384563277390075703)
XLA Ops:
  0.0 0.1 pad_add_fusion.pos_ref
  0.1 1.4 %shard_map.73.refs_0_ = bf16[8,4224]{1,0:T(8,128)(2,1)S(1)} custom-call(s32[2]{0:T(128)S(1)} %pad_add_fusion.pos_ref, s32[8,16]{1,0:T(8,128)} %bitcast.4, f32[8,16]{1,0:T(8,128)} %bitcast.5, bf16[8,4096]{1,0:T(8,128)(2,1)} %values_ref.1), custom_call_target="tpu_custom_call" | custom-call | tf_op jit(solution)/shard_map/pallas_call | solution.py:313
  1.5 5.1 %collective-permute-start.2 = (bf16[8,4224]{1,0:T(8,128)(2,1)S(1)}, bf16[8,4224]{1,0:T(8,128)(2,1)S(1)}, u32[]{:S(2)}, u32[]{:S(2)}) collective-permute-start(bf16[8,4224]{1,0:T(8,128)(2,1)S(1)} %shard_map.73.refs_0_), channel_id=1, source_target_pairs={{0,12},{1,13},{2,14},{3,15},{4,0},{5,1},{6,2},{7,3},{8,4},{9,5},{1... | collective-permute-start | bytes 202760 | tf_op jit(solution)/shard_map/ppermute | solution.py:31
  6.6 0.0 collective-permute-start.1
  6.6 1.0 %collective-permute-start = (bf16[8,4224]{1,0:T(8,128)(2,1)S(1)}, bf16[8,4224]{1,0:T(8,128)(2,1)S(1)}, u32[]{:S(2)}, u32[]{:S(2)}) collective-permute-start(bf16[8,4224]{1,0:T(8,128)(2,1)S(1)} %shard_map.73.refs_0_), channel_id=1, source_target_pairs={{0,4},{1,5},{2,6},{3,7},{4,8},{5,9},{6,10},{7,11},{8,12},{9,13},{1... | collective-permute-start | bytes 202760 | tf_op jit(solution)/shard_map/ppermute | solution.py:31
  7.6 0.7 %reshape.3.refs_2_.gain_ref = bf16[1,4096]{1,0:T(2,128)(2,1)S(1)} reshape(bf16[4096]{0:T(1024)(128)(2,1)} %param.8) | data formatting | bytes 16384 | tf_op jit(solution)/shard_map/reshape | solution.py:392
  8.3 3.5 %shard_map.74 = (f32[8,128]{1,0:T(8,128)S(1)}, bf16[4096,512]{1,0:T(8,128)(2,1)S(1)}, bf16[4096,512]{1,0:T(8,128)(2,1)S(1)}) custom-call(bf16[4,4096,512]{2,1,0:T(8,128)(2,1)} %refs_1_.4, bf16[4,4096,512]{2,1,0:T(8,128)(2,1)} %refs_1_.4, bf16[1,4096]{1,0:T(2,128)(2,1)S(1)} %reshape.3.refs_2_.gain_ref), custom_call_target="tpu_custom_call" | custom-call | bytes 8388608 | tf_op jit(solution)/shard_map/pallas_call | solution.py:313
  11.8 0.0 collective-permute-done.2.refs_3_
  11.8 1.4 %collective-permute-done.1.refs_2_ = bf16[8,4224]{1,0:T(8,128)(2,1)S(1)} collective-permute-done((bf16[8,4224]{1,0:T(8,128)(2,1)S(1)}, bf16[8,4224]{1,0:T(8,128)(2,1)S(1)}, u32[]{:S(2)}, u32[]{:S(2)}) %collective-permute-start.1) | collective-permute-done | bytes 67616 | tf_op jit(solution)/shard_map/ppermute | solution.py:31
  13.3 0.0 collective-permute-done.refs_1_
  13.3 1.6 %collective-permute-start.3 = (bf16[32,2176]{1,0:T(8,128)(2,1)S(1)}, bf16[32,2176]{1,0:T(8,128)(2,1)S(1)}, u32[]{:S(2)}, u32[]{:S(2)}) collective-permute-start(bf16[32,2176]{1,0:T(8,128)(2,1)S(1)} %get-tuple-element.53.refs_0_), channel_id=1, source_target_pairs={{0,2},{1,3},{2,0},{3,1},{4,6},{5,7},{6,4},{7,5},{8,10},{9,11},{10,... | collective-permute-start | bytes 417800 | tf_op jit(solution)/shard_map/ppermute | solution.py:31
  14.9 1.5 %collective-permute-start.5 = (bf16[32,2048]{1,0:T(8,128)(2,1)S(1)}, bf16[32,2048]{1,0:T(8,128)(2,1)S(1)}, u32[]{:S(2)}, u32[]{:S(2)}) collective-permute-start(bf16[32,2048]{1,0:T(8,128)(2,1)S(1)} %get-tuple-element.60.refs_0_), channel_id=1, source_target_pairs={{0,16},{16,0},{1,17},{17,1},{2,18},{18,2},{3,19},{19,3},{4,20},{20... | collective-permute-start | bytes 393224 | tf_op jit(solution)/shard_map/ppermute | solution.py:31
  16.4 3.5 %shard_map.76 = (f32[8,128]{1,0:T(8,128)S(1)}, bf16[4096,512]{1,0:T(8,128)(2,1)S(1)}, bf16[4096,512]{1,0:T(8,128)(2,1)S(1)}) custom-call(bf16[4,4096,512]{2,1,0:T(8,128)(2,1)} %refs_1_.4, bf16[4,4096,512]{2,1,0:T(8,128)(2,1)} %refs_1_.4, f32[8,128]{1,0:T(8,128)S(1)} %get-tuple-element.54.refs_2_), custom_call_target="tpu_custom_call" | custom-call | bytes 8388608 | tf_op jit(solution)/shard_map/pallas_call | solution.py:313
  19.9 0.0 collective-permute-done.3.refs_1_
  19.9 0.6 collective-permute-start.4
  20.5 0.0 collective-permute-done.5.refs_1_
  20.5 1.5 %collective-permute-start.6 = (bf16[64,2048]{1,0:T(8,128)(2,1)S(1)}, bf16[64,2048]{1,0:T(8,128)(2,1)S(1)}, u32[]{:S(2)}, u32[]{:S(2)}) collective-permute-start(bf16[64,2048]{1,0:T(8,128)(2,1)S(1)} %shard_map.80.refs_0_), channel_id=1, source_target_pairs={{0,2},{1,3},{2,0},{3,1},{4,6},{5,7},{6,4},{7,5},{8,10},{9,11},{10,... | collective-permute-start | bytes 786440 | tf_op jit(solution)/shard_map/ppermute | solution.py:31
  22.0 4.7 %shard_map.78 = (f32[8,128]{1,0:T(8,128)S(1)}, bf16[4096,512]{1,0:T(8,128)(2,1)S(1)}, bf16[4096,512]{1,0:T(8,128)(2,1)S(1)}, bf16[1024,2048]{1,0:T(8,128)(2,1)S(1)}) custom-call(bf16[4,4096,512]{2,1,0:T(8,128)(2,1)} %refs_9_.1, bf16[4,4096,512]{2,1,0:T(8,128)(2,1)} %refs_9_.1, bf16[4,1024,2048]{2,1,0:T(8,128)(2,1)} %refs_4_.1, ...), custom_call_target="tpu_custom_call" | custom-call | bytes 12582912 | tf_op jit(solution)/shard_map/pallas_call | solution.py:313
  26.8 1.1 %collective-permute-done.4.refs_1_ = bf16[64,2176]{1,0:T(8,128)(2,1)S(1)} collective-permute-done((bf16[64,2176]{1,0:T(8,128)(2,1)S(1)}, bf16[64,2176]{1,0:T(8,128)(2,1)S(1)}, u32[]{:S(2)}, u32[]{:S(2)}) %collective-permute-start.4) | collective-permute-done | bytes 278560 | tf_op jit(solution)/shard_map/ppermute | solution.py:31
  27.9 0.1 collective-permute-start.7
  28.0 0.0 collective-permute-done.6.refs_1_
  28.1 0.6 collective-permute-start.8
  28.6 2.2 %shard_map.82 = (f32[8,128]{1,0:T(8,128)S(1)}, bf16[1024,2048]{1,0:T(8,128)(2,1)S(1)}) custom-call(bf16[4,1024,2048]{2,1,0:T(8,128)(2,1)} %refs_4_.1, f32[8,128]{1,0:T(8,128)S(1)} %get-tuple-element.65.refs_1_), custom_call_target="tpu_custom_call" | custom-call | bytes 4194304 | tf_op jit(solution)/shard_map/pallas_call | solution.py:313
  30.8 0.0 collective-permute-done.8.refs_3_
  30.8 0.0 collective-permute-done.7.refs_1_
  30.8 6.1 %shard_map.83 = (bf16[2,64,512]{2,1,0:T(8,128)(2,1)S(1)}, bf16[4,64,4096]{2,1,0:T(8,128)(2,1)S(1)}, bf16[2,256,256]{2,1,0:T(8,128)(2,1)S(1)}, bf16[2,256,256]{2,...) custom-call(s32[2]{0:T(128)S(1)} %pad_add_fusion.pos_ref, ...), custom_call_target="tpu_custom_call" | custom-call | flops 1610612736 | bytes 16777216 | tf_op jit(solution)/shard_map/pallas_call | solution.py:313
  36.9 0.9 %collective-permute-start.9 = (bf16[2,64,512]{2,1,0:T(8,128)(2,1)S(1)}, bf16[2,64,512]{2,1,0:T(8,128)(2,1)S(1)}, u32[]{:S(2)}, u32[]{:S(2)}) collective-permute-start(bf16[2,64,512]{2,1,0:T(8,128)(2,1)S(1)} %get-tuple-element.74.refs_0_), channel_id=1, source_target_pairs={{0,16},{16,0},{1,17},{17,1},{2,18},{18,2},{3,19},{19,3},{4,20},{20... | collective-permute-start | bytes 393224 | tf_op jit(solution)/shard_map/ppermute | solution.py:31
  37.9 4.0 %shard_map.84 = (bf16[2,64,512]{2,1,0:T(8,128)(2,1)S(1)}, bf16[1024,2048]{1,0:T(8,128)(2,1)S(1)}, bf16[1024,2048]{1,0:T(8,128)(2,1)S(1)}) custom-call(s32[2]{0:T(128)S(1)} %pad_add_fusion.pos_ref, bf16[4,64,4096]{2,1,0:T(8,128)(2,1)S(1)} %get-tuple-element.68.normed_ref, bf16[4096,512]{1,0:T(8,128)(2,1)S(1)} %get-tuple-element.69.refs_0_, ...), custom_call_target="tpu_custom_call" | custom-call | flops 1073741824 | bytes 16777216 | tf_op jit(solution)/shard_map/pallas_call | solution.py:313
  41.9 1.2 %collective-permute-start.10 = (bf16[2,64,512]{2,1,0:T(8,128)(2,1)S(1)}, bf16[2,64,512]{2,1,0:T(8,128)(2,1)S(1)}, u32[]{:S(2)}, u32[]{:S(2)}) collective-permute-start(bf16[2,64,512]{2,1,0:T(8,128)(2,1)S(1)} %get-tuple-element.73.own_ref), channel_id=1, source_target_pairs={{0,16},{16,0},{1,17},{17,1},{2,18},{18,2},{3,19},{19,3},{4,20},{20... | collective-permute-start | bytes 393224 | tf_op jit(solution)/shard_map/ppermute | solution.py:31
  43.1 0.0 collective-permute-done.9.refs_1_
  43.1 2.8 %shard_map.85 = (bf16[128,2048]{1,0:T(8,128)(2,1)S(1)}, f32[128,2048]{1,0:T(8,128)S(1)}) custom-call(s32[2]{0:T(128)S(1)} %pad_add_fusion.pos_ref, bf16[2,64,512]{2,1,0:T(8,128)(2,1)S(1)} %get-tuple-element.73.own_ref, bf16[2,64,512]{2,1,0:T(8,128)(2,1)S(1)} %get-tuple-element.74.refs_0_, bf16[2,64,512]{2,1,0:T(8,128)(2,1)S(1)} %collective-permute-done.9.refs_1_, ...), custom_call_target="tpu_custom_call" | custom-call | flops 536870912 | bytes 8388608 | tf_op jit(solution)/shard_map/pallas_call | solution.py:313
  45.9 1.6 %collective-permute-done.10.refs_0_ = bf16[2,64,512]{2,1,0:T(8,128)(2,1)S(1)} collective-permute-done((bf16[2,64,512]{2,1,0:T(8,128)(2,1)S(1)}, bf16[2,64,512]{2,1,0:T(8,128)(2,1)S(1)}, u32[]{:S(2)}, u32[]{:S(2)}) %collective-permute-start.10) | collective-permute-done | bytes 131104 | tf_op jit(solution)/shard_map/ppermute | solution.py:31
  47.6 1.3 %shard_map.86 = (bf16[128,1024]{1,0:T(8,128)(2,1)S(1)}, bf16[128,1024]{1,0:T(8,128)(2,1)S(1)}) custom-call(s32[2]{0:T(128)S(1)} %pad_add_fusion.pos_ref, bf16[2,256,256]{2,1,0:T(8,128)(2,1)S(1)} %get-tuple-element.67.mix_ref, bf16[128,2048]{1,0:T(8,128)(2,1)S(1)} %get-tuple-element.79.done_ref, f32[128,2048]{1,0:T(8,128)S(1)} %get-tuple-element.80.part_ref, ...), custom_call_target="tpu_custom_call" | custom-call | flops 536870912 | bytes 8388608 | tf_op jit(solution)/shard_map/pallas_call | solution.py:313
  48.9 0.1 collective-permute-start.11
  49.0 1.4 %shard_map.89 = (bf16[128,1024]{1,0:T(8,128)(2,1)S(1)}, bf16[128,1024]{1,0:T(8,128)(2,1)S(1)}) custom-call(s32[2]{0:T(128)S(1)} %pad_add_fusion.pos_ref, bf16[2,256,256]{2,1,0:T(8,128)(2,1)S(1)} %get-tuple-element.89.mix_ref, bf16[128,2048]{1,0:T(8,128)(2,1)S(1)} %get-tuple-element.79.done_ref, f32[128,2048]{1,0:T(8,128)S(1)} %get-tuple-element.80.part_ref, ...), custom_call_target="tpu_custom_call" | custom-call | flops 536870912 | bytes 8388608 | tf_op jit(solution)/shard_map/pallas_call | solution.py:313
  50.4 0.6 collective-permute-start.16
  50.9 0.0 collective-permute-done.11.refs_1_
  50.9 0.1 shard_map.87
  51.0 0.6 collective-permute-start.12
  51.6 0.5 collective-permute-done.16.refs_1_
  52.1 0.1 shard_map.90
  52.2 1.0 %collective-permute-start.17 = (bf16[32,1024]{1,0:T(8,128)(2,1)S(1)}, bf16[32,1024]{1,0:T(8,128)(2,1)S(1)}, u32[]{:S(2)}, u32[]{:S(2)}) collective-permute-start(bf16[32,1024]{1,0:T(8,128)(2,1)S(1)} %get-tuple-element.93), channel_id=1, source_target_pairs={{0,12},{1,13},{2,14},{3,15},{4,0},{5,1},{6,2},{7,3},{8,4},{9,5},{1... | collective-permute-start | bytes 196616 | tf_op jit(solution)/shard_map/ppermute | solution.py:31
  53.2 0.7 %collective-permute-start.18 = (bf16[32,1024]{1,0:T(8,128)(2,1)S(1)}, bf16[32,1024]{1,0:T(8,128)(2,1)S(1)}, u32[]{:S(2)}, u32[]{:S(2)}) collective-permute-start(bf16[32,1024]{1,0:T(8,128)(2,1)S(1)} %get-tuple-element.94), channel_id=1, source_target_pairs={{0,8},{1,9},{2,10},{3,11},{4,12},{5,13},{6,14},{7,15},{8,0},{9,1},... | collective-permute-start | bytes 196616 | tf_op jit(solution)/shard_map/ppermute | solution.py:31
  53.8 1.7 %collective-permute-start.19 = (bf16[32,1024]{1,0:T(8,128)(2,1)S(1)}, bf16[32,1024]{1,0:T(8,128)(2,1)S(1)}, u32[]{:S(2)}, u32[]{:S(2)}) collective-permute-start(bf16[32,1024]{1,0:T(8,128)(2,1)S(1)} %get-tuple-element.95), channel_id=1, source_target_pairs={{0,4},{1,5},{2,6},{3,7},{4,8},{5,9},{6,10},{7,11},{8,12},{9,13},{1... | collective-permute-start | bytes 196616 | tf_op jit(solution)/shard_map/ppermute | solution.py:31
  55.5 0.9 %collective-permute-done.12.refs_1_ = bf16[64,1024]{1,0:T(8,128)(2,1)S(1)} collective-permute-done((bf16[64,1024]{1,0:T(8,128)(2,1)S(1)}, bf16[64,1024]{1,0:T(8,128)(2,1)S(1)}, u32[]{:S(2)}, u32[]{:S(2)}) %collective-permute-start.12) | collective-permute-done | bytes 131104 | tf_op jit(solution)/shard_map/ppermute | solution.py:31
  56.5 1.2 %collective-permute-start.13 = (bf16[16,1024]{1,0:T(8,128)(2,1)S(1)}, bf16[16,1024]{1,0:T(8,128)(2,1)S(1)}, u32[]{:S(2)}, u32[]{:S(2)}) collective-permute-start(bf16[16,1024]{1,0:T(8,128)(2,1)S(1)} %get-tuple-element.86), channel_id=1, source_target_pairs={{0,12},{1,13},{2,14},{3,15},{4,0},{5,1},{6,2},{7,3},{8,4},{9,5},{1... | collective-permute-start | bytes 98312 | tf_op jit(solution)/shard_map/ppermute | solution.py:31
  57.8 0.4 collective-permute-start.14
  58.2 0.0 collective-permute-done.17.refs_1_
  58.2 1.7 %collective-permute-start.15 = (bf16[16,1024]{1,0:T(8,128)(2,1)S(1)}, bf16[16,1024]{1,0:T(8,128)(2,1)S(1)}, u32[]{:S(2)}, u32[]{:S(2)}) collective-permute-start(bf16[16,1024]{1,0:T(8,128)(2,1)S(1)} %get-tuple-element.88), channel_id=1, source_target_pairs={{0,4},{1,5},{2,6},{3,7},{4,8},{5,9},{6,10},{7,11},{8,12},{9,13},{1... | collective-permute-start | bytes 98312 | tf_op jit(solution)/shard_map/ppermute | solution.py:31
  59.9 2.3 %collective-permute-done.18.refs_2_ = bf16[32,1024]{1,0:T(8,128)(2,1)S(1)} collective-permute-done((bf16[32,1024]{1,0:T(8,128)(2,1)S(1)}, bf16[32,1024]{1,0:T(8,128)(2,1)S(1)}, u32[]{:S(2)}, u32[]{:S(2)}) %collective-permute-start.18) | collective-permute-done | bytes 65568 | tf_op jit(solution)/shard_map/ppermute | solution.py:31
  62.3 0.0 collective-permute-done.19.refs_3_
  62.3 0.8 %collective-permute-start.20 = (bf16[16,1024]{1,0:T(8,128)(2,1)S(1)}, bf16[16,1024]{1,0:T(8,128)(2,1)S(1)}, u32[]{:S(2)}, u32[]{:S(2)}) collective-permute-start(bf16[16,1024]{1,0:T(8,128)(2,1)S(1)} %get-tuple-element.98), channel_id=1, source_target_pairs={{0,2},{1,3},{2,0},{3,1},{4,6},{5,7},{6,4},{7,5},{8,10},{9,11},{10,... | collective-permute-start | bytes 98312 | tf_op jit(solution)/shard_map/ppermute | solution.py:31
  63.1 0.0 collective-permute-done.13.refs_1_
  63.1 0.3 collective-permute-done.14.refs_2_
  63.4 0.5 collective-permute-done.15.refs_3_
  63.9 2.4 %collective-permute-done.20.refs_5_ = bf16[16,1024]{1,0:T(8,128)(2,1)S(1)} collective-permute-done((bf16[16,1024]{1,0:T(8,128)(2,1)S(1)}, bf16[16,1024]{1,0:T(8,128)(2,1)S(1)}, u32[]{:S(2)}, u32[]{:S(2)}) %collective-permute-start.20) | collective-permute-done | bytes 32800 | tf_op jit(solution)/shard_map/ppermute | solution.py:31
  66.3 1.2 %shard_map.92 = bf16[16,2048]{1,0:T(8,128)(2,1)} custom-call(s32[2]{0:T(128)S(1)} %pad_add_fusion.pos_ref, bf16[128,2176]{1,0:T(8,128)(2,1)S(1)} %get-tuple-element.59.refs_0_.first_ref, bf16[128,2048]{1,0:T(8,128)(2,1)S(1)} %shard_map.81.refs_2_.second_ref, bf16[16,1024]{1,0:T(8,128)(2,1)S(1)} %get-tuple-element.85.refs_0_, ...), custom_call_target="tpu_custom_call" | custom-call | bytes 524288 | tf_op jit(solution)/shard_map/pallas_call | solution.py:313
  (7 shorter events, 0.2 us)
Async XLA Ops:
  1.5 10.3 %collective-permute-start.2 = (bf16[8,4224]{1,0:T(8,128)(2,1)S(1)}, bf16[8,4224]{1,0:T(8,128)(2,1)S(1)}, u32[]{:S(2)}, u32[]{:S(2)}) collective-permute-start(bf16[8,4224]{1,0:T(8,128)(2,1)S(1)} %shard_map.73.refs_0_), channel_id=1, source_target_pairs={{0,12},{1,13},{2,14},{3,15},{4,0},{5,1},{6,2},{7,3},{8,4},{9,5},{1... | collective-permute-start | bytes 202760 | tf_op jit(solution)/shard_map/ppermute | solution.py:31
  6.6 6.6 %collective-permute-start.1 = (bf16[8,4224]{1,0:T(8,128)(2,1)S(1)}, bf16[8,4224]{1,0:T(8,128)(2,1)S(1)}, u32[]{:S(2)}, u32[]{:S(2)}) collective-permute-start(bf16[8,4224]{1,0:T(8,128)(2,1)S(1)} %shard_map.73.refs_0_), channel_id=1, source_target_pairs={{0,8},{1,9},{2,10},{3,11},{4,12},{5,13},{6,14},{7,15},{8,0},{9,1},... | collective-permute-start | bytes 202760 | tf_op jit(solution)/shard_map/ppermute | solution.py:31
  6.6 6.6 %collective-permute-start = (bf16[8,4224]{1,0:T(8,128)(2,1)S(1)}, bf16[8,4224]{1,0:T(8,128)(2,1)S(1)}, u32[]{:S(2)}, u32[]{:S(2)}) collective-permute-start(bf16[8,4224]{1,0:T(8,128)(2,1)S(1)} %shard_map.73.refs_0_), channel_id=1, source_target_pairs={{0,4},{1,5},{2,6},{3,7},{4,8},{5,9},{6,10},{7,11},{8,12},{9,13},{1... | collective-permute-start | bytes 202760 | tf_op jit(solution)/shard_map/ppermute | solution.py:31
  13.3 6.6 %collective-permute-start.3 = (bf16[32,2176]{1,0:T(8,128)(2,1)S(1)}, bf16[32,2176]{1,0:T(8,128)(2,1)S(1)}, u32[]{:S(2)}, u32[]{:S(2)}) collective-permute-start(bf16[32,2176]{1,0:T(8,128)(2,1)S(1)} %get-tuple-element.53.refs_0_), channel_id=1, source_target_pairs={{0,2},{1,3},{2,0},{3,1},{4,6},{5,7},{6,4},{7,5},{8,10},{9,11},{10,... | collective-permute-start | bytes 417800 | tf_op jit(solution)/shard_map/ppermute | solution.py:31
  14.9 5.6 %collective-permute-start.5 = (bf16[32,2048]{1,0:T(8,128)(2,1)S(1)}, bf16[32,2048]{1,0:T(8,128)(2,1)S(1)}, u32[]{:S(2)}, u32[]{:S(2)}) collective-permute-start(bf16[32,2048]{1,0:T(8,128)(2,1)S(1)} %get-tuple-element.60.refs_0_), channel_id=1, source_target_pairs={{0,16},{16,0},{1,17},{17,1},{2,18},{18,2},{3,19},{19,3},{4,20},{20... | collective-permute-start | bytes 393224 | tf_op jit(solution)/shard_map/ppermute | solution.py:31
  19.9 8.0 %collective-permute-start.4 = (bf16[64,2176]{1,0:T(8,128)(2,1)S(1)}, bf16[64,2176]{1,0:T(8,128)(2,1)S(1)}, u32[]{:S(2)}, u32[]{:S(2)}) collective-permute-start(bf16[64,2176]{1,0:T(8,128)(2,1)S(1)} %get-tuple-element.56.refs_0_), channel_id=1, source_target_pairs={{0,16},{16,0},{1,17},{17,1},{2,18},{18,2},{3,19},{19,3},{4,20},{20... | collective-permute-start | bytes 835592 | tf_op jit(solution)/shard_map/ppermute | solution.py:31
  20.5 7.5 %collective-permute-start.6 = (bf16[64,2048]{1,0:T(8,128)(2,1)S(1)}, bf16[64,2048]{1,0:T(8,128)(2,1)S(1)}, u32[]{:S(2)}, u32[]{:S(2)}) collective-permute-start(bf16[64,2048]{1,0:T(8,128)(2,1)S(1)} %shard_map.80.refs_0_), channel_id=1, source_target_pairs={{0,2},{1,3},{2,0},{3,1},{4,6},{5,7},{6,4},{7,5},{8,10},{9,11},{10,... | collective-permute-start | bytes 786440 | tf_op jit(solution)/shard_map/ppermute | solution.py:31
  27.9 2.9 %collective-permute-start.7 = (bf16[128,2176]{1,0:T(8,128)(2,1)S(1)}, bf16[128,2176]{1,0:T(8,128)(2,1)S(1)}, u32[]{:S(2)}, u32[]{:S(2)}) collective-permute-start(bf16[128,2176]{1,0:T(8,128)(2,1)S(1)} %get-tuple-element.59.refs_0_.first_ref), channel_id=1, source_target_pairs={{0,1},{1,0},{2,3},{3,2},{4,5},{5,4},{6,7},{7,6},{8,9},{9,8},{10,11... | collective-permute-start | bytes 1671176 | tf_op jit(solution)/shard_map/ppermute | solution.py:31
  28.1 2.8 %collective-permute-start.8 = (bf16[128,2048]{1,0:T(8,128)(2,1)S(1)}, bf16[128,2048]{1,0:T(8,128)(2,1)S(1)}, u32[]{:S(2)}, u32[]{:S(2)}) collective-permute-start(bf16[128,2048]{1,0:T(8,128)(2,1)S(1)} %shard_map.81.refs_2_.second_ref), channel_id=1, source_target_pairs={{0,1},{1,0},{2,3},{3,2},{4,5},{5,4},{6,7},{7,6},{8,9},{9,8},{10,11... | collective-permute-start | bytes 1572872 | tf_op jit(solution)/shard_map/ppermute | solution.py:31
  36.9 6.2 %collective-permute-start.9 = (bf16[2,64,512]{2,1,0:T(8,128)(2,1)S(1)}, bf16[2,64,512]{2,1,0:T(8,128)(2,1)S(1)}, u32[]{:S(2)}, u32[]{:S(2)}) collective-permute-start(bf16[2,64,512]{2,1,0:T(8,128)(2,1)S(1)} %get-tuple-element.74.refs_0_), channel_id=1, source_target_pairs={{0,16},{16,0},{1,17},{17,1},{2,18},{18,2},{3,19},{19,3},{4,20},{20... | collective-permute-start | bytes 393224 | tf_op jit(solution)/shard_map/ppermute | solution.py:31
  41.9 5.7 %collective-permute-start.10 = (bf16[2,64,512]{2,1,0:T(8,128)(2,1)S(1)}, bf16[2,64,512]{2,1,0:T(8,128)(2,1)S(1)}, u32[]{:S(2)}, u32[]{:S(2)}) collective-permute-start(bf16[2,64,512]{2,1,0:T(8,128)(2,1)S(1)} %get-tuple-element.73.own_ref), channel_id=1, source_target_pairs={{0,16},{16,0},{1,17},{17,1},{2,18},{18,2},{3,19},{19,3},{4,20},{20... | collective-permute-start | bytes 393224 | tf_op jit(solution)/shard_map/ppermute | solution.py:31
  48.9 2.0 %collective-permute-start.11 = (bf16[128,1024]{1,0:T(8,128)(2,1)S(1)}, bf16[128,1024]{1,0:T(8,128)(2,1)S(1)}, u32[]{:S(2)}, u32[]{:S(2)}) collective-permute-start(bf16[128,1024]{1,0:T(8,128)(2,1)S(1)} %get-tuple-element.82), channel_id=1, source_target_pairs={{0,1},{1,0},{2,3},{3,2},{4,5},{5,4},{6,7},{7,6},{8,9},{9,8},{10,11... | collective-permute-start | bytes 786440 | tf_op jit(solution)/shard_map/ppermute | solution.py:31
  50.4 1.7 %collective-permute-start.16 = (bf16[128,1024]{1,0:T(8,128)(2,1)S(1)}, bf16[128,1024]{1,0:T(8,128)(2,1)S(1)}, u32[]{:S(2)}, u32[]{:S(2)}) collective-permute-start(bf16[128,1024]{1,0:T(8,128)(2,1)S(1)} %get-tuple-element.91), channel_id=1, source_target_pairs={{0,1},{1,0},{2,3},{3,2},{4,5},{5,4},{6,7},{7,6},{8,9},{9,8},{10,11... | collective-permute-start | bytes 786440 | tf_op jit(solution)/shard_map/ppermute | solution.py:31
  51.0 5.5 %collective-permute-start.12 = (bf16[64,1024]{1,0:T(8,128)(2,1)S(1)}, bf16[64,1024]{1,0:T(8,128)(2,1)S(1)}, u32[]{:S(2)}, u32[]{:S(2)}) collective-permute-start(bf16[64,1024]{1,0:T(8,128)(2,1)S(1)} %get-tuple-element.84), channel_id=1, source_target_pairs={{0,2},{1,3},{2,0},{3,1},{4,6},{5,7},{6,4},{7,5},{8,10},{9,11},{10,... | collective-permute-start | bytes 393224 | tf_op jit(solution)/shard_map/ppermute | solution.py:31
  52.2 6.1 %collective-permute-start.17 = (bf16[32,1024]{1,0:T(8,128)(2,1)S(1)}, bf16[32,1024]{1,0:T(8,128)(2,1)S(1)}, u32[]{:S(2)}, u32[]{:S(2)}) collective-permute-start(bf16[32,1024]{1,0:T(8,128)(2,1)S(1)} %get-tuple-element.93), channel_id=1, source_target_pairs={{0,12},{1,13},{2,14},{3,15},{4,0},{5,1},{6,2},{7,3},{8,4},{9,5},{1... | collective-permute-start | bytes 196616 | tf_op jit(solution)/shard_map/ppermute | solution.py:31
  53.2 9.1 %collective-permute-start.18 = (bf16[32,1024]{1,0:T(8,128)(2,1)S(1)}, bf16[32,1024]{1,0:T(8,128)(2,1)S(1)}, u32[]{:S(2)}, u32[]{:S(2)}) collective-permute-start(bf16[32,1024]{1,0:T(8,128)(2,1)S(1)} %get-tuple-element.94), channel_id=1, source_target_pairs={{0,8},{1,9},{2,10},{3,11},{4,12},{5,13},{6,14},{7,15},{8,0},{9,1},... | collective-permute-start | bytes 196616 | tf_op jit(solution)/shard_map/ppermute | solution.py:31
  53.8 8.4 %collective-permute-start.19 = (bf16[32,1024]{1,0:T(8,128)(2,1)S(1)}, bf16[32,1024]{1,0:T(8,128)(2,1)S(1)}, u32[]{:S(2)}, u32[]{:S(2)}) collective-permute-start(bf16[32,1024]{1,0:T(8,128)(2,1)S(1)} %get-tuple-element.95), channel_id=1, source_target_pairs={{0,4},{1,5},{2,6},{3,7},{4,8},{5,9},{6,10},{7,11},{8,12},{9,13},{1... | collective-permute-start | bytes 196616 | tf_op jit(solution)/shard_map/ppermute | solution.py:31
  56.5 6.6 %collective-permute-start.13 = (bf16[16,1024]{1,0:T(8,128)(2,1)S(1)}, bf16[16,1024]{1,0:T(8,128)(2,1)S(1)}, u32[]{:S(2)}, u32[]{:S(2)}) collective-permute-start(bf16[16,1024]{1,0:T(8,128)(2,1)S(1)} %get-tuple-element.86), channel_id=1, source_target_pairs={{0,12},{1,13},{2,14},{3,15},{4,0},{5,1},{6,2},{7,3},{8,4},{9,5},{1... | collective-permute-start | bytes 98312 | tf_op jit(solution)/shard_map/ppermute | solution.py:31
  57.8 5.6 %collective-permute-start.14 = (bf16[16,1024]{1,0:T(8,128)(2,1)S(1)}, bf16[16,1024]{1,0:T(8,128)(2,1)S(1)}, u32[]{:S(2)}, u32[]{:S(2)}) collective-permute-start(bf16[16,1024]{1,0:T(8,128)(2,1)S(1)} %get-tuple-element.87), channel_id=1, source_target_pairs={{0,8},{1,9},{2,10},{3,11},{4,12},{5,13},{6,14},{7,15},{8,0},{9,1},... | collective-permute-start | bytes 98312 | tf_op jit(solution)/shard_map/ppermute | solution.py:31
  58.2 5.7 %collective-permute-start.15 = (bf16[16,1024]{1,0:T(8,128)(2,1)S(1)}, bf16[16,1024]{1,0:T(8,128)(2,1)S(1)}, u32[]{:S(2)}, u32[]{:S(2)}) collective-permute-start(bf16[16,1024]{1,0:T(8,128)(2,1)S(1)} %get-tuple-element.88), channel_id=1, source_target_pairs={{0,4},{1,5},{2,6},{3,7},{4,8},{5,9},{6,10},{7,11},{8,12},{9,13},{1... | collective-permute-start | bytes 98312 | tf_op jit(solution)/shard_map/ppermute | solution.py:31
  62.3 4.0 %collective-permute-start.20 = (bf16[16,1024]{1,0:T(8,128)(2,1)S(1)}, bf16[16,1024]{1,0:T(8,128)(2,1)S(1)}, u32[]{:S(2)}, u32[]{:S(2)}) collective-permute-start(bf16[16,1024]{1,0:T(8,128)(2,1)S(1)} %get-tuple-element.98), channel_id=1, source_target_pairs={{0,2},{1,3},{2,0},{3,1},{4,6},{5,7},{6,4},{7,5},{8,10},{9,11},{10,... | collective-permute-start | bytes 98312 | tf_op jit(solution)/shard_map/ppermute | solution.py:31

commit v10 on v9

--- a/solution.py
+++ b/solution.py
@@ -40,7 +40,9 @@
     copies = [
         pltpu.make_async_copy(ids_ref, ids, sems.at[0]),
         pltpu.make_async_copy(weights_ref, weights, sems.at[1]),
-        pltpu.make_async_copy(values_ref, message_ref.at[:, pl.ds(0, width)], sems.at[2]),
+    ] + [
+        pltpu.make_async_copy(values_ref, message_ref.at[k, :, pl.ds(0, width)], sems.at[2 + k])
+        for k in range(message_ref.shape[0])
     ]
     for copy in copies:
         copy.start()
@@ -58,14 +60,15 @@
     routing = lax.dot_general(
         own.astype(jnp.bfloat16), table, (((1,), (1,)), ((), ())), preferred_element_type=jnp.float32
     )
-    message_ref[:, width:] = routing.astype(jnp.bfloat16)
-    copies[2].wait()
-
-
-def split_kernel(half, *refs):
-    pieces, (first_ref, second_ref, token_ref) = refs[:-3], refs[-3:]
-    pieces = [ref for ref in pieces if ref.shape[1] > 2 * half]
-    whole = jnp.concatenate([ref[...].astype(jnp.float32) for ref in pieces], axis=0).astype(jnp.bfloat16)
+    for k in range(message_ref.shape[0]):
+        message_ref[k, :, width:] = routing.astype(jnp.bfloat16)
+    for copy in copies[2:]:
+        copy.wait()
+
+
+def split_kernel(half, whole_ref, sign_ref, first_ref, second_ref, token_ref):
+    pieces = [whole_ref[k].astype(jnp.float32) for k in range(whole_ref.shape[0])]
+    whole = jnp.concatenate(pieces, axis=0).astype(jnp.bfloat16)
     second_ref[...] = whole[:, :half]
     first_ref[...] = whole[:, half:]
     token_ref[...] = jnp.zeros_like(token_ref)
@@ -164,21 +167,22 @@
 
     part = n_mid * n_tp * run
     pick = jnp.concatenate(picks, axis=1)
-    chosen, swapped = [], []
-    for f in range(n_fast):
-        own = pick[f * part : (f + 1) * part]
-        runs = [
-            own[(t * n_mid + m) * run : (t * n_mid + m + 1) * run] for m in range(n_mid) for t in range(n_tp)
-        ]
-        chosen.append(own.T.astype(jnp.bfloat16))
-        swapped.append(jnp.concatenate(runs, axis=0).T.astype(jnp.bfloat16))
+    swapped = jnp.concatenate(
+        [
+            pick[f * part + (t * n_mid + m) * run : f * part + (t * n_mid + m + 1) * run]
+            for f in range(n_fast)
+            for m in range(n_mid)
+            for t in range(n_tp)
+        ],
+        axis=0,
+    )
+    chosen, swapped = pick.T.astype(jnp.bfloat16), swapped.T.astype(jnp.bfloat16)
     size = min(half, 4 * LANES)
     squares = 0.0
     for begin in range(0, 2 * half, size):
         table, side, at = (swapped, second, begin) if begin < half else (chosen, first, begin - half)
-        values = 0.0
-        for f in range(n_fast):
-            values = values + jnp.dot(table[f], side[f][:, at : at + size], preferred_element_type=jnp.float32)
+        values = jnp.concatenate([ref[:, at : at + size] for ref in side], axis=0)
+        values = jnp.dot(table, values, preferred_element_type=jnp.float32)
         squares = squares + jnp.sum(values * values, axis=1, keepdims=True)
         values = values.astype(jnp.bfloat16)
         for e in range(exp_loc):
@@ -267,21 +271,37 @@
 
 def sum_kernel(count, signs, blocks, *refs):
     out_refs = refs[count + signs :]
-    in_blocks(total_of(refs[:count]), out_refs[:blocks])
+    pieces = refs[:count]
+    if count == 1:
+        pieces = [pieces[0].at[k] for k in range(pieces[0].shape[0])]
+    total = total_of(pieces)
+    if len(out_refs[0].shape) == 3:
+        rows = out_refs[0].shape[1]
+        for k in range(out_refs[0].shape[0]):
+            out_refs[0][k] = total[k * rows : (k + 1) * rows].astype(jnp.bfloat16)
+    else:
+        in_blocks(total, out_refs[:blocks])
     for ref in out_refs[blocks:]:
         ref[...] = jnp.zeros_like(ref)
 
 
-def final_kernel(dims, count, pos_ref, first_ref, second_ref, *refs):
+def final_kernel(dims, pos_ref, first_ref, second_ref, *refs):
     n_mid, n_tp, slow_n, tok_dev, half = dims
-    left, right, (out_ref, own_ref) = refs[:count], refs[count:-2], refs[-2:]
+    (left_ref, *right), (out_ref, own_ref) = refs[:-2], refs[-2:]
+    left = [left_ref.at[k] for k in range(left_ref.shape[0])]
     tp_pos = pos_ref[0]
     col_part = out_ref.shape[1]
-    for s in range(n_tp):
-        at = s * n_mid * slow_n * tok_dev
-        own_ref[s * tok_dev : (s + 1) * tok_dev, half:] = first_ref[at : at + tok_dev, :half].astype(jnp.float32)
-        at = s * slow_n * tok_dev
-        own_ref[s * tok_dev : (s + 1) * tok_dev, :half] = second_ref[at : at + tok_dev].astype(jnp.float32)
+    run = slow_n * tok_dev
+    group = n_tp * tok_dev
+
+    def own(ref, step):
+        row = lax.broadcasted_iota(jnp.int32, (group, ref.shape[0]), 0)
+        at = lax.div(row, tok_dev) * step + pos_ref[2] * tok_dev + lax.rem(row, tok_dev)
+        table = (at == lax.broadcasted_iota(jnp.int32, (group, ref.shape[0]), 1)).astype(jnp.float32)
+        return jnp.dot(table.astype(jnp.bfloat16), ref[:, :half], preferred_element_type=jnp.float32)
+
+    own_ref[:, half:] = own(first_ref, n_mid * run)
+    own_ref[:, :half] = own(second_ref, run)
     total = jnp.concatenate([total_of(left), total_of(right)], axis=1)
     total = total + own_ref[:, pl.ds(pl.multiple_of(tp_pos * col_part, col_part), col_part)]
     rows = []
@@ -342,11 +362,13 @@
     return near, sign
 
 
-def summed(pieces, blocks, after, signed):
-    rows, columns = pieces[0].shape
+def summed(pieces, blocks, stacked, after, signed):
+    rows, columns = pieces[0].shape[-2:]
+    shape = (blocks, rows // blocks, columns) if stacked else (rows // blocks, columns)
+    outs = 1 if stacked else blocks
     return local_call(
-        functools.partial(sum_kernel, len(pieces), len(after), blocks),
-        [jax.ShapeDtypeStruct((rows // blocks, columns), pieces[0].dtype)] * blocks + [TOKEN] * signed,
+        functools.partial(sum_kernel, len(pieces), len(after), outs),
+        [jax.ShapeDtypeStruct(shape, pieces[0].dtype)] * outs + [TOKEN] * signed,
         list(pieces) + after,
         limit=4 << 20,
         moved=2 * (len(pieces) + 1) * rows * columns,
@@ -378,44 +400,45 @@
     rows = cap * n_ep
     tokens = group * n_ep
     digits = factors_of(n_ep)
-    fast, mid, slow = digits[0], digits[1:2], digits[2:]
+    fast, mid = digits[0], digits[1:2]
     half = width // 2
     slow_n = n_ep
     for _, radix in [fast] + mid:
         slow_n //= radix
-    n_fast, n_mid = fast[1], mid[0][1] if mid else 1
+    n_fast, n_mid = fast[1], mid[0][1]
 
     bf16 = functools.partial(jax.ShapeDtypeStruct, dtype=jnp.bfloat16)
     slots = exp_loc * rows
     lead = exp_loc - exp_loc // 2
     tail = exp_loc - lead
     gain = norm_gain.reshape(1, width)
-    position = jnp.stack([tp_pos, ep_pos * exp_loc])
+    position = jnp.stack([tp_pos, ep_pos * exp_loc, ep_pos // (n_ep // slow_n)])
     (message,) = local_call(
         functools.partial(pack_kernel, top),
-        [bf16((tok_dev, width + LANES))],
+        [bf16((slow_n, tok_dev, width + LANES))],
         [position, expert_ids.T, gate_weights.T, hidden_in],
         far=[1, 2, 3],
         scratch=[
             pltpu.VMEM((top, group), jnp.int32),
             pltpu.VMEM((top, group), jnp.float32),
-            pltpu.SemaphoreType.DMA((3,)),
+            pltpu.SemaphoreType.DMA((2 + slow_n,)),
         ],
         limit=4 << 20,
     )
-    around = [message]
-    for digit in reversed(slow):
-        around = [a for piece in around for a in arrivals(piece, "ep", n_ep, *digit)]
+    stride = n_ep // slow_n
+    alike = [[at + k * stride for k in range(slow_n)] for at in range(stride)]
+    along_slow = lambda a: lax.all_to_all(a, "ep", 0, 0, axis_index_groups=alike, tiled=True)
+    around = along_slow(message)
     gate_lead, sign = loaded([(w_gate, e) for e in range(lead)], [gain])
     first, second, sign = local_call(
         functools.partial(split_kernel, half),
         [bf16((slow_n * tok_dev, width + LANES - half)), bf16((slow_n * tok_dev, half)), TOKEN],
-        around + [sign],
+        [around, sign],
         limit=4 << 20,
     )
     gate_tail, sign = loaded([(w_gate, e) for e in range(lead, exp_loc)], [sign])
     along_tp = lambda a: arrivals(a, "tp", n_tp, 1, n_tp)
-    along_mid = lambda a: arrivals(a, "ep", n_ep, *mid[0]) if mid else [a]
+    along_mid = lambda a: arrivals(a, "ep", n_ep, *mid[0])
     first, second = along_mid(first), along_tp(second)
     first, sign = joined(first, [sign], 1)
     (second,) = joined(second, [], 0)
@@ -480,23 +503,16 @@
         stride, radix = digit
         return [blocks[0]] + [shifted(blocks[s], "ep", n_ep, stride, radix, radix - s) for s in range(1, radix)]
 
-    slow = list(reversed(slow))
-    right_way, left_way = slow + mid, mid + slow
-    right = summed(swapped(mixed_of(turned, col_half), fast), right_way[0][1], [], 0)
-    left = summed(swapped(mixed_of(mix, 0), fast), left_way[0][1], [], 0)
-    signs = []
-    for digit, later in zip(left_way[:-1], left_way[1:]):
-        *left, sign = summed(swapped(left, digit), later[1], [], 1)
-        signs.append(sign)
-    for digit, later in zip(right_way[:-1], right_way[1:]):
-        right = summed(swapped(right, digit), later[1], signs, 0)
-        signs = []
-    left = swapped(left, left_way[-1])
-    right = swapped(right, right_way[-1])
+    (right,) = summed(swapped(mixed_of(turned, col_half), fast), slow_n, True, [], 0)
+    left = summed(swapped(mixed_of(mix, 0), fast), n_mid, False, [], 0)
+    right = along_slow(right)
+    left, sign = summed(swapped(left, mid[0]), slow_n, True, [], 1)
+    left = along_slow(left)
+    right = swapped(summed([right], n_mid, False, [sign], 0), mid[0])
     (mixed,) = local_call(
-        functools.partial(final_kernel, (n_mid, n_tp, slow_n, tok_dev, half), len(left)),
+        functools.partial(final_kernel, (n_mid, n_tp, slow_n, tok_dev, half)),
         [bf16((group, col_part))],
-        [position, first[0], second[0]] + left + right,
+        [position, first[0], second[0], left] + right,
         scratch=[pltpu.VMEM((group, width), jnp.float32)],
         limit=4 << 20,
         moved=2 * group * (width + 6 * col_part),
@@ -560,7 +576,8 @@
     group, top = expert_ids.shape
     exp_loc = w_gate.shape[0]
     cap = max(2, 2 * top * group // (exp_loc * lax.axis_size("ep")))
-    plan = by_tokens if exp_loc > 1 and exp_loc * cap >= group else by_slots
+    whole = exp_loc > 1 and len(factors_of(lax.axis_size("ep"))) > 2 and exp_loc * cap >= group
+    plan = by_tokens if whole else by_slots
     return plan(hidden_in, norm_gain, expert_ids, gate_weights, w_gate, w_up, w_down)
 
 

time: 67.7 us -> 82 us (1.21)
  local copies, waits for them, and re-layouts: 0.71 us -> 7.03 us
  waiting for transfers between devices: 11.2 us -> 16.4 us
  Pallas kernels: 32.5 us -> 34.6 us
    all_to_all x0 -> x3, starting transfers between devices: none -> 14.1 us  [by_tokens(): lax.all_to_all(a, 'ep', 0, 0, axis_index_groups=alike, tiled=True)]
    ppermute x21 -> x12, starting transfers between devices: 22.8 us -> 9.12 us  [shifted(): return lax.ppermute(x, axis, pairs)]
    all_to_all x0 -> x3, waiting for transfers between devices: none -> 9.31 us  [by_tokens(): lax.all_to_all(a, 'ep', 0, 0, axis_index_groups=alike, tiled=True)]
    unnamed x0 -> x8, local copies, waits for them, and re-layouts: none -> 6.32 us
    ppermute x21 -> x12, waiting for transfers between devices: 11.2 us -> 7.13 us  [shifted(): return lax.ppermute(x, axis, pairs)]
    pallas_call x20, Pallas kernels: 32.5 us -> 34.6 us  [local_call(): pl.pallas_call(kernel, out_shape=shapes, in_specs=specs, out_specs=[VMEM]...]
  transfers between devices with their start and end apart: 21 -> 15, of which waited for: 9 -> 7; matrix products, arithmetic and copies ran while one was open for 1% -> 1% of each run, Pallas kernels for 33% -> 29%
where the time goes in v10:
time: 82 us; the launch traced here: 81.5 us
  Pallas kernels  34.6 us (42%)
  starting transfers between devices  23.2 us (28%)
  waiting for transfers between devices  16.4 us (20%)
  local copies, waits for them, and re-layouts  7.03 us (9%)
    pallas_call x20, Pallas kernels, local_call(): pl.pallas_call(kernel, out_shape=shapes, in_specs=specs, out_specs=[VMEM]...  34.6 us
    all_to_all x3, starting transfers between devices, by_tokens(): lax.all_to_all(a, 'ep', 0, 0, axis_index_groups=alike, tiled=True)  14.1 us
    all_to_all x3, waiting for transfers between devices, by_tokens(): lax.all_to_all(a, 'ep', 0, 0, axis_index_groups=alike, tiled=True)  9.31 us
    ppermute x12, starting transfers between devices, shifted(): return lax.ppermute(x, axis, pairs)  9.12 us
    ppermute x12, waiting for transfers between devices, shifted(): return lax.ppermute(x, axis, pairs)  7.13 us
    unnamed x8, local copies, waits for them, and re-layouts  6.32 us
  transfers between devices with their start and end apart: 15, of which 7 were waited for; matrix products, arithmetic and copies ran while one was open for 1% of the time, Pallas kernels for 29%

profile of v10, /device:TPU:0, one launch (start us, length us, event | category | flops | bytes accessed | tf_op | source)
XLA Modules:
  0.0 81.5 jit_solution(5452281140263165585)
XLA Ops:
  0.0 0.1 pad_add_fusion.pos_ref
  0.1 2.3 %shard_map.73 = bf16[4,8,4224]{2,1,0:T(8,128)(2,1)} custom-call(s32[3]{0:T(128)S(1)} %pad_add_fusion.pos_ref, s32[8,16]{1,0:T(8,128)} %bitcast.5, f32[8,16]{1,0:T(8,128)} %bitcast.6, bf16[8,4096]{1,0:T(8,128)(2,1)} %values_ref.1), custom_call_target="tpu_custom_call" | custom-call | tf_op jit(solution)/shard_map/pallas_call | solution.py:333
  2.4 6.3 %all-to-all-start = ((bf16[4,8,4224]{2,1,0:T(8,128)(2,1)}), bf16[4,8,4224]{2,1,0:T(8,128)(2,1)S(1)}, u32[]{:S(2)}, u32[]{:S(2)}) async-start(bf16[4,8,4224]{2,1,0:T(8,128)(2,1)} %shard_map.73), calls=%async_computation | async-start | bytes 540672 | tf_op jit(solution)/shard_map/all_to_all | solution.py:430
  8.7 0.7 reshape.3.refs_2_.gain_ref
  9.4 3.5 %shard_map.74 = (f32[8,128]{1,0:T(8,128)S(1)}, bf16[4096,512]{1,0:T(8,128)(2,1)S(1)}, bf16[4096,512]{1,0:T(8,128)(2,1)S(1)}) custom-call(bf16[4,4096,512]{2,1,0:T(8,128)(2,1)} %refs_1_.4, bf16[4,4096,512]{2,1,0:T(8,128)(2,1)} %refs_1_.4, bf16[1,4096]{1,0:T(2,128)(2,1)S(1)} %reshape.3.refs_2_.gain_ref), custom_call_target="tpu_custom_call" | custom-call | bytes 8388608 | tf_op jit(solution)/shard_map/pallas_call | solution.py:333
  12.9 0.0 copy-start
  12.9 2.0 %copy-done = bf16[4096,512]{1,0:T(8,128)(2,1)} copy-done((bf16[4096,512]{1,0:T(8,128)(2,1)}, bf16[4096,512]{1,0:T(8,128)(2,1)S(1)}, u32[]{:S(2)}) %copy-start) | copy-done | bytes 4194328
  14.9 0.0 copy-start.2
  14.9 2.0 %copy-done.2 = bf16[4096,512]{1,0:T(8,128)(2,1)} copy-done((bf16[4096,512]{1,0:T(8,128)(2,1)}, bf16[4096,512]{1,0:T(8,128)(2,1)S(1)}, u32[]{:S(2)}) %copy-start.2) | copy-done | bytes 4194328
  16.9 0.9 %all-to-all-done.whole_ref = bf16[4,8,4224]{2,1,0:T(8,128)(2,1)S(1)} async-done(((bf16[4,8,4224]{2,1,0:T(8,128)(2,1)}), bf16[4,8,4224]{2,1,0:T(8,128)(2,1)S(1)}, u32[]{:S(2)}, u32[]{:S(2)}) %all-to-all-start) | async-done | bytes 270368 | tf_op jit(solution)/shard_map/all_to_all | solution.py:430
  17.8 1.6 %collective-permute-start = (bf16[32,2176]{1,0:T(8,128)(2,1)S(1)}, bf16[32,2176]{1,0:T(8,128)(2,1)S(1)}, u32[]{:S(2)}, u32[]{:S(2)}) collective-permute-start(bf16[32,2176]{1,0:T(8,128)(2,1)S(1)} %get-tuple-element.46.refs_0_), channel_id=1, source_target_pairs={{0,2},{1,3},{2,0},{3,1},{4,6},{5,7},{6,4},{7,5},{8,10},{9,11},{10,... | collective-permute-start | bytes 417800 | tf_op jit(solution)/shard_map/ppermute | solution.py:31
  19.4 1.5 %collective-permute-start.2 = (bf16[32,2048]{1,0:T(8,128)(2,1)S(1)}, bf16[32,2048]{1,0:T(8,128)(2,1)S(1)}, u32[]{:S(2)}, u32[]{:S(2)}) collective-permute-start(bf16[32,2048]{1,0:T(8,128)(2,1)S(1)} %get-tuple-element.53.refs_0_), channel_id=1, source_target_pairs={{0,16},{16,0},{1,17},{17,1},{2,18},{18,2},{3,19},{19,3},{4,20},{20... | collective-permute-start | bytes 393224 | tf_op jit(solution)/shard_map/ppermute | solution.py:31
  20.9 3.5 %shard_map.76 = (f32[8,128]{1,0:T(8,128)S(1)}, bf16[4096,512]{1,0:T(8,128)(2,1)S(1)}, bf16[4096,512]{1,0:T(8,128)(2,1)S(1)}) custom-call(bf16[4,4096,512]{2,1,0:T(8,128)(2,1)} %refs_1_.4, bf16[4,4096,512]{2,1,0:T(8,128)(2,1)} %refs_1_.4, f32[8,128]{1,0:T(8,128)S(1)} %get-tuple-element.47.refs_2_), custom_call_target="tpu_custom_call" | custom-call | bytes 8388608 | tf_op jit(solution)/shard_map/pallas_call | solution.py:333
  24.4 0.0 collective-permute-done.refs_1_
  24.4 0.6 collective-permute-start.1
  25.0 0.0 collective-permute-done.2.refs_1_
  25.1 1.1 %collective-permute-start.3 = (bf16[64,2048]{1,0:T(8,128)(2,1)S(1)}, bf16[64,2048]{1,0:T(8,128)(2,1)S(1)}, u32[]{:S(2)}, u32[]{:S(2)}) collective-permute-start(bf16[64,2048]{1,0:T(8,128)(2,1)S(1)} %shard_map.80.refs_0_), channel_id=1, source_target_pairs={{0,2},{1,3},{2,0},{3,1},{4,6},{5,7},{6,4},{7,5},{8,10},{9,11},{10,... | collective-permute-start | bytes 786440 | tf_op jit(solution)/shard_map/ppermute | solution.py:31
  26.1 4.7 %shard_map.78 = (f32[8,128]{1,0:T(8,128)S(1)}, bf16[4096,512]{1,0:T(8,128)(2,1)S(1)}, bf16[4096,512]{1,0:T(8,128)(2,1)S(1)}, bf16[1024,2048]{1,0:T(8,128)(2,1)S(1)}) custom-call(bf16[4,4096,512]{2,1,0:T(8,128)(2,1)} %refs_9_.1, bf16[4,4096,512]{2,1,0:T(8,128)(2,1)} %refs_9_.1, bf16[4,1024,2048]{2,1,0:T(8,128)(2,1)} %refs_4_.1, ...), custom_call_target="tpu_custom_call" | custom-call | bytes 12582912 | tf_op jit(solution)/shard_map/pallas_call | solution.py:333
  30.9 0.3 collective-permute-done.1.refs_1_
  31.2 0.1 collective-permute-start.4
  31.3 0.2 collective-permute-done.3.refs_1_
  31.5 0.3 collective-permute-start.5
  31.9 0.0 copy-start.1
  31.9 0.0 copy-start.3
  31.9 2.4 %shard_map.82 = (f32[8,128]{1,0:T(8,128)S(1)}, bf16[1024,2048]{1,0:T(8,128)(2,1)S(1)}) custom-call(bf16[4,1024,2048]{2,1,0:T(8,128)(2,1)} %refs_4_.1, f32[8,128]{1,0:T(8,128)S(1)} %get-tuple-element.58.refs_1_), custom_call_target="tpu_custom_call" | custom-call | bytes 4194304 | tf_op jit(solution)/shard_map/pallas_call | solution.py:333
  34.3 0.0 collective-permute-done.5.refs_3_
  34.3 0.0 collective-permute-done.4.refs_1_
  34.3 1.1 %copy-done.1 = bf16[4096,512]{1,0:T(8,128)(2,1)S(1)} copy-done((bf16[4096,512]{1,0:T(8,128)(2,1)S(1)}, bf16[4096,512]{1,0:T(8,128)(2,1)}, u32[]{:S(2)}) %copy-start.1) | copy-done | bytes 4194328
  35.3 1.3 %copy-done.3 = bf16[4096,512]{1,0:T(8,128)(2,1)S(1)} copy-done((bf16[4096,512]{1,0:T(8,128)(2,1)S(1)}, bf16[4096,512]{1,0:T(8,128)(2,1)}, u32[]{:S(2)}) %copy-start.3) | copy-done | bytes 4194328
  36.6 5.5 %shard_map.83 = (bf16[2,64,512]{2,1,0:T(8,128)(2,1)S(1)}, bf16[4,64,4096]{2,1,0:T(8,128)(2,1)S(1)}, bf16[2,256,256]{2,1,0:T(8,128)(2,1)S(1)}, bf16[2,256,256]{2,...) custom-call(s32[3]{0:T(128)S(1)} %pad_add_fusion.pos_ref, ...), custom_call_target="tpu_custom_call" | custom-call | flops 1610612736 | bytes 16777216 | tf_op jit(solution)/shard_map/pallas_call | solution.py:333
  42.2 1.3 %collective-permute-start.6 = (bf16[2,64,512]{2,1,0:T(8,128)(2,1)S(1)}, bf16[2,64,512]{2,1,0:T(8,128)(2,1)S(1)}, u32[]{:S(2)}, u32[]{:S(2)}) collective-permute-start(bf16[2,64,512]{2,1,0:T(8,128)(2,1)S(1)} %get-tuple-element.67.refs_0_), channel_id=1, source_target_pairs={{0,16},{16,0},{1,17},{17,1},{2,18},{18,2},{3,19},{19,3},{4,20},{20... | collective-permute-start | bytes 393224 | tf_op jit(solution)/shard_map/ppermute | solution.py:31
  43.5 4.0 %shard_map.84 = (bf16[2,64,512]{2,1,0:T(8,128)(2,1)S(1)}, bf16[1024,2048]{1,0:T(8,128)(2,1)S(1)}, bf16[1024,2048]{1,0:T(8,128)(2,1)S(1)}) custom-call(s32[3]{0:T(128)S(1)} %pad_add_fusion.pos_ref, bf16[4,64,4096]{2,1,0:T(8,128)(2,1)S(1)} %get-tuple-element.61.normed_ref, bf16[4096,512]{1,0:T(8,128)(2,1)S(1)} %get-tuple-element.62.refs_0_, ...), custom_call_target="tpu_custom_call" | custom-call | flops 1073741824 | bytes 16777216 | tf_op jit(solution)/shard_map/pallas_call | solution.py:333
  47.5 0.9 %collective-permute-start.7 = (bf16[2,64,512]{2,1,0:T(8,128)(2,1)S(1)}, bf16[2,64,512]{2,1,0:T(8,128)(2,1)S(1)}, u32[]{:S(2)}, u32[]{:S(2)}) collective-permute-start(bf16[2,64,512]{2,1,0:T(8,128)(2,1)S(1)} %get-tuple-element.66.own_ref), channel_id=1, source_target_pairs={{0,16},{16,0},{1,17},{17,1},{2,18},{18,2},{3,19},{19,3},{4,20},{20... | collective-permute-start | bytes 393224 | tf_op jit(solution)/shard_map/ppermute | solution.py:31
  48.3 0.0 collective-permute-done.6.refs_1_
  48.3 2.9 %shard_map.85 = (bf16[128,2048]{1,0:T(8,128)(2,1)S(1)}, f32[128,2048]{1,0:T(8,128)S(1)}) custom-call(s32[3]{0:T(128)S(1)} %pad_add_fusion.pos_ref, bf16[2,64,512]{2,1,0:T(8,128)(2,1)S(1)} %get-tuple-element.66.own_ref, bf16[2,64,512]{2,1,0:T(8,128)(2,1)S(1)} %get-tuple-element.67.refs_0_, bf16[2,64,512]{2,1,0:T(8,128)(2,1)S(1)} %collective-permute-done.6.refs_1_, ...), custom_call_target="tpu_custom_call" | custom-call | flops 536870912 | bytes 8388608 | tf_op jit(solution)/shard_map/pallas_call | solution.py:333
  51.2 2.0 %collective-permute-done.7.refs_0_ = bf16[2,64,512]{2,1,0:T(8,128)(2,1)S(1)} collective-permute-done((bf16[2,64,512]{2,1,0:T(8,128)(2,1)S(1)}, bf16[2,64,512]{2,1,0:T(8,128)(2,1)S(1)}, u32[]{:S(2)}, u32[]{:S(2)}) %collective-permute-start.7) | collective-permute-done | bytes 131104 | tf_op jit(solution)/shard_map/ppermute | solution.py:31
  53.2 1.4 %shard_map.89 = (bf16[128,1024]{1,0:T(8,128)(2,1)S(1)}, bf16[128,1024]{1,0:T(8,128)(2,1)S(1)}) custom-call(s32[3]{0:T(128)S(1)} %pad_add_fusion.pos_ref, bf16[2,256,256]{2,1,0:T(8,128)(2,1)S(1)} %get-tuple-element.79.mix_ref, bf16[128,2048]{1,0:T(8,128)(2,1)S(1)} %get-tuple-element.72.done_ref, f32[128,2048]{1,0:T(8,128)S(1)} %get-tuple-element.73.part_ref, ...), custom_call_target="tpu_custom_call" | custom-call | flops 536870912 | bytes 8388608 | tf_op jit(solution)/shard_map/pallas_call | solution.py:333
  54.5 0.1 collective-permute-start.10
  54.6 1.4 %shard_map.86 = (bf16[128,1024]{1,0:T(8,128)(2,1)S(1)}, bf16[128,1024]{1,0:T(8,128)(2,1)S(1)}) custom-call(s32[3]{0:T(128)S(1)} %pad_add_fusion.pos_ref, bf16[2,256,256]{2,1,0:T(8,128)(2,1)S(1)} %get-tuple-element.60.mix_ref, bf16[128,2048]{1,0:T(8,128)(2,1)S(1)} %get-tuple-element.72.done_ref, f32[128,2048]{1,0:T(8,128)S(1)} %get-tuple-element.73.part_ref, ...), custom_call_target="tpu_custom_call" | custom-call | flops 536870912 | bytes 8388608 | tf_op jit(solution)/shard_map/pallas_call | solution.py:333
  56.0 0.6 collective-permute-start.8
  56.5 0.0 collective-permute-done.10.refs_1_
  56.5 0.8 shard_map.90
  57.3 4.5 %all-to-all-start.2 = ((bf16[4,32,1024]{2,1,0:T(8,128)(2,1)}), bf16[4,32,1024]{2,1,0:T(8,128)(2,1)S(1)}, u32[]{:S(2)}, u32[]{:S(2)}) async-start(bf16[4,32,1024]{2,1,0:T(8,128)(2,1)} %shard_map.90), calls=%async_computation.2 | async-start | bytes 524288 | tf_op jit(solution)/shard_map/all_to_all | solution.py:430
  61.7 0.0 collective-permute-done.8.refs_1_
  61.7 0.1 shard_map.87
  61.8 0.6 collective-permute-start.9
  62.4 4.6 %collective-permute-done.9.refs_1_ = bf16[64,1024]{1,0:T(8,128)(2,1)S(1)} collective-permute-done((bf16[64,1024]{1,0:T(8,128)(2,1)S(1)}, bf16[64,1024]{1,0:T(8,128)(2,1)S(1)}, u32[]{:S(2)}, u32[]{:S(2)}) %collective-permute-start.9) | collective-permute-done | bytes 131104 | tf_op jit(solution)/shard_map/ppermute | solution.py:31
  67.0 0.7 shard_map.88
  67.7 3.1 %all-to-all-done.2.refs_0_ = bf16[4,32,1024]{2,1,0:T(8,128)(2,1)S(1)} async-done(((bf16[4,32,1024]{2,1,0:T(8,128)(2,1)}), bf16[4,32,1024]{2,1,0:T(8,128)(2,1)S(1)}, u32[]{:S(2)}, u32[]{:S(2)}) %all-to-all-start.2) | async-done | bytes 262176 | tf_op jit(solution)/shard_map/all_to_all | solution.py:430
  70.8 3.3 %all-to-all-start.1 = ((bf16[4,16,1024]{2,1,0:T(8,128)(2,1)}), bf16[4,16,1024]{2,1,0:T(8,128)(2,1)S(1)}, u32[]{:S(2)}, u32[]{:S(2)}) async-start(bf16[4,16,1024]{2,1,0:T(8,128)(2,1)} %get-tuple-element.78), calls=%async_computation.1 | async-start | bytes 262144 | tf_op jit(solution)/shard_map/all_to_all | solution.py:430
  74.2 0.6 collective-permute-start.11
  74.8 5.3 %all-to-all-done.1.refs_0_ = bf16[4,16,1024]{2,1,0:T(8,128)(2,1)S(1)} async-done(((bf16[4,16,1024]{2,1,0:T(8,128)(2,1)}), bf16[4,16,1024]{2,1,0:T(8,128)(2,1)S(1)}, u32[]{:S(2)}, u32[]{:S(2)}) %all-to-all-start.1) | async-done | bytes 131104 | tf_op jit(solution)/shard_map/all_to_all | solution.py:430
  80.1 0.0 collective-permute-done.11.refs_2_
  80.1 1.4 %shard_map.92 = bf16[16,2048]{1,0:T(8,128)(2,1)} custom-call(s32[3]{0:T(128)S(1)} %pad_add_fusion.pos_ref, bf16[128,2176]{1,0:T(8,128)(2,1)S(1)} %get-tuple-element.52.refs_0_.first_ref, bf16[128,2048]{1,0:T(8,128)(2,1)S(1)} %shard_map.81.refs_2_.second_ref, bf16[4,16,1024]{2,1,0:T(8,128)(2,1)S(1)} %all-to-all-done.1.refs_0_, ...), custom_call_target="tpu_custom_call" | custom-call | bytes 524288 | tf_op jit(solution)/shard_map/pallas_call | solution.py:333
  (6 shorter events, 0.2 us)
Async XLA Ops:
  2.4 15.4 %all-to-all-start = ((bf16[4,8,4224]{2,1,0:T(8,128)(2,1)}), bf16[4,8,4224]{2,1,0:T(8,128)(2,1)S(1)}, u32[]{:S(2)}, u32[]{:S(2)}) async-start(bf16[4,8,4224]{2,1,0:T(8,128)(2,1)} %shard_map.73), calls=%async_computation | async-start | bytes 540672 | tf_op jit(solution)/shard_map/all_to_all | solution.py:430
  12.9 2.0 %copy-start = (bf16[4096,512]{1,0:T(8,128)(2,1)}, bf16[4096,512]{1,0:T(8,128)(2,1)S(1)}, u32[]{:S(2)}) copy-start(bf16[4096,512]{1,0:T(8,128)(2,1)S(1)} %get-tuple-element.54.refs_4_) | copy-start | bytes 12582916
  14.9 2.0 %copy-start.2 = (bf16[4096,512]{1,0:T(8,128)(2,1)}, bf16[4096,512]{1,0:T(8,128)(2,1)S(1)}, u32[]{:S(2)}) copy-start(bf16[4096,512]{1,0:T(8,128)(2,1)S(1)} %get-tuple-element.55.refs_5_) | copy-start | bytes 12582916
  17.8 6.6 %collective-permute-start = (bf16[32,2176]{1,0:T(8,128)(2,1)S(1)}, bf16[32,2176]{1,0:T(8,128)(2,1)S(1)}, u32[]{:S(2)}, u32[]{:S(2)}) collective-permute-start(bf16[32,2176]{1,0:T(8,128)(2,1)S(1)} %get-tuple-element.46.refs_0_), channel_id=1, source_target_pairs={{0,2},{1,3},{2,0},{3,1},{4,6},{5,7},{6,4},{7,5},{8,10},{9,11},{10,... | collective-permute-start | bytes 417800 | tf_op jit(solution)/shard_map/ppermute | solution.py:31
  19.4 5.6 %collective-permute-start.2 = (bf16[32,2048]{1,0:T(8,128)(2,1)S(1)}, bf16[32,2048]{1,0:T(8,128)(2,1)S(1)}, u32[]{:S(2)}, u32[]{:S(2)}) collective-permute-start(bf16[32,2048]{1,0:T(8,128)(2,1)S(1)} %get-tuple-element.53.refs_0_), channel_id=1, source_target_pairs={{0,16},{16,0},{1,17},{17,1},{2,18},{18,2},{3,19},{19,3},{4,20},{20... | collective-permute-start | bytes 393224 | tf_op jit(solution)/shard_map/ppermute | solution.py:31
  24.4 6.7 %collective-permute-start.1 = (bf16[64,2176]{1,0:T(8,128)(2,1)S(1)}, bf16[64,2176]{1,0:T(8,128)(2,1)S(1)}, u32[]{:S(2)}, u32[]{:S(2)}) collective-permute-start(bf16[64,2176]{1,0:T(8,128)(2,1)S(1)} %get-tuple-element.49.refs_0_), channel_id=1, source_target_pairs={{0,16},{16,0},{1,17},{17,1},{2,18},{18,2},{3,19},{19,3},{4,20},{20... | collective-permute-start | bytes 835592 | tf_op jit(solution)/shard_map/ppermute | solution.py:31
  25.1 6.4 %collective-permute-start.3 = (bf16[64,2048]{1,0:T(8,128)(2,1)S(1)}, bf16[64,2048]{1,0:T(8,128)(2,1)S(1)}, u32[]{:S(2)}, u32[]{:S(2)}) collective-permute-start(bf16[64,2048]{1,0:T(8,128)(2,1)S(1)} %shard_map.80.refs_0_), channel_id=1, source_target_pairs={{0,2},{1,3},{2,0},{3,1},{4,6},{5,7},{6,4},{7,5},{8,10},{9,11},{10,... | collective-permute-start | bytes 786440 | tf_op jit(solution)/shard_map/ppermute | solution.py:31
  31.2 3.1 %collective-permute-start.4 = (bf16[128,2176]{1,0:T(8,128)(2,1)S(1)}, bf16[128,2176]{1,0:T(8,128)(2,1)S(1)}, u32[]{:S(2)}, u32[]{:S(2)}) collective-permute-start(bf16[128,2176]{1,0:T(8,128)(2,1)S(1)} %get-tuple-element.52.refs_0_.first_ref), channel_id=1, source_target_pairs={{0,1},{1,0},{2,3},{3,2},{4,5},{5,4},{6,7},{7,6},{8,9},{9,8},{10,11... | collective-permute-start | bytes 1671176 | tf_op jit(solution)/shard_map/ppermute | solution.py:31
  31.5 2.7 %collective-permute-start.5 = (bf16[128,2048]{1,0:T(8,128)(2,1)S(1)}, bf16[128,2048]{1,0:T(8,128)(2,1)S(1)}, u32[]{:S(2)}, u32[]{:S(2)}) collective-permute-start(bf16[128,2048]{1,0:T(8,128)(2,1)S(1)} %shard_map.81.refs_2_.second_ref), channel_id=1, source_target_pairs={{0,1},{1,0},{2,3},{3,2},{4,5},{5,4},{6,7},{7,6},{8,9},{9,8},{10,11... | collective-permute-start | bytes 1572872 | tf_op jit(solution)/shard_map/ppermute | solution.py:31
  31.9 3.4 %copy-start.1 = (bf16[4096,512]{1,0:T(8,128)(2,1)S(1)}, bf16[4096,512]{1,0:T(8,128)(2,1)}, u32[]{:S(2)}) copy-start(bf16[4096,512]{1,0:T(8,128)(2,1)} %copy-done) | copy-start | bytes 12582916
  31.9 4.7 %copy-start.3 = (bf16[4096,512]{1,0:T(8,128)(2,1)S(1)}, bf16[4096,512]{1,0:T(8,128)(2,1)}, u32[]{:S(2)}) copy-start(bf16[4096,512]{1,0:T(8,128)(2,1)} %copy-done.2) | copy-start | bytes 12582916
  42.2 6.2 %collective-permute-start.6 = (bf16[2,64,512]{2,1,0:T(8,128)(2,1)S(1)}, bf16[2,64,512]{2,1,0:T(8,128)(2,1)S(1)}, u32[]{:S(2)}, u32[]{:S(2)}) collective-permute-start(bf16[2,64,512]{2,1,0:T(8,128)(2,1)S(1)} %get-tuple-element.67.refs_0_), channel_id=1, source_target_pairs={{0,16},{16,0},{1,17},{17,1},{2,18},{18,2},{3,19},{19,3},{4,20},{20... | collective-permute-start | bytes 393224 | tf_op jit(solution)/shard_map/ppermute | solution.py:31
  47.5 5.7 %collective-permute-start.7 = (bf16[2,64,512]{2,1,0:T(8,128)(2,1)S(1)}, bf16[2,64,512]{2,1,0:T(8,128)(2,1)S(1)}, u32[]{:S(2)}, u32[]{:S(2)}) collective-permute-start(bf16[2,64,512]{2,1,0:T(8,128)(2,1)S(1)} %get-tuple-element.66.own_ref), channel_id=1, source_target_pairs={{0,16},{16,0},{1,17},{17,1},{2,18},{18,2},{3,19},{19,3},{4,20},{20... | collective-permute-start | bytes 393224 | tf_op jit(solution)/shard_map/ppermute | solution.py:31
  54.5 2.0 %collective-permute-start.10 = (bf16[128,1024]{1,0:T(8,128)(2,1)S(1)}, bf16[128,1024]{1,0:T(8,128)(2,1)S(1)}, u32[]{:S(2)}, u32[]{:S(2)}) collective-permute-start(bf16[128,1024]{1,0:T(8,128)(2,1)S(1)} %get-tuple-element.81), channel_id=1, source_target_pairs={{0,1},{1,0},{2,3},{3,2},{4,5},{5,4},{6,7},{7,6},{8,9},{9,8},{10,11... | collective-permute-start | bytes 786440 | tf_op jit(solution)/shard_map/ppermute | solution.py:31
  56.0 5.8 %collective-permute-start.8 = (bf16[128,1024]{1,0:T(8,128)(2,1)S(1)}, bf16[128,1024]{1,0:T(8,128)(2,1)S(1)}, u32[]{:S(2)}, u32[]{:S(2)}) collective-permute-start(bf16[128,1024]{1,0:T(8,128)(2,1)S(1)} %get-tuple-element.75), channel_id=1, source_target_pairs={{0,1},{1,0},{2,3},{3,2},{4,5},{5,4},{6,7},{7,6},{8,9},{9,8},{10,11... | collective-permute-start | bytes 786440 | tf_op jit(solution)/shard_map/ppermute | solution.py:31
  57.3 13.6 %all-to-all-start.2 = ((bf16[4,32,1024]{2,1,0:T(8,128)(2,1)}), bf16[4,32,1024]{2,1,0:T(8,128)(2,1)S(1)}, u32[]{:S(2)}, u32[]{:S(2)}) async-start(bf16[4,32,1024]{2,1,0:T(8,128)(2,1)} %shard_map.90), calls=%async_computation.2 | async-start | bytes 524288 | tf_op jit(solution)/shard_map/all_to_all | solution.py:430
  61.8 5.2 %collective-permute-start.9 = (bf16[64,1024]{1,0:T(8,128)(2,1)S(1)}, bf16[64,1024]{1,0:T(8,128)(2,1)S(1)}, u32[]{:S(2)}, u32[]{:S(2)}) collective-permute-start(bf16[64,1024]{1,0:T(8,128)(2,1)S(1)} %get-tuple-element.77), channel_id=1, source_target_pairs={{0,2},{1,3},{2,0},{3,1},{4,6},{5,7},{6,4},{7,5},{8,10},{9,11},{10,... | collective-permute-start | bytes 393224 | tf_op jit(solution)/shard_map/ppermute | solution.py:31
  70.8 9.2 %all-to-all-start.1 = ((bf16[4,16,1024]{2,1,0:T(8,128)(2,1)}), bf16[4,16,1024]{2,1,0:T(8,128)(2,1)S(1)}, u32[]{:S(2)}, u32[]{:S(2)}) async-start(bf16[4,16,1024]{2,1,0:T(8,128)(2,1)} %get-tuple-element.78), calls=%async_computation.1 | async-start | bytes 262144 | tf_op jit(solution)/shard_map/all_to_all | solution.py:430
  74.2 5.8 %collective-permute-start.11 = (bf16[16,1024]{1,0:T(8,128)(2,1)S(1)}, bf16[16,1024]{1,0:T(8,128)(2,1)S(1)}, u32[]{:S(2)}, u32[]{:S(2)}) collective-permute-start(bf16[16,1024]{1,0:T(8,128)(2,1)S(1)} %get-tuple-element.84), channel_id=1, source_target_pairs={{0,2},{1,3},{2,0},{3,1},{4,6},{5,7},{6,4},{7,5},{8,10},{9,11},{10,... | collective-permute-start | bytes 98312 | tf_op jit(solution)/shard_map/ppermute | solution.py:31

commit v11 on v9

--- a/solution.py
+++ b/solution.py
@@ -17,22 +17,27 @@
             digits.append((stride, 2))
             stride, n = stride * 2, n // 2
     while n > 1:
-        radix = next(r for r in (4, 3, 2, n) if n % r == 0)
+        radix = 4 if n % 4 == 0 else 2
         digits.append((stride, radix))
         stride, n = stride * radix, n // radix
     return digits
 
 
-def shifted(x, axis, size, stride, radix, by):
+def traded(x, axis, size, stride, radix, by):
     pairs = []
     for i in range(size):
         digit = i // stride % radix
-        pairs.append((i, i + ((digit + by) % radix - digit) * stride))
+        pairs.append((i, i + ((digit ^ by) - digit) * stride))
     return lax.ppermute(x, axis, pairs)
 
 
+def trades(blocks, axis, size, stride, radix):
+    came = {s: traded(blocks[s], axis, size, stride, radix, s) for s in reversed(range(1, radix))}
+    return [blocks[0]] + [came[s] for s in range(1, radix)]
+
+
 def arrivals(x, axis, size, stride, radix):
-    return [x] + [shifted(x, axis, size, stride, radix, s) for s in range(1, radix)]
+    return trades([x] * radix, axis, size, stride, radix)
 
 
 def pack_kernel(top, pos_ref, ids_ref, weights_ref, values_ref, message_ref, ids, weights, sems):
@@ -164,28 +169,31 @@
 
     part = n_mid * n_tp * run
     pick = jnp.concatenate(picks, axis=1)
-    chosen, swapped = [], []
-    for f in range(n_fast):
-        own = pick[f * part : (f + 1) * part]
-        runs = [
-            own[(t * n_mid + m) * run : (t * n_mid + m + 1) * run] for m in range(n_mid) for t in range(n_tp)
-        ]
-        chosen.append(own.T.astype(jnp.bfloat16))
-        swapped.append(jnp.concatenate(runs, axis=0).T.astype(jnp.bfloat16))
+    swapped = jnp.concatenate(
+        [
+            pick[f * part + (t * n_mid + m) * run : f * part + (t * n_mid + m + 1) * run]
+            for f in range(n_fast)
+            for m in range(n_mid)
+            for t in range(n_tp)
+        ],
+        axis=0,
+    )
+    chosen, swapped = pick.T.astype(jnp.bfloat16), swapped.T.astype(jnp.bfloat16)
     size = min(half, 4 * LANES)
     squares = 0.0
     for begin in range(0, 2 * half, size):
         table, side, at = (swapped, second, begin) if begin < half else (chosen, first, begin - half)
-        values = 0.0
-        for f in range(n_fast):
-            values = values + jnp.dot(table[f], side[f][:, at : at + size], preferred_element_type=jnp.float32)
+        values = jnp.concatenate([ref[:, at : at + size] for ref in side], axis=0)
+        values = jnp.dot(table, values, preferred_element_type=jnp.float32)
         squares = squares + jnp.sum(values * values, axis=1, keepdims=True)
         values = values.astype(jnp.bfloat16)
         for e in range(exp_loc):
             normed_ref[e, :, begin : begin + size] = values[e * rows : (e + 1) * rows]
     scale = lax.rsqrt(squares / (2 * half) + 1e-06)
+    gain_all = gain_ref[...].astype(jnp.float32)
     for begin in range(0, 2 * half, size):
-        gain = gain_ref[:, begin : begin + size].astype(jnp.float32)
+        gain = [gain_all[r : r + 1] for r in range(begin // LANES, (begin + size) // LANES)]
+        gain = jnp.concatenate(gain, axis=1)
         for e in range(exp_loc):
             values = normed_ref[e, :, begin : begin + size].astype(jnp.float32)
             values = values * scale[e * rows : (e + 1) * rows] * gain
@@ -389,7 +397,7 @@
     slots = exp_loc * rows
     lead = exp_loc - exp_loc // 2
     tail = exp_loc - lead
-    gain = norm_gain.reshape(1, width)
+    gain = norm_gain.reshape(width // LANES, LANES)
     position = jnp.stack([tp_pos, ep_pos * exp_loc])
     (message,) = local_call(
         functools.partial(pack_kernel, top),
@@ -406,7 +414,7 @@
     around = [message]
     for digit in reversed(slow):
         around = [a for piece in around for a in arrivals(piece, "ep", n_ep, *digit)]
-    gate_lead, sign = loaded([(w_gate, e) for e in range(lead)], [gain])
+    gate_lead, sign = loaded([(w_gate, e) for e in range(lead)], [])
     first, second, sign = local_call(
         functools.partial(split_kernel, half),
         [bf16((slow_n * tok_dev, width + LANES - half)), bf16((slow_n * tok_dev, half)), TOKEN],
@@ -477,8 +485,8 @@
     )
 
     def swapped(blocks, digit):
-        stride, radix = digit
-        return [blocks[0]] + [shifted(blocks[s], "ep", n_ep, stride, radix, radix - s) for s in range(1, radix)]
+        own, *others = trades(blocks, "ep", n_ep, *digit)
+        return [own] + others[::-1]
 
     slow = list(reversed(slow))
     right_way, left_way = slow + mid, mid + slow
@@ -560,7 +568,9 @@
     group, top = expert_ids.shape
     exp_loc = w_gate.shape[0]
     cap = max(2, 2 * top * group // (exp_loc * lax.axis_size("ep")))
-    plan = by_tokens if exp_loc > 1 and exp_loc * cap >= group else by_slots
+    n_ep = lax.axis_size("ep")
+    whole = exp_loc > 1 and exp_loc * cap >= group and n_ep > 4 and n_ep & (n_ep - 1) == 0
+    plan = by_tokens if whole else by_slots
     return plan(hidden_in, norm_gain, expert_ids, gate_weights, w_gate, w_up, w_down)
 
 

time: 67.7 us -> 65.8 us (0.972)
  waiting for transfers between devices: 11.2 us -> 9.58 us
  starting transfers between devices: 22.8 us -> 23.9 us
  local copies, waits for them, and re-layouts: 0.71 us -> 0.01 us
    ppermute x21, waiting for transfers between devices: 11.2 us -> 9.58 us  [traded(): return lax.ppermute(x, axis, pairs)]
    ppermute x21, starting transfers between devices: 22.8 us -> 23.9 us  [traded(): return lax.ppermute(x, axis, pairs)]
    reshape x1 -> x0, local copies, waits for them, and re-layouts: 0.71 us -> none  [by_tokens(): gain = norm_gain.reshape(1, width)]
  transfers between devices with their start and end apart: 21 -> 21, of which waited for: 9 -> 8; matrix products, arithmetic and copies ran while one was open for 1% -> 0% of each run, Pallas kernels for 33% -> 34%
where the time goes in v11:
time: 65.8 us; the launch traced here: 65.7 us
  Pallas kernels  31.9 us (48%)
  starting transfers between devices  23.9 us (36%)
  waiting for transfers between devices  9.58 us (15%)
    pallas_call x20, Pallas kernels, local_call(): pl.pallas_call(kernel, out_shape=shapes, in_specs=specs, out_specs=[VMEM]...  31.9 us
    ppermute x21, starting transfers between devices, traded(): return lax.ppermute(x, axis, pairs)  23.9 us
    ppermute x21, waiting for transfers between devices, traded(): return lax.ppermute(x, axis, pairs)  9.58 us
  transfers between devices with their start and end apart: 21, of which 8 were waited for; matrix products, arithmetic and copies ran while one was open for 0% of the time, Pallas kernels for 34%

profile of v11, /device:TPU:0, one launch (start us, length us, event | category | flops | bytes accessed | tf_op | source)
XLA Modules:
  0.0 65.7 jit_solution(9423722510001503014)
XLA Ops:
  0.0 0.1 pad_add_fusion.pos_ref
  0.1 1.4 %shard_map.73.refs_0_ = bf16[8,4224]{1,0:T(8,128)(2,1)S(1)} custom-call(s32[2]{0:T(128)S(1)} %pad_add_fusion.pos_ref, s32[8,16]{1,0:T(8,128)} %bitcast.6, f32[8,16]{1,0:T(8,128)} %bitcast.7, bf16[8,4096]{1,0:T(8,128)(2,1)} %values_ref.1), custom_call_target="tpu_custom_call" | custom-call | tf_op jit(solution)/shard_map/pallas_call | solution.py:321
  1.5 5.1 %collective-permute-start.2 = (bf16[8,4224]{1,0:T(8,128)(2,1)S(1)}, bf16[8,4224]{1,0:T(8,128)(2,1)S(1)}, u32[]{:S(2)}, u32[]{:S(2)}) collective-permute-start(bf16[8,4224]{1,0:T(8,128)(2,1)S(1)} %shard_map.73.refs_0_), channel_id=1, source_target_pairs={{0,12},{1,13},{2,14},{3,15},{4,8},{5,9},{6,10},{7,11},{8,4},{9,5},... | collective-permute-start | bytes 202760 | tf_op jit(solution)/shard_map/ppermute | solution.py:31
  6.6 0.0 collective-permute-start.1
  6.6 0.6 collective-permute-start
  7.3 3.5 %shard_map.74 = (f32[8,128]{1,0:T(8,128)S(1)}, bf16[4096,512]{1,0:T(8,128)(2,1)S(1)}, bf16[4096,512]{1,0:T(8,128)(2,1)S(1)}) custom-call(bf16[4,4096,512]{2,1,0:T(8,128)(2,1)} %refs_1_.4, bf16[4,4096,512]{2,1,0:T(8,128)(2,1)} %refs_1_.4), custom_call_target="tpu_custom_call" | custom-call | bytes 8388608 | tf_op jit(solution)/shard_map/pallas_call | solution.py:321
  10.8 0.0 collective-permute-done.2.refs_3_
  10.8 1.6 %collective-permute-done.1.refs_2_ = bf16[8,4224]{1,0:T(8,128)(2,1)S(1)} collective-permute-done((bf16[8,4224]{1,0:T(8,128)(2,1)S(1)}, bf16[8,4224]{1,0:T(8,128)(2,1)S(1)}, u32[]{:S(2)}, u32[]{:S(2)}) %collective-permute-start.1) | collective-permute-done | bytes 67616 | tf_op jit(solution)/shard_map/ppermute | solution.py:31
  12.4 0.0 collective-permute-done.refs_1_
  12.4 1.6 %collective-permute-start.3 = (bf16[32,2176]{1,0:T(8,128)(2,1)S(1)}, bf16[32,2176]{1,0:T(8,128)(2,1)S(1)}, u32[]{:S(2)}, u32[]{:S(2)}) collective-permute-start(bf16[32,2176]{1,0:T(8,128)(2,1)S(1)} %get-tuple-element.53.refs_0_), channel_id=1, source_target_pairs={{0,2},{1,3},{2,0},{3,1},{4,6},{5,7},{6,4},{7,5},{8,10},{9,11},{10,... | collective-permute-start | bytes 417800 | tf_op jit(solution)/shard_map/ppermute | solution.py:31
  14.0 1.5 %collective-permute-start.5 = (bf16[32,2048]{1,0:T(8,128)(2,1)S(1)}, bf16[32,2048]{1,0:T(8,128)(2,1)S(1)}, u32[]{:S(2)}, u32[]{:S(2)}) collective-permute-start(bf16[32,2048]{1,0:T(8,128)(2,1)S(1)} %get-tuple-element.60.refs_0_), channel_id=1, source_target_pairs={{0,16},{16,0},{1,17},{17,1},{2,18},{18,2},{3,19},{19,3},{4,20},{20... | collective-permute-start | bytes 393224 | tf_op jit(solution)/shard_map/ppermute | solution.py:31
  15.5 3.5 %shard_map.76 = (f32[8,128]{1,0:T(8,128)S(1)}, bf16[4096,512]{1,0:T(8,128)(2,1)S(1)}, bf16[4096,512]{1,0:T(8,128)(2,1)S(1)}) custom-call(bf16[4,4096,512]{2,1,0:T(8,128)(2,1)} %refs_1_.4, bf16[4,4096,512]{2,1,0:T(8,128)(2,1)} %refs_1_.4, f32[8,128]{1,0:T(8,128)S(1)} %get-tuple-element.54.refs_2_), custom_call_target="tpu_custom_call" | custom-call | bytes 8388608 | tf_op jit(solution)/shard_map/pallas_call | solution.py:321
  19.0 0.0 collective-permute-done.3.refs_1_
  19.0 0.6 collective-permute-start.4
  19.6 0.0 collective-permute-done.5.refs_1_
  19.6 1.5 %collective-permute-start.6 = (bf16[64,2048]{1,0:T(8,128)(2,1)S(1)}, bf16[64,2048]{1,0:T(8,128)(2,1)S(1)}, u32[]{:S(2)}, u32[]{:S(2)}) collective-permute-start(bf16[64,2048]{1,0:T(8,128)(2,1)S(1)} %shard_map.80.refs_0_), channel_id=1, source_target_pairs={{0,2},{1,3},{2,0},{3,1},{4,6},{5,7},{6,4},{7,5},{8,10},{9,11},{10,... | collective-permute-start | bytes 786440 | tf_op jit(solution)/shard_map/ppermute | solution.py:31
  21.1 4.7 %shard_map.78 = (f32[8,128]{1,0:T(8,128)S(1)}, bf16[4096,512]{1,0:T(8,128)(2,1)S(1)}, bf16[4096,512]{1,0:T(8,128)(2,1)S(1)}, bf16[1024,2048]{1,0:T(8,128)(2,1)S(1)}) custom-call(bf16[4,4096,512]{2,1,0:T(8,128)(2,1)} %refs_9_.1, bf16[4,4096,512]{2,1,0:T(8,128)(2,1)} %refs_9_.1, bf16[4,1024,2048]{2,1,0:T(8,128)(2,1)} %refs_4_.1, ...), custom_call_target="tpu_custom_call" | custom-call | bytes 12582912 | tf_op jit(solution)/shard_map/pallas_call | solution.py:321
  25.8 1.1 %collective-permute-done.4.refs_1_ = bf16[64,2176]{1,0:T(8,128)(2,1)S(1)} collective-permute-done((bf16[64,2176]{1,0:T(8,128)(2,1)S(1)}, bf16[64,2176]{1,0:T(8,128)(2,1)S(1)}, u32[]{:S(2)}, u32[]{:S(2)}) %collective-permute-start.4) | collective-permute-done | bytes 278560 | tf_op jit(solution)/shard_map/ppermute | solution.py:31
  27.0 0.1 collective-permute-start.7
  27.1 0.0 collective-permute-done.6.refs_1_
  27.1 0.6 collective-permute-start.8
  27.7 0.0 copy-start
  27.7 2.2 %shard_map.82 = (f32[8,128]{1,0:T(8,128)S(1)}, bf16[1024,2048]{1,0:T(8,128)(2,1)S(1)}) custom-call(bf16[4,1024,2048]{2,1,0:T(8,128)(2,1)} %refs_4_.1, f32[8,128]{1,0:T(8,128)S(1)} %get-tuple-element.65.refs_1_), custom_call_target="tpu_custom_call" | custom-call | bytes 4194304 | tf_op jit(solution)/shard_map/pallas_call | solution.py:321
  29.9 0.0 collective-permute-done.8.refs_3_
  29.9 0.0 collective-permute-done.7.refs_1_
  29.9 0.0 copy-done
  29.9 5.4 %shard_map.83 = (bf16[2,64,512]{2,1,0:T(8,128)(2,1)S(1)}, bf16[4,64,4096]{2,1,0:T(8,128)(2,1)S(1)}, bf16[2,256,256]{2,1,0:T(8,128)(2,1)S(1)}, bf16[2,256,256]{2,...) custom-call(s32[2]{0:T(128)S(1)} %pad_add_fusion.pos_ref, ...), custom_call_target="tpu_custom_call" | custom-call | flops 1610612736 | bytes 16777216 | tf_op jit(solution)/shard_map/pallas_call | solution.py:321
  35.4 0.9 %collective-permute-start.9 = (bf16[2,64,512]{2,1,0:T(8,128)(2,1)S(1)}, bf16[2,64,512]{2,1,0:T(8,128)(2,1)S(1)}, u32[]{:S(2)}, u32[]{:S(2)}) collective-permute-start(bf16[2,64,512]{2,1,0:T(8,128)(2,1)S(1)} %get-tuple-element.74.refs_0_), channel_id=1, source_target_pairs={{0,16},{16,0},{1,17},{17,1},{2,18},{18,2},{3,19},{19,3},{4,20},{20... | collective-permute-start | bytes 393224 | tf_op jit(solution)/shard_map/ppermute | solution.py:31
  36.3 4.0 %shard_map.84 = (bf16[2,64,512]{2,1,0:T(8,128)(2,1)S(1)}, bf16[1024,2048]{1,0:T(8,128)(2,1)S(1)}, bf16[1024,2048]{1,0:T(8,128)(2,1)S(1)}) custom-call(s32[2]{0:T(128)S(1)} %pad_add_fusion.pos_ref, bf16[4,64,4096]{2,1,0:T(8,128)(2,1)S(1)} %get-tuple-element.68.normed_ref, bf16[4096,512]{1,0:T(8,128)(2,1)S(1)} %get-tuple-element.69.refs_0_, ...), custom_call_target="tpu_custom_call" | custom-call | flops 1073741824 | bytes 16777216 | tf_op jit(solution)/shard_map/pallas_call | solution.py:321
  40.3 1.2 %collective-permute-start.10 = (bf16[2,64,512]{2,1,0:T(8,128)(2,1)S(1)}, bf16[2,64,512]{2,1,0:T(8,128)(2,1)S(1)}, u32[]{:S(2)}, u32[]{:S(2)}) collective-permute-start(bf16[2,64,512]{2,1,0:T(8,128)(2,1)S(1)} %get-tuple-element.73.own_ref), channel_id=1, source_target_pairs={{0,16},{16,0},{1,17},{17,1},{2,18},{18,2},{3,19},{19,3},{4,20},{20... | collective-permute-start | bytes 393224 | tf_op jit(solution)/shard_map/ppermute | solution.py:31
  41.5 0.0 collective-permute-done.9.refs_1_
  41.6 2.9 %shard_map.85 = (bf16[128,2048]{1,0:T(8,128)(2,1)S(1)}, f32[128,2048]{1,0:T(8,128)S(1)}) custom-call(s32[2]{0:T(128)S(1)} %pad_add_fusion.pos_ref, bf16[2,64,512]{2,1,0:T(8,128)(2,1)S(1)} %get-tuple-element.73.own_ref, bf16[2,64,512]{2,1,0:T(8,128)(2,1)S(1)} %get-tuple-element.74.refs_0_, bf16[2,64,512]{2,1,0:T(8,128)(2,1)S(1)} %collective-permute-done.9.refs_1_, ...), custom_call_target="tpu_custom_call" | custom-call | flops 536870912 | bytes 8388608 | tf_op jit(solution)/shard_map/pallas_call | solution.py:321
  44.4 1.6 %collective-permute-done.10.refs_0_ = bf16[2,64,512]{2,1,0:T(8,128)(2,1)S(1)} collective-permute-done((bf16[2,64,512]{2,1,0:T(8,128)(2,1)S(1)}, bf16[2,64,512]{2,1,0:T(8,128)(2,1)S(1)}, u32[]{:S(2)}, u32[]{:S(2)}) %collective-permute-start.10) | collective-permute-done | bytes 131104 | tf_op jit(solution)/shard_map/ppermute | solution.py:31
  46.0 1.4 %shard_map.86 = (bf16[128,1024]{1,0:T(8,128)(2,1)S(1)}, bf16[128,1024]{1,0:T(8,128)(2,1)S(1)}) custom-call(s32[2]{0:T(128)S(1)} %pad_add_fusion.pos_ref, bf16[2,256,256]{2,1,0:T(8,128)(2,1)S(1)} %get-tuple-element.67.mix_ref, bf16[128,2048]{1,0:T(8,128)(2,1)S(1)} %get-tuple-element.79.done_ref, f32[128,2048]{1,0:T(8,128)S(1)} %get-tuple-element.80.part_ref, ...), custom_call_target="tpu_custom_call" | custom-call | flops 536870912 | bytes 8388608 | tf_op jit(solution)/shard_map/pallas_call | solution.py:321
  47.4 0.1 collective-permute-start.11
  47.4 1.4 %shard_map.89 = (bf16[128,1024]{1,0:T(8,128)(2,1)S(1)}, bf16[128,1024]{1,0:T(8,128)(2,1)S(1)}) custom-call(s32[2]{0:T(128)S(1)} %pad_add_fusion.pos_ref, bf16[2,256,256]{2,1,0:T(8,128)(2,1)S(1)} %get-tuple-element.89.mix_ref, bf16[128,2048]{1,0:T(8,128)(2,1)S(1)} %get-tuple-element.79.done_ref, f32[128,2048]{1,0:T(8,128)S(1)} %get-tuple-element.80.part_ref, ...), custom_call_target="tpu_custom_call" | custom-call | flops 536870912 | bytes 8388608 | tf_op jit(solution)/shard_map/pallas_call | solution.py:321
  48.8 0.6 collective-permute-start.16
  49.4 0.0 collective-permute-done.11.refs_1_
  49.4 0.1 shard_map.87
  49.4 0.6 collective-permute-start.12
  50.0 0.5 collective-permute-done.16.refs_1_
  50.5 0.1 shard_map.90
  50.6 1.9 %collective-permute-start.17 = (bf16[32,1024]{1,0:T(8,128)(2,1)S(1)}, bf16[32,1024]{1,0:T(8,128)(2,1)S(1)}, u32[]{:S(2)}, u32[]{:S(2)}) collective-permute-start(bf16[32,1024]{1,0:T(8,128)(2,1)S(1)} %get-tuple-element.93), channel_id=1, source_target_pairs={{0,12},{1,13},{2,14},{3,15},{4,8},{5,9},{6,10},{7,11},{8,4},{9,5},... | collective-permute-start | bytes 196616 | tf_op jit(solution)/shard_map/ppermute | solution.py:31
  52.5 0.0 collective-permute-start.18
  52.5 2.5 %collective-permute-start.19 = (bf16[32,1024]{1,0:T(8,128)(2,1)S(1)}, bf16[32,1024]{1,0:T(8,128)(2,1)S(1)}, u32[]{:S(2)}, u32[]{:S(2)}) collective-permute-start(bf16[32,1024]{1,0:T(8,128)(2,1)S(1)} %get-tuple-element.95), channel_id=1, source_target_pairs={{0,4},{1,5},{2,6},{3,7},{4,0},{5,1},{6,2},{7,3},{8,12},{9,13},{10,... | collective-permute-start | bytes 196616 | tf_op jit(solution)/shard_map/ppermute | solution.py:31
  55.1 0.0 collective-permute-done.12.refs_1_
  55.1 1.9 %collective-permute-start.13 = (bf16[16,1024]{1,0:T(8,128)(2,1)S(1)}, bf16[16,1024]{1,0:T(8,128)(2,1)S(1)}, u32[]{:S(2)}, u32[]{:S(2)}) collective-permute-start(bf16[16,1024]{1,0:T(8,128)(2,1)S(1)} %get-tuple-element.86), channel_id=1, source_target_pairs={{0,12},{1,13},{2,14},{3,15},{4,8},{5,9},{6,10},{7,11},{8,4},{9,5},... | collective-permute-start | bytes 98312 | tf_op jit(solution)/shard_map/ppermute | solution.py:31
  57.0 0.0 collective-permute-start.14
  57.0 0.4 collective-permute-done.17.refs_1_
  57.5 2.1 %collective-permute-start.15 = (bf16[16,1024]{1,0:T(8,128)(2,1)S(1)}, bf16[16,1024]{1,0:T(8,128)(2,1)S(1)}, u32[]{:S(2)}, u32[]{:S(2)}) collective-permute-start(bf16[16,1024]{1,0:T(8,128)(2,1)S(1)} %get-tuple-element.88), channel_id=1, source_target_pairs={{0,4},{1,5},{2,6},{3,7},{4,0},{5,1},{6,2},{7,3},{8,12},{9,13},{10,... | collective-permute-start | bytes 98312 | tf_op jit(solution)/shard_map/ppermute | solution.py:31
  59.6 0.9 %collective-permute-done.18.refs_2_ = bf16[32,1024]{1,0:T(8,128)(2,1)S(1)} collective-permute-done((bf16[32,1024]{1,0:T(8,128)(2,1)S(1)}, bf16[32,1024]{1,0:T(8,128)(2,1)S(1)}, u32[]{:S(2)}, u32[]{:S(2)}) %collective-permute-start.18) | collective-permute-done | bytes 65568 | tf_op jit(solution)/shard_map/ppermute | solution.py:31
  60.4 0.0 collective-permute-done.19.refs_3_
  60.5 0.6 collective-permute-start.20
  61.1 0.0 collective-permute-done.13.refs_1_
  61.1 1.4 %collective-permute-done.14.refs_2_ = bf16[16,1024]{1,0:T(8,128)(2,1)S(1)} collective-permute-done((bf16[16,1024]{1,0:T(8,128)(2,1)S(1)}, bf16[16,1024]{1,0:T(8,128)(2,1)S(1)}, u32[]{:S(2)}, u32[]{:S(2)}) %collective-permute-start.14) | collective-permute-done | bytes 32800 | tf_op jit(solution)/shard_map/ppermute | solution.py:31
  62.4 0.0 collective-permute-done.15.refs_3_
  62.5 2.0 %collective-permute-done.20.refs_5_ = bf16[16,1024]{1,0:T(8,128)(2,1)S(1)} collective-permute-done((bf16[16,1024]{1,0:T(8,128)(2,1)S(1)}, bf16[16,1024]{1,0:T(8,128)(2,1)S(1)}, u32[]{:S(2)}, u32[]{:S(2)}) %collective-permute-start.20) | collective-permute-done | bytes 32800 | tf_op jit(solution)/shard_map/ppermute | solution.py:31
  64.4 1.2 %shard_map.92 = bf16[16,2048]{1,0:T(8,128)(2,1)} custom-call(s32[2]{0:T(128)S(1)} %pad_add_fusion.pos_ref, bf16[128,2176]{1,0:T(8,128)(2,1)S(1)} %get-tuple-element.59.refs_0_.first_ref, bf16[128,2048]{1,0:T(8,128)(2,1)S(1)} %shard_map.81.refs_2_.second_ref, bf16[16,1024]{1,0:T(8,128)(2,1)S(1)} %get-tuple-element.85.refs_0_, ...), custom_call_target="tpu_custom_call" | custom-call | bytes 524288 | tf_op jit(solution)/shard_map/pallas_call | solution.py:321
  (7 shorter events, 0.2 us)
Async XLA Ops:
  1.5 9.2 %collective-permute-start.2 = (bf16[8,4224]{1,0:T(8,128)(2,1)S(1)}, bf16[8,4224]{1,0:T(8,128)(2,1)S(1)}, u32[]{:S(2)}, u32[]{:S(2)}) collective-permute-start(bf16[8,4224]{1,0:T(8,128)(2,1)S(1)} %shard_map.73.refs_0_), channel_id=1, source_target_pairs={{0,12},{1,13},{2,14},{3,15},{4,8},{5,9},{6,10},{7,11},{8,4},{9,5},... | collective-permute-start | bytes 202760 | tf_op jit(solution)/shard_map/ppermute | solution.py:31
  6.6 5.8 %collective-permute-start.1 = (bf16[8,4224]{1,0:T(8,128)(2,1)S(1)}, bf16[8,4224]{1,0:T(8,128)(2,1)S(1)}, u32[]{:S(2)}, u32[]{:S(2)}) collective-permute-start(bf16[8,4224]{1,0:T(8,128)(2,1)S(1)} %shard_map.73.refs_0_), channel_id=1, source_target_pairs={{0,8},{1,9},{2,10},{3,11},{4,12},{5,13},{6,14},{7,15},{8,0},{9,1},... | collective-permute-start | bytes 202760 | tf_op jit(solution)/shard_map/ppermute | solution.py:31
  6.6 5.8 %collective-permute-start = (bf16[8,4224]{1,0:T(8,128)(2,1)S(1)}, bf16[8,4224]{1,0:T(8,128)(2,1)S(1)}, u32[]{:S(2)}, u32[]{:S(2)}) collective-permute-start(bf16[8,4224]{1,0:T(8,128)(2,1)S(1)} %shard_map.73.refs_0_), channel_id=1, source_target_pairs={{0,4},{1,5},{2,6},{3,7},{4,0},{5,1},{6,2},{7,3},{8,12},{9,13},{10,... | collective-permute-start | bytes 202760 | tf_op jit(solution)/shard_map/ppermute | solution.py:31
  12.4 6.6 %collective-permute-start.3 = (bf16[32,2176]{1,0:T(8,128)(2,1)S(1)}, bf16[32,2176]{1,0:T(8,128)(2,1)S(1)}, u32[]{:S(2)}, u32[]{:S(2)}) collective-permute-start(bf16[32,2176]{1,0:T(8,128)(2,1)S(1)} %get-tuple-element.53.refs_0_), channel_id=1, source_target_pairs={{0,2},{1,3},{2,0},{3,1},{4,6},{5,7},{6,4},{7,5},{8,10},{9,11},{10,... | collective-permute-start | bytes 417800 | tf_op jit(solution)/shard_map/ppermute | solution.py:31
  14.0 5.6 %collective-permute-start.5 = (bf16[32,2048]{1,0:T(8,128)(2,1)S(1)}, bf16[32,2048]{1,0:T(8,128)(2,1)S(1)}, u32[]{:S(2)}, u32[]{:S(2)}) collective-permute-start(bf16[32,2048]{1,0:T(8,128)(2,1)S(1)} %get-tuple-element.60.refs_0_), channel_id=1, source_target_pairs={{0,16},{16,0},{1,17},{17,1},{2,18},{18,2},{3,19},{19,3},{4,20},{20... | collective-permute-start | bytes 393224 | tf_op jit(solution)/shard_map/ppermute | solution.py:31
  19.0 7.9 %collective-permute-start.4 = (bf16[64,2176]{1,0:T(8,128)(2,1)S(1)}, bf16[64,2176]{1,0:T(8,128)(2,1)S(1)}, u32[]{:S(2)}, u32[]{:S(2)}) collective-permute-start(bf16[64,2176]{1,0:T(8,128)(2,1)S(1)} %get-tuple-element.56.refs_0_), channel_id=1, source_target_pairs={{0,16},{16,0},{1,17},{17,1},{2,18},{18,2},{3,19},{19,3},{4,20},{20... | collective-permute-start | bytes 835592 | tf_op jit(solution)/shard_map/ppermute | solution.py:31
  19.6 7.4 %collective-permute-start.6 = (bf16[64,2048]{1,0:T(8,128)(2,1)S(1)}, bf16[64,2048]{1,0:T(8,128)(2,1)S(1)}, u32[]{:S(2)}, u32[]{:S(2)}) collective-permute-start(bf16[64,2048]{1,0:T(8,128)(2,1)S(1)} %shard_map.80.refs_0_), channel_id=1, source_target_pairs={{0,2},{1,3},{2,0},{3,1},{4,6},{5,7},{6,4},{7,5},{8,10},{9,11},{10,... | collective-permute-start | bytes 786440 | tf_op jit(solution)/shard_map/ppermute | solution.py:31
  27.0 2.9 %collective-permute-start.7 = (bf16[128,2176]{1,0:T(8,128)(2,1)S(1)}, bf16[128,2176]{1,0:T(8,128)(2,1)S(1)}, u32[]{:S(2)}, u32[]{:S(2)}) collective-permute-start(bf16[128,2176]{1,0:T(8,128)(2,1)S(1)} %get-tuple-element.59.refs_0_.first_ref), channel_id=1, source_target_pairs={{0,1},{1,0},{2,3},{3,2},{4,5},{5,4},{6,7},{7,6},{8,9},{9,8},{10,11... | collective-permute-start | bytes 1671176 | tf_op jit(solution)/shard_map/ppermute | solution.py:31
  27.1 2.8 %collective-permute-start.8 = (bf16[128,2048]{1,0:T(8,128)(2,1)S(1)}, bf16[128,2048]{1,0:T(8,128)(2,1)S(1)}, u32[]{:S(2)}, u32[]{:S(2)}) collective-permute-start(bf16[128,2048]{1,0:T(8,128)(2,1)S(1)} %shard_map.81.refs_2_.second_ref), channel_id=1, source_target_pairs={{0,1},{1,0},{2,3},{3,2},{4,5},{5,4},{6,7},{7,6},{8,9},{9,8},{10,11... | collective-permute-start | bytes 1572872 | tf_op jit(solution)/shard_map/ppermute | solution.py:31
  27.7 2.3 %copy-start = (bf16[4096]{0:T(1024)(128)(2,1)S(1)}, bf16[4096]{0:T(1024)(128)(2,1)}, u32[]{:S(2)}) copy-start(bf16[4096]{0:T(1024)(128)(2,1)} %param.8) | copy-start | bytes 24580
  35.4 6.2 %collective-permute-start.9 = (bf16[2,64,512]{2,1,0:T(8,128)(2,1)S(1)}, bf16[2,64,512]{2,1,0:T(8,128)(2,1)S(1)}, u32[]{:S(2)}, u32[]{:S(2)}) collective-permute-start(bf16[2,64,512]{2,1,0:T(8,128)(2,1)S(1)} %get-tuple-element.74.refs_0_), channel_id=1, source_target_pairs={{0,16},{16,0},{1,17},{17,1},{2,18},{18,2},{3,19},{19,3},{4,20},{20... | collective-permute-start | bytes 393224 | tf_op jit(solution)/shard_map/ppermute | solution.py:31
  40.3 5.7 %collective-permute-start.10 = (bf16[2,64,512]{2,1,0:T(8,128)(2,1)S(1)}, bf16[2,64,512]{2,1,0:T(8,128)(2,1)S(1)}, u32[]{:S(2)}, u32[]{:S(2)}) collective-permute-start(bf16[2,64,512]{2,1,0:T(8,128)(2,1)S(1)} %get-tuple-element.73.own_ref), channel_id=1, source_target_pairs={{0,16},{16,0},{1,17},{17,1},{2,18},{18,2},{3,19},{19,3},{4,20},{20... | collective-permute-start | bytes 393224 | tf_op jit(solution)/shard_map/ppermute | solution.py:31
  47.4 2.0 %collective-permute-start.11 = (bf16[128,1024]{1,0:T(8,128)(2,1)S(1)}, bf16[128,1024]{1,0:T(8,128)(2,1)S(1)}, u32[]{:S(2)}, u32[]{:S(2)}) collective-permute-start(bf16[128,1024]{1,0:T(8,128)(2,1)S(1)} %get-tuple-element.82), channel_id=1, source_target_pairs={{0,1},{1,0},{2,3},{3,2},{4,5},{5,4},{6,7},{7,6},{8,9},{9,8},{10,11... | collective-permute-start | bytes 786440 | tf_op jit(solution)/shard_map/ppermute | solution.py:31
  48.8 1.7 %collective-permute-start.16 = (bf16[128,1024]{1,0:T(8,128)(2,1)S(1)}, bf16[128,1024]{1,0:T(8,128)(2,1)S(1)}, u32[]{:S(2)}, u32[]{:S(2)}) collective-permute-start(bf16[128,1024]{1,0:T(8,128)(2,1)S(1)} %get-tuple-element.91), channel_id=1, source_target_pairs={{0,1},{1,0},{2,3},{3,2},{4,5},{5,4},{6,7},{7,6},{8,9},{9,8},{10,11... | collective-permute-start | bytes 786440 | tf_op jit(solution)/shard_map/ppermute | solution.py:31
  49.4 5.6 %collective-permute-start.12 = (bf16[64,1024]{1,0:T(8,128)(2,1)S(1)}, bf16[64,1024]{1,0:T(8,128)(2,1)S(1)}, u32[]{:S(2)}, u32[]{:S(2)}) collective-permute-start(bf16[64,1024]{1,0:T(8,128)(2,1)S(1)} %get-tuple-element.84), channel_id=1, source_target_pairs={{0,2},{1,3},{2,0},{3,1},{4,6},{5,7},{6,4},{7,5},{8,10},{9,11},{10,... | collective-permute-start | bytes 393224 | tf_op jit(solution)/shard_map/ppermute | solution.py:31
  50.6 6.9 %collective-permute-start.17 = (bf16[32,1024]{1,0:T(8,128)(2,1)S(1)}, bf16[32,1024]{1,0:T(8,128)(2,1)S(1)}, u32[]{:S(2)}, u32[]{:S(2)}) collective-permute-start(bf16[32,1024]{1,0:T(8,128)(2,1)S(1)} %get-tuple-element.93), channel_id=1, source_target_pairs={{0,12},{1,13},{2,14},{3,15},{4,8},{5,9},{6,10},{7,11},{8,4},{9,5},... | collective-permute-start | bytes 196616 | tf_op jit(solution)/shard_map/ppermute | solution.py:31
  52.5 7.9 %collective-permute-start.18 = (bf16[32,1024]{1,0:T(8,128)(2,1)S(1)}, bf16[32,1024]{1,0:T(8,128)(2,1)S(1)}, u32[]{:S(2)}, u32[]{:S(2)}) collective-permute-start(bf16[32,1024]{1,0:T(8,128)(2,1)S(1)} %get-tuple-element.94), channel_id=1, source_target_pairs={{0,8},{1,9},{2,10},{3,11},{4,12},{5,13},{6,14},{7,15},{8,0},{9,1},... | collective-permute-start | bytes 196616 | tf_op jit(solution)/shard_map/ppermute | solution.py:31
  52.5 7.9 %collective-permute-start.19 = (bf16[32,1024]{1,0:T(8,128)(2,1)S(1)}, bf16[32,1024]{1,0:T(8,128)(2,1)S(1)}, u32[]{:S(2)}, u32[]{:S(2)}) collective-permute-start(bf16[32,1024]{1,0:T(8,128)(2,1)S(1)} %get-tuple-element.95), channel_id=1, source_target_pairs={{0,4},{1,5},{2,6},{3,7},{4,0},{5,1},{6,2},{7,3},{8,12},{9,13},{10,... | collective-permute-start | bytes 196616 | tf_op jit(solution)/shard_map/ppermute | solution.py:31
  55.1 6.0 %collective-permute-start.13 = (bf16[16,1024]{1,0:T(8,128)(2,1)S(1)}, bf16[16,1024]{1,0:T(8,128)(2,1)S(1)}, u32[]{:S(2)}, u32[]{:S(2)}) collective-permute-start(bf16[16,1024]{1,0:T(8,128)(2,1)S(1)} %get-tuple-element.86), channel_id=1, source_target_pairs={{0,12},{1,13},{2,14},{3,15},{4,8},{5,9},{6,10},{7,11},{8,4},{9,5},... | collective-permute-start | bytes 98312 | tf_op jit(solution)/shard_map/ppermute | solution.py:31
  57.0 5.4 %collective-permute-start.14 = (bf16[16,1024]{1,0:T(8,128)(2,1)S(1)}, bf16[16,1024]{1,0:T(8,128)(2,1)S(1)}, u32[]{:S(2)}, u32[]{:S(2)}) collective-permute-start(bf16[16,1024]{1,0:T(8,128)(2,1)S(1)} %get-tuple-element.87), channel_id=1, source_target_pairs={{0,8},{1,9},{2,10},{3,11},{4,12},{5,13},{6,14},{7,15},{8,0},{9,1},... | collective-permute-start | bytes 98312 | tf_op jit(solution)/shard_map/ppermute | solution.py:31
  57.5 5.0 %collective-permute-start.15 = (bf16[16,1024]{1,0:T(8,128)(2,1)S(1)}, bf16[16,1024]{1,0:T(8,128)(2,1)S(1)}, u32[]{:S(2)}, u32[]{:S(2)}) collective-permute-start(bf16[16,1024]{1,0:T(8,128)(2,1)S(1)} %get-tuple-element.88), channel_id=1, source_target_pairs={{0,4},{1,5},{2,6},{3,7},{4,0},{5,1},{6,2},{7,3},{8,12},{9,13},{10,... | collective-permute-start | bytes 98312 | tf_op jit(solution)/shard_map/ppermute | solution.py:31
  60.5 4.0 %collective-permute-start.20 = (bf16[16,1024]{1,0:T(8,128)(2,1)S(1)}, bf16[16,1024]{1,0:T(8,128)(2,1)S(1)}, u32[]{:S(2)}, u32[]{:S(2)}) collective-permute-start(bf16[16,1024]{1,0:T(8,128)(2,1)S(1)} %get-tuple-element.98), channel_id=1, source_target_pairs={{0,2},{1,3},{2,0},{3,1},{4,6},{5,7},{6,4},{7,5},{8,10},{9,11},{10,... | collective-permute-start | bytes 98312 | tf_op jit(solution)/shard_map/ppermute | solution.py:31

commit v12 on v11

--- a/solution.py
+++ b/solution.py
@@ -205,8 +205,9 @@
     n_fast = dims[0]
     first, second, refs = refs[:n_fast], refs[n_fast : 2 * n_fast], refs[2 * n_fast :]
     gates, ups, refs = refs[:lead], refs[lead : 2 * lead], refs[2 * lead :]
-    _, far_ref, hidden_ref, normed_ref, mix_ref, turned_ref, *near, sems = refs
-    copies = load_copies([far_ref] * tail, near, sems, range(lead, lead + tail))
+    gate_far, up_far, hidden_ref, normed_ref, mix_ref, turned_ref, *near, sems = refs
+    wanted = [(gate_far, lead + tail - 1)] + [(up_far, e) for e in range(lead, lead + tail)]
+    copies = load_copies([ref for ref, _ in wanted], near, sems, [e for _, e in wanted])
 
     @pl.when(pos_ref[0] >= 0)
     def _():
@@ -280,26 +281,32 @@
         ref[...] = jnp.zeros_like(ref)
 
 
-def final_kernel(dims, count, pos_ref, first_ref, second_ref, *refs):
+def own_kernel(dims, pos_ref, first_ref, second_ref, _, out_ref, own_ref):
     n_mid, n_tp, slow_n, tok_dev, half = dims
-    left, right, (out_ref, own_ref) = refs[:count], refs[count:-2], refs[-2:]
-    tp_pos = pos_ref[0]
     col_part = out_ref.shape[1]
     for s in range(n_tp):
         at = s * n_mid * slow_n * tok_dev
         own_ref[s * tok_dev : (s + 1) * tok_dev, half:] = first_ref[at : at + tok_dev, :half].astype(jnp.float32)
         at = s * slow_n * tok_dev
         own_ref[s * tok_dev : (s + 1) * tok_dev, :half] = second_ref[at : at + tok_dev].astype(jnp.float32)
-    total = jnp.concatenate([total_of(left), total_of(right)], axis=1)
-    total = total + own_ref[:, pl.ds(pl.multiple_of(tp_pos * col_part, col_part), col_part)]
-    rows = []
-    for j in range(n_tp):
-        row = total[:tok_dev]
-        for s in range(1, n_tp):
-            here = lax.rem(tp_pos - s + n_tp, n_tp) == j
-            row = jnp.where(here, total[s * tok_dev : (s + 1) * tok_dev], row)
-        rows.append(row)
-    out_ref[...] = jnp.concatenate(rows, axis=0).astype(jnp.bfloat16)
+    out_ref[...] = own_ref[:, pl.ds(pl.multiple_of(pos_ref[0] * col_part, col_part), col_part)]
+
+
+def final_kernel(n_tp, count, pos_ref, own_ref, *refs):
+    left, right, out_ref = refs[:count], refs[count:-1], refs[-1]
+    begin, tok_dev = 0, own_ref.shape[0] // n_tp
+    for side in (left, right):
+        columns = pl.ds(begin, side[0].shape[1])
+        total = total_of(side) + own_ref[:, columns]
+        rows = []
+        for j in range(n_tp):
+            row = total[:tok_dev]
+            for s in range(1, n_tp):
+                here = lax.rem(pos_ref[0] - s + n_tp, n_tp) == j
+                row = jnp.where(here, total[s * tok_dev : (s + 1) * tok_dev], row)
+            rows.append(row)
+        out_ref[:, columns] = jnp.concatenate(rows, axis=0).astype(jnp.bfloat16)
+        begin += side[0].shape[1]
 
 
 VMEM = pl.BlockSpec(memory_space=pltpu.VMEM)
@@ -414,33 +421,32 @@
     around = [message]
     for digit in reversed(slow):
         around = [a for piece in around for a in arrivals(piece, "ep", n_ep, *digit)]
-    gate_lead, sign = loaded([(w_gate, e) for e in range(lead)], [])
+    loads, sign = loaded([(w_gate, e) for e in range(lead)] + [(w_up, 0)], [])
+    gate_lead, up_lead = loads[:lead], loads[lead:]
     first, second, sign = local_call(
         functools.partial(split_kernel, half),
         [bf16((slow_n * tok_dev, width + LANES - half)), bf16((slow_n * tok_dev, half)), TOKEN],
         around + [sign],
         limit=4 << 20,
     )
-    gate_tail, sign = loaded([(w_gate, e) for e in range(lead, exp_loc)], [sign])
+    gate_tail, sign = loaded([(w_gate, e) for e in range(lead, exp_loc - 1)], [sign]) if tail > 1 else ([], sign)
     along_tp = lambda a: arrivals(a, "tp", n_tp, 1, n_tp)
     along_mid = lambda a: arrivals(a, "ep", n_ep, *mid[0]) if mid else [a]
     first, second = along_mid(first), along_tp(second)
     first, sign = joined(first, [sign], 1)
     (second,) = joined(second, [], 0)
-    up_lead, sign = loaded([(w_up, e) for e in range(lead)] + [(w_down, 0)], [sign])
-    *up_lead, down_first = up_lead
+    loads, sign = loaded([(w_up, e) for e in range(1, lead)] + [(w_down, e) for e in range(lead)], [sign])
+    up_lead, down_lead = up_lead + loads[: lead - 1], loads[lead - 1 :]
     first, second = along_tp(first), along_mid(second)
-    first, sign = joined(first, [sign], 1)
-    down_lead, sign = loaded([(w_down, e) for e in range(1, lead)], [sign]) if lead > 1 else ([], sign)
-    down_lead = [down_first] + down_lead
+    (first,) = joined(first, [sign], 0)
     (second,) = joined(second, [], 0)
     first = arrivals(first, "ep", n_ep, *fast)
     second = arrivals(second, "ep", n_ep, *fast)
 
     dims = (n_fast, n_mid, n_tp, slow_n, tok_dev, top, exp_loc, rows, half)
     sems = lambda array, count: pltpu.SemaphoreType.DMA((count, runs_of(array)))
-    operands = [position, gain] + first + second + gate_lead + up_lead + [sign, w_up]
-    hidden, normed, mix, turned, *up_tail = local_call(
+    operands = [position, gain] + first + second + gate_lead + up_lead + [w_gate, w_up]
+    hidden, normed, mix, turned, gate_last, *up_tail = local_call(
         functools.partial(select_kernel, dims, lead, tail),
         [
             bf16((lead, rows, hid_part)),
@@ -448,15 +454,16 @@
             bf16((2, tokens, slots)),
             bf16((2, tokens, slots)),
         ]
+        + kept(w_gate, 1)
         + kept(w_up, tail),
         operands,
-        far=[len(operands) - 1],
-        scratch=[sems(w_up, tail)],
+        far=[len(operands) - 2, len(operands) - 1],
+        scratch=[sems(w_up, 1 + tail)],
         flops=2 * slots * tokens * width + 4 * lead * rows * width * hid_part,
         moved=4 * lead * width * hid_part,
     )
     pieces = along_tp(hidden)
-    operands = [position, normed] + gate_tail + up_tail + [w_down]
+    operands = [position, normed] + gate_tail + [gate_last] + up_tail + [w_down]
     hidden, *down_tail = local_call(
         functools.partial(up_kernel, lead, tail, range(lead, exp_loc)),
         [bf16((tail, rows, hid_part))] + kept(w_down, tail),
@@ -494,20 +501,27 @@
     left = summed(swapped(mixed_of(mix, 0), fast), left_way[0][1], [], 0)
     signs = []
     for digit, later in zip(left_way[:-1], left_way[1:]):
-        *left, sign = summed(swapped(left, digit), later[1], [], 1)
-        signs.append(sign)
+        *left, late_sign = summed(swapped(left, digit), later[1], [], 1)
+        signs.append(late_sign)
     for digit, later in zip(right_way[:-1], right_way[1:]):
         right = summed(swapped(right, digit), later[1], signs, 0)
         signs = []
     left = swapped(left, left_way[-1])
     right = swapped(right, right_way[-1])
-    (mixed,) = local_call(
-        functools.partial(final_kernel, (n_mid, n_tp, slow_n, tok_dev, half), len(left)),
-        [bf16((group, col_part))],
-        [position, first[0], second[0]] + left + right,
+    (own,) = local_call(
+        functools.partial(own_kernel, (n_mid, n_tp, slow_n, tok_dev, half)),
+        [jax.ShapeDtypeStruct((group, col_part), jnp.float32)],
+        [position, first[0], second[0], late_sign],
         scratch=[pltpu.VMEM((group, width), jnp.float32)],
         limit=4 << 20,
-        moved=2 * group * (width + 6 * col_part),
+        moved=4 * group * width,
+    )
+    (mixed,) = local_call(
+        functools.partial(final_kernel, n_tp, len(left)),
+        [bf16((group, col_part))],
+        [position, own] + left + right,
+        limit=4 << 20,
+        moved=2 * group * 8 * col_part,
     )
     return mixed
 

time: 65.8 us -> 64.8 us (0.985)
  starting transfers between devices: 23.9 us -> 27 us
  waiting for transfers between devices: 9.58 us -> 7.11 us
  Pallas kernels: 31.9 us -> 30.3 us
    ppermute x21, starting transfers between devices: 23.9 us -> 27 us  [traded(): return lax.ppermute(x, axis, pairs)]
    ppermute x21, waiting for transfers between devices: 9.58 us -> 7.11 us  [traded(): return lax.ppermute(x, axis, pairs)]
    pallas_call x20, Pallas kernels: 31.9 us -> 30.3 us  [local_call(): pl.pallas_call(kernel, out_shape=shapes, in_specs=specs, out_specs=[VMEM]...]
  transfers between devices with their start and end apart: 21 -> 21, of which waited for: 8 -> 7; matrix products, arithmetic and copies ran while one was open for 0% -> 0% of each run, Pallas kernels for 34% -> 32%
where the time goes in v12:
time: 64.8 us; the launch traced here: 64.7 us
  Pallas kernels  30.3 us (47%)
  starting transfers between devices  27 us (42%)
  waiting for transfers between devices  7.11 us (11%)
    pallas_call x20, Pallas kernels, local_call(): pl.pallas_call(kernel, out_shape=shapes, in_specs=specs, out_specs=[VMEM]...  30.3 us
    ppermute x21, starting transfers between devices, traded(): return lax.ppermute(x, axis, pairs)  27 us
    ppermute x21, waiting for transfers between devices, traded(): return lax.ppermute(x, axis, pairs)  7.11 us
  transfers between devices with their start and end apart: 21, of which 7 were waited for; matrix products, arithmetic and copies ran while one was open for 0% of the time, Pallas kernels for 32%

profile of v12, /device:TPU:0, one launch (start us, length us, event | category | flops | bytes accessed | tf_op | source)
XLA Modules:
  0.0 64.7 jit_solution(18341603531203884598)
XLA Ops:
  0.0 0.1 pad_add_fusion.pos_ref
  0.1 1.4 %shard_map.73.refs_0_ = bf16[8,4224]{1,0:T(8,128)(2,1)S(1)} custom-call(s32[2]{0:T(128)S(1)} %pad_add_fusion.pos_ref, s32[8,16]{1,0:T(8,128)} %bitcast.6, f32[8,16]{1,0:T(8,128)} %bitcast.7, bf16[8,4096]{1,0:T(8,128)(2,1)} %values_ref.1), custom_call_target="tpu_custom_call" | custom-call | tf_op jit(solution)/shard_map/pallas_call | solution.py:328
  1.5 5.1 %collective-permute-start.2 = (bf16[8,4224]{1,0:T(8,128)(2,1)S(1)}, bf16[8,4224]{1,0:T(8,128)(2,1)S(1)}, u32[]{:S(2)}, u32[]{:S(2)}) collective-permute-start(bf16[8,4224]{1,0:T(8,128)(2,1)S(1)} %shard_map.73.refs_0_), channel_id=1, source_target_pairs={{0,12},{1,13},{2,14},{3,15},{4,8},{5,9},{6,10},{7,11},{8,4},{9,5},... | collective-permute-start | bytes 202760 | tf_op jit(solution)/shard_map/ppermute | solution.py:31
  6.6 0.0 collective-permute-start.1
  6.6 0.6 collective-permute-start
  7.3 4.7 %shard_map.74 = (f32[8,128]{1,0:T(8,128)S(1)}, bf16[4096,512]{1,0:T(8,128)(2,1)S(1)}, bf16[4096,512]{1,0:T(8,128)(2,1)S(1)}, bf16[4096,512]{1,0:T(8,128)(2,1)S(1)}) custom-call(bf16[4,4096,512]{2,1,0:T(8,128)(2,1)} %refs_8_.1, bf16[4,4096,512]{2,1,0:T(8,128)(2,1)} %refs_8_.1, bf16[4,4096,512]{2,1,0:T(8,128)(2,1)} %refs_9_.1), custom_call_target="tpu_custom_call" | custom-call | bytes 12582912 | tf_op jit(solution)/shard_map/pallas_call | solution.py:328
  12.0 0.0 collective-permute-done.2.refs_3_
  12.0 0.4 collective-permute-done.1.refs_2_
  12.4 0.0 collective-permute-done.refs_1_
  12.4 1.6 %collective-permute-start.3 = (bf16[32,2176]{1,0:T(8,128)(2,1)S(1)}, bf16[32,2176]{1,0:T(8,128)(2,1)S(1)}, u32[]{:S(2)}, u32[]{:S(2)}) collective-permute-start(bf16[32,2176]{1,0:T(8,128)(2,1)S(1)} %get-tuple-element.50.refs_0_), channel_id=1, source_target_pairs={{0,2},{1,3},{2,0},{3,1},{4,6},{5,7},{6,4},{7,5},{8,10},{9,11},{10,... | collective-permute-start | bytes 417800 | tf_op jit(solution)/shard_map/ppermute | solution.py:31
  14.0 1.5 %collective-permute-start.5 = (bf16[32,2048]{1,0:T(8,128)(2,1)S(1)}, bf16[32,2048]{1,0:T(8,128)(2,1)S(1)}, u32[]{:S(2)}, u32[]{:S(2)}) collective-permute-start(bf16[32,2048]{1,0:T(8,128)(2,1)S(1)} %get-tuple-element.56.refs_0_), channel_id=1, source_target_pairs={{0,16},{16,0},{1,17},{17,1},{2,18},{18,2},{3,19},{19,3},{4,20},{20... | collective-permute-start | bytes 393224 | tf_op jit(solution)/shard_map/ppermute | solution.py:31
  15.5 2.2 %shard_map.76 = (f32[8,128]{1,0:T(8,128)S(1)}, bf16[4096,512]{1,0:T(8,128)(2,1)S(1)}) custom-call(bf16[4,4096,512]{2,1,0:T(8,128)(2,1)} %refs_8_.1, f32[8,128]{1,0:T(8,128)S(1)} %get-tuple-element.51.refs_1_), custom_call_target="tpu_custom_call" | custom-call | bytes 4194304 | tf_op jit(solution)/shard_map/pallas_call | solution.py:328
  17.7 0.0 collective-permute-done.3.refs_1_
  17.8 1.7 %collective-permute-start.4 = (bf16[64,2176]{1,0:T(8,128)(2,1)S(1)}, bf16[64,2176]{1,0:T(8,128)(2,1)S(1)}, u32[]{:S(2)}, u32[]{:S(2)}) collective-permute-start(bf16[64,2176]{1,0:T(8,128)(2,1)S(1)} %get-tuple-element.53.refs_0_), channel_id=1, source_target_pairs={{0,16},{16,0},{1,17},{17,1},{2,18},{18,2},{3,19},{19,3},{4,20},{20... | collective-permute-start | bytes 835592 | tf_op jit(solution)/shard_map/ppermute | solution.py:31
  19.5 0.0 collective-permute-done.5.refs_1_
  19.5 1.6 %collective-permute-start.6 = (bf16[64,2048]{1,0:T(8,128)(2,1)S(1)}, bf16[64,2048]{1,0:T(8,128)(2,1)S(1)}, u32[]{:S(2)}, u32[]{:S(2)}) collective-permute-start(bf16[64,2048]{1,0:T(8,128)(2,1)S(1)} %shard_map.80.refs_0_), channel_id=1, source_target_pairs={{0,2},{1,3},{2,0},{3,1},{4,6},{5,7},{6,4},{7,5},{8,10},{9,11},{10,... | collective-permute-start | bytes 786440 | tf_op jit(solution)/shard_map/ppermute | solution.py:31
  21.1 0.0 copy-start
  21.1 4.7 %shard_map.78 = (f32[8,128]{1,0:T(8,128)S(1)}, bf16[4096,512]{1,0:T(8,128)(2,1)S(1)}, bf16[1024,2048]{1,0:T(8,128)(2,1)S(1)}, bf16[1024,2048]{1,0:T(8,128)(2,1)S(1)}) custom-call(bf16[4,4096,512]{2,1,0:T(8,128)(2,1)} %refs_9_.1, bf16[4,1024,2048]{2,1,0:T(8,128)(2,1)} %refs_4_.1, bf16[4,1024,2048]{2,1,0:T(8,128)(2,1)} %refs_4_.1, ...), custom_call_target="tpu_custom_call" | custom-call | bytes 12582912 | tf_op jit(solution)/shard_map/pallas_call | solution.py:328
  25.8 0.0 collective-permute-done.4.refs_1_
  25.9 0.1 collective-permute-start.7
  26.0 0.5 collective-permute-done.6.refs_1_
  26.5 0.1 collective-permute-start.8
  26.6 2.0 %collective-permute-done.8.refs_3_ = bf16[128,2048]{1,0:T(8,128)(2,1)S(1)} collective-permute-done((bf16[128,2048]{1,0:T(8,128)(2,1)S(1)}, bf16[128,2048]{1,0:T(8,128)(2,1)S(1)}, u32[]{:S(2)}, u32[]{:S(2)}) %collective-permute-start.8) | collective-permute-done | bytes 524320 | tf_op jit(solution)/shard_map/ppermute | solution.py:31
  28.7 0.0 collective-permute-done.7.refs_1_
  28.7 0.0 copy-done
  28.7 5.6 %shard_map.82 = (bf16[2,64,512]{2,1,0:T(8,128)(2,1)S(1)}, bf16[4,64,4096]{2,1,0:T(8,128)(2,1)S(1)}, bf16[2,256,256]{2,1,0:T(8,128)(2,1)S(1)}, bf16[2,256,256]{2,...) custom-call(s32[2]{0:T(128)S(1)} %pad_add_fusion.pos_ref, ...), custom_call_target="tpu_custom_call" | custom-call | flops 1610612736 | bytes 16777216 | tf_op jit(solution)/shard_map/pallas_call | solution.py:328
  34.3 1.3 %collective-permute-start.9 = (bf16[2,64,512]{2,1,0:T(8,128)(2,1)S(1)}, bf16[2,64,512]{2,1,0:T(8,128)(2,1)S(1)}, u32[]{:S(2)}, u32[]{:S(2)}) collective-permute-start(bf16[2,64,512]{2,1,0:T(8,128)(2,1)S(1)} %get-tuple-element.68.refs_0_), channel_id=1, source_target_pairs={{0,16},{16,0},{1,17},{17,1},{2,18},{18,2},{3,19},{19,3},{4,20},{20... | collective-permute-start | bytes 393224 | tf_op jit(solution)/shard_map/ppermute | solution.py:31
  35.5 4.0 %shard_map.83 = (bf16[2,64,512]{2,1,0:T(8,128)(2,1)S(1)}, bf16[1024,2048]{1,0:T(8,128)(2,1)S(1)}, bf16[1024,2048]{1,0:T(8,128)(2,1)S(1)}) custom-call(s32[2]{0:T(128)S(1)} %pad_add_fusion.pos_ref, bf16[4,64,4096]{2,1,0:T(8,128)(2,1)S(1)} %get-tuple-element.62.normed_ref, bf16[4096,512]{1,0:T(8,128)(2,1)S(1)} %get-tuple-element.63.refs_0_, ...), custom_call_target="tpu_custom_call" | custom-call | flops 1073741824 | bytes 16777216 | tf_op jit(solution)/shard_map/pallas_call | solution.py:328
  39.5 0.9 %collective-permute-start.10 = (bf16[2,64,512]{2,1,0:T(8,128)(2,1)S(1)}, bf16[2,64,512]{2,1,0:T(8,128)(2,1)S(1)}, u32[]{:S(2)}, u32[]{:S(2)}) collective-permute-start(bf16[2,64,512]{2,1,0:T(8,128)(2,1)S(1)} %get-tuple-element.67.own_ref), channel_id=1, source_target_pairs={{0,16},{16,0},{1,17},{17,1},{2,18},{18,2},{3,19},{19,3},{4,20},{20... | collective-permute-start | bytes 393224 | tf_op jit(solution)/shard_map/ppermute | solution.py:31
  40.4 0.0 collective-permute-done.9.refs_1_
  40.4 2.8 %shard_map.84 = (bf16[128,2048]{1,0:T(8,128)(2,1)S(1)}, f32[128,2048]{1,0:T(8,128)S(1)}) custom-call(s32[2]{0:T(128)S(1)} %pad_add_fusion.pos_ref, bf16[2,64,512]{2,1,0:T(8,128)(2,1)S(1)} %get-tuple-element.67.own_ref, bf16[2,64,512]{2,1,0:T(8,128)(2,1)S(1)} %get-tuple-element.68.refs_0_, bf16[2,64,512]{2,1,0:T(8,128)(2,1)S(1)} %collective-permute-done.9.refs_1_, ...), custom_call_target="tpu_custom_call" | custom-call | flops 536870912 | bytes 8388608 | tf_op jit(solution)/shard_map/pallas_call | solution.py:328
  43.3 1.6 %collective-permute-done.10.refs_0_ = bf16[2,64,512]{2,1,0:T(8,128)(2,1)S(1)} collective-permute-done((bf16[2,64,512]{2,1,0:T(8,128)(2,1)S(1)}, bf16[2,64,512]{2,1,0:T(8,128)(2,1)S(1)}, u32[]{:S(2)}, u32[]{:S(2)}) %collective-permute-start.10) | collective-permute-done | bytes 131104 | tf_op jit(solution)/shard_map/ppermute | solution.py:31
  44.9 1.4 %shard_map.85 = (bf16[128,1024]{1,0:T(8,128)(2,1)S(1)}, bf16[128,1024]{1,0:T(8,128)(2,1)S(1)}) custom-call(s32[2]{0:T(128)S(1)} %pad_add_fusion.pos_ref, bf16[2,256,256]{2,1,0:T(8,128)(2,1)S(1)} %get-tuple-element.61.mix_ref, bf16[128,2048]{1,0:T(8,128)(2,1)S(1)} %get-tuple-element.73.done_ref, f32[128,2048]{1,0:T(8,128)S(1)} %get-tuple-element.74.part_ref, ...), custom_call_target="tpu_custom_call" | custom-call | flops 536870912 | bytes 8388608 | tf_op jit(solution)/shard_map/pallas_call | solution.py:328
  46.2 0.1 collective-permute-start.11
  46.3 1.4 %shard_map.89 = (bf16[128,1024]{1,0:T(8,128)(2,1)S(1)}, bf16[128,1024]{1,0:T(8,128)(2,1)S(1)}) custom-call(s32[2]{0:T(128)S(1)} %pad_add_fusion.pos_ref, bf16[2,256,256]{2,1,0:T(8,128)(2,1)S(1)} %get-tuple-element.84.mix_ref, bf16[128,2048]{1,0:T(8,128)(2,1)S(1)} %get-tuple-element.73.done_ref, f32[128,2048]{1,0:T(8,128)S(1)} %get-tuple-element.74.part_ref, ...), custom_call_target="tpu_custom_call" | custom-call | flops 536870912 | bytes 8388608 | tf_op jit(solution)/shard_map/pallas_call | solution.py:328
  47.7 0.6 collective-permute-start.16
  48.2 0.0 collective-permute-done.11.refs_1_
  48.2 0.1 shard_map.86
  48.3 1.6 %collective-permute-start.12 = (bf16[64,1024]{1,0:T(8,128)(2,1)S(1)}, bf16[64,1024]{1,0:T(8,128)(2,1)S(1)}, u32[]{:S(2)}, u32[]{:S(2)}) collective-permute-start(bf16[64,1024]{1,0:T(8,128)(2,1)S(1)} %get-tuple-element.78), channel_id=1, source_target_pairs={{0,2},{1,3},{2,0},{3,1},{4,6},{5,7},{6,4},{7,5},{8,10},{9,11},{10,... | collective-permute-start | bytes 393224 | tf_op jit(solution)/shard_map/ppermute | solution.py:31
  49.9 0.0 collective-permute-done.16.refs_1_
  49.9 0.1 shard_map.90
  50.0 3.2 %collective-permute-start.17 = (bf16[32,1024]{1,0:T(8,128)(2,1)S(1)}, bf16[32,1024]{1,0:T(8,128)(2,1)S(1)}, u32[]{:S(2)}, u32[]{:S(2)}) collective-permute-start(bf16[32,1024]{1,0:T(8,128)(2,1)S(1)} %get-tuple-element.88), channel_id=1, source_target_pairs={{0,12},{1,13},{2,14},{3,15},{4,8},{5,9},{6,10},{7,11},{8,4},{9,5},... | collective-permute-start | bytes 196616 | tf_op jit(solution)/shard_map/ppermute | solution.py:31
  53.1 0.0 collective-permute-start.18
  53.1 1.3 %collective-permute-start.19 = (bf16[32,1024]{1,0:T(8,128)(2,1)S(1)}, bf16[32,1024]{1,0:T(8,128)(2,1)S(1)}, u32[]{:S(2)}, u32[]{:S(2)}) collective-permute-start(bf16[32,1024]{1,0:T(8,128)(2,1)S(1)} %get-tuple-element.90), channel_id=1, source_target_pairs={{0,4},{1,5},{2,6},{3,7},{4,0},{5,1},{6,2},{7,3},{8,12},{9,13},{10,... | collective-permute-start | bytes 196616 | tf_op jit(solution)/shard_map/ppermute | solution.py:31
  54.4 0.0 collective-permute-done.12.refs_1_
  54.4 3.2 %collective-permute-start.13 = (bf16[16,1024]{1,0:T(8,128)(2,1)S(1)}, bf16[16,1024]{1,0:T(8,128)(2,1)S(1)}, u32[]{:S(2)}, u32[]{:S(2)}) collective-permute-start(bf16[16,1024]{1,0:T(8,128)(2,1)S(1)} %get-tuple-element.81), channel_id=1, source_target_pairs={{0,12},{1,13},{2,14},{3,15},{4,8},{5,9},{6,10},{7,11},{8,4},{9,5},... | collective-permute-start | bytes 98312 | tf_op jit(solution)/shard_map/ppermute | solution.py:31
  57.6 0.0 collective-permute-start.14
  57.6 0.0 collective-permute-done.17.refs_1_
  57.6 1.3 %collective-permute-start.15 = (bf16[16,1024]{1,0:T(8,128)(2,1)S(1)}, bf16[16,1024]{1,0:T(8,128)(2,1)S(1)}, u32[]{:S(2)}, u32[]{:S(2)}) collective-permute-start(bf16[16,1024]{1,0:T(8,128)(2,1)S(1)} %get-tuple-element.83), channel_id=1, source_target_pairs={{0,4},{1,5},{2,6},{3,7},{4,0},{5,1},{6,2},{7,3},{8,12},{9,13},{10,... | collective-permute-start | bytes 98312 | tf_op jit(solution)/shard_map/ppermute | solution.py:31
  58.9 0.5 collective-permute-done.18.refs_2_
  59.4 0.0 collective-permute-done.19.refs_3_
  59.5 1.4 %collective-permute-start.20 = (bf16[16,1024]{1,0:T(8,128)(2,1)S(1)}, bf16[16,1024]{1,0:T(8,128)(2,1)S(1)}, u32[]{:S(2)}, u32[]{:S(2)}) collective-permute-start(bf16[16,1024]{1,0:T(8,128)(2,1)S(1)} %get-tuple-element.92), channel_id=1, source_target_pairs={{0,2},{1,3},{2,0},{3,1},{4,6},{5,7},{6,4},{7,5},{8,10},{9,11},{10,... | collective-permute-start | bytes 98312 | tf_op jit(solution)/shard_map/ppermute | solution.py:31
  60.9 0.6 shard_map.88.own_ref
  61.5 0.0 collective-permute-done.13.refs_1_
  61.5 1.0 %collective-permute-done.14.refs_2_ = bf16[16,1024]{1,0:T(8,128)(2,1)S(1)} collective-permute-done((bf16[16,1024]{1,0:T(8,128)(2,1)S(1)}, bf16[16,1024]{1,0:T(8,128)(2,1)S(1)}, u32[]{:S(2)}, u32[]{:S(2)}) %collective-permute-start.14) | collective-permute-done | bytes 32800 | tf_op jit(solution)/shard_map/ppermute | solution.py:31
  62.4 0.0 collective-permute-done.15.refs_3_
  62.4 1.0 %collective-permute-done.20.refs_5_ = bf16[16,1024]{1,0:T(8,128)(2,1)S(1)} collective-permute-done((bf16[16,1024]{1,0:T(8,128)(2,1)S(1)}, bf16[16,1024]{1,0:T(8,128)(2,1)S(1)}, u32[]{:S(2)}, u32[]{:S(2)}) %collective-permute-start.20) | collective-permute-done | bytes 32800 | tf_op jit(solution)/shard_map/ppermute | solution.py:31
  63.5 1.2 %shard_map.92 = bf16[16,2048]{1,0:T(8,128)(2,1)} custom-call(s32[2]{0:T(128)S(1)} %pad_add_fusion.pos_ref, f32[16,2048]{1,0:T(8,128)S(1)} %shard_map.88.own_ref, bf16[16,1024]{1,0:T(8,128)(2,1)S(1)} %get-tuple-element.80.refs_0_, bf16[16,1024]{1,0:T(8,128)(2,1)S(1)} %collective-permute-done.13.refs_1_, bf16[16,1024]{1,0:T(8,128)(2,1)S(1)} %collective-permute-done.14.refs_2_, ...), custom_call_target="tpu_custom_call" | custom-call | bytes 524288 | tf_op jit(solution)/shard_map/pallas_call | solution.py:328
  (7 shorter events, 0.2 us)
Async XLA Ops:
  1.5 10.5 %collective-permute-start.2 = (bf16[8,4224]{1,0:T(8,128)(2,1)S(1)}, bf16[8,4224]{1,0:T(8,128)(2,1)S(1)}, u32[]{:S(2)}, u32[]{:S(2)}) collective-permute-start(bf16[8,4224]{1,0:T(8,128)(2,1)S(1)} %shard_map.73.refs_0_), channel_id=1, source_target_pairs={{0,12},{1,13},{2,14},{3,15},{4,8},{5,9},{6,10},{7,11},{8,4},{9,5},... | collective-permute-start | bytes 202760 | tf_op jit(solution)/shard_map/ppermute | solution.py:31
  6.6 5.8 %collective-permute-start.1 = (bf16[8,4224]{1,0:T(8,128)(2,1)S(1)}, bf16[8,4224]{1,0:T(8,128)(2,1)S(1)}, u32[]{:S(2)}, u32[]{:S(2)}) collective-permute-start(bf16[8,4224]{1,0:T(8,128)(2,1)S(1)} %shard_map.73.refs_0_), channel_id=1, source_target_pairs={{0,8},{1,9},{2,10},{3,11},{4,12},{5,13},{6,14},{7,15},{8,0},{9,1},... | collective-permute-start | bytes 202760 | tf_op jit(solution)/shard_map/ppermute | solution.py:31
  6.6 5.8 %collective-permute-start = (bf16[8,4224]{1,0:T(8,128)(2,1)S(1)}, bf16[8,4224]{1,0:T(8,128)(2,1)S(1)}, u32[]{:S(2)}, u32[]{:S(2)}) collective-permute-start(bf16[8,4224]{1,0:T(8,128)(2,1)S(1)} %shard_map.73.refs_0_), channel_id=1, source_target_pairs={{0,4},{1,5},{2,6},{3,7},{4,0},{5,1},{6,2},{7,3},{8,12},{9,13},{10,... | collective-permute-start | bytes 202760 | tf_op jit(solution)/shard_map/ppermute | solution.py:31
  12.4 5.3 %collective-permute-start.3 = (bf16[32,2176]{1,0:T(8,128)(2,1)S(1)}, bf16[32,2176]{1,0:T(8,128)(2,1)S(1)}, u32[]{:S(2)}, u32[]{:S(2)}) collective-permute-start(bf16[32,2176]{1,0:T(8,128)(2,1)S(1)} %get-tuple-element.50.refs_0_), channel_id=1, source_target_pairs={{0,2},{1,3},{2,0},{3,1},{4,6},{5,7},{6,4},{7,5},{8,10},{9,11},{10,... | collective-permute-start | bytes 417800 | tf_op jit(solution)/shard_map/ppermute | solution.py:31
  14.0 5.5 %collective-permute-start.5 = (bf16[32,2048]{1,0:T(8,128)(2,1)S(1)}, bf16[32,2048]{1,0:T(8,128)(2,1)S(1)}, u32[]{:S(2)}, u32[]{:S(2)}) collective-permute-start(bf16[32,2048]{1,0:T(8,128)(2,1)S(1)} %get-tuple-element.56.refs_0_), channel_id=1, source_target_pairs={{0,16},{16,0},{1,17},{17,1},{2,18},{18,2},{3,19},{19,3},{4,20},{20... | collective-permute-start | bytes 393224 | tf_op jit(solution)/shard_map/ppermute | solution.py:31
  17.8 8.1 %collective-permute-start.4 = (bf16[64,2176]{1,0:T(8,128)(2,1)S(1)}, bf16[64,2176]{1,0:T(8,128)(2,1)S(1)}, u32[]{:S(2)}, u32[]{:S(2)}) collective-permute-start(bf16[64,2176]{1,0:T(8,128)(2,1)S(1)} %get-tuple-element.53.refs_0_), channel_id=1, source_target_pairs={{0,16},{16,0},{1,17},{17,1},{2,18},{18,2},{3,19},{19,3},{4,20},{20... | collective-permute-start | bytes 835592 | tf_op jit(solution)/shard_map/ppermute | solution.py:31
  19.5 7.0 %collective-permute-start.6 = (bf16[64,2048]{1,0:T(8,128)(2,1)S(1)}, bf16[64,2048]{1,0:T(8,128)(2,1)S(1)}, u32[]{:S(2)}, u32[]{:S(2)}) collective-permute-start(bf16[64,2048]{1,0:T(8,128)(2,1)S(1)} %shard_map.80.refs_0_), channel_id=1, source_target_pairs={{0,2},{1,3},{2,0},{3,1},{4,6},{5,7},{6,4},{7,5},{8,10},{9,11},{10,... | collective-permute-start | bytes 786440 | tf_op jit(solution)/shard_map/ppermute | solution.py:31
  21.1 7.6 %copy-start = (bf16[4096]{0:T(1024)(128)(2,1)S(1)}, bf16[4096]{0:T(1024)(128)(2,1)}, u32[]{:S(2)}) copy-start(bf16[4096]{0:T(1024)(128)(2,1)} %param.8) | copy-start | bytes 24580
  25.9 2.8 %collective-permute-start.7 = (bf16[128,2176]{1,0:T(8,128)(2,1)S(1)}, bf16[128,2176]{1,0:T(8,128)(2,1)S(1)}, u32[]{:S(2)}, u32[]{:S(2)}) collective-permute-start(bf16[128,2176]{1,0:T(8,128)(2,1)S(1)} %shard_map.79.refs_0_.first_ref), channel_id=1, source_target_pairs={{0,1},{1,0},{2,3},{3,2},{4,5},{5,4},{6,7},{7,6},{8,9},{9,8},{10,11... | collective-permute-start | bytes 1671176 | tf_op jit(solution)/shard_map/ppermute | solution.py:31
  26.5 2.1 %collective-permute-start.8 = (bf16[128,2048]{1,0:T(8,128)(2,1)S(1)}, bf16[128,2048]{1,0:T(8,128)(2,1)S(1)}, u32[]{:S(2)}, u32[]{:S(2)}) collective-permute-start(bf16[128,2048]{1,0:T(8,128)(2,1)S(1)} %shard_map.81.refs_2_.second_ref), channel_id=1, source_target_pairs={{0,1},{1,0},{2,3},{3,2},{4,5},{5,4},{6,7},{7,6},{8,9},{9,8},{10,11... | collective-permute-start | bytes 1572872 | tf_op jit(solution)/shard_map/ppermute | solution.py:31
  34.3 6.2 %collective-permute-start.9 = (bf16[2,64,512]{2,1,0:T(8,128)(2,1)S(1)}, bf16[2,64,512]{2,1,0:T(8,128)(2,1)S(1)}, u32[]{:S(2)}, u32[]{:S(2)}) collective-permute-start(bf16[2,64,512]{2,1,0:T(8,128)(2,1)S(1)} %get-tuple-element.68.refs_0_), channel_id=1, source_target_pairs={{0,16},{16,0},{1,17},{17,1},{2,18},{18,2},{3,19},{19,3},{4,20},{20... | collective-permute-start | bytes 393224 | tf_op jit(solution)/shard_map/ppermute | solution.py:31
  39.5 5.3 %collective-permute-start.10 = (bf16[2,64,512]{2,1,0:T(8,128)(2,1)S(1)}, bf16[2,64,512]{2,1,0:T(8,128)(2,1)S(1)}, u32[]{:S(2)}, u32[]{:S(2)}) collective-permute-start(bf16[2,64,512]{2,1,0:T(8,128)(2,1)S(1)} %get-tuple-element.67.own_ref), channel_id=1, source_target_pairs={{0,16},{16,0},{1,17},{17,1},{2,18},{18,2},{3,19},{19,3},{4,20},{20... | collective-permute-start | bytes 393224 | tf_op jit(solution)/shard_map/ppermute | solution.py:31
  46.2 2.0 %collective-permute-start.11 = (bf16[128,1024]{1,0:T(8,128)(2,1)S(1)}, bf16[128,1024]{1,0:T(8,128)(2,1)S(1)}, u32[]{:S(2)}, u32[]{:S(2)}) collective-permute-start(bf16[128,1024]{1,0:T(8,128)(2,1)S(1)} %get-tuple-element.76), channel_id=1, source_target_pairs={{0,1},{1,0},{2,3},{3,2},{4,5},{5,4},{6,7},{7,6},{8,9},{9,8},{10,11... | collective-permute-start | bytes 786440 | tf_op jit(solution)/shard_map/ppermute | solution.py:31
  47.7 2.2 %collective-permute-start.16 = (bf16[128,1024]{1,0:T(8,128)(2,1)S(1)}, bf16[128,1024]{1,0:T(8,128)(2,1)S(1)}, u32[]{:S(2)}, u32[]{:S(2)}) collective-permute-start(bf16[128,1024]{1,0:T(8,128)(2,1)S(1)} %get-tuple-element.86), channel_id=1, source_target_pairs={{0,1},{1,0},{2,3},{3,2},{4,5},{5,4},{6,7},{7,6},{8,9},{9,8},{10,11... | collective-permute-start | bytes 786440 | tf_op jit(solution)/shard_map/ppermute | solution.py:31
  48.3 6.1 %collective-permute-start.12 = (bf16[64,1024]{1,0:T(8,128)(2,1)S(1)}, bf16[64,1024]{1,0:T(8,128)(2,1)S(1)}, u32[]{:S(2)}, u32[]{:S(2)}) collective-permute-start(bf16[64,1024]{1,0:T(8,128)(2,1)S(1)} %get-tuple-element.78), channel_id=1, source_target_pairs={{0,2},{1,3},{2,0},{3,1},{4,6},{5,7},{6,4},{7,5},{8,10},{9,11},{10,... | collective-permute-start | bytes 393224 | tf_op jit(solution)/shard_map/ppermute | solution.py:31
  50.0 7.7 %collective-permute-start.17 = (bf16[32,1024]{1,0:T(8,128)(2,1)S(1)}, bf16[32,1024]{1,0:T(8,128)(2,1)S(1)}, u32[]{:S(2)}, u32[]{:S(2)}) collective-permute-start(bf16[32,1024]{1,0:T(8,128)(2,1)S(1)} %get-tuple-element.88), channel_id=1, source_target_pairs={{0,12},{1,13},{2,14},{3,15},{4,8},{5,9},{6,10},{7,11},{8,4},{9,5},... | collective-permute-start | bytes 196616 | tf_op jit(solution)/shard_map/ppermute | solution.py:31
  53.1 6.3 %collective-permute-start.18 = (bf16[32,1024]{1,0:T(8,128)(2,1)S(1)}, bf16[32,1024]{1,0:T(8,128)(2,1)S(1)}, u32[]{:S(2)}, u32[]{:S(2)}) collective-permute-start(bf16[32,1024]{1,0:T(8,128)(2,1)S(1)} %get-tuple-element.89), channel_id=1, source_target_pairs={{0,8},{1,9},{2,10},{3,11},{4,12},{5,13},{6,14},{7,15},{8,0},{9,1},... | collective-permute-start | bytes 196616 | tf_op jit(solution)/shard_map/ppermute | solution.py:31
  53.1 6.3 %collective-permute-start.19 = (bf16[32,1024]{1,0:T(8,128)(2,1)S(1)}, bf16[32,1024]{1,0:T(8,128)(2,1)S(1)}, u32[]{:S(2)}, u32[]{:S(2)}) collective-permute-start(bf16[32,1024]{1,0:T(8,128)(2,1)S(1)} %get-tuple-element.90), channel_id=1, source_target_pairs={{0,4},{1,5},{2,6},{3,7},{4,0},{5,1},{6,2},{7,3},{8,12},{9,13},{10,... | collective-permute-start | bytes 196616 | tf_op jit(solution)/shard_map/ppermute | solution.py:31
  54.4 7.0 %collective-permute-start.13 = (bf16[16,1024]{1,0:T(8,128)(2,1)S(1)}, bf16[16,1024]{1,0:T(8,128)(2,1)S(1)}, u32[]{:S(2)}, u32[]{:S(2)}) collective-permute-start(bf16[16,1024]{1,0:T(8,128)(2,1)S(1)} %get-tuple-element.81), channel_id=1, source_target_pairs={{0,12},{1,13},{2,14},{3,15},{4,8},{5,9},{6,10},{7,11},{8,4},{9,5},... | collective-permute-start | bytes 98312 | tf_op jit(solution)/shard_map/ppermute | solution.py:31
  57.6 4.8 %collective-permute-start.14 = (bf16[16,1024]{1,0:T(8,128)(2,1)S(1)}, bf16[16,1024]{1,0:T(8,128)(2,1)S(1)}, u32[]{:S(2)}, u32[]{:S(2)}) collective-permute-start(bf16[16,1024]{1,0:T(8,128)(2,1)S(1)} %get-tuple-element.82), channel_id=1, source_target_pairs={{0,8},{1,9},{2,10},{3,11},{4,12},{5,13},{6,14},{7,15},{8,0},{9,1},... | collective-permute-start | bytes 98312 | tf_op jit(solution)/shard_map/ppermute | solution.py:31
  57.6 4.8 %collective-permute-start.15 = (bf16[16,1024]{1,0:T(8,128)(2,1)S(1)}, bf16[16,1024]{1,0:T(8,128)(2,1)S(1)}, u32[]{:S(2)}, u32[]{:S(2)}) collective-permute-start(bf16[16,1024]{1,0:T(8,128)(2,1)S(1)} %get-tuple-element.83), channel_id=1, source_target_pairs={{0,4},{1,5},{2,6},{3,7},{4,0},{5,1},{6,2},{7,3},{8,12},{9,13},{10,... | collective-permute-start | bytes 98312 | tf_op jit(solution)/shard_map/ppermute | solution.py:31
  59.5 4.0 %collective-permute-start.20 = (bf16[16,1024]{1,0:T(8,128)(2,1)S(1)}, bf16[16,1024]{1,0:T(8,128)(2,1)S(1)}, u32[]{:S(2)}, u32[]{:S(2)}) collective-permute-start(bf16[16,1024]{1,0:T(8,128)(2,1)S(1)} %get-tuple-element.92), channel_id=1, source_target_pairs={{0,2},{1,3},{2,0},{3,1},{4,6},{5,7},{6,4},{7,5},{8,10},{9,11},{10,... | collective-permute-start | bytes 98312 | tf_op jit(solution)/shard_map/ppermute | solution.py:31

commit v13 on v12

--- a/solution.py
+++ b/solution.py
@@ -481,14 +481,15 @@
         flops=2 * lead * rows * n_tp * hid_part * col_part,
         moved=2 * lead * n_tp * hid_part * col_part,
     )
-    col_half = col_part // 2
-    mixed_of = lambda table, begin: local_call(
+    left_cols = col_part * 5 // 8 // LANES * LANES
+    right_cols = col_part - left_cols
+    mixed_of = lambda table, begin, size: local_call(
         functools.partial(mix_kernel, n_tp, tail, begin),
-        [bf16((tokens // n_fast, col_half))] * n_fast,
+        [bf16((tokens // n_fast, size))] * n_fast,
         [position, table, done, part] + late[1:] + down_tail,
-        scratch=[pltpu.VMEM((slots, col_half), jnp.bfloat16)],
-        flops=slots * n_tp * hid_part * col_part,
-        moved=exp_loc * n_tp * hid_part * col_part,
+        scratch=[pltpu.VMEM((slots, size), jnp.bfloat16)],
+        flops=2 * slots * n_tp * hid_part * size,
+        moved=2 * tail * n_tp * hid_part * size,
     )
 
     def swapped(blocks, digit):
@@ -497,8 +498,8 @@
 
     slow = list(reversed(slow))
     right_way, left_way = slow + mid, mid + slow
-    right = summed(swapped(mixed_of(turned, col_half), fast), right_way[0][1], [], 0)
-    left = summed(swapped(mixed_of(mix, 0), fast), left_way[0][1], [], 0)
+    right = summed(swapped(mixed_of(turned, left_cols, right_cols), fast), right_way[0][1], [], 0)
+    left = summed(swapped(mixed_of(mix, 0, left_cols), fast), left_way[0][1], [], 0)
     signs = []
     for digit, later in zip(left_way[:-1], left_way[1:]):
         *left, late_sign = summed(swapped(left, digit), later[1], [], 1)

time: 64.8 us -> 64.4 us (level)
  waiting for transfers between devices: 7.11 us -> 6.43 us
    ppermute x21, waiting for transfers between devices: 7.11 us -> 6.43 us  [traded(): return lax.ppermute(x, axis, pairs)]
  transfers between devices with their start and end apart: 21 -> 21, of which waited for: 7 -> 6; matrix products, arithmetic and copies ran while one was open for 0% -> 0% of each run, Pallas kernels for 32% -> 32%
where the time goes in v13:
time: 64.4 us; the launch traced here: 64.2 us
  Pallas kernels  30.4 us (47%)
  starting transfers between devices  27.2 us (42%)
  waiting for transfers between devices  6.43 us (10%)
    pallas_call x20, Pallas kernels, local_call(): pl.pallas_call(kernel, out_shape=shapes, in_specs=specs, out_specs=[VMEM]...  30.4 us
    ppermute x21, starting transfers between devices, traded(): return lax.ppermute(x, axis, pairs)  27.2 us
    ppermute x21, waiting for transfers between devices, traded(): return lax.ppermute(x, axis, pairs)  6.43 us
  transfers between devices with their start and end apart: 21, of which 6 were waited for; matrix products, arithmetic and copies ran while one was open for 0% of the time, Pallas kernels for 32%

profile of v13, /device:TPU:0, one launch (start us, length us, event | category | flops | bytes accessed | tf_op | source)
XLA Modules:
  0.0 64.2 jit_solution(8431545179806366317)
XLA Ops:
  0.0 0.1 pad_add_fusion.pos_ref
  0.1 1.4 %shard_map.73.refs_0_ = bf16[8,4224]{1,0:T(8,128)(2,1)S(1)} custom-call(s32[2]{0:T(128)S(1)} %pad_add_fusion.pos_ref, s32[8,16]{1,0:T(8,128)} %bitcast.6, f32[8,16]{1,0:T(8,128)} %bitcast.7, bf16[8,4096]{1,0:T(8,128)(2,1)} %values_ref.1), custom_call_target="tpu_custom_call" | custom-call | tf_op jit(solution)/shard_map/pallas_call | solution.py:328
  1.5 5.1 %collective-permute-start.2 = (bf16[8,4224]{1,0:T(8,128)(2,1)S(1)}, bf16[8,4224]{1,0:T(8,128)(2,1)S(1)}, u32[]{:S(2)}, u32[]{:S(2)}) collective-permute-start(bf16[8,4224]{1,0:T(8,128)(2,1)S(1)} %shard_map.73.refs_0_), channel_id=1, source_target_pairs={{0,12},{1,13},{2,14},{3,15},{4,8},{5,9},{6,10},{7,11},{8,4},{9,5},... | collective-permute-start | bytes 202760 | tf_op jit(solution)/shard_map/ppermute | solution.py:31
  6.6 0.0 collective-permute-start.1
  6.6 0.6 collective-permute-start
  7.3 4.7 %shard_map.74 = (f32[8,128]{1,0:T(8,128)S(1)}, bf16[4096,512]{1,0:T(8,128)(2,1)S(1)}, bf16[4096,512]{1,0:T(8,128)(2,1)S(1)}, bf16[4096,512]{1,0:T(8,128)(2,1)S(1)}) custom-call(bf16[4,4096,512]{2,1,0:T(8,128)(2,1)} %refs_8_.1, bf16[4,4096,512]{2,1,0:T(8,128)(2,1)} %refs_8_.1, bf16[4,4096,512]{2,1,0:T(8,128)(2,1)} %refs_9_.1), custom_call_target="tpu_custom_call" | custom-call | bytes 12582912 | tf_op jit(solution)/shard_map/pallas_call | solution.py:328
  12.0 0.0 collective-permute-done.2.refs_3_
  12.0 0.4 collective-permute-done.1.refs_2_
  12.4 0.0 collective-permute-done.refs_1_
  12.4 1.6 %collective-permute-start.3 = (bf16[32,2176]{1,0:T(8,128)(2,1)S(1)}, bf16[32,2176]{1,0:T(8,128)(2,1)S(1)}, u32[]{:S(2)}, u32[]{:S(2)}) collective-permute-start(bf16[32,2176]{1,0:T(8,128)(2,1)S(1)} %get-tuple-element.50.refs_0_), channel_id=1, source_target_pairs={{0,2},{1,3},{2,0},{3,1},{4,6},{5,7},{6,4},{7,5},{8,10},{9,11},{10,... | collective-permute-start | bytes 417800 | tf_op jit(solution)/shard_map/ppermute | solution.py:31
  14.0 1.5 %collective-permute-start.5 = (bf16[32,2048]{1,0:T(8,128)(2,1)S(1)}, bf16[32,2048]{1,0:T(8,128)(2,1)S(1)}, u32[]{:S(2)}, u32[]{:S(2)}) collective-permute-start(bf16[32,2048]{1,0:T(8,128)(2,1)S(1)} %get-tuple-element.56.refs_0_), channel_id=1, source_target_pairs={{0,16},{16,0},{1,17},{17,1},{2,18},{18,2},{3,19},{19,3},{4,20},{20... | collective-permute-start | bytes 393224 | tf_op jit(solution)/shard_map/ppermute | solution.py:31
  15.5 2.2 %shard_map.76 = (f32[8,128]{1,0:T(8,128)S(1)}, bf16[4096,512]{1,0:T(8,128)(2,1)S(1)}) custom-call(bf16[4,4096,512]{2,1,0:T(8,128)(2,1)} %refs_8_.1, f32[8,128]{1,0:T(8,128)S(1)} %get-tuple-element.51.refs_1_), custom_call_target="tpu_custom_call" | custom-call | bytes 4194304 | tf_op jit(solution)/shard_map/pallas_call | solution.py:328
  17.7 0.0 collective-permute-done.3.refs_1_
  17.8 1.7 %collective-permute-start.4 = (bf16[64,2176]{1,0:T(8,128)(2,1)S(1)}, bf16[64,2176]{1,0:T(8,128)(2,1)S(1)}, u32[]{:S(2)}, u32[]{:S(2)}) collective-permute-start(bf16[64,2176]{1,0:T(8,128)(2,1)S(1)} %get-tuple-element.53.refs_0_), channel_id=1, source_target_pairs={{0,16},{16,0},{1,17},{17,1},{2,18},{18,2},{3,19},{19,3},{4,20},{20... | collective-permute-start | bytes 835592 | tf_op jit(solution)/shard_map/ppermute | solution.py:31
  19.5 0.0 collective-permute-done.5.refs_1_
  19.5 1.6 %collective-permute-start.6 = (bf16[64,2048]{1,0:T(8,128)(2,1)S(1)}, bf16[64,2048]{1,0:T(8,128)(2,1)S(1)}, u32[]{:S(2)}, u32[]{:S(2)}) collective-permute-start(bf16[64,2048]{1,0:T(8,128)(2,1)S(1)} %shard_map.80.refs_0_), channel_id=1, source_target_pairs={{0,2},{1,3},{2,0},{3,1},{4,6},{5,7},{6,4},{7,5},{8,10},{9,11},{10,... | collective-permute-start | bytes 786440 | tf_op jit(solution)/shard_map/ppermute | solution.py:31
  21.1 0.0 copy-start
  21.1 4.7 %shard_map.78 = (f32[8,128]{1,0:T(8,128)S(1)}, bf16[4096,512]{1,0:T(8,128)(2,1)S(1)}, bf16[1024,2048]{1,0:T(8,128)(2,1)S(1)}, bf16[1024,2048]{1,0:T(8,128)(2,1)S(1)}) custom-call(bf16[4,4096,512]{2,1,0:T(8,128)(2,1)} %refs_9_.1, bf16[4,1024,2048]{2,1,0:T(8,128)(2,1)} %refs_4_.1, bf16[4,1024,2048]{2,1,0:T(8,128)(2,1)} %refs_4_.1, ...), custom_call_target="tpu_custom_call" | custom-call | bytes 12582912 | tf_op jit(solution)/shard_map/pallas_call | solution.py:328
  25.8 0.0 collective-permute-done.4.refs_1_
  25.9 0.1 collective-permute-start.7
  26.0 0.5 collective-permute-done.6.refs_1_
  26.5 0.1 collective-permute-start.8
  26.6 2.0 %collective-permute-done.8.refs_3_ = bf16[128,2048]{1,0:T(8,128)(2,1)S(1)} collective-permute-done((bf16[128,2048]{1,0:T(8,128)(2,1)S(1)}, bf16[128,2048]{1,0:T(8,128)(2,1)S(1)}, u32[]{:S(2)}, u32[]{:S(2)}) %collective-permute-start.8) | collective-permute-done | bytes 524320 | tf_op jit(solution)/shard_map/ppermute | solution.py:31
  28.7 0.0 collective-permute-done.7.refs_1_
  28.7 0.0 copy-done
  28.7 5.6 %shard_map.82 = (bf16[2,64,512]{2,1,0:T(8,128)(2,1)S(1)}, bf16[4,64,4096]{2,1,0:T(8,128)(2,1)S(1)}, bf16[2,256,256]{2,1,0:T(8,128)(2,1)S(1)}, bf16[2,256,256]{2,...) custom-call(s32[2]{0:T(128)S(1)} %pad_add_fusion.pos_ref, ...), custom_call_target="tpu_custom_call" | custom-call | flops 1610612736 | bytes 16777216 | tf_op jit(solution)/shard_map/pallas_call | solution.py:328
  34.3 1.3 %collective-permute-start.9 = (bf16[2,64,512]{2,1,0:T(8,128)(2,1)S(1)}, bf16[2,64,512]{2,1,0:T(8,128)(2,1)S(1)}, u32[]{:S(2)}, u32[]{:S(2)}) collective-permute-start(bf16[2,64,512]{2,1,0:T(8,128)(2,1)S(1)} %get-tuple-element.68.refs_0_), channel_id=1, source_target_pairs={{0,16},{16,0},{1,17},{17,1},{2,18},{18,2},{3,19},{19,3},{4,20},{20... | collective-permute-start | bytes 393224 | tf_op jit(solution)/shard_map/ppermute | solution.py:31
  35.5 4.0 %shard_map.83 = (bf16[2,64,512]{2,1,0:T(8,128)(2,1)S(1)}, bf16[1024,2048]{1,0:T(8,128)(2,1)S(1)}, bf16[1024,2048]{1,0:T(8,128)(2,1)S(1)}) custom-call(s32[2]{0:T(128)S(1)} %pad_add_fusion.pos_ref, bf16[4,64,4096]{2,1,0:T(8,128)(2,1)S(1)} %get-tuple-element.62.normed_ref, bf16[4096,512]{1,0:T(8,128)(2,1)S(1)} %get-tuple-element.63.refs_0_, ...), custom_call_target="tpu_custom_call" | custom-call | flops 1073741824 | bytes 16777216 | tf_op jit(solution)/shard_map/pallas_call | solution.py:328
  39.5 0.9 %collective-permute-start.10 = (bf16[2,64,512]{2,1,0:T(8,128)(2,1)S(1)}, bf16[2,64,512]{2,1,0:T(8,128)(2,1)S(1)}, u32[]{:S(2)}, u32[]{:S(2)}) collective-permute-start(bf16[2,64,512]{2,1,0:T(8,128)(2,1)S(1)} %get-tuple-element.67.own_ref), channel_id=1, source_target_pairs={{0,16},{16,0},{1,17},{17,1},{2,18},{18,2},{3,19},{19,3},{4,20},{20... | collective-permute-start | bytes 393224 | tf_op jit(solution)/shard_map/ppermute | solution.py:31
  40.4 0.0 collective-permute-done.9.refs_1_
  40.4 2.8 %shard_map.84 = (bf16[128,2048]{1,0:T(8,128)(2,1)S(1)}, f32[128,2048]{1,0:T(8,128)S(1)}) custom-call(s32[2]{0:T(128)S(1)} %pad_add_fusion.pos_ref, bf16[2,64,512]{2,1,0:T(8,128)(2,1)S(1)} %get-tuple-element.67.own_ref, bf16[2,64,512]{2,1,0:T(8,128)(2,1)S(1)} %get-tuple-element.68.refs_0_, bf16[2,64,512]{2,1,0:T(8,128)(2,1)S(1)} %collective-permute-done.9.refs_1_, ...), custom_call_target="tpu_custom_call" | custom-call | flops 536870912 | bytes 8388608 | tf_op jit(solution)/shard_map/pallas_call | solution.py:328
  43.3 1.6 %collective-permute-done.10.refs_0_ = bf16[2,64,512]{2,1,0:T(8,128)(2,1)S(1)} collective-permute-done((bf16[2,64,512]{2,1,0:T(8,128)(2,1)S(1)}, bf16[2,64,512]{2,1,0:T(8,128)(2,1)S(1)}, u32[]{:S(2)}, u32[]{:S(2)}) %collective-permute-start.10) | collective-permute-done | bytes 131104 | tf_op jit(solution)/shard_map/ppermute | solution.py:31
  44.9 1.5 %shard_map.85 = (bf16[128,1280]{1,0:T(8,128)(2,1)S(1)}, bf16[128,1280]{1,0:T(8,128)(2,1)S(1)}) custom-call(s32[2]{0:T(128)S(1)} %pad_add_fusion.pos_ref, bf16[2,256,256]{2,1,0:T(8,128)(2,1)S(1)} %get-tuple-element.61.mix_ref, bf16[128,2048]{1,0:T(8,128)(2,1)S(1)} %get-tuple-element.73.done_ref, f32[128,2048]{1,0:T(8,128)S(1)} %get-tuple-element.74.part_ref, ...), custom_call_target="tpu_custom_call" | custom-call | flops 671088640 | bytes 5242880 | tf_op jit(solution)/shard_map/pallas_call | solution.py:328
  46.4 0.1 collective-permute-start.11
  46.5 1.3 %shard_map.89 = (bf16[128,768]{1,0:T(8,128)(2,1)S(1)}, bf16[128,768]{1,0:T(8,128)(2,1)S(1)}) custom-call(s32[2]{0:T(128)S(1)} %pad_add_fusion.pos_ref, bf16[2,256,256]{2,1,0:T(8,128)(2,1)S(1)} %get-tuple-element.84.mix_ref, bf16[128,2048]{1,0:T(8,128)(2,1)S(1)} %get-tuple-element.73.done_ref, f32[128,2048]{1,0:T(8,128)S(1)} %get-tuple-element.74.part_ref, ...), custom_call_target="tpu_custom_call" | custom-call | flops 402653184 | bytes 3145728 | tf_op jit(solution)/shard_map/pallas_call | solution.py:328
  47.7 0.6 collective-permute-start.16
  48.3 0.0 collective-permute-done.11.refs_1_
  48.3 0.1 shard_map.86
  48.4 1.6 %collective-permute-start.12 = (bf16[64,1280]{1,0:T(8,128)(2,1)S(1)}, bf16[64,1280]{1,0:T(8,128)(2,1)S(1)}, u32[]{:S(2)}, u32[]{:S(2)}) collective-permute-start(bf16[64,1280]{1,0:T(8,128)(2,1)S(1)} %get-tuple-element.78), channel_id=1, source_target_pairs={{0,2},{1,3},{2,0},{3,1},{4,6},{5,7},{6,4},{7,5},{8,10},{9,11},{10,... | collective-permute-start | bytes 491528 | tf_op jit(solution)/shard_map/ppermute | solution.py:31
  50.0 0.0 collective-permute-done.16.refs_1_
  50.0 3.2 %collective-permute-start.17 = (bf16[32,768]{1,0:T(8,128)(2,1)S(1)}, bf16[32,768]{1,0:T(8,128)(2,1)S(1)}, u32[]{:S(2)}, u32[]{:S(2)}) collective-permute-start(bf16[32,768]{1,0:T(8,128)(2,1)S(1)} %get-tuple-element.88), channel_id=1, source_target_pairs={{0,12},{1,13},{2,14},{3,15},{4,8},{5,9},{6,10},{7,11},{8,4},{9,5},... | collective-permute-start | bytes 147464 | tf_op jit(solution)/shard_map/ppermute | solution.py:31
  53.2 0.0 collective-permute-start.18
  53.2 1.3 %collective-permute-start.19 = (bf16[32,768]{1,0:T(8,128)(2,1)S(1)}, bf16[32,768]{1,0:T(8,128)(2,1)S(1)}, u32[]{:S(2)}, u32[]{:S(2)}) collective-permute-start(bf16[32,768]{1,0:T(8,128)(2,1)S(1)} %get-tuple-element.90), channel_id=1, source_target_pairs={{0,4},{1,5},{2,6},{3,7},{4,0},{5,1},{6,2},{7,3},{8,12},{9,13},{10,... | collective-permute-start | bytes 147464 | tf_op jit(solution)/shard_map/ppermute | solution.py:31
  54.5 0.1 collective-permute-done.12.refs_1_
  54.6 3.5 %collective-permute-start.13 = (bf16[16,1280]{1,0:T(8,128)(2,1)S(1)}, bf16[16,1280]{1,0:T(8,128)(2,1)S(1)}, u32[]{:S(2)}, u32[]{:S(2)}) collective-permute-start(bf16[16,1280]{1,0:T(8,128)(2,1)S(1)} %get-tuple-element.81), channel_id=1, source_target_pairs={{0,12},{1,13},{2,14},{3,15},{4,8},{5,9},{6,10},{7,11},{8,4},{9,5},... | collective-permute-start | bytes 122888 | tf_op jit(solution)/shard_map/ppermute | solution.py:31
  58.1 0.0 collective-permute-start.14
  58.1 0.0 collective-permute-done.17.refs_1_
  58.1 1.0 %collective-permute-start.15 = (bf16[16,1280]{1,0:T(8,128)(2,1)S(1)}, bf16[16,1280]{1,0:T(8,128)(2,1)S(1)}, u32[]{:S(2)}, u32[]{:S(2)}) collective-permute-start(bf16[16,1280]{1,0:T(8,128)(2,1)S(1)} %get-tuple-element.83), channel_id=1, source_target_pairs={{0,4},{1,5},{2,6},{3,7},{4,0},{5,1},{6,2},{7,3},{8,12},{9,13},{10,... | collective-permute-start | bytes 122888 | tf_op jit(solution)/shard_map/ppermute | solution.py:31
  59.1 0.0 collective-permute-done.18.refs_2_
  59.1 0.0 collective-permute-done.19.refs_3_
  59.1 1.6 %collective-permute-start.20 = (bf16[16,768]{1,0:T(8,128)(2,1)S(1)}, bf16[16,768]{1,0:T(8,128)(2,1)S(1)}, u32[]{:S(2)}, u32[]{:S(2)}) collective-permute-start(bf16[16,768]{1,0:T(8,128)(2,1)S(1)} %get-tuple-element.92), channel_id=1, source_target_pairs={{0,2},{1,3},{2,0},{3,1},{4,6},{5,7},{6,4},{7,5},{8,10},{9,11},{10,... | collective-permute-start | bytes 73736 | tf_op jit(solution)/shard_map/ppermute | solution.py:31
  60.7 0.6 shard_map.88.own_ref
  61.3 1.7 %collective-permute-done.20.refs_5_ = bf16[16,768]{1,0:T(8,128)(2,1)S(1)} collective-permute-done((bf16[16,768]{1,0:T(8,128)(2,1)S(1)}, bf16[16,768]{1,0:T(8,128)(2,1)S(1)}, u32[]{:S(2)}, u32[]{:S(2)}) %collective-permute-start.20) | collective-permute-done | bytes 24608 | tf_op jit(solution)/shard_map/ppermute | solution.py:31
  63.0 0.0 collective-permute-done.13.refs_1_
  63.0 0.0 collective-permute-done.14.refs_2_
  63.0 0.0 collective-permute-done.15.refs_3_
  63.0 1.2 %shard_map.92 = bf16[16,2048]{1,0:T(8,128)(2,1)} custom-call(s32[2]{0:T(128)S(1)} %pad_add_fusion.pos_ref, f32[16,2048]{1,0:T(8,128)S(1)} %shard_map.88.own_ref, bf16[16,1280]{1,0:T(8,128)(2,1)S(1)} %get-tuple-element.80.refs_0_, bf16[16,1280]{1,0:T(8,128)(2,1)S(1)} %collective-permute-done.13.refs_1_, bf16[16,1280]{1,0:T(8,128)(2,1)S(1)} %collective-permute-done.14.refs_2_, ...), custom_call_target="tpu_custom_call" | custom-call | bytes 524288 | tf_op jit(solution)/shard_map/pallas_call | solution.py:328
  (8 shorter events, 0.3 us)
Async XLA Ops:
  1.5 10.5 %collective-permute-start.2 = (bf16[8,4224]{1,0:T(8,128)(2,1)S(1)}, bf16[8,4224]{1,0:T(8,128)(2,1)S(1)}, u32[]{:S(2)}, u32[]{:S(2)}) collective-permute-start(bf16[8,4224]{1,0:T(8,128)(2,1)S(1)} %shard_map.73.refs_0_), channel_id=1, source_target_pairs={{0,12},{1,13},{2,14},{3,15},{4,8},{5,9},{6,10},{7,11},{8,4},{9,5},... | collective-permute-start | bytes 202760 | tf_op jit(solution)/shard_map/ppermute | solution.py:31
  6.6 5.8 %collective-permute-start.1 = (bf16[8,4224]{1,0:T(8,128)(2,1)S(1)}, bf16[8,4224]{1,0:T(8,128)(2,1)S(1)}, u32[]{:S(2)}, u32[]{:S(2)}) collective-permute-start(bf16[8,4224]{1,0:T(8,128)(2,1)S(1)} %shard_map.73.refs_0_), channel_id=1, source_target_pairs={{0,8},{1,9},{2,10},{3,11},{4,12},{5,13},{6,14},{7,15},{8,0},{9,1},... | collective-permute-start | bytes 202760 | tf_op jit(solution)/shard_map/ppermute | solution.py:31
  6.6 5.8 %collective-permute-start = (bf16[8,4224]{1,0:T(8,128)(2,1)S(1)}, bf16[8,4224]{1,0:T(8,128)(2,1)S(1)}, u32[]{:S(2)}, u32[]{:S(2)}) collective-permute-start(bf16[8,4224]{1,0:T(8,128)(2,1)S(1)} %shard_map.73.refs_0_), channel_id=1, source_target_pairs={{0,4},{1,5},{2,6},{3,7},{4,0},{5,1},{6,2},{7,3},{8,12},{9,13},{10,... | collective-permute-start | bytes 202760 | tf_op jit(solution)/shard_map/ppermute | solution.py:31
  12.4 5.3 %collective-permute-start.3 = (bf16[32,2176]{1,0:T(8,128)(2,1)S(1)}, bf16[32,2176]{1,0:T(8,128)(2,1)S(1)}, u32[]{:S(2)}, u32[]{:S(2)}) collective-permute-start(bf16[32,2176]{1,0:T(8,128)(2,1)S(1)} %get-tuple-element.50.refs_0_), channel_id=1, source_target_pairs={{0,2},{1,3},{2,0},{3,1},{4,6},{5,7},{6,4},{7,5},{8,10},{9,11},{10,... | collective-permute-start | bytes 417800 | tf_op jit(solution)/shard_map/ppermute | solution.py:31
  14.0 5.5 %collective-permute-start.5 = (bf16[32,2048]{1,0:T(8,128)(2,1)S(1)}, bf16[32,2048]{1,0:T(8,128)(2,1)S(1)}, u32[]{:S(2)}, u32[]{:S(2)}) collective-permute-start(bf16[32,2048]{1,0:T(8,128)(2,1)S(1)} %get-tuple-element.56.refs_0_), channel_id=1, source_target_pairs={{0,16},{16,0},{1,17},{17,1},{2,18},{18,2},{3,19},{19,3},{4,20},{20... | collective-permute-start | bytes 393224 | tf_op jit(solution)/shard_map/ppermute | solution.py:31
  17.8 8.1 %collective-permute-start.4 = (bf16[64,2176]{1,0:T(8,128)(2,1)S(1)}, bf16[64,2176]{1,0:T(8,128)(2,1)S(1)}, u32[]{:S(2)}, u32[]{:S(2)}) collective-permute-start(bf16[64,2176]{1,0:T(8,128)(2,1)S(1)} %get-tuple-element.53.refs_0_), channel_id=1, source_target_pairs={{0,16},{16,0},{1,17},{17,1},{2,18},{18,2},{3,19},{19,3},{4,20},{20... | collective-permute-start | bytes 835592 | tf_op jit(solution)/shard_map/ppermute | solution.py:31
  19.5 7.0 %collective-permute-start.6 = (bf16[64,2048]{1,0:T(8,128)(2,1)S(1)}, bf16[64,2048]{1,0:T(8,128)(2,1)S(1)}, u32[]{:S(2)}, u32[]{:S(2)}) collective-permute-start(bf16[64,2048]{1,0:T(8,128)(2,1)S(1)} %shard_map.80.refs_0_), channel_id=1, source_target_pairs={{0,2},{1,3},{2,0},{3,1},{4,6},{5,7},{6,4},{7,5},{8,10},{9,11},{10,... | collective-permute-start | bytes 786440 | tf_op jit(solution)/shard_map/ppermute | solution.py:31
  21.1 7.6 %copy-start = (bf16[4096]{0:T(1024)(128)(2,1)S(1)}, bf16[4096]{0:T(1024)(128)(2,1)}, u32[]{:S(2)}) copy-start(bf16[4096]{0:T(1024)(128)(2,1)} %param.8) | copy-start | bytes 24580
  25.9 2.8 %collective-permute-start.7 = (bf16[128,2176]{1,0:T(8,128)(2,1)S(1)}, bf16[128,2176]{1,0:T(8,128)(2,1)S(1)}, u32[]{:S(2)}, u32[]{:S(2)}) collective-permute-start(bf16[128,2176]{1,0:T(8,128)(2,1)S(1)} %shard_map.79.refs_0_.first_ref), channel_id=1, source_target_pairs={{0,1},{1,0},{2,3},{3,2},{4,5},{5,4},{6,7},{7,6},{8,9},{9,8},{10,11... | collective-permute-start | bytes 1671176 | tf_op jit(solution)/shard_map/ppermute | solution.py:31
  26.5 2.1 %collective-permute-start.8 = (bf16[128,2048]{1,0:T(8,128)(2,1)S(1)}, bf16[128,2048]{1,0:T(8,128)(2,1)S(1)}, u32[]{:S(2)}, u32[]{:S(2)}) collective-permute-start(bf16[128,2048]{1,0:T(8,128)(2,1)S(1)} %shard_map.81.refs_2_.second_ref), channel_id=1, source_target_pairs={{0,1},{1,0},{2,3},{3,2},{4,5},{5,4},{6,7},{7,6},{8,9},{9,8},{10,11... | collective-permute-start | bytes 1572872 | tf_op jit(solution)/shard_map/ppermute | solution.py:31
  34.3 6.2 %collective-permute-start.9 = (bf16[2,64,512]{2,1,0:T(8,128)(2,1)S(1)}, bf16[2,64,512]{2,1,0:T(8,128)(2,1)S(1)}, u32[]{:S(2)}, u32[]{:S(2)}) collective-permute-start(bf16[2,64,512]{2,1,0:T(8,128)(2,1)S(1)} %get-tuple-element.68.refs_0_), channel_id=1, source_target_pairs={{0,16},{16,0},{1,17},{17,1},{2,18},{18,2},{3,19},{19,3},{4,20},{20... | collective-permute-start | bytes 393224 | tf_op jit(solution)/shard_map/ppermute | solution.py:31
  39.5 5.3 %collective-permute-start.10 = (bf16[2,64,512]{2,1,0:T(8,128)(2,1)S(1)}, bf16[2,64,512]{2,1,0:T(8,128)(2,1)S(1)}, u32[]{:S(2)}, u32[]{:S(2)}) collective-permute-start(bf16[2,64,512]{2,1,0:T(8,128)(2,1)S(1)} %get-tuple-element.67.own_ref), channel_id=1, source_target_pairs={{0,16},{16,0},{1,17},{17,1},{2,18},{18,2},{3,19},{19,3},{4,20},{20... | collective-permute-start | bytes 393224 | tf_op jit(solution)/shard_map/ppermute | solution.py:31
  46.4 1.9 %collective-permute-start.11 = (bf16[128,1280]{1,0:T(8,128)(2,1)S(1)}, bf16[128,1280]{1,0:T(8,128)(2,1)S(1)}, u32[]{:S(2)}, u32[]{:S(2)}) collective-permute-start(bf16[128,1280]{1,0:T(8,128)(2,1)S(1)} %get-tuple-element.76), channel_id=1, source_target_pairs={{0,1},{1,0},{2,3},{3,2},{4,5},{5,4},{6,7},{7,6},{8,9},{9,8},{10,11... | collective-permute-start | bytes 983048 | tf_op jit(solution)/shard_map/ppermute | solution.py:31
  47.7 2.2 %collective-permute-start.16 = (bf16[128,768]{1,0:T(8,128)(2,1)S(1)}, bf16[128,768]{1,0:T(8,128)(2,1)S(1)}, u32[]{:S(2)}, u32[]{:S(2)}) collective-permute-start(bf16[128,768]{1,0:T(8,128)(2,1)S(1)} %get-tuple-element.86), channel_id=1, source_target_pairs={{0,1},{1,0},{2,3},{3,2},{4,5},{5,4},{6,7},{7,6},{8,9},{9,8},{10,11... | collective-permute-start | bytes 589832 | tf_op jit(solution)/shard_map/ppermute | solution.py:31
  48.4 6.2 %collective-permute-start.12 = (bf16[64,1280]{1,0:T(8,128)(2,1)S(1)}, bf16[64,1280]{1,0:T(8,128)(2,1)S(1)}, u32[]{:S(2)}, u32[]{:S(2)}) collective-permute-start(bf16[64,1280]{1,0:T(8,128)(2,1)S(1)} %get-tuple-element.78), channel_id=1, source_target_pairs={{0,2},{1,3},{2,0},{3,1},{4,6},{5,7},{6,4},{7,5},{8,10},{9,11},{10,... | collective-permute-start | bytes 491528 | tf_op jit(solution)/shard_map/ppermute | solution.py:31
  50.0 8.1 %collective-permute-start.17 = (bf16[32,768]{1,0:T(8,128)(2,1)S(1)}, bf16[32,768]{1,0:T(8,128)(2,1)S(1)}, u32[]{:S(2)}, u32[]{:S(2)}) collective-permute-start(bf16[32,768]{1,0:T(8,128)(2,1)S(1)} %get-tuple-element.88), channel_id=1, source_target_pairs={{0,12},{1,13},{2,14},{3,15},{4,8},{5,9},{6,10},{7,11},{8,4},{9,5},... | collective-permute-start | bytes 147464 | tf_op jit(solution)/shard_map/ppermute | solution.py:31
  53.2 5.9 %collective-permute-start.18 = (bf16[32,768]{1,0:T(8,128)(2,1)S(1)}, bf16[32,768]{1,0:T(8,128)(2,1)S(1)}, u32[]{:S(2)}, u32[]{:S(2)}) collective-permute-start(bf16[32,768]{1,0:T(8,128)(2,1)S(1)} %get-tuple-element.89), channel_id=1, source_target_pairs={{0,8},{1,9},{2,10},{3,11},{4,12},{5,13},{6,14},{7,15},{8,0},{9,1},... | collective-permute-start | bytes 147464 | tf_op jit(solution)/shard_map/ppermute | solution.py:31
  53.2 5.9 %collective-permute-start.19 = (bf16[32,768]{1,0:T(8,128)(2,1)S(1)}, bf16[32,768]{1,0:T(8,128)(2,1)S(1)}, u32[]{:S(2)}, u32[]{:S(2)}) collective-permute-start(bf16[32,768]{1,0:T(8,128)(2,1)S(1)} %get-tuple-element.90), channel_id=1, source_target_pairs={{0,4},{1,5},{2,6},{3,7},{4,0},{5,1},{6,2},{7,3},{8,12},{9,13},{10,... | collective-permute-start | bytes 147464 | tf_op jit(solution)/shard_map/ppermute | solution.py:31
  54.6 8.4 %collective-permute-start.13 = (bf16[16,1280]{1,0:T(8,128)(2,1)S(1)}, bf16[16,1280]{1,0:T(8,128)(2,1)S(1)}, u32[]{:S(2)}, u32[]{:S(2)}) collective-permute-start(bf16[16,1280]{1,0:T(8,128)(2,1)S(1)} %get-tuple-element.81), channel_id=1, source_target_pairs={{0,12},{1,13},{2,14},{3,15},{4,8},{5,9},{6,10},{7,11},{8,4},{9,5},... | collective-permute-start | bytes 122888 | tf_op jit(solution)/shard_map/ppermute | solution.py:31
  58.1 4.9 %collective-permute-start.14 = (bf16[16,1280]{1,0:T(8,128)(2,1)S(1)}, bf16[16,1280]{1,0:T(8,128)(2,1)S(1)}, u32[]{:S(2)}, u32[]{:S(2)}) collective-permute-start(bf16[16,1280]{1,0:T(8,128)(2,1)S(1)} %get-tuple-element.82), channel_id=1, source_target_pairs={{0,8},{1,9},{2,10},{3,11},{4,12},{5,13},{6,14},{7,15},{8,0},{9,1},... | collective-permute-start | bytes 122888 | tf_op jit(solution)/shard_map/ppermute | solution.py:31
  58.1 4.9 %collective-permute-start.15 = (bf16[16,1280]{1,0:T(8,128)(2,1)S(1)}, bf16[16,1280]{1,0:T(8,128)(2,1)S(1)}, u32[]{:S(2)}, u32[]{:S(2)}) collective-permute-start(bf16[16,1280]{1,0:T(8,128)(2,1)S(1)} %get-tuple-element.83), channel_id=1, source_target_pairs={{0,4},{1,5},{2,6},{3,7},{4,0},{5,1},{6,2},{7,3},{8,12},{9,13},{10,... | collective-permute-start | bytes 122888 | tf_op jit(solution)/shard_map/ppermute | solution.py:31
  59.1 3.9 %collective-permute-start.20 = (bf16[16,768]{1,0:T(8,128)(2,1)S(1)}, bf16[16,768]{1,0:T(8,128)(2,1)S(1)}, u32[]{:S(2)}, u32[]{:S(2)}) collective-permute-start(bf16[16,768]{1,0:T(8,128)(2,1)S(1)} %get-tuple-element.92), channel_id=1, source_target_pairs={{0,2},{1,3},{2,0},{3,1},{4,6},{5,7},{6,4},{7,5},{8,10},{9,11},{10,... | collective-permute-start | bytes 73736 | tf_op jit(solution)/shard_map/ppermute | solution.py:31

commit v14 on v13

--- a/solution.py
+++ b/solution.py
@@ -116,8 +116,9 @@
         hidden_ref[i] = (gate_act / (1.0 + jnp.exp(-gate_act)) * up_act).astype(jnp.bfloat16)
 
 
-def select_body(dims, pos_ref, gain_ref, first, second, gates, ups, hidden_ref, normed_ref, mix_ref, turned_ref):
+def route_kernel(dims, pos_ref, *refs):
     n_fast, n_mid, n_tp, slow_n, tok_dev, top, exp_loc, rows, half = dims
+    first, (right_ref, squares_ref, swapped_ref, mix_ref, turned_ref) = refs[:n_fast], refs[n_fast:]
     tp_pos, base = pos_ref[0], pos_ref[1]
     run = slow_n * tok_dev
     tokens = n_fast * n_mid * n_tp * run
@@ -178,40 +179,51 @@
         ],
         axis=0,
     )
-    chosen, swapped = pick.T.astype(jnp.bfloat16), swapped.T.astype(jnp.bfloat16)
-    size = min(half, 4 * LANES)
-    squares = 0.0
-    for begin in range(0, 2 * half, size):
-        table, side, at = (swapped, second, begin) if begin < half else (chosen, first, begin - half)
-        values = jnp.concatenate([ref[:, at : at + size] for ref in side], axis=0)
+    swapped_ref[...] = swapped.T.astype(jnp.bfloat16)
+    squares = choose(pick.T.astype(jnp.bfloat16), first, right_ref, half)
+    squares_ref[...] = jnp.broadcast_to(squares, squares_ref.shape)
+
+
+def choose(table, pieces, out_ref, half):
+    exp_loc, rows, _ = out_ref.shape
+    size, squares = min(half, 4 * LANES), 0.0
+    for begin in range(0, half, size):
+        values = jnp.concatenate([ref[:, begin : begin + size] for ref in pieces], axis=0)
         values = jnp.dot(table, values, preferred_element_type=jnp.float32)
         squares = squares + jnp.sum(values * values, axis=1, keepdims=True)
         values = values.astype(jnp.bfloat16)
         for e in range(exp_loc):
-            normed_ref[e, :, begin : begin + size] = values[e * rows : (e + 1) * rows]
+            out_ref[e, :, begin : begin + size] = values[e * rows : (e + 1) * rows]
+    return squares
+
+
+def select_body(half, gain_ref, right_ref, squares_ref, swapped_ref, second, gates, ups, hidden_ref, normed_ref):
+    exp_loc, rows, _ = normed_ref.shape
+    squares = squares_ref[:, :1] + choose(swapped_ref[...], second, normed_ref, half)
     scale = lax.rsqrt(squares / (2 * half) + 1e-06)
     gain_all = gain_ref[...].astype(jnp.float32)
+    size = min(half, 4 * LANES)
     for begin in range(0, 2 * half, size):
         gain = [gain_all[r : r + 1] for r in range(begin // LANES, (begin + size) // LANES)]
         gain = jnp.concatenate(gain, axis=1)
+        source, at = (normed_ref, begin) if begin < half else (right_ref, begin - half)
         for e in range(exp_loc):
-            values = normed_ref[e, :, begin : begin + size].astype(jnp.float32)
+            values = source[e, :, at : at + size].astype(jnp.float32)
             values = values * scale[e * rows : (e + 1) * rows] * gain
             normed_ref[e, :, begin : begin + size] = values.astype(jnp.bfloat16)
     swiglu(normed_ref, gates, ups, hidden_ref, 0)
 
 
-def select_kernel(dims, lead, tail, pos_ref, gain_ref, *refs):
-    n_fast = dims[0]
-    first, second, refs = refs[:n_fast], refs[n_fast : 2 * n_fast], refs[2 * n_fast :]
+def select_kernel(half, n_fast, lead, tail, pos_ref, gain_ref, right_ref, squares_ref, swapped_ref, *refs):
+    second, refs = refs[:n_fast], refs[n_fast:]
     gates, ups, refs = refs[:lead], refs[lead : 2 * lead], refs[2 * lead :]
-    gate_far, up_far, hidden_ref, normed_ref, mix_ref, turned_ref, *near, sems = refs
+    gate_far, up_far, hidden_ref, normed_ref, *near, sems = refs
     wanted = [(gate_far, lead + tail - 1)] + [(up_far, e) for e in range(lead, lead + tail)]
     copies = load_copies([ref for ref, _ in wanted], near, sems, [e for _, e in wanted])
 
     @pl.when(pos_ref[0] >= 0)
     def _():
-        select_body(dims, pos_ref, gain_ref, first, second, gates, ups, hidden_ref, normed_ref, mix_ref, turned_ref)
+        select_body(half, gain_ref, right_ref, squares_ref, swapped_ref, second, gates, ups, hidden_ref, normed_ref)
 
     for copy in copies:
         copy.wait()
@@ -435,7 +447,7 @@
     first, second = along_mid(first), along_tp(second)
     first, sign = joined(first, [sign], 1)
     (second,) = joined(second, [], 0)
-    loads, sign = loaded([(w_up, e) for e in range(1, lead)] + [(w_down, e) for e in range(lead)], [sign])
+    loads, sign = loaded([(w_up, e) for e in range(1, lead)] + [(w_down, e) for e in range(lead - 1)], [sign])
     up_lead, down_lead = up_lead + loads[: lead - 1], loads[lead - 1 :]
     first, second = along_tp(first), along_mid(second)
     (first,) = joined(first, [sign], 0)
@@ -445,34 +457,43 @@
 
     dims = (n_fast, n_mid, n_tp, slow_n, tok_dev, top, exp_loc, rows, half)
     sems = lambda array, count: pltpu.SemaphoreType.DMA((count, runs_of(array)))
-    operands = [position, gain] + first + second + gate_lead + up_lead + [w_gate, w_up]
-    hidden, normed, mix, turned, gate_last, *up_tail = local_call(
-        functools.partial(select_kernel, dims, lead, tail),
+    right, squares, swapped, mix, turned = local_call(
+        functools.partial(route_kernel, dims),
         [
-            bf16((lead, rows, hid_part)),
-            bf16((exp_loc, rows, width)),
+            bf16((exp_loc, rows, half)),
+            jax.ShapeDtypeStruct((slots, LANES), jnp.float32),
+            bf16((slots, tokens)),
             bf16((2, tokens, slots)),
             bf16((2, tokens, slots)),
-        ]
+        ],
+        [position] + first,
+        flops=slots * tokens * width,
+        moved=4 * slots * width,
+    )
+    operands = [position, gain, right, squares, swapped] + second + gate_lead + up_lead + [w_gate, w_up]
+    hidden, normed, gate_last, *up_tail = local_call(
+        functools.partial(select_kernel, half, n_fast, lead, tail),
+        [bf16((lead, rows, hid_part)), bf16((exp_loc, rows, width))]
         + kept(w_gate, 1)
         + kept(w_up, tail),
         operands,
         far=[len(operands) - 2, len(operands) - 1],
         scratch=[sems(w_up, 1 + tail)],
-        flops=2 * slots * tokens * width + 4 * lead * rows * width * hid_part,
+        flops=slots * tokens * width + 4 * lead * rows * width * hid_part,
         moved=4 * lead * width * hid_part,
     )
     pieces = along_tp(hidden)
     operands = [position, normed] + gate_tail + [gate_last] + up_tail + [w_down]
     hidden, *down_tail = local_call(
-        functools.partial(up_kernel, lead, tail, range(lead, exp_loc)),
-        [bf16((tail, rows, hid_part))] + kept(w_down, tail),
+        functools.partial(up_kernel, lead, tail, range(lead - 1, exp_loc)),
+        [bf16((tail, rows, hid_part))] + kept(w_down, tail + 1),
         operands,
         far=[len(operands) - 1],
-        scratch=[sems(w_down, tail)],
+        scratch=[sems(w_down, tail + 1)],
         flops=4 * tail * rows * width * hid_part,
         moved=4 * tail * width * hid_part,
     )
+    down_lead, down_tail = down_lead + down_tail[:1], down_tail[1:]
     late = along_tp(hidden)
     done, part = local_call(
         functools.partial(down_kernel, n_tp, lead),
@@ -492,23 +513,23 @@
         moved=2 * tail * n_tp * hid_part * size,
     )
 
-    def swapped(blocks, digit):
+    def around(blocks, digit):
         own, *others = trades(blocks, "ep", n_ep, *digit)
         return [own] + others[::-1]
 
     slow = list(reversed(slow))
     right_way, left_way = slow + mid, mid + slow
-    right = summed(swapped(mixed_of(turned, left_cols, right_cols), fast), right_way[0][1], [], 0)
-    left = summed(swapped(mixed_of(mix, 0, left_cols), fast), left_way[0][1], [], 0)
+    right = summed(around(mixed_of(turned, left_cols, right_cols), fast), right_way[0][1], [], 0)
+    left = summed(around(mixed_of(mix, 0, left_cols), fast), left_way[0][1], [], 0)
     signs = []
     for digit, later in zip(left_way[:-1], left_way[1:]):
-        *left, late_sign = summed(swapped(left, digit), later[1], [], 1)
+        *left, late_sign = summed(around(left, digit), later[1], [], 1)
         signs.append(late_sign)
     for digit, later in zip(right_way[:-1], right_way[1:]):
-        right = summed(swapped(right, digit), later[1], signs, 0)
+        right = summed(around(right, digit), later[1], signs, 0)
         signs = []
-    left = swapped(left, left_way[-1])
-    right = swapped(right, right_way[-1])
+    left = around(left, left_way[-1])
+    right = around(right, right_way[-1])
     (own,) = local_call(
         functools.partial(own_kernel, (n_mid, n_tp, slow_n, tok_dev, half)),
         [jax.ShapeDtypeStruct((group, col_part), jnp.float32)],

time: 64.4 us -> 66.5 us (1.033)
  Pallas kernels: 30.4 us -> 32 us
    pallas_call x20 -> x21, Pallas kernels: 30.4 us -> 32 us  [local_call(): pl.pallas_call(kernel, out_shape=shapes, in_specs=specs, out_specs=[VMEM]...]
  transfers between devices with their start and end apart: 21 -> 21, of which waited for: 6 -> 7; matrix products, arithmetic and copies ran while one was open for 0% -> 0% of each run, Pallas kernels for 32% -> 34%
where the time goes in v14:
time: 66.5 us; the launch traced here: 66.4 us
  Pallas kernels  32 us (48%)
  starting transfers between devices  27.2 us (41%)
  waiting for transfers between devices  6.92 us (10%)
    pallas_call x21, Pallas kernels, local_call(): pl.pallas_call(kernel, out_shape=shapes, in_specs=specs, out_specs=[VMEM]...  32 us
    ppermute x21, starting transfers between devices, traded(): return lax.ppermute(x, axis, pairs)  27.2 us
    ppermute x21, waiting for transfers between devices, traded(): return lax.ppermute(x, axis, pairs)  6.92 us
  transfers between devices with their start and end apart: 21, of which 7 were waited for; matrix products, arithmetic and copies ran while one was open for 0% of the time, Pallas kernels for 34%

profile of v14, /device:TPU:0, one launch (start us, length us, event | category | flops | bytes accessed | tf_op | source)
XLA Modules:
  0.0 66.4 jit_solution(8535988908940318203)
XLA Ops:
  0.0 0.1 pad_add_fusion.pos_ref
  0.1 1.4 %shard_map.73.refs_0_ = bf16[8,4224]{1,0:T(8,128)(2,1)S(1)} custom-call(s32[2]{0:T(128)S(1)} %pad_add_fusion.pos_ref, s32[8,16]{1,0:T(8,128)} %bitcast.6, f32[8,16]{1,0:T(8,128)} %bitcast.7, bf16[8,4096]{1,0:T(8,128)(2,1)} %values_ref.1), custom_call_target="tpu_custom_call" | custom-call | tf_op jit(solution)/shard_map/pallas_call | solution.py:340
  1.5 5.1 %collective-permute-start.2 = (bf16[8,4224]{1,0:T(8,128)(2,1)S(1)}, bf16[8,4224]{1,0:T(8,128)(2,1)S(1)}, u32[]{:S(2)}, u32[]{:S(2)}) collective-permute-start(bf16[8,4224]{1,0:T(8,128)(2,1)S(1)} %shard_map.73.refs_0_), channel_id=1, source_target_pairs={{0,12},{1,13},{2,14},{3,15},{4,8},{5,9},{6,10},{7,11},{8,4},{9,5},... | collective-permute-start | bytes 202760 | tf_op jit(solution)/shard_map/ppermute | solution.py:31
  6.6 0.0 collective-permute-start.1
  6.6 0.6 collective-permute-start
  7.3 4.7 %shard_map.74 = (f32[8,128]{1,0:T(8,128)S(1)}, bf16[4096,512]{1,0:T(8,128)(2,1)S(1)}, bf16[4096,512]{1,0:T(8,128)(2,1)S(1)}, bf16[4096,512]{1,0:T(8,128)(2,1)S(1)}) custom-call(bf16[4,4096,512]{2,1,0:T(8,128)(2,1)} %refs_6_.1, bf16[4,4096,512]{2,1,0:T(8,128)(2,1)} %refs_6_.1, bf16[4,4096,512]{2,1,0:T(8,128)(2,1)} %refs_7_.1), custom_call_target="tpu_custom_call" | custom-call | bytes 12582912 | tf_op jit(solution)/shard_map/pallas_call | solution.py:340
  12.0 0.0 collective-permute-done.2.refs_3_
  12.0 0.4 collective-permute-done.1.refs_2_
  12.4 0.0 collective-permute-done.refs_1_
  12.4 1.6 %collective-permute-start.3 = (bf16[32,2176]{1,0:T(8,128)(2,1)S(1)}, bf16[32,2176]{1,0:T(8,128)(2,1)S(1)}, u32[]{:S(2)}, u32[]{:S(2)}) collective-permute-start(bf16[32,2176]{1,0:T(8,128)(2,1)S(1)} %get-tuple-element.53.refs_0_), channel_id=1, source_target_pairs={{0,2},{1,3},{2,0},{3,1},{4,6},{5,7},{6,4},{7,5},{8,10},{9,11},{10,... | collective-permute-start | bytes 417800 | tf_op jit(solution)/shard_map/ppermute | solution.py:31
  14.0 1.5 %collective-permute-start.5 = (bf16[32,2048]{1,0:T(8,128)(2,1)S(1)}, bf16[32,2048]{1,0:T(8,128)(2,1)S(1)}, u32[]{:S(2)}, u32[]{:S(2)}) collective-permute-start(bf16[32,2048]{1,0:T(8,128)(2,1)S(1)} %get-tuple-element.59.refs_0_), channel_id=1, source_target_pairs={{0,16},{16,0},{1,17},{17,1},{2,18},{18,2},{3,19},{19,3},{4,20},{20... | collective-permute-start | bytes 393224 | tf_op jit(solution)/shard_map/ppermute | solution.py:31
  15.5 2.2 %shard_map.76 = (f32[8,128]{1,0:T(8,128)S(1)}, bf16[4096,512]{1,0:T(8,128)(2,1)S(1)}) custom-call(bf16[4,4096,512]{2,1,0:T(8,128)(2,1)} %refs_6_.1, f32[8,128]{1,0:T(8,128)S(1)} %get-tuple-element.54.refs_1_), custom_call_target="tpu_custom_call" | custom-call | bytes 4194304 | tf_op jit(solution)/shard_map/pallas_call | solution.py:340
  17.7 0.0 collective-permute-done.3.refs_1_
  17.8 1.7 %collective-permute-start.4 = (bf16[64,2176]{1,0:T(8,128)(2,1)S(1)}, bf16[64,2176]{1,0:T(8,128)(2,1)S(1)}, u32[]{:S(2)}, u32[]{:S(2)}) collective-permute-start(bf16[64,2176]{1,0:T(8,128)(2,1)S(1)} %get-tuple-element.56.refs_0_), channel_id=1, source_target_pairs={{0,16},{16,0},{1,17},{17,1},{2,18},{18,2},{3,19},{19,3},{4,20},{20... | collective-permute-start | bytes 835592 | tf_op jit(solution)/shard_map/ppermute | solution.py:31
  19.5 0.0 collective-permute-done.5.refs_1_
  19.5 1.6 %collective-permute-start.6 = (bf16[64,2048]{1,0:T(8,128)(2,1)S(1)}, bf16[64,2048]{1,0:T(8,128)(2,1)S(1)}, u32[]{:S(2)}, u32[]{:S(2)}) collective-permute-start(bf16[64,2048]{1,0:T(8,128)(2,1)S(1)} %shard_map.80.refs_0_), channel_id=1, source_target_pairs={{0,2},{1,3},{2,0},{3,1},{4,6},{5,7},{6,4},{7,5},{8,10},{9,11},{10,... | collective-permute-start | bytes 786440 | tf_op jit(solution)/shard_map/ppermute | solution.py:31
  21.1 0.0 copy-start
  21.1 3.5 %shard_map.78 = (f32[8,128]{1,0:T(8,128)S(1)}, bf16[4096,512]{1,0:T(8,128)(2,1)S(1)}, bf16[1024,2048]{1,0:T(8,128)(2,1)S(1)}) custom-call(bf16[4,4096,512]{2,1,0:T(8,128)(2,1)} %refs_7_.1, bf16[4,1024,2048]{2,1,0:T(8,128)(2,1)} %refs_4_.1, f32[8,128]{1,0:T(8,128)S(1)} %get-tuple-element.57.refs_2_), custom_call_target="tpu_custom_call" | custom-call | bytes 8388608 | tf_op jit(solution)/shard_map/pallas_call | solution.py:340
  24.6 1.1 %collective-permute-done.4.refs_1_ = bf16[64,2176]{1,0:T(8,128)(2,1)S(1)} collective-permute-done((bf16[64,2176]{1,0:T(8,128)(2,1)S(1)}, bf16[64,2176]{1,0:T(8,128)(2,1)S(1)}, u32[]{:S(2)}, u32[]{:S(2)}) %collective-permute-start.4) | collective-permute-done | bytes 278560 | tf_op jit(solution)/shard_map/ppermute | solution.py:31
  25.7 0.1 collective-permute-start.7
  25.8 0.7 %collective-permute-done.6.refs_1_ = bf16[64,2048]{1,0:T(8,128)(2,1)S(1)} collective-permute-done((bf16[64,2048]{1,0:T(8,128)(2,1)S(1)}, bf16[64,2048]{1,0:T(8,128)(2,1)S(1)}, u32[]{:S(2)}, u32[]{:S(2)}) %collective-permute-start.6) | collective-permute-done | bytes 262176 | tf_op jit(solution)/shard_map/ppermute | solution.py:31
  26.5 0.1 collective-permute-start.8
  26.6 1.1 %collective-permute-done.7.refs_1_ = bf16[128,2176]{1,0:T(8,128)(2,1)S(1)} collective-permute-done((bf16[128,2176]{1,0:T(8,128)(2,1)S(1)}, bf16[128,2176]{1,0:T(8,128)(2,1)S(1)}, u32[]{:S(2)}, u32[]{:S(2)}) %collective-permute-start.7) | collective-permute-done | bytes 557088 | tf_op jit(solution)/shard_map/ppermute | solution.py:31
  27.7 1.9 %shard_map.82 = (bf16[4,64,2048]{2,1,0:T(8,128)(2,1)S(1)}, f32[256,128]{1,0:T(8,128)S(1)}, bf16[256,256]{1,0:T(8,128)(2,1)S(1)}, bf16[2,256,256]{2,1,0:T(8,128)(2,1)S(1)}, bf16[2,256,256]{2,1,0:T(8,128)(2,1)S(1)}) custom-call(s32[2]{0:T(128)S(1)} %pad_add_fusion.pos_ref, bf16[128,2176]{1,0:T(8,128)(2,1)S(1)} %shard_map.79.refs_0_.first_ref, ...), custom_call_target="tpu_custom_call" | custom-call | flops 268435456 | bytes 4194304 | tf_op jit(solution)/shard_map/pallas_call | solution.py:340
  29.7 0.0 collective-permute-done.8.refs_1_
  29.7 0.0 copy-done
  29.7 5.3 %shard_map.83 = (bf16[2,64,512]{2,1,0:T(8,128)(2,1)S(1)}, bf16[4,64,4096]{2,1,0:T(8,128)(2,1)S(1)}, bf16[4096,512]{1,0:T(8,128)(2,1)S(1)}, bf16[4096,512]{1,0:T(8,128)(2,1)S(1)}, bf16[4096,512]{1,0:T(8,128)(2,1)S(1)}) custom-call(s32[2]{0:T(128)S(1)} %pad_add_fusion.pos_ref, bf16[32,128]{1,0:T(8,128)(2,1)S(1)} %bitcast.5, ...), custom_call_target="tpu_custom_call" | custom-call | flops 1342177280 | bytes 16777216 | tf_op jit(solution)/shard_map/pallas_call | solution.py:340
  35.0 1.4 %collective-permute-start.9 = (bf16[2,64,512]{2,1,0:T(8,128)(2,1)S(1)}, bf16[2,64,512]{2,1,0:T(8,128)(2,1)S(1)}, u32[]{:S(2)}, u32[]{:S(2)}) collective-permute-start(bf16[2,64,512]{2,1,0:T(8,128)(2,1)S(1)} %get-tuple-element.74.refs_0_), channel_id=1, source_target_pairs={{0,16},{16,0},{1,17},{17,1},{2,18},{18,2},{3,19},{19,3},{4,20},{20... | collective-permute-start | bytes 393224 | tf_op jit(solution)/shard_map/ppermute | solution.py:31
  36.4 5.2 %shard_map.84 = (bf16[2,64,512]{2,1,0:T(8,128)(2,1)S(1)}, bf16[1024,2048]{1,0:T(8,128)(2,1)S(1)}, bf16[1024,2048]{1,0:T(8,128)(2,1)S(1)}, bf16[1024,2048]{1,0:T(8,128)(2,1)S(1)}) custom-call(s32[2]{0:T(128)S(1)} %pad_add_fusion.pos_ref, bf16[4,64,4096]{2,1,0:T(8,128)(2,1)S(1)} %get-tuple-element.68.normed_ref, ...), custom_call_target="tpu_custom_call" | custom-call | flops 1073741824 | bytes 16777216 | tf_op jit(solution)/shard_map/pallas_call | solution.py:340
  41.6 0.7 %collective-permute-start.10 = (bf16[2,64,512]{2,1,0:T(8,128)(2,1)S(1)}, bf16[2,64,512]{2,1,0:T(8,128)(2,1)S(1)}, u32[]{:S(2)}, u32[]{:S(2)}) collective-permute-start(bf16[2,64,512]{2,1,0:T(8,128)(2,1)S(1)} %get-tuple-element.73.own_ref), channel_id=1, source_target_pairs={{0,16},{16,0},{1,17},{17,1},{2,18},{18,2},{3,19},{19,3},{4,20},{20... | collective-permute-start | bytes 393224 | tf_op jit(solution)/shard_map/ppermute | solution.py:31
  42.4 0.0 collective-permute-done.9.refs_1_
  42.4 2.8 %shard_map.85 = (bf16[128,2048]{1,0:T(8,128)(2,1)S(1)}, f32[128,2048]{1,0:T(8,128)S(1)}) custom-call(s32[2]{0:T(128)S(1)} %pad_add_fusion.pos_ref, bf16[2,64,512]{2,1,0:T(8,128)(2,1)S(1)} %get-tuple-element.73.own_ref, bf16[2,64,512]{2,1,0:T(8,128)(2,1)S(1)} %get-tuple-element.74.refs_0_, bf16[2,64,512]{2,1,0:T(8,128)(2,1)S(1)} %collective-permute-done.9.refs_1_, ...), custom_call_target="tpu_custom_call" | custom-call | flops 536870912 | bytes 8388608 | tf_op jit(solution)/shard_map/pallas_call | solution.py:340
  45.2 1.8 %collective-permute-done.10.refs_0_ = bf16[2,64,512]{2,1,0:T(8,128)(2,1)S(1)} collective-permute-done((bf16[2,64,512]{2,1,0:T(8,128)(2,1)S(1)}, bf16[2,64,512]{2,1,0:T(8,128)(2,1)S(1)}, u32[]{:S(2)}, u32[]{:S(2)}) %collective-permute-start.10) | collective-permute-done | bytes 131104 | tf_op jit(solution)/shard_map/ppermute | solution.py:31
  47.0 1.5 %shard_map.86 = (bf16[128,1280]{1,0:T(8,128)(2,1)S(1)}, bf16[128,1280]{1,0:T(8,128)(2,1)S(1)}) custom-call(s32[2]{0:T(128)S(1)} %pad_add_fusion.pos_ref, bf16[2,256,256]{2,1,0:T(8,128)(2,1)S(1)} %get-tuple-element.60.mix_ref, bf16[128,2048]{1,0:T(8,128)(2,1)S(1)} %get-tuple-element.79.done_ref, f32[128,2048]{1,0:T(8,128)S(1)} %get-tuple-element.80.part_ref, ...), custom_call_target="tpu_custom_call" | custom-call | flops 671088640 | bytes 5242880 | tf_op jit(solution)/shard_map/pallas_call | solution.py:340
  48.5 0.1 collective-permute-start.11
  48.6 1.3 %shard_map.90 = (bf16[128,768]{1,0:T(8,128)(2,1)S(1)}, bf16[128,768]{1,0:T(8,128)(2,1)S(1)}) custom-call(s32[2]{0:T(128)S(1)} %pad_add_fusion.pos_ref, bf16[2,256,256]{2,1,0:T(8,128)(2,1)S(1)} %get-tuple-element.90.mix_ref, bf16[128,2048]{1,0:T(8,128)(2,1)S(1)} %get-tuple-element.79.done_ref, f32[128,2048]{1,0:T(8,128)S(1)} %get-tuple-element.80.part_ref, ...), custom_call_target="tpu_custom_call" | custom-call | flops 402653184 | bytes 3145728 | tf_op jit(solution)/shard_map/pallas_call | solution.py:340
  49.9 0.6 collective-permute-start.16
  50.4 0.0 collective-permute-done.11.refs_1_
  50.4 0.1 shard_map.87
  50.5 1.6 %collective-permute-start.12 = (bf16[64,1280]{1,0:T(8,128)(2,1)S(1)}, bf16[64,1280]{1,0:T(8,128)(2,1)S(1)}, u32[]{:S(2)}, u32[]{:S(2)}) collective-permute-start(bf16[64,1280]{1,0:T(8,128)(2,1)S(1)} %get-tuple-element.84), channel_id=1, source_target_pairs={{0,2},{1,3},{2,0},{3,1},{4,6},{5,7},{6,4},{7,5},{8,10},{9,11},{10,... | collective-permute-start | bytes 491528 | tf_op jit(solution)/shard_map/ppermute | solution.py:31
  52.1 0.0 collective-permute-done.16.refs_1_
  52.1 2.2 %collective-permute-start.17 = (bf16[32,768]{1,0:T(8,128)(2,1)S(1)}, bf16[32,768]{1,0:T(8,128)(2,1)S(1)}, u32[]{:S(2)}, u32[]{:S(2)}) collective-permute-start(bf16[32,768]{1,0:T(8,128)(2,1)S(1)} %get-tuple-element.94), channel_id=1, source_target_pairs={{0,12},{1,13},{2,14},{3,15},{4,8},{5,9},{6,10},{7,11},{8,4},{9,5},... | collective-permute-start | bytes 147464 | tf_op jit(solution)/shard_map/ppermute | solution.py:31
  54.4 0.0 collective-permute-start.18
  54.4 2.2 %collective-permute-start.19 = (bf16[32,768]{1,0:T(8,128)(2,1)S(1)}, bf16[32,768]{1,0:T(8,128)(2,1)S(1)}, u32[]{:S(2)}, u32[]{:S(2)}) collective-permute-start(bf16[32,768]{1,0:T(8,128)(2,1)S(1)} %get-tuple-element.96), channel_id=1, source_target_pairs={{0,4},{1,5},{2,6},{3,7},{4,0},{5,1},{6,2},{7,3},{8,12},{9,13},{10,... | collective-permute-start | bytes 147464 | tf_op jit(solution)/shard_map/ppermute | solution.py:31
  56.6 0.1 collective-permute-done.12.refs_1_
  56.7 2.8 %collective-permute-start.13 = (bf16[16,1280]{1,0:T(8,128)(2,1)S(1)}, bf16[16,1280]{1,0:T(8,128)(2,1)S(1)}, u32[]{:S(2)}, u32[]{:S(2)}) collective-permute-start(bf16[16,1280]{1,0:T(8,128)(2,1)S(1)} %get-tuple-element.87), channel_id=1, source_target_pairs={{0,12},{1,13},{2,14},{3,15},{4,8},{5,9},{6,10},{7,11},{8,4},{9,5},... | collective-permute-start | bytes 122888 | tf_op jit(solution)/shard_map/ppermute | solution.py:31
  59.6 0.0 collective-permute-start.14
  59.6 0.0 collective-permute-done.17.refs_1_
  59.6 1.6 %collective-permute-start.15 = (bf16[16,1280]{1,0:T(8,128)(2,1)S(1)}, bf16[16,1280]{1,0:T(8,128)(2,1)S(1)}, u32[]{:S(2)}, u32[]{:S(2)}) collective-permute-start(bf16[16,1280]{1,0:T(8,128)(2,1)S(1)} %get-tuple-element.89), channel_id=1, source_target_pairs={{0,4},{1,5},{2,6},{3,7},{4,0},{5,1},{6,2},{7,3},{8,12},{9,13},{10,... | collective-permute-start | bytes 122888 | tf_op jit(solution)/shard_map/ppermute | solution.py:31
  61.2 0.0 collective-permute-done.18.refs_2_
  61.2 0.0 collective-permute-done.19.refs_3_
  61.2 1.6 %collective-permute-start.20 = (bf16[16,768]{1,0:T(8,128)(2,1)S(1)}, bf16[16,768]{1,0:T(8,128)(2,1)S(1)}, u32[]{:S(2)}, u32[]{:S(2)}) collective-permute-start(bf16[16,768]{1,0:T(8,128)(2,1)S(1)} %get-tuple-element.98), channel_id=1, source_target_pairs={{0,2},{1,3},{2,0},{3,1},{4,6},{5,7},{6,4},{7,5},{8,10},{9,11},{10,... | collective-permute-start | bytes 73736 | tf_op jit(solution)/shard_map/ppermute | solution.py:31
  62.8 0.6 shard_map.89.own_ref
  63.4 1.7 %collective-permute-done.20.refs_5_ = bf16[16,768]{1,0:T(8,128)(2,1)S(1)} collective-permute-done((bf16[16,768]{1,0:T(8,128)(2,1)S(1)}, bf16[16,768]{1,0:T(8,128)(2,1)S(1)}, u32[]{:S(2)}, u32[]{:S(2)}) %collective-permute-start.20) | collective-permute-done | bytes 24608 | tf_op jit(solution)/shard_map/ppermute | solution.py:31
  65.1 0.0 collective-permute-done.13.refs_1_
  65.1 0.0 collective-permute-done.14.refs_2_
  65.1 0.0 collective-permute-done.15.refs_3_
  65.1 1.2 %shard_map.93 = bf16[16,2048]{1,0:T(8,128)(2,1)} custom-call(s32[2]{0:T(128)S(1)} %pad_add_fusion.pos_ref, f32[16,2048]{1,0:T(8,128)S(1)} %shard_map.89.own_ref, bf16[16,1280]{1,0:T(8,128)(2,1)S(1)} %get-tuple-element.86.refs_0_, bf16[16,1280]{1,0:T(8,128)(2,1)S(1)} %collective-permute-done.13.refs_1_, bf16[16,1280]{1,0:T(8,128)(2,1)S(1)} %collective-permute-done.14.refs_2_, ...), custom_call_target="tpu_custom_call" | custom-call | bytes 524288 | tf_op jit(solution)/shard_map/pallas_call | solution.py:340
  (8 shorter events, 0.3 us)
Async XLA Ops:
  1.5 10.5 %collective-permute-start.2 = (bf16[8,4224]{1,0:T(8,128)(2,1)S(1)}, bf16[8,4224]{1,0:T(8,128)(2,1)S(1)}, u32[]{:S(2)}, u32[]{:S(2)}) collective-permute-start(bf16[8,4224]{1,0:T(8,128)(2,1)S(1)} %shard_map.73.refs_0_), channel_id=1, source_target_pairs={{0,12},{1,13},{2,14},{3,15},{4,8},{5,9},{6,10},{7,11},{8,4},{9,5},... | collective-permute-start | bytes 202760 | tf_op jit(solution)/shard_map/ppermute | solution.py:31
  6.6 5.8 %collective-permute-start.1 = (bf16[8,4224]{1,0:T(8,128)(2,1)S(1)}, bf16[8,4224]{1,0:T(8,128)(2,1)S(1)}, u32[]{:S(2)}, u32[]{:S(2)}) collective-permute-start(bf16[8,4224]{1,0:T(8,128)(2,1)S(1)} %shard_map.73.refs_0_), channel_id=1, source_target_pairs={{0,8},{1,9},{2,10},{3,11},{4,12},{5,13},{6,14},{7,15},{8,0},{9,1},... | collective-permute-start | bytes 202760 | tf_op jit(solution)/shard_map/ppermute | solution.py:31
  6.6 5.8 %collective-permute-start = (bf16[8,4224]{1,0:T(8,128)(2,1)S(1)}, bf16[8,4224]{1,0:T(8,128)(2,1)S(1)}, u32[]{:S(2)}, u32[]{:S(2)}) collective-permute-start(bf16[8,4224]{1,0:T(8,128)(2,1)S(1)} %shard_map.73.refs_0_), channel_id=1, source_target_pairs={{0,4},{1,5},{2,6},{3,7},{4,0},{5,1},{6,2},{7,3},{8,12},{9,13},{10,... | collective-permute-start | bytes 202760 | tf_op jit(solution)/shard_map/ppermute | solution.py:31
  12.4 5.3 %collective-permute-start.3 = (bf16[32,2176]{1,0:T(8,128)(2,1)S(1)}, bf16[32,2176]{1,0:T(8,128)(2,1)S(1)}, u32[]{:S(2)}, u32[]{:S(2)}) collective-permute-start(bf16[32,2176]{1,0:T(8,128)(2,1)S(1)} %get-tuple-element.53.refs_0_), channel_id=1, source_target_pairs={{0,2},{1,3},{2,0},{3,1},{4,6},{5,7},{6,4},{7,5},{8,10},{9,11},{10,... | collective-permute-start | bytes 417800 | tf_op jit(solution)/shard_map/ppermute | solution.py:31
  14.0 5.5 %collective-permute-start.5 = (bf16[32,2048]{1,0:T(8,128)(2,1)S(1)}, bf16[32,2048]{1,0:T(8,128)(2,1)S(1)}, u32[]{:S(2)}, u32[]{:S(2)}) collective-permute-start(bf16[32,2048]{1,0:T(8,128)(2,1)S(1)} %get-tuple-element.59.refs_0_), channel_id=1, source_target_pairs={{0,16},{16,0},{1,17},{17,1},{2,18},{18,2},{3,19},{19,3},{4,20},{20... | collective-permute-start | bytes 393224 | tf_op jit(solution)/shard_map/ppermute | solution.py:31
  17.8 7.9 %collective-permute-start.4 = (bf16[64,2176]{1,0:T(8,128)(2,1)S(1)}, bf16[64,2176]{1,0:T(8,128)(2,1)S(1)}, u32[]{:S(2)}, u32[]{:S(2)}) collective-permute-start(bf16[64,2176]{1,0:T(8,128)(2,1)S(1)} %get-tuple-element.56.refs_0_), channel_id=1, source_target_pairs={{0,16},{16,0},{1,17},{17,1},{2,18},{18,2},{3,19},{19,3},{4,20},{20... | collective-permute-start | bytes 835592 | tf_op jit(solution)/shard_map/ppermute | solution.py:31
  19.5 7.0 %collective-permute-start.6 = (bf16[64,2048]{1,0:T(8,128)(2,1)S(1)}, bf16[64,2048]{1,0:T(8,128)(2,1)S(1)}, u32[]{:S(2)}, u32[]{:S(2)}) collective-permute-start(bf16[64,2048]{1,0:T(8,128)(2,1)S(1)} %shard_map.80.refs_0_), channel_id=1, source_target_pairs={{0,2},{1,3},{2,0},{3,1},{4,6},{5,7},{6,4},{7,5},{8,10},{9,11},{10,... | collective-permute-start | bytes 786440 | tf_op jit(solution)/shard_map/ppermute | solution.py:31
  21.1 8.6 %copy-start = (bf16[4096]{0:T(1024)(128)(2,1)S(1)}, bf16[4096]{0:T(1024)(128)(2,1)}, u32[]{:S(2)}) copy-start(bf16[4096]{0:T(1024)(128)(2,1)} %param.8) | copy-start | bytes 24580
  25.7 2.0 %collective-permute-start.7 = (bf16[128,2176]{1,0:T(8,128)(2,1)S(1)}, bf16[128,2176]{1,0:T(8,128)(2,1)S(1)}, u32[]{:S(2)}, u32[]{:S(2)}) collective-permute-start(bf16[128,2176]{1,0:T(8,128)(2,1)S(1)} %shard_map.79.refs_0_.first_ref), channel_id=1, source_target_pairs={{0,1},{1,0},{2,3},{3,2},{4,5},{5,4},{6,7},{7,6},{8,9},{9,8},{10,11... | collective-permute-start | bytes 1671176 | tf_op jit(solution)/shard_map/ppermute | solution.py:31
  26.5 3.1 %collective-permute-start.8 = (bf16[128,2048]{1,0:T(8,128)(2,1)S(1)}, bf16[128,2048]{1,0:T(8,128)(2,1)S(1)}, u32[]{:S(2)}, u32[]{:S(2)}) collective-permute-start(bf16[128,2048]{1,0:T(8,128)(2,1)S(1)} %shard_map.81.refs_0_.second_ref), channel_id=1, source_target_pairs={{0,1},{1,0},{2,3},{3,2},{4,5},{5,4},{6,7},{7,6},{8,9},{9,8},{10,11... | collective-permute-start | bytes 1572872 | tf_op jit(solution)/shard_map/ppermute | solution.py:31
  35.0 7.4 %collective-permute-start.9 = (bf16[2,64,512]{2,1,0:T(8,128)(2,1)S(1)}, bf16[2,64,512]{2,1,0:T(8,128)(2,1)S(1)}, u32[]{:S(2)}, u32[]{:S(2)}) collective-permute-start(bf16[2,64,512]{2,1,0:T(8,128)(2,1)S(1)} %get-tuple-element.74.refs_0_), channel_id=1, source_target_pairs={{0,16},{16,0},{1,17},{17,1},{2,18},{18,2},{3,19},{19,3},{4,20},{20... | collective-permute-start | bytes 393224 | tf_op jit(solution)/shard_map/ppermute | solution.py:31
  41.6 5.3 %collective-permute-start.10 = (bf16[2,64,512]{2,1,0:T(8,128)(2,1)S(1)}, bf16[2,64,512]{2,1,0:T(8,128)(2,1)S(1)}, u32[]{:S(2)}, u32[]{:S(2)}) collective-permute-start(bf16[2,64,512]{2,1,0:T(8,128)(2,1)S(1)} %get-tuple-element.73.own_ref), channel_id=1, source_target_pairs={{0,16},{16,0},{1,17},{17,1},{2,18},{18,2},{3,19},{19,3},{4,20},{20... | collective-permute-start | bytes 393224 | tf_op jit(solution)/shard_map/ppermute | solution.py:31
  48.5 1.9 %collective-permute-start.11 = (bf16[128,1280]{1,0:T(8,128)(2,1)S(1)}, bf16[128,1280]{1,0:T(8,128)(2,1)S(1)}, u32[]{:S(2)}, u32[]{:S(2)}) collective-permute-start(bf16[128,1280]{1,0:T(8,128)(2,1)S(1)} %get-tuple-element.82), channel_id=1, source_target_pairs={{0,1},{1,0},{2,3},{3,2},{4,5},{5,4},{6,7},{7,6},{8,9},{9,8},{10,11... | collective-permute-start | bytes 983048 | tf_op jit(solution)/shard_map/ppermute | solution.py:31
  49.9 2.2 %collective-permute-start.16 = (bf16[128,768]{1,0:T(8,128)(2,1)S(1)}, bf16[128,768]{1,0:T(8,128)(2,1)S(1)}, u32[]{:S(2)}, u32[]{:S(2)}) collective-permute-start(bf16[128,768]{1,0:T(8,128)(2,1)S(1)} %get-tuple-element.92), channel_id=1, source_target_pairs={{0,1},{1,0},{2,3},{3,2},{4,5},{5,4},{6,7},{7,6},{8,9},{9,8},{10,11... | collective-permute-start | bytes 589832 | tf_op jit(solution)/shard_map/ppermute | solution.py:31
  50.5 6.2 %collective-permute-start.12 = (bf16[64,1280]{1,0:T(8,128)(2,1)S(1)}, bf16[64,1280]{1,0:T(8,128)(2,1)S(1)}, u32[]{:S(2)}, u32[]{:S(2)}) collective-permute-start(bf16[64,1280]{1,0:T(8,128)(2,1)S(1)} %get-tuple-element.84), channel_id=1, source_target_pairs={{0,2},{1,3},{2,0},{3,1},{4,6},{5,7},{6,4},{7,5},{8,10},{9,11},{10,... | collective-permute-start | bytes 491528 | tf_op jit(solution)/shard_map/ppermute | solution.py:31
  52.1 7.4 %collective-permute-start.17 = (bf16[32,768]{1,0:T(8,128)(2,1)S(1)}, bf16[32,768]{1,0:T(8,128)(2,1)S(1)}, u32[]{:S(2)}, u32[]{:S(2)}) collective-permute-start(bf16[32,768]{1,0:T(8,128)(2,1)S(1)} %get-tuple-element.94), channel_id=1, source_target_pairs={{0,12},{1,13},{2,14},{3,15},{4,8},{5,9},{6,10},{7,11},{8,4},{9,5},... | collective-permute-start | bytes 147464 | tf_op jit(solution)/shard_map/ppermute | solution.py:31
  54.4 6.8 %collective-permute-start.18 = (bf16[32,768]{1,0:T(8,128)(2,1)S(1)}, bf16[32,768]{1,0:T(8,128)(2,1)S(1)}, u32[]{:S(2)}, u32[]{:S(2)}) collective-permute-start(bf16[32,768]{1,0:T(8,128)(2,1)S(1)} %get-tuple-element.95), channel_id=1, source_target_pairs={{0,8},{1,9},{2,10},{3,11},{4,12},{5,13},{6,14},{7,15},{8,0},{9,1},... | collective-permute-start | bytes 147464 | tf_op jit(solution)/shard_map/ppermute | solution.py:31
  54.4 6.8 %collective-permute-start.19 = (bf16[32,768]{1,0:T(8,128)(2,1)S(1)}, bf16[32,768]{1,0:T(8,128)(2,1)S(1)}, u32[]{:S(2)}, u32[]{:S(2)}) collective-permute-start(bf16[32,768]{1,0:T(8,128)(2,1)S(1)} %get-tuple-element.96), channel_id=1, source_target_pairs={{0,4},{1,5},{2,6},{3,7},{4,0},{5,1},{6,2},{7,3},{8,12},{9,13},{10,... | collective-permute-start | bytes 147464 | tf_op jit(solution)/shard_map/ppermute | solution.py:31
  56.7 8.4 %collective-permute-start.13 = (bf16[16,1280]{1,0:T(8,128)(2,1)S(1)}, bf16[16,1280]{1,0:T(8,128)(2,1)S(1)}, u32[]{:S(2)}, u32[]{:S(2)}) collective-permute-start(bf16[16,1280]{1,0:T(8,128)(2,1)S(1)} %get-tuple-element.87), channel_id=1, source_target_pairs={{0,12},{1,13},{2,14},{3,15},{4,8},{5,9},{6,10},{7,11},{8,4},{9,5},... | collective-permute-start | bytes 122888 | tf_op jit(solution)/shard_map/ppermute | solution.py:31
  59.6 5.6 %collective-permute-start.14 = (bf16[16,1280]{1,0:T(8,128)(2,1)S(1)}, bf16[16,1280]{1,0:T(8,128)(2,1)S(1)}, u32[]{:S(2)}, u32[]{:S(2)}) collective-permute-start(bf16[16,1280]{1,0:T(8,128)(2,1)S(1)} %get-tuple-element.88), channel_id=1, source_target_pairs={{0,8},{1,9},{2,10},{3,11},{4,12},{5,13},{6,14},{7,15},{8,0},{9,1},... | collective-permute-start | bytes 122888 | tf_op jit(solution)/shard_map/ppermute | solution.py:31
  59.6 5.6 %collective-permute-start.15 = (bf16[16,1280]{1,0:T(8,128)(2,1)S(1)}, bf16[16,1280]{1,0:T(8,128)(2,1)S(1)}, u32[]{:S(2)}, u32[]{:S(2)}) collective-permute-start(bf16[16,1280]{1,0:T(8,128)(2,1)S(1)} %get-tuple-element.89), channel_id=1, source_target_pairs={{0,4},{1,5},{2,6},{3,7},{4,0},{5,1},{6,2},{7,3},{8,12},{9,13},{10,... | collective-permute-start | bytes 122888 | tf_op jit(solution)/shard_map/ppermute | solution.py:31
  61.2 3.9 %collective-permute-start.20 = (bf16[16,768]{1,0:T(8,128)(2,1)S(1)}, bf16[16,768]{1,0:T(8,128)(2,1)S(1)}, u32[]{:S(2)}, u32[]{:S(2)}) collective-permute-start(bf16[16,768]{1,0:T(8,128)(2,1)S(1)} %get-tuple-element.98), channel_id=1, source_target_pairs={{0,2},{1,3},{2,0},{3,1},{4,6},{5,7},{6,4},{7,5},{8,10},{9,11},{10,... | collective-permute-start | bytes 73736 | tf_op jit(solution)/shard_map/ppermute | solution.py:31

commit v15 on v13

--- a/solution.py
+++ b/solution.py
@@ -494,7 +494,7 @@
 
     def swapped(blocks, digit):
         own, *others = trades(blocks, "ep", n_ep, *digit)
-        return [own] + others[::-1]
+        return [own] + others
 
     slow = list(reversed(slow))
     right_way, left_way = slow + mid, mid + slow

time: 64.4 us -> 65.9 us (1.023)
  waiting for transfers between devices: 6.43 us -> 8.08 us
    ppermute x21, waiting for transfers between devices: 6.43 us -> 8.08 us  [traded(): return lax.ppermute(x, axis, pairs)]
  transfers between devices with their start and end apart: 21 -> 21, of which waited for: 6 -> 8; matrix products, arithmetic and copies ran while one was open for 0% -> 0% of each run, Pallas kernels for 32% -> 31%
where the time goes in v15:
time: 65.9 us; the launch traced here: 65.7 us
  Pallas kernels  30.4 us (46%)
  starting transfers between devices  27 us (41%)
  waiting for transfers between devices  8.08 us (12%)
    pallas_call x20, Pallas kernels, local_call(): pl.pallas_call(kernel, out_shape=shapes, in_specs=specs, out_specs=[VMEM]...  30.4 us
    ppermute x21, starting transfers between devices, traded(): return lax.ppermute(x, axis, pairs)  27 us
    ppermute x21, waiting for transfers between devices, traded(): return lax.ppermute(x, axis, pairs)  8.08 us
  transfers between devices with their start and end apart: 21, of which 8 were waited for; matrix products, arithmetic and copies ran while one was open for 0% of the time, Pallas kernels for 31%

profile of v15, /device:TPU:0, one launch (start us, length us, event | category | flops | bytes accessed | tf_op | source)
XLA Modules:
  0.0 65.7 jit_solution(5594426495865661046)
XLA Ops:
  0.0 0.1 pad_add_fusion.pos_ref
  0.1 1.4 %shard_map.73.refs_0_ = bf16[8,4224]{1,0:T(8,128)(2,1)S(1)} custom-call(s32[2]{0:T(128)S(1)} %pad_add_fusion.pos_ref, s32[8,16]{1,0:T(8,128)} %bitcast.6, f32[8,16]{1,0:T(8,128)} %bitcast.7, bf16[8,4096]{1,0:T(8,128)(2,1)} %values_ref.1), custom_call_target="tpu_custom_call" | custom-call | tf_op jit(solution)/shard_map/pallas_call | solution.py:328
  1.5 5.1 %collective-permute-start.2 = (bf16[8,4224]{1,0:T(8,128)(2,1)S(1)}, bf16[8,4224]{1,0:T(8,128)(2,1)S(1)}, u32[]{:S(2)}, u32[]{:S(2)}) collective-permute-start(bf16[8,4224]{1,0:T(8,128)(2,1)S(1)} %shard_map.73.refs_0_), channel_id=1, source_target_pairs={{0,12},{1,13},{2,14},{3,15},{4,8},{5,9},{6,10},{7,11},{8,4},{9,5},... | collective-permute-start | bytes 202760 | tf_op jit(solution)/shard_map/ppermute | solution.py:31
  6.6 0.0 collective-permute-start.1
  6.6 0.6 collective-permute-start
  7.3 4.7 %shard_map.74 = (f32[8,128]{1,0:T(8,128)S(1)}, bf16[4096,512]{1,0:T(8,128)(2,1)S(1)}, bf16[4096,512]{1,0:T(8,128)(2,1)S(1)}, bf16[4096,512]{1,0:T(8,128)(2,1)S(1)}) custom-call(bf16[4,4096,512]{2,1,0:T(8,128)(2,1)} %refs_8_.1, bf16[4,4096,512]{2,1,0:T(8,128)(2,1)} %refs_8_.1, bf16[4,4096,512]{2,1,0:T(8,128)(2,1)} %refs_9_.1), custom_call_target="tpu_custom_call" | custom-call | bytes 12582912 | tf_op jit(solution)/shard_map/pallas_call | solution.py:328
  12.0 0.0 collective-permute-done.2.refs_3_
  12.0 0.4 collective-permute-done.1.refs_2_
  12.4 0.0 collective-permute-done.refs_1_
  12.4 1.6 %collective-permute-start.3 = (bf16[32,2176]{1,0:T(8,128)(2,1)S(1)}, bf16[32,2176]{1,0:T(8,128)(2,1)S(1)}, u32[]{:S(2)}, u32[]{:S(2)}) collective-permute-start(bf16[32,2176]{1,0:T(8,128)(2,1)S(1)} %get-tuple-element.50.refs_0_), channel_id=1, source_target_pairs={{0,2},{1,3},{2,0},{3,1},{4,6},{5,7},{6,4},{7,5},{8,10},{9,11},{10,... | collective-permute-start | bytes 417800 | tf_op jit(solution)/shard_map/ppermute | solution.py:31
  14.0 1.5 %collective-permute-start.5 = (bf16[32,2048]{1,0:T(8,128)(2,1)S(1)}, bf16[32,2048]{1,0:T(8,128)(2,1)S(1)}, u32[]{:S(2)}, u32[]{:S(2)}) collective-permute-start(bf16[32,2048]{1,0:T(8,128)(2,1)S(1)} %get-tuple-element.56.refs_0_), channel_id=1, source_target_pairs={{0,16},{16,0},{1,17},{17,1},{2,18},{18,2},{3,19},{19,3},{4,20},{20... | collective-permute-start | bytes 393224 | tf_op jit(solution)/shard_map/ppermute | solution.py:31
  15.5 2.2 %shard_map.76 = (f32[8,128]{1,0:T(8,128)S(1)}, bf16[4096,512]{1,0:T(8,128)(2,1)S(1)}) custom-call(bf16[4,4096,512]{2,1,0:T(8,128)(2,1)} %refs_8_.1, f32[8,128]{1,0:T(8,128)S(1)} %get-tuple-element.51.refs_1_), custom_call_target="tpu_custom_call" | custom-call | bytes 4194304 | tf_op jit(solution)/shard_map/pallas_call | solution.py:328
  17.7 0.0 collective-permute-done.3.refs_1_
  17.8 1.7 %collective-permute-start.4 = (bf16[64,2176]{1,0:T(8,128)(2,1)S(1)}, bf16[64,2176]{1,0:T(8,128)(2,1)S(1)}, u32[]{:S(2)}, u32[]{:S(2)}) collective-permute-start(bf16[64,2176]{1,0:T(8,128)(2,1)S(1)} %get-tuple-element.53.refs_0_), channel_id=1, source_target_pairs={{0,16},{16,0},{1,17},{17,1},{2,18},{18,2},{3,19},{19,3},{4,20},{20... | collective-permute-start | bytes 835592 | tf_op jit(solution)/shard_map/ppermute | solution.py:31
  19.5 0.0 collective-permute-done.5.refs_1_
  19.5 1.6 %collective-permute-start.6 = (bf16[64,2048]{1,0:T(8,128)(2,1)S(1)}, bf16[64,2048]{1,0:T(8,128)(2,1)S(1)}, u32[]{:S(2)}, u32[]{:S(2)}) collective-permute-start(bf16[64,2048]{1,0:T(8,128)(2,1)S(1)} %shard_map.80.refs_0_), channel_id=1, source_target_pairs={{0,2},{1,3},{2,0},{3,1},{4,6},{5,7},{6,4},{7,5},{8,10},{9,11},{10,... | collective-permute-start | bytes 786440 | tf_op jit(solution)/shard_map/ppermute | solution.py:31
  21.1 0.0 copy-start
  21.1 4.7 %shard_map.78 = (f32[8,128]{1,0:T(8,128)S(1)}, bf16[4096,512]{1,0:T(8,128)(2,1)S(1)}, bf16[1024,2048]{1,0:T(8,128)(2,1)S(1)}, bf16[1024,2048]{1,0:T(8,128)(2,1)S(1)}) custom-call(bf16[4,4096,512]{2,1,0:T(8,128)(2,1)} %refs_9_.1, bf16[4,1024,2048]{2,1,0:T(8,128)(2,1)} %refs_4_.1, bf16[4,1024,2048]{2,1,0:T(8,128)(2,1)} %refs_4_.1, ...), custom_call_target="tpu_custom_call" | custom-call | bytes 12582912 | tf_op jit(solution)/shard_map/pallas_call | solution.py:328
  25.8 0.0 collective-permute-done.4.refs_1_
  25.9 0.1 collective-permute-start.7
  26.0 0.5 collective-permute-done.6.refs_1_
  26.5 0.1 collective-permute-start.8
  26.6 2.0 %collective-permute-done.8.refs_3_ = bf16[128,2048]{1,0:T(8,128)(2,1)S(1)} collective-permute-done((bf16[128,2048]{1,0:T(8,128)(2,1)S(1)}, bf16[128,2048]{1,0:T(8,128)(2,1)S(1)}, u32[]{:S(2)}, u32[]{:S(2)}) %collective-permute-start.8) | collective-permute-done | bytes 524320 | tf_op jit(solution)/shard_map/ppermute | solution.py:31
  28.7 0.0 collective-permute-done.7.refs_1_
  28.7 0.0 copy-done
  28.7 5.6 %shard_map.82 = (bf16[2,64,512]{2,1,0:T(8,128)(2,1)S(1)}, bf16[4,64,4096]{2,1,0:T(8,128)(2,1)S(1)}, bf16[2,256,256]{2,1,0:T(8,128)(2,1)S(1)}, bf16[2,256,256]{2,...) custom-call(s32[2]{0:T(128)S(1)} %pad_add_fusion.pos_ref, ...), custom_call_target="tpu_custom_call" | custom-call | flops 1610612736 | bytes 16777216 | tf_op jit(solution)/shard_map/pallas_call | solution.py:328
  34.3 1.3 %collective-permute-start.9 = (bf16[2,64,512]{2,1,0:T(8,128)(2,1)S(1)}, bf16[2,64,512]{2,1,0:T(8,128)(2,1)S(1)}, u32[]{:S(2)}, u32[]{:S(2)}) collective-permute-start(bf16[2,64,512]{2,1,0:T(8,128)(2,1)S(1)} %get-tuple-element.68.refs_0_), channel_id=1, source_target_pairs={{0,16},{16,0},{1,17},{17,1},{2,18},{18,2},{3,19},{19,3},{4,20},{20... | collective-permute-start | bytes 393224 | tf_op jit(solution)/shard_map/ppermute | solution.py:31
  35.5 4.0 %shard_map.83 = (bf16[2,64,512]{2,1,0:T(8,128)(2,1)S(1)}, bf16[1024,2048]{1,0:T(8,128)(2,1)S(1)}, bf16[1024,2048]{1,0:T(8,128)(2,1)S(1)}) custom-call(s32[2]{0:T(128)S(1)} %pad_add_fusion.pos_ref, bf16[4,64,4096]{2,1,0:T(8,128)(2,1)S(1)} %get-tuple-element.62.normed_ref, bf16[4096,512]{1,0:T(8,128)(2,1)S(1)} %get-tuple-element.63.refs_0_, ...), custom_call_target="tpu_custom_call" | custom-call | flops 1073741824 | bytes 16777216 | tf_op jit(solution)/shard_map/pallas_call | solution.py:328
  39.5 0.9 %collective-permute-start.10 = (bf16[2,64,512]{2,1,0:T(8,128)(2,1)S(1)}, bf16[2,64,512]{2,1,0:T(8,128)(2,1)S(1)}, u32[]{:S(2)}, u32[]{:S(2)}) collective-permute-start(bf16[2,64,512]{2,1,0:T(8,128)(2,1)S(1)} %get-tuple-element.67.own_ref), channel_id=1, source_target_pairs={{0,16},{16,0},{1,17},{17,1},{2,18},{18,2},{3,19},{19,3},{4,20},{20... | collective-permute-start | bytes 393224 | tf_op jit(solution)/shard_map/ppermute | solution.py:31
  40.4 0.0 collective-permute-done.9.refs_1_
  40.4 2.8 %shard_map.84 = (bf16[128,2048]{1,0:T(8,128)(2,1)S(1)}, f32[128,2048]{1,0:T(8,128)S(1)}) custom-call(s32[2]{0:T(128)S(1)} %pad_add_fusion.pos_ref, bf16[2,64,512]{2,1,0:T(8,128)(2,1)S(1)} %get-tuple-element.67.own_ref, bf16[2,64,512]{2,1,0:T(8,128)(2,1)S(1)} %get-tuple-element.68.refs_0_, bf16[2,64,512]{2,1,0:T(8,128)(2,1)S(1)} %collective-permute-done.9.refs_1_, ...), custom_call_target="tpu_custom_call" | custom-call | flops 536870912 | bytes 8388608 | tf_op jit(solution)/shard_map/pallas_call | solution.py:328
  43.3 1.6 %collective-permute-done.10.refs_0_ = bf16[2,64,512]{2,1,0:T(8,128)(2,1)S(1)} collective-permute-done((bf16[2,64,512]{2,1,0:T(8,128)(2,1)S(1)}, bf16[2,64,512]{2,1,0:T(8,128)(2,1)S(1)}, u32[]{:S(2)}, u32[]{:S(2)}) %collective-permute-start.10) | collective-permute-done | bytes 131104 | tf_op jit(solution)/shard_map/ppermute | solution.py:31
  44.9 1.5 %shard_map.85 = (bf16[128,1280]{1,0:T(8,128)(2,1)S(1)}, bf16[128,1280]{1,0:T(8,128)(2,1)S(1)}) custom-call(s32[2]{0:T(128)S(1)} %pad_add_fusion.pos_ref, bf16[2,256,256]{2,1,0:T(8,128)(2,1)S(1)} %get-tuple-element.61.mix_ref, bf16[128,2048]{1,0:T(8,128)(2,1)S(1)} %get-tuple-element.73.done_ref, f32[128,2048]{1,0:T(8,128)S(1)} %get-tuple-element.74.part_ref, ...), custom_call_target="tpu_custom_call" | custom-call | flops 671088640 | bytes 5242880 | tf_op jit(solution)/shard_map/pallas_call | solution.py:328
  46.4 0.1 collective-permute-start.11
  46.5 1.3 %shard_map.89 = (bf16[128,768]{1,0:T(8,128)(2,1)S(1)}, bf16[128,768]{1,0:T(8,128)(2,1)S(1)}) custom-call(s32[2]{0:T(128)S(1)} %pad_add_fusion.pos_ref, bf16[2,256,256]{2,1,0:T(8,128)(2,1)S(1)} %get-tuple-element.84.mix_ref, bf16[128,2048]{1,0:T(8,128)(2,1)S(1)} %get-tuple-element.73.done_ref, f32[128,2048]{1,0:T(8,128)S(1)} %get-tuple-element.74.part_ref, ...), custom_call_target="tpu_custom_call" | custom-call | flops 402653184 | bytes 3145728 | tf_op jit(solution)/shard_map/pallas_call | solution.py:328
  47.7 0.6 collective-permute-start.16
  48.3 0.0 collective-permute-done.11.refs_1_
  48.3 0.1 shard_map.86
  48.4 1.6 %collective-permute-start.12 = (bf16[64,1280]{1,0:T(8,128)(2,1)S(1)}, bf16[64,1280]{1,0:T(8,128)(2,1)S(1)}, u32[]{:S(2)}, u32[]{:S(2)}) collective-permute-start(bf16[64,1280]{1,0:T(8,128)(2,1)S(1)} %get-tuple-element.78), channel_id=1, source_target_pairs={{0,2},{1,3},{2,0},{3,1},{4,6},{5,7},{6,4},{7,5},{8,10},{9,11},{10,... | collective-permute-start | bytes 491528 | tf_op jit(solution)/shard_map/ppermute | solution.py:31
  50.0 0.0 collective-permute-done.16.refs_1_
  50.0 0.6 collective-permute-start.17
  50.6 3.2 %collective-permute-start.18 = (bf16[32,768]{1,0:T(8,128)(2,1)S(1)}, bf16[32,768]{1,0:T(8,128)(2,1)S(1)}, u32[]{:S(2)}, u32[]{:S(2)}) collective-permute-start(bf16[32,768]{1,0:T(8,128)(2,1)S(1)} %get-tuple-element.89), channel_id=1, source_target_pairs={{0,8},{1,9},{2,10},{3,11},{4,12},{5,13},{6,14},{7,15},{8,0},{9,1},... | collective-permute-start | bytes 147464 | tf_op jit(solution)/shard_map/ppermute | solution.py:31
  53.8 0.7 %collective-permute-start.19 = (bf16[32,768]{1,0:T(8,128)(2,1)S(1)}, bf16[32,768]{1,0:T(8,128)(2,1)S(1)}, u32[]{:S(2)}, u32[]{:S(2)}) collective-permute-start(bf16[32,768]{1,0:T(8,128)(2,1)S(1)} %get-tuple-element.90), channel_id=1, source_target_pairs={{0,12},{1,13},{2,14},{3,15},{4,8},{5,9},{6,10},{7,11},{8,4},{9,5},... | collective-permute-start | bytes 147464 | tf_op jit(solution)/shard_map/ppermute | solution.py:31
  54.5 0.1 collective-permute-done.12.refs_1_
  54.6 0.9 %collective-permute-start.13 = (bf16[16,1280]{1,0:T(8,128)(2,1)S(1)}, bf16[16,1280]{1,0:T(8,128)(2,1)S(1)}, u32[]{:S(2)}, u32[]{:S(2)}) collective-permute-start(bf16[16,1280]{1,0:T(8,128)(2,1)S(1)} %get-tuple-element.81), channel_id=1, source_target_pairs={{0,4},{1,5},{2,6},{3,7},{4,0},{5,1},{6,2},{7,3},{8,12},{9,13},{10,... | collective-permute-start | bytes 122888 | tf_op jit(solution)/shard_map/ppermute | solution.py:31
  55.5 3.1 %collective-permute-start.14 = (bf16[16,1280]{1,0:T(8,128)(2,1)S(1)}, bf16[16,1280]{1,0:T(8,128)(2,1)S(1)}, u32[]{:S(2)}, u32[]{:S(2)}) collective-permute-start(bf16[16,1280]{1,0:T(8,128)(2,1)S(1)} %get-tuple-element.82), channel_id=1, source_target_pairs={{0,8},{1,9},{2,10},{3,11},{4,12},{5,13},{6,14},{7,15},{8,0},{9,1},... | collective-permute-start | bytes 122888 | tf_op jit(solution)/shard_map/ppermute | solution.py:31
  58.7 0.0 collective-permute-done.17.refs_1_
  58.7 0.4 collective-permute-start.15
  59.1 0.0 collective-permute-done.18.refs_2_
  59.1 0.6 collective-permute-done.19.refs_3_
  59.8 1.4 %collective-permute-start.20 = (bf16[16,768]{1,0:T(8,128)(2,1)S(1)}, bf16[16,768]{1,0:T(8,128)(2,1)S(1)}, u32[]{:S(2)}, u32[]{:S(2)}) collective-permute-start(bf16[16,768]{1,0:T(8,128)(2,1)S(1)} %get-tuple-element.92), channel_id=1, source_target_pairs={{0,2},{1,3},{2,0},{3,1},{4,6},{5,7},{6,4},{7,5},{8,10},{9,11},{10,... | collective-permute-start | bytes 73736 | tf_op jit(solution)/shard_map/ppermute | solution.py:31
  61.1 0.6 shard_map.88.own_ref
  61.7 1.9 %collective-permute-done.20.refs_5_ = bf16[16,768]{1,0:T(8,128)(2,1)S(1)} collective-permute-done((bf16[16,768]{1,0:T(8,128)(2,1)S(1)}, bf16[16,768]{1,0:T(8,128)(2,1)S(1)}, u32[]{:S(2)}, u32[]{:S(2)}) %collective-permute-start.20) | collective-permute-done | bytes 24608 | tf_op jit(solution)/shard_map/ppermute | solution.py:31
  63.6 0.0 collective-permute-done.13.refs_1_
  63.6 0.0 collective-permute-done.14.refs_2_
  63.6 0.8 %collective-permute-done.15.refs_3_ = bf16[16,1280]{1,0:T(8,128)(2,1)S(1)} collective-permute-done((bf16[16,1280]{1,0:T(8,128)(2,1)S(1)}, bf16[16,1280]{1,0:T(8,128)(2,1)S(1)}, u32[]{:S(2)}, u32[]{:S(2)}) %collective-permute-start.15) | collective-permute-done | bytes 40992 | tf_op jit(solution)/shard_map/ppermute | solution.py:31
  64.5 1.2 %shard_map.92 = bf16[16,2048]{1,0:T(8,128)(2,1)} custom-call(s32[2]{0:T(128)S(1)} %pad_add_fusion.pos_ref, f32[16,2048]{1,0:T(8,128)S(1)} %shard_map.88.own_ref, bf16[16,1280]{1,0:T(8,128)(2,1)S(1)} %get-tuple-element.80.refs_0_, bf16[16,1280]{1,0:T(8,128)(2,1)S(1)} %collective-permute-done.13.refs_1_, bf16[16,1280]{1,0:T(8,128)(2,1)S(1)} %collective-permute-done.14.refs_2_, ...), custom_call_target="tpu_custom_call" | custom-call | bytes 524288 | tf_op jit(solution)/shard_map/pallas_call | solution.py:328
  (8 shorter events, 0.3 us)
Async XLA Ops:
  1.5 10.5 %collective-permute-start.2 = (bf16[8,4224]{1,0:T(8,128)(2,1)S(1)}, bf16[8,4224]{1,0:T(8,128)(2,1)S(1)}, u32[]{:S(2)}, u32[]{:S(2)}) collective-permute-start(bf16[8,4224]{1,0:T(8,128)(2,1)S(1)} %shard_map.73.refs_0_), channel_id=1, source_target_pairs={{0,12},{1,13},{2,14},{3,15},{4,8},{5,9},{6,10},{7,11},{8,4},{9,5},... | collective-permute-start | bytes 202760 | tf_op jit(solution)/shard_map/ppermute | solution.py:31
  6.6 5.8 %collective-permute-start.1 = (bf16[8,4224]{1,0:T(8,128)(2,1)S(1)}, bf16[8,4224]{1,0:T(8,128)(2,1)S(1)}, u32[]{:S(2)}, u32[]{:S(2)}) collective-permute-start(bf16[8,4224]{1,0:T(8,128)(2,1)S(1)} %shard_map.73.refs_0_), channel_id=1, source_target_pairs={{0,8},{1,9},{2,10},{3,11},{4,12},{5,13},{6,14},{7,15},{8,0},{9,1},... | collective-permute-start | bytes 202760 | tf_op jit(solution)/shard_map/ppermute | solution.py:31
  6.6 5.8 %collective-permute-start = (bf16[8,4224]{1,0:T(8,128)(2,1)S(1)}, bf16[8,4224]{1,0:T(8,128)(2,1)S(1)}, u32[]{:S(2)}, u32[]{:S(2)}) collective-permute-start(bf16[8,4224]{1,0:T(8,128)(2,1)S(1)} %shard_map.73.refs_0_), channel_id=1, source_target_pairs={{0,4},{1,5},{2,6},{3,7},{4,0},{5,1},{6,2},{7,3},{8,12},{9,13},{10,... | collective-permute-start | bytes 202760 | tf_op jit(solution)/shard_map/ppermute | solution.py:31
  12.4 5.3 %collective-permute-start.3 = (bf16[32,2176]{1,0:T(8,128)(2,1)S(1)}, bf16[32,2176]{1,0:T(8,128)(2,1)S(1)}, u32[]{:S(2)}, u32[]{:S(2)}) collective-permute-start(bf16[32,2176]{1,0:T(8,128)(2,1)S(1)} %get-tuple-element.50.refs_0_), channel_id=1, source_target_pairs={{0,2},{1,3},{2,0},{3,1},{4,6},{5,7},{6,4},{7,5},{8,10},{9,11},{10,... | collective-permute-start | bytes 417800 | tf_op jit(solution)/shard_map/ppermute | solution.py:31
  14.0 5.5 %collective-permute-start.5 = (bf16[32,2048]{1,0:T(8,128)(2,1)S(1)}, bf16[32,2048]{1,0:T(8,128)(2,1)S(1)}, u32[]{:S(2)}, u32[]{:S(2)}) collective-permute-start(bf16[32,2048]{1,0:T(8,128)(2,1)S(1)} %get-tuple-element.56.refs_0_), channel_id=1, source_target_pairs={{0,16},{16,0},{1,17},{17,1},{2,18},{18,2},{3,19},{19,3},{4,20},{20... | collective-permute-start | bytes 393224 | tf_op jit(solution)/shard_map/ppermute | solution.py:31
  17.8 8.1 %collective-permute-start.4 = (bf16[64,2176]{1,0:T(8,128)(2,1)S(1)}, bf16[64,2176]{1,0:T(8,128)(2,1)S(1)}, u32[]{:S(2)}, u32[]{:S(2)}) collective-permute-start(bf16[64,2176]{1,0:T(8,128)(2,1)S(1)} %get-tuple-element.53.refs_0_), channel_id=1, source_target_pairs={{0,16},{16,0},{1,17},{17,1},{2,18},{18,2},{3,19},{19,3},{4,20},{20... | collective-permute-start | bytes 835592 | tf_op jit(solution)/shard_map/ppermute | solution.py:31
  19.5 7.0 %collective-permute-start.6 = (bf16[64,2048]{1,0:T(8,128)(2,1)S(1)}, bf16[64,2048]{1,0:T(8,128)(2,1)S(1)}, u32[]{:S(2)}, u32[]{:S(2)}) collective-permute-start(bf16[64,2048]{1,0:T(8,128)(2,1)S(1)} %shard_map.80.refs_0_), channel_id=1, source_target_pairs={{0,2},{1,3},{2,0},{3,1},{4,6},{5,7},{6,4},{7,5},{8,10},{9,11},{10,... | collective-permute-start | bytes 786440 | tf_op jit(solution)/shard_map/ppermute | solution.py:31
  21.1 7.6 %copy-start = (bf16[4096]{0:T(1024)(128)(2,1)S(1)}, bf16[4096]{0:T(1024)(128)(2,1)}, u32[]{:S(2)}) copy-start(bf16[4096]{0:T(1024)(128)(2,1)} %param.8) | copy-start | bytes 24580
  25.9 2.8 %collective-permute-start.7 = (bf16[128,2176]{1,0:T(8,128)(2,1)S(1)}, bf16[128,2176]{1,0:T(8,128)(2,1)S(1)}, u32[]{:S(2)}, u32[]{:S(2)}) collective-permute-start(bf16[128,2176]{1,0:T(8,128)(2,1)S(1)} %shard_map.79.refs_0_.first_ref), channel_id=1, source_target_pairs={{0,1},{1,0},{2,3},{3,2},{4,5},{5,4},{6,7},{7,6},{8,9},{9,8},{10,11... | collective-permute-start | bytes 1671176 | tf_op jit(solution)/shard_map/ppermute | solution.py:31
  26.5 2.1 %collective-permute-start.8 = (bf16[128,2048]{1,0:T(8,128)(2,1)S(1)}, bf16[128,2048]{1,0:T(8,128)(2,1)S(1)}, u32[]{:S(2)}, u32[]{:S(2)}) collective-permute-start(bf16[128,2048]{1,0:T(8,128)(2,1)S(1)} %shard_map.81.refs_2_.second_ref), channel_id=1, source_target_pairs={{0,1},{1,0},{2,3},{3,2},{4,5},{5,4},{6,7},{7,6},{8,9},{9,8},{10,11... | collective-permute-start | bytes 1572872 | tf_op jit(solution)/shard_map/ppermute | solution.py:31
  34.3 6.2 %collective-permute-start.9 = (bf16[2,64,512]{2,1,0:T(8,128)(2,1)S(1)}, bf16[2,64,512]{2,1,0:T(8,128)(2,1)S(1)}, u32[]{:S(2)}, u32[]{:S(2)}) collective-permute-start(bf16[2,64,512]{2,1,0:T(8,128)(2,1)S(1)} %get-tuple-element.68.refs_0_), channel_id=1, source_target_pairs={{0,16},{16,0},{1,17},{17,1},{2,18},{18,2},{3,19},{19,3},{4,20},{20... | collective-permute-start | bytes 393224 | tf_op jit(solution)/shard_map/ppermute | solution.py:31
  39.5 5.3 %collective-permute-start.10 = (bf16[2,64,512]{2,1,0:T(8,128)(2,1)S(1)}, bf16[2,64,512]{2,1,0:T(8,128)(2,1)S(1)}, u32[]{:S(2)}, u32[]{:S(2)}) collective-permute-start(bf16[2,64,512]{2,1,0:T(8,128)(2,1)S(1)} %get-tuple-element.67.own_ref), channel_id=1, source_target_pairs={{0,16},{16,0},{1,17},{17,1},{2,18},{18,2},{3,19},{19,3},{4,20},{20... | collective-permute-start | bytes 393224 | tf_op jit(solution)/shard_map/ppermute | solution.py:31
  46.4 1.9 %collective-permute-start.11 = (bf16[128,1280]{1,0:T(8,128)(2,1)S(1)}, bf16[128,1280]{1,0:T(8,128)(2,1)S(1)}, u32[]{:S(2)}, u32[]{:S(2)}) collective-permute-start(bf16[128,1280]{1,0:T(8,128)(2,1)S(1)} %get-tuple-element.76), channel_id=1, source_target_pairs={{0,1},{1,0},{2,3},{3,2},{4,5},{5,4},{6,7},{7,6},{8,9},{9,8},{10,11... | collective-permute-start | bytes 983048 | tf_op jit(solution)/shard_map/ppermute | solution.py:31
  47.7 2.2 %collective-permute-start.16 = (bf16[128,768]{1,0:T(8,128)(2,1)S(1)}, bf16[128,768]{1,0:T(8,128)(2,1)S(1)}, u32[]{:S(2)}, u32[]{:S(2)}) collective-permute-start(bf16[128,768]{1,0:T(8,128)(2,1)S(1)} %get-tuple-element.86), channel_id=1, source_target_pairs={{0,1},{1,0},{2,3},{3,2},{4,5},{5,4},{6,7},{7,6},{8,9},{9,8},{10,11... | collective-permute-start | bytes 589832 | tf_op jit(solution)/shard_map/ppermute | solution.py:31
  48.4 6.2 %collective-permute-start.12 = (bf16[64,1280]{1,0:T(8,128)(2,1)S(1)}, bf16[64,1280]{1,0:T(8,128)(2,1)S(1)}, u32[]{:S(2)}, u32[]{:S(2)}) collective-permute-start(bf16[64,1280]{1,0:T(8,128)(2,1)S(1)} %get-tuple-element.78), channel_id=1, source_target_pairs={{0,2},{1,3},{2,0},{3,1},{4,6},{5,7},{6,4},{7,5},{8,10},{9,11},{10,... | collective-permute-start | bytes 491528 | tf_op jit(solution)/shard_map/ppermute | solution.py:31
  50.0 8.7 %collective-permute-start.17 = (bf16[32,768]{1,0:T(8,128)(2,1)S(1)}, bf16[32,768]{1,0:T(8,128)(2,1)S(1)}, u32[]{:S(2)}, u32[]{:S(2)}) collective-permute-start(bf16[32,768]{1,0:T(8,128)(2,1)S(1)} %get-tuple-element.88), channel_id=1, source_target_pairs={{0,4},{1,5},{2,6},{3,7},{4,0},{5,1},{6,2},{7,3},{8,12},{9,13},{10,... | collective-permute-start | bytes 147464 | tf_op jit(solution)/shard_map/ppermute | solution.py:31
  50.6 8.5 %collective-permute-start.18 = (bf16[32,768]{1,0:T(8,128)(2,1)S(1)}, bf16[32,768]{1,0:T(8,128)(2,1)S(1)}, u32[]{:S(2)}, u32[]{:S(2)}) collective-permute-start(bf16[32,768]{1,0:T(8,128)(2,1)S(1)} %get-tuple-element.89), channel_id=1, source_target_pairs={{0,8},{1,9},{2,10},{3,11},{4,12},{5,13},{6,14},{7,15},{8,0},{9,1},... | collective-permute-start | bytes 147464 | tf_op jit(solution)/shard_map/ppermute | solution.py:31
  53.8 6.0 %collective-permute-start.19 = (bf16[32,768]{1,0:T(8,128)(2,1)S(1)}, bf16[32,768]{1,0:T(8,128)(2,1)S(1)}, u32[]{:S(2)}, u32[]{:S(2)}) collective-permute-start(bf16[32,768]{1,0:T(8,128)(2,1)S(1)} %get-tuple-element.90), channel_id=1, source_target_pairs={{0,12},{1,13},{2,14},{3,15},{4,8},{5,9},{6,10},{7,11},{8,4},{9,5},... | collective-permute-start | bytes 147464 | tf_op jit(solution)/shard_map/ppermute | solution.py:31
  54.6 9.0 %collective-permute-start.13 = (bf16[16,1280]{1,0:T(8,128)(2,1)S(1)}, bf16[16,1280]{1,0:T(8,128)(2,1)S(1)}, u32[]{:S(2)}, u32[]{:S(2)}) collective-permute-start(bf16[16,1280]{1,0:T(8,128)(2,1)S(1)} %get-tuple-element.81), channel_id=1, source_target_pairs={{0,4},{1,5},{2,6},{3,7},{4,0},{5,1},{6,2},{7,3},{8,12},{9,13},{10,... | collective-permute-start | bytes 122888 | tf_op jit(solution)/shard_map/ppermute | solution.py:31
  55.5 8.1 %collective-permute-start.14 = (bf16[16,1280]{1,0:T(8,128)(2,1)S(1)}, bf16[16,1280]{1,0:T(8,128)(2,1)S(1)}, u32[]{:S(2)}, u32[]{:S(2)}) collective-permute-start(bf16[16,1280]{1,0:T(8,128)(2,1)S(1)} %get-tuple-element.82), channel_id=1, source_target_pairs={{0,8},{1,9},{2,10},{3,11},{4,12},{5,13},{6,14},{7,15},{8,0},{9,1},... | collective-permute-start | bytes 122888 | tf_op jit(solution)/shard_map/ppermute | solution.py:31
  58.7 5.8 %collective-permute-start.15 = (bf16[16,1280]{1,0:T(8,128)(2,1)S(1)}, bf16[16,1280]{1,0:T(8,128)(2,1)S(1)}, u32[]{:S(2)}, u32[]{:S(2)}) collective-permute-start(bf16[16,1280]{1,0:T(8,128)(2,1)S(1)} %get-tuple-element.83), channel_id=1, source_target_pairs={{0,12},{1,13},{2,14},{3,15},{4,8},{5,9},{6,10},{7,11},{8,4},{9,5},... | collective-permute-start | bytes 122888 | tf_op jit(solution)/shard_map/ppermute | solution.py:31
  59.8 3.9 %collective-permute-start.20 = (bf16[16,768]{1,0:T(8,128)(2,1)S(1)}, bf16[16,768]{1,0:T(8,128)(2,1)S(1)}, u32[]{:S(2)}, u32[]{:S(2)}) collective-permute-start(bf16[16,768]{1,0:T(8,128)(2,1)S(1)} %get-tuple-element.92), channel_id=1, source_target_pairs={{0,2},{1,3},{2,0},{3,1},{4,6},{5,7},{6,4},{7,5},{8,10},{9,11},{10,... | collective-permute-start | bytes 73736 | tf_op jit(solution)/shard_map/ppermute | solution.py:31
